TPU v7x, 32 devices: a whole 2x2x4 slice. The times are simulated.
32 devices in a mesh: blk: 8 (over z, x), span: 4 (over y, core).
Axes of the slice: x: 2, y: 2, z: 4, core: 2. Of those that a mesh axis runs over, the one named last changes fastest.
Arguments:
- fluid_adjoint_in: float32 [5, 64, 128, 128], P(None, 'blk', 'span'), may hold values from -4 to 4
- fluid_source: float32 [5, 64, 128, 128], P(None, 'blk', 'span'), may hold values from -24 to 24
- velocity: float32 [3, 64, 128, 128], P(None, 'blk', 'span'), may hold values from 0.1 to 1
- diffusion: float32 [5], replicated, may hold values from 0.5 to 2
- jacobian: float32 [5, 5], replicated, may hold values from -0.4 to 0.4
- wall_coefficient: float32 [8, 128, 128], P('blk', 'span'), may hold values from 0.5 to 2
- metal_costate_prior: float32 [128, 128, 128], P('blk', 'span'), may hold values from -4 to 4
- solid_source: float32 [128, 128, 128], P('blk', 'span'), may hold values from -12 to 12
- conductivity: float32 [128, 128, 128], P('blk', 'span'), may hold values from 0.3 to 3
- tile_owner: int32 [4, 256, 1], P('span', 'blk'), may hold values from 0 to 7; in each aligned block of 32 rows (0 to 31, 32 to 63, ..., all dimensions but the last counted through in order) at most 12 rows name the same one
- tile_target: int32 [4, 256], P('span', 'blk'), may hold values from 0 to 31
Outputs:
- fluid_adjoint: float32 [5, 64, 128, 128], P(None, 'blk', 'span')
- solid_adjoint: float32 [128, 128, 128], P('blk', 'span')
- residual_norms: float32 [6], replicated
Inputs may be any that keep to these rules, and one draw needn't show every extreme that they name: `tile_owner`: within the 32 wall tiles of one fluid block (the rows of one device), no owner is named more than 12 times, a bound that some block reaches; every owner is named by some tile.
All inputs are finite; a program needn't handle non-finite values.
Results may differ from a plain program's by a relative error of at most 0.004.
Values sent between devices are 32-bit elements; how exact they have to be, the bound alone decides.
No kernel may reach another device: no remote copies, remote signals or barrier semaphores. Data moves between devices by JAX's collectives and lax.ppermute only.
A program may use at most 64 MiB of HBM per device.

v0:
```python
import jax
import jax.numpy as jnp
from jax import lax
from jax.sharding import PartitionSpec as P

FSWEEPS = 4
SSWEEPS = 4


damping_weight = 0.8


def padded(block, sides, width):
    for axis, dim in sides:
        count = lax.axis_size(axis)
        forward = [(i, i + 1) for i in range(count - 1)]
        backward = [(target, source) for source, target in forward]
        low = lax.ppermute(
            lax.slice_in_dim(block, block.shape[dim] - width, None, axis=dim), axis, forward
        )
        high = lax.ppermute(lax.slice_in_dim(block, 0, width, axis=dim), axis, backward)
        block = jnp.concatenate([low, block, high], axis=dim)
    return block


def fluid_operator(bordered_grid_data, velocity, spread, jacobian):
    centre = bordered_grid_data[:, 1:-1, 1:-1, 1:-1]
    x_next = bordered_grid_data[:, 2:, 1:-1, 1:-1]
    y_next = bordered_grid_data[:, 1:-1, 2:, 1:-1]
    z_next = bordered_grid_data[:, 1:-1, 1:-1, 2:]
    beside_all = (
        x_next
        + bordered_grid_data[:, :-2, 1:-1, 1:-1]
        + y_next
        + bordered_grid_data[:, 1:-1, :-2, 1:-1]
        + z_next
        + bordered_grid_data[:, 1:-1, 1:-1, :-2]
    )
    mixing = jnp.einsum("fg,gxyz->fxyz", jacobian, centre, precision=lax.Precision.HIGHEST)
    velocity_sum = velocity[0] + velocity[1] + velocity[2]
    return (
        (6.0 * spread + velocity_sum) * centre
        - spread * beside_all
        - velocity[0] * x_next
        - velocity[1] * y_next
        - velocity[2] * z_next
        + mixing
    )


def face_conductance(kappa_rim):
    centre = kappa_rim[1:-1, 1:-1, 1:-1]
    return (
        0.5 * (centre + kappa_rim[2:, 1:-1, 1:-1]),
        0.5 * (centre + kappa_rim[:-2, 1:-1, 1:-1]),
        0.5 * (centre + kappa_rim[1:-1, 2:, 1:-1]),
        0.5 * (centre + kappa_rim[1:-1, :-2, 1:-1]),
        0.5 * (centre + kappa_rim[1:-1, 1:-1, 2:]),
        0.5 * (centre + kappa_rim[1:-1, 1:-1, :-2]),
    )


def solid_operator(bordered_grid_data, faces, diagonal):
    centre = bordered_grid_data[1:-1, 1:-1, 1:-1]
    flows = (
        faces[0] * bordered_grid_data[2:, 1:-1, 1:-1]
        + faces[1] * bordered_grid_data[:-2, 1:-1, 1:-1]
    )
    flows = (
        flows
        + faces[2] * bordered_grid_data[1:-1, 2:, 1:-1]
        + faces[3] * bordered_grid_data[1:-1, :-2, 1:-1]
    )
    flows = (
        flows
        + faces[4] * bordered_grid_data[1:-1, 1:-1, 2:]
        + faces[5] * bordered_grid_data[1:-1, 1:-1, :-2]
    )
    return diagonal * centre - flows


def pad_depth(array):
    widths = [(0, 0)] * (array.ndim - 1) + [(1, 1)]
    return jnp.pad(array, widths)


def shards(
    fluid_adjoint_in,
    fluid_source,
    velocity,
    diffusion,
    jacobian,
    wall_coefficient,
    metal_costate_prior,
    solid_source,
    conductivity,
    tile_owner,
    tile_target,
):
    highest = lax.Precision.HIGHEST
    spread = diffusion[:, None, None, None]
    fluid_diagonal = (
        6.0 * spread
        + (velocity[0] + velocity[1] + velocity[2])
        + jnp.diagonal(jacobian)[:, None, None, None]
    )
    adjoint = fluid_adjoint_in
    for iteration in range(FSWEEPS):
        bordered_grid_data = padded(adjoint, (("blk", 1), ("span", 2)), 1)
        bordered_grid_data = pad_depth(bordered_grid_data)
        fluid_residual = fluid_source - fluid_operator(
            bordered_grid_data, velocity, spread, jacobian
        )
        adjoint = adjoint + damping_weight * fluid_residual / fluid_diagonal
    fluid_squares = jnp.sum(fluid_residual * fluid_residual, axis=(1, 2, 3))
    wall_flux = wall_coefficient[0] * adjoint[4, 0]
    rows = wall_flux.shape[0]
    blocks = lax.axis_size("blk")
    myself = lax.axis_index("blk")
    owner_local = tile_owner[0, :, 0]
    target_local = tile_target[0, :]
    owners_all, targets_all = (
        lax.all_gather(owner_local, "blk", axis=0, tiled=True),
        lax.all_gather(target_local, "blk", axis=0, tiled=True),
    )
    owner_grid = owners_all.reshape(blocks, rows)
    target_grid = targets_all.reshape(blocks, rows)
    to_myself = owner_grid == myself
    target_hot = target_grid[:, :, None] == jnp.arange(rows, dtype=jnp.int32)[None, None, :]
    placing = (target_hot & to_myself[:, :, None]).astype(jnp.float32).reshape(blocks * rows, rows)
    arrived = lax.all_gather(wall_flux, "blk", axis=0, tiled=True)
    surface = jnp.dot(placing.T, arrived, precision=highest)
    heat_source = solid_source.at[-1].add(surface)
    thermal_state_grid = metal_costate_prior
    kappa_rim = padded(conductivity, (("blk", 0), ("span", 1)), 1)
    kappa_rim = pad_depth(kappa_rim)
    faces = face_conductance(kappa_rim)
    metal_pivot_entries = faces[0] + faces[1] + faces[2] + faces[3] + faces[4] + faces[5]
    for iteration in range(SSWEEPS):
        bordered_grid_data = padded(thermal_state_grid, (("blk", 0), ("span", 1)), 1)
        bordered_grid_data = pad_depth(bordered_grid_data)
        metal_imbalance_grid = heat_source - solid_operator(
            bordered_grid_data, faces, metal_pivot_entries
        )
        thermal_state_grid = (
            thermal_state_grid + damping_weight * metal_imbalance_grid / metal_pivot_entries
        )
    interface_heat_level = thermal_state_grid[-1]
    boundary_patches_finished = lax.all_gather(interface_heat_level, "blk", axis=0, tiled=True)
    output_entries = jnp.take(boundary_patches_finished, owner_local * rows + target_local, axis=0)
    gas_outcome = adjoint.at[4, 0].add(wall_coefficient[0] * output_entries)
    solid_squares = jnp.sum(metal_imbalance_grid * metal_imbalance_grid)[None]
    totals = lax.psum(jnp.concatenate([fluid_squares, solid_squares]), ("blk", "span"))
    every_processor = lax.axis_size("blk") * lax.axis_size("span")
    fluid_cells = float(adjoint.shape[1] * adjoint.shape[2] * adjoint.shape[3] * every_processor)
    solid_cells = float(
        thermal_state_grid.shape[0]
        * thermal_state_grid.shape[1]
        * thermal_state_grid.shape[2]
        * every_processor
    )
    counts = jnp.array([fluid_cells] * 5 + [solid_cells], jnp.float32)
    magnitude_list = jnp.sqrt(totals / counts)
    return (gas_outcome, thermal_state_grid, magnitude_list)


def solution(mesh):
    placed = (
        P(None, "blk", "span", None),
        P(None, "blk", "span", None),
        P(None, "blk", "span", None),
        P(),
        P(),
        P("blk", "span", None),
        P("blk", "span", None),
        P("blk", "span", None),
        P("blk", "span", None),
        P("span", "blk", None),
        P("span", "blk"),
    )
    return jax.shard_map(
        shards,
        mesh=mesh,
        in_specs=placed,
        out_specs=(P(None, "blk", "span", None), P("blk", "span", None), P()),
        check_vma=False,
    )
```

profile of v0, /device:TPU:0, one launch (start us, length us, event | category | flops | bytes accessed | tf_op | source)
XLA Modules:
  0.0 273.7 jit_solution(14079116844969162105)
XLA Ops:
  0.7 1.6 copy.36
  3.0 4.8 %collective-permute-start.1 = (f32[5,1,32,128]{3,0,2,1:T(8,128)}, f32[5,1,32,128]{3,0,2,1:T(8,128)S(1)}, u32[]{:S(2)}, u32[]{:S(2)}) collective-permute-start(f32[5,1,32,128]{3,0,2,1:T(8,128)} %get-tuple-element.59), channel_id=1, source_target_pairs={{0,4},{4,8},{8,12},{12,16},{16,20},{20,24},{24,28},{1,5},{5,9},{9,... | collective-permute-start | bytes 245768 | tf_op jit(solution)/shard_map/ppermute | solution.py:18
  7.9 1.3 collective-permute-start
  9.9 4.5 %collective-permute-start.17 = (f32[1,32,128]{2,1,0:T(8,128)S(1)}, f32[1,32,128]{2,1,0:T(8,128)S(1)}, u32[]{:S(2)}, u32[]{:S(2)}) collective-permute-start(f32[1,32,128]{2,1,0:T(8,128)S(1)} %get-tuple-element.80), channel_id=1, source_target_pairs={{0,4},{4,8},{8,12},{12,16},{16,20},{20,24},{24,28},{1,5},{5,9},{9,... | collective-permute-start | bytes 49160 | tf_op jit(solution)/shard_map/ppermute | solution.py:18
  14.5 1.3 collective-permute-start.16
  15.8 5.0 %collective-permute-start.21 = (f32[1,32,128]{2,1,0:T(8,128)S(1)}, f32[1,32,128]{2,1,0:T(8,128)S(1)}, u32[]{:S(2)}, u32[]{:S(2)}) collective-permute-start(f32[1,32,128]{2,1,0:T(8,128)S(1)} %get-tuple-element.83), channel_id=1, source_target_pairs={{0,4},{4,8},{8,12},{12,16},{16,20},{20,24},{24,28},{1,5},{5,9},{9,... | collective-permute-start | bytes 49160 | tf_op jit(solution)/shard_map/ppermute | solution.py:18
  22.4 11.5 %all-reduce.11 = (s32[256]{0:T(256)S(1)}, s32[256]{0:T(256)S(1)}) all-reduce(s32[256]{0:T(256)S(1)} %bitcast_dynamic-update-slice_fusion.1, s32[256]{0:T(256)S(1)} %bitcast_dynamic-update-slice_fusion), channel_id=2, replica_groups=mesh['blk'=8,'span'=4] {'blk'}, use_global_device_ids=true, to_apply=%add.9 | all-reduce | flops 512 | bytes 4096
  36.4 1.3 collective-permute-start.2
  37.7 3.0 %collective-permute-start.3 = (f32[5,10,1,128]{3,0,2,1:T(8,128)S(1)}, f32[5,10,1,128]{3,0,2,1:T(8,128)S(1)}, u32[]{:S(2)}, u32[]{:S(2)}) collective-permute-start(f32[5,10,1,128]{3,0,2,1:T(8,128)S(1)} %get-tuple-element.48), channel_id=1, source_target_pairs={{0,1},{1,2},{2,3},{4,5},{5,6},{6,7},{8,9},{9,10},{10,11},{12,13},{... | collective-permute-start | bytes 76808 | tf_op jit(solution)/shard_map/ppermute | solution.py:18
  40.8 1.3 collective-permute-start.18
  42.1 3.7 %collective-permute-start.19 = (f32[18,1,128]{2,1,0:T(1,128)S(1)}, f32[18,1,128]{2,1,0:T(1,128)S(1)}, u32[]{:S(2)}, u32[]{:S(2)}) collective-permute-start(f32[18,1,128]{2,1,0:T(1,128)S(1)} %get-tuple-element.70), channel_id=1, source_target_pairs={{0,1},{1,2},{2,3},{4,5},{5,6},{6,7},{8,9},{9,10},{10,11},{12,13},{... | collective-permute-start | bytes 27656 | tf_op jit(solution)/shard_map/ppermute | solution.py:18
  46.6 2.7 fusion.10
  49.3 1.3 collective-permute-start.4
  50.6 5.2 %collective-permute-start.5 = (f32[5,1,32,128]{3,0,2,1:T(8,128)S(1)}, f32[5,1,32,128]{3,0,2,1:T(8,128)S(1)}, u32[]{:S(2)}, u32[]{:S(2)}) collective-permute-start(f32[5,1,32,128]{3,0,2,1:T(8,128)S(1)} %get-tuple-element.56), channel_id=1, source_target_pairs={{0,4},{4,8},{8,12},{12,16},{16,20},{20,24},{24,28},{1,5},{5,9},{9,... | collective-permute-start | bytes 245768 | tf_op jit(solution)/shard_map/ppermute | solution.py:18
  55.8 1.3 collective-permute-done.4
  57.2 4.2 %collective-permute-done.5 = f32[5,1,32,128]{3,0,2,1:T(8,128)S(1)} collective-permute-done((f32[5,1,32,128]{3,0,2,1:T(8,128)S(1)}, f32[5,1,32,128]{3,0,2,1:T(8,128)S(1)}, u32[]{:S(2)}, u32[]{:S(2)}) %collective-permute-start.5) | collective-permute-done | bytes 81952 | tf_op jit(solution)/shard_map/ppermute | solution.py:18
  61.4 1.3 collective-permute-start.6
  62.7 3.0 %collective-permute-start.7 = (f32[5,10,1,128]{3,0,2,1:T(8,128)S(1)}, f32[5,10,1,128]{3,0,2,1:T(8,128)S(1)}, u32[]{:S(2)}, u32[]{:S(2)}) collective-permute-start(f32[5,10,1,128]{3,0,2,1:T(8,128)S(1)} %get-tuple-element.46), channel_id=1, source_target_pairs={{0,1},{1,2},{2,3},{4,5},{5,6},{6,7},{8,9},{9,10},{10,11},{12,13},{... | collective-permute-start | bytes 76808 | tf_op jit(solution)/shard_map/ppermute | solution.py:18
  67.4 2.2 fusion.11
  69.6 1.3 collective-permute-start.8
  70.9 5.0 %collective-permute-start.9 = (f32[5,1,32,128]{3,0,2,1:T(8,128)S(1)}, f32[5,1,32,128]{3,0,2,1:T(8,128)S(1)}, u32[]{:S(2)}, u32[]{:S(2)}) collective-permute-start(f32[5,1,32,128]{3,0,2,1:T(8,128)S(1)} %get-tuple-element.54), channel_id=1, source_target_pairs={{0,4},{4,8},{8,12},{12,16},{16,20},{20,24},{24,28},{1,5},{5,9},{9,... | collective-permute-start | bytes 245768 | tf_op jit(solution)/shard_map/ppermute | solution.py:18
  75.9 1.5 collective-permute-done.8
  77.4 4.1 %collective-permute-done.9 = f32[5,1,32,128]{3,0,2,1:T(8,128)S(1)} collective-permute-done((f32[5,1,32,128]{3,0,2,1:T(8,128)S(1)}, f32[5,1,32,128]{3,0,2,1:T(8,128)S(1)}, u32[]{:S(2)}, u32[]{:S(2)}) %collective-permute-start.9) | collective-permute-done | bytes 81952 | tf_op jit(solution)/shard_map/ppermute | solution.py:18
  81.5 1.3 collective-permute-start.10
  82.8 3.0 %collective-permute-start.11 = (f32[5,10,1,128]{3,0,2,1:T(8,128)S(1)}, f32[5,10,1,128]{3,0,2,1:T(8,128)S(1)}, u32[]{:S(2)}, u32[]{:S(2)}) collective-permute-start(f32[5,10,1,128]{3,0,2,1:T(8,128)S(1)} %get-tuple-element.44), channel_id=1, source_target_pairs={{0,1},{1,2},{2,3},{4,5},{5,6},{6,7},{8,9},{9,10},{10,11},{12,13},{... | collective-permute-start | bytes 76808 | tf_op jit(solution)/shard_map/ppermute | solution.py:18
  85.9 1.3 collective-permute-start.22
  87.2 4.2 %collective-permute-start.23 = (f32[18,1,128]{2,1,0:T(1,128)S(1)}, f32[18,1,128]{2,1,0:T(1,128)S(1)}, u32[]{:S(2)}, u32[]{:S(2)}) collective-permute-start(f32[18,1,128]{2,1,0:T(1,128)S(1)} %get-tuple-element.72), channel_id=1, source_target_pairs={{0,1},{1,2},{2,3},{4,5},{5,6},{6,7},{8,9},{9,10},{10,11},{12,13},{... | collective-permute-start | bytes 27656 | tf_op jit(solution)/shard_map/ppermute | solution.py:18
  92.2 2.2 fusion.12
  94.4 1.3 collective-permute-start.12
  95.7 4.9 %collective-permute-start.13 = (f32[5,1,32,128]{3,0,2,1:T(8,128)S(1)}, f32[5,1,32,128]{3,0,2,1:T(8,128)S(1)}, u32[]{:S(2)}, u32[]{:S(2)}) collective-permute-start(f32[5,1,32,128]{3,0,2,1:T(8,128)S(1)} %get-tuple-element.52), channel_id=1, source_target_pairs={{0,4},{4,8},{8,12},{12,16},{16,20},{20,24},{24,28},{1,5},{5,9},{9,... | collective-permute-start | bytes 245768 | tf_op jit(solution)/shard_map/ppermute | solution.py:18
  102.0 4.2 %collective-permute-done.13 = f32[5,1,32,128]{3,0,2,1:T(8,128)S(1)} collective-permute-done((f32[5,1,32,128]{3,0,2,1:T(8,128)S(1)}, f32[5,1,32,128]{3,0,2,1:T(8,128)S(1)}, u32[]{:S(2)}, u32[]{:S(2)}) %collective-permute-start.13) | collective-permute-done | bytes 81952 | tf_op jit(solution)/shard_map/ppermute | solution.py:18
  106.3 1.4 collective-permute-start.14
  107.7 3.0 %collective-permute-start.15 = (f32[5,10,1,128]{3,0,2,1:T(8,128)S(1)}, f32[5,10,1,128]{3,0,2,1:T(8,128)S(1)}, u32[]{:S(2)}, u32[]{:S(2)}) collective-permute-start(f32[5,10,1,128]{3,0,2,1:T(8,128)S(1)} %get-tuple-element.42), channel_id=1, source_target_pairs={{0,1},{1,2},{2,3},{4,5},{5,6},{6,7},{8,9},{9,10},{10,11},{12,13},{... | collective-permute-start | bytes 76808 | tf_op jit(solution)/shard_map/ppermute | solution.py:18
  112.4 2.5 multiply_reduce_fusion
  115.0 31.4 %all_gather.14 = f32[256,128]{1,0:T(8,128)S(1)} all-gather(f32[32,128]{1,0:T(8,128)S(1)} %bitcast_multiply_fusion), channel_id=1, replica_groups=mesh['blk'=8,'span'=4] {'blk'}, dimensions={0}, use_global_device_ids=true | all-gather | bytes 147456 | tf_op jit(solution)/shard_map/all_gather | solution.py:131
  147.4 1.3 collective-permute-start.24
  148.7 4.5 %collective-permute-start.25 = (f32[1,32,128]{2,1,0:T(8,128)S(1)}, f32[1,32,128]{2,1,0:T(8,128)S(1)}, u32[]{:S(2)}, u32[]{:S(2)}) collective-permute-start(f32[1,32,128]{2,1,0:T(8,128)S(1)} %get-tuple-element.78), channel_id=1, source_target_pairs={{0,4},{4,8},{8,12},{12,16},{16,20},{20,24},{24,28},{1,5},{5,9},{9,... | collective-permute-start | bytes 49160 | tf_op jit(solution)/shard_map/ppermute | solution.py:18
  153.2 1.4 collective-permute-done.25
  154.7 1.3 collective-permute-start.26
  156.0 3.0 %collective-permute-start.27 = (f32[18,1,128]{2,1,0:T(1,128)S(1)}, f32[18,1,128]{2,1,0:T(1,128)S(1)}, u32[]{:S(2)}, u32[]{:S(2)}) collective-permute-start(f32[18,1,128]{2,1,0:T(1,128)S(1)} %get-tuple-element.68), channel_id=1, source_target_pairs={{0,1},{1,2},{2,3},{4,5},{5,6},{6,7},{8,9},{9,10},{10,11},{12,13},{... | collective-permute-start | bytes 27656 | tf_op jit(solution)/shard_map/ppermute | solution.py:18
  161.8 4.9 %collective-permute-start.29 = (f32[1,32,128]{2,1,0:T(8,128)S(1)}, f32[1,32,128]{2,1,0:T(8,128)S(1)}, u32[]{:S(2)}, u32[]{:S(2)}) collective-permute-start(f32[1,32,128]{2,1,0:T(8,128)S(1)} %get-tuple-element.76), channel_id=1, source_target_pairs={{0,4},{4,8},{8,12},{12,16},{16,20},{20,24},{24,28},{1,5},{5,9},{9,... | collective-permute-start | bytes 49160 | tf_op jit(solution)/shard_map/ppermute | solution.py:18
  166.7 1.4 collective-permute-done.29
  169.4 5.4 %collective-permute-start.31 = (f32[18,1,128]{2,1,0:T(1,128)S(1)}, f32[18,1,128]{2,1,0:T(1,128)S(1)}, u32[]{:S(2)}, u32[]{:S(2)}) collective-permute-start(f32[18,1,128]{2,1,0:T(1,128)S(1)} %get-tuple-element.66), channel_id=1, source_target_pairs={{0,1},{1,2},{2,3},{4,5},{5,6},{6,7},{8,9},{9,10},{10,11},{12,13},{... | collective-permute-start | bytes 27656 | tf_op jit(solution)/shard_map/ppermute | solution.py:18
  177.7 5.4 %collective-permute-start.33 = (f32[1,32,128]{2,1,0:T(8,128)S(1)}, f32[1,32,128]{2,1,0:T(8,128)S(1)}, u32[]{:S(2)}, u32[]{:S(2)}) collective-permute-start(f32[1,32,128]{2,1,0:T(8,128)S(1)} %get-tuple-element.74), channel_id=1, source_target_pairs={{0,4},{4,8},{8,12},{12,16},{16,20},{20,24},{24,28},{1,5},{5,9},{9,... | collective-permute-start | bytes 49160 | tf_op jit(solution)/shard_map/ppermute | solution.py:18
  183.1 1.4 collective-permute-done.33
  185.9 4.8 %collective-permute-start.35 = (f32[18,1,128]{2,1,0:T(1,128)S(1)}, f32[18,1,128]{2,1,0:T(1,128)S(1)}, u32[]{:S(2)}, u32[]{:S(2)}) collective-permute-start(f32[18,1,128]{2,1,0:T(1,128)S(1)} %get-tuple-element.64), channel_id=1, source_target_pairs={{0,1},{1,2},{2,3},{4,5},{5,6},{6,7},{8,9},{9,10},{10,11},{12,13},{... | collective-permute-start | bytes 27656 | tf_op jit(solution)/shard_map/ppermute | solution.py:18
  193.6 47.1 %psum.7 = f32[6]{0:T(128)S(1)} all-reduce(f32[6]{0:T(128)S(1)} %pad_maximum_fusion.78), channel_id=1, replica_groups=mesh['blk'=8,'span'=4] {'blk','span'}, use_global_device_ids=true, to_apply=%region_2.3 | all-reduce | flops 6 | bytes 48 | tf_op jit(solution)/shard_map/psum | solution.py:153
  240.8 30.6 %all-gather.2 = f32[1,256,128]{2,1,0:T(8,128)S(1)} all-gather(f32[1,32,128]{2,1,0:T(8,128)S(1)} %slice.616), channel_id=4, replica_groups=mesh['blk'=8,'span'=4] {'blk'}, dimensions={1}, use_global_device_ids=true | all-gather | bytes 147456 | tf_op jit(solution)/shard_map/all_gather | solution.py:149
  (137 shorter events, 25.6 us)
Async XLA Ops:
  0.6 33.3 %copy-start = (f32[5,5]{1,0:T(8,128)S(1)}, f32[5,5]{1,0:T(8,128)}, u32[]{:S(2)}) copy-start(f32[5,5]{1,0:T(8,128)} %param.20) | copy-start | bytes 304
  0.6 20.3 %copy-start.19 = (u32[32]{0:T(128)S(1)}, u32[32]{0:T(128)}, u32[]{:S(2)}) copy-start(u32[32]{0:T(128)} %constant.140) | copy-start | bytes 388
  0.7 35.3 %copy-start.3 = (f32[5,8,32,128]{3,2,1,0:T(8,128)S(1)}, f32[5,8,32,128]{3,2,1,0:T(8,128)}, u32[]{:S(2)}) copy-start(f32[5,8,32,128]{3,2,1,0:T(8,128)} %param.16) | copy-start | bytes 1966084
  0.7 35.2 %copy-start.1 = (f32[16,32,128]{2,1,0:T(8,128)S(1)}, f32[16,32,128]{2,1,0:T(8,128)}, u32[]{:S(2)}) copy-start(f32[16,32,128]{2,1,0:T(8,128)} %param.24) | copy-start | bytes 786436
  0.7 21.5 %copy-start.17 = (s32[1,32,1]{1,2,0:T(1,128)S(1)}, s32[1,32,1]{1,2,0:T(1,128)}, u32[]{:S(2)}) copy-start(s32[1,32,1]{1,2,0:T(1,128)} %param.25) | copy-start | bytes 388
  0.7 21.6 %copy-start.16 = (s32[1,32]{1,0:T(1,128)S(1)}, s32[1,32]{1,0:T(1,128)}, u32[]{:S(2)}) copy-start(s32[1,32]{1,0:T(1,128)} %param.26) | copy-start | bytes 388
  3.0 32.9 %collective-permute-start.1 = (f32[5,1,32,128]{3,0,2,1:T(8,128)}, f32[5,1,32,128]{3,0,2,1:T(8,128)S(1)}, u32[]{:S(2)}, u32[]{:S(2)}) collective-permute-start(f32[5,1,32,128]{3,0,2,1:T(8,128)} %get-tuple-element.59), channel_id=1, source_target_pairs={{0,4},{4,8},{8,12},{12,16},{16,20},{20,24},{24,28},{1,5},{5,9},{9,... | collective-permute-start | bytes 245768 | tf_op jit(solution)/shard_map/ppermute | solution.py:18
  7.9 28.5 %collective-permute-start = (f32[5,1,32,128]{3,0,2,1:T(8,128)}, f32[5,1,32,128]{3,0,2,1:T(8,128)S(1)}, u32[]{:S(2)}, u32[]{:S(2)}) collective-permute-start(f32[5,1,32,128]{3,0,2,1:T(8,128)} %get-tuple-element.58), channel_id=1, source_target_pairs={{4,0},{8,4},{12,8},{16,12},{20,16},{24,20},{28,24},{5,1},{9,5},{13... | collective-permute-start | bytes 245768 | tf_op jit(solution)/shard_map/ppermute | solution.py:21
  9.9 24.6 %collective-permute-start.17 = (f32[1,32,128]{2,1,0:T(8,128)S(1)}, f32[1,32,128]{2,1,0:T(8,128)S(1)}, u32[]{:S(2)}, u32[]{:S(2)}) collective-permute-start(f32[1,32,128]{2,1,0:T(8,128)S(1)} %get-tuple-element.80), channel_id=1, source_target_pairs={{0,4},{4,8},{8,12},{12,16},{16,20},{20,24},{24,28},{1,5},{5,9},{9,... | collective-permute-start | bytes 49160 | tf_op jit(solution)/shard_map/ppermute | solution.py:18
  14.5 21.4 %collective-permute-start.16 = (f32[1,32,128]{2,1,0:T(8,128)S(1)}, f32[1,32,128]{2,1,0:T(8,128)S(1)}, u32[]{:S(2)}, u32[]{:S(2)}) collective-permute-start(f32[1,32,128]{2,1,0:T(8,128)S(1)} %get-tuple-element.81), channel_id=1, source_target_pairs={{4,0},{8,4},{12,8},{16,12},{20,16},{24,20},{28,24},{5,1},{9,5},{13... | collective-permute-start | bytes 49160 | tf_op jit(solution)/shard_map/ppermute | solution.py:21
  15.8 34.8 %collective-permute-start.21 = (f32[1,32,128]{2,1,0:T(8,128)S(1)}, f32[1,32,128]{2,1,0:T(8,128)S(1)}, u32[]{:S(2)}, u32[]{:S(2)}) collective-permute-start(f32[1,32,128]{2,1,0:T(8,128)S(1)} %get-tuple-element.83), channel_id=1, source_target_pairs={{0,4},{4,8},{8,12},{12,16},{16,20},{20,24},{24,28},{1,5},{5,9},{9,... | collective-permute-start | bytes 49160 | tf_op jit(solution)/shard_map/ppermute | solution.py:18
  20.9 71.3 %copy-start.7 = (f32[8,32,128]{2,1,0:T(8,128)}, f32[8,32,128]{2,1,0:T(8,128)S(1)}, u32[]{:S(2)}) copy-start(f32[8,32,128]{2,1,0:T(8,128)S(1)} %get-tuple-element.61) | copy-start | bytes 393220
  20.9 71.3 %copy-start.9 = (f32[8,32,128]{2,1,0:T(8,128)}, f32[8,32,128]{2,1,0:T(8,128)S(1)}, u32[]{:S(2)}) copy-start(f32[8,32,128]{2,1,0:T(8,128)S(1)} %get-tuple-element.62) | copy-start | bytes 393220
  20.9 71.3 %copy-start.11 = (f32[8,32,128]{2,1,0:T(8,128)}, f32[8,32,128]{2,1,0:T(8,128)S(1)}, u32[]{:S(2)}) copy-start(f32[8,32,128]{2,1,0:T(8,128)S(1)} %get-tuple-element.63) | copy-start | bytes 393220
  34.6 41.4 %collective-permute-start.20 = (f32[1,32,128]{2,1,0:T(8,128)S(1)}, f32[1,32,128]{2,1,0:T(8,128)S(1)}, u32[]{:S(2)}, u32[]{:S(2)}) collective-permute-start(f32[1,32,128]{2,1,0:T(8,128)S(1)} %get-tuple-element.82), channel_id=1, source_target_pairs={{4,0},{8,4},{12,8},{16,12},{20,16},{24,20},{28,24},{5,1},{9,5},{13... | collective-permute-start | bytes 49160 | tf_op jit(solution)/shard_map/ppermute | solution.py:21
  36.4 5.7 %collective-permute-start.2 = (f32[5,10,1,128]{3,0,2,1:T(8,128)S(1)}, f32[5,10,1,128]{3,0,2,1:T(8,128)S(1)}, u32[]{:S(2)}, u32[]{:S(2)}) collective-permute-start(f32[5,10,1,128]{3,0,2,1:T(8,128)S(1)} %get-tuple-element.49), channel_id=1, source_target_pairs={{1,0},{2,1},{3,2},{5,4},{6,5},{7,6},{9,8},{10,9},{11,10},{13,12},{... | collective-permute-start | bytes 76808 | tf_op jit(solution)/shard_map/ppermute | solution.py:21
  37.7 8.1 %collective-permute-start.3 = (f32[5,10,1,128]{3,0,2,1:T(8,128)S(1)}, f32[5,10,1,128]{3,0,2,1:T(8,128)S(1)}, u32[]{:S(2)}, u32[]{:S(2)}) collective-permute-start(f32[5,10,1,128]{3,0,2,1:T(8,128)S(1)} %get-tuple-element.48), channel_id=1, source_target_pairs={{0,1},{1,2},{2,3},{4,5},{5,6},{6,7},{8,9},{9,10},{10,11},{12,13},{... | collective-permute-start | bytes 76808 | tf_op jit(solution)/shard_map/ppermute | solution.py:18
  40.8 54.9 %collective-permute-start.18 = (f32[18,1,128]{2,1,0:T(1,128)S(1)}, f32[18,1,128]{2,1,0:T(1,128)S(1)}, u32[]{:S(2)}, u32[]{:S(2)}) collective-permute-start(f32[18,1,128]{2,1,0:T(1,128)S(1)} %get-tuple-element.71), channel_id=1, source_target_pairs={{1,0},{2,1},{3,2},{5,4},{6,5},{7,6},{9,8},{10,9},{11,10},{13,12},{... | collective-permute-start | bytes 27656 | tf_op jit(solution)/shard_map/ppermute | solution.py:21
  42.1 58.6 %collective-permute-start.19 = (f32[18,1,128]{2,1,0:T(1,128)S(1)}, f32[18,1,128]{2,1,0:T(1,128)S(1)}, u32[]{:S(2)}, u32[]{:S(2)}) collective-permute-start(f32[18,1,128]{2,1,0:T(1,128)S(1)} %get-tuple-element.70), channel_id=1, source_target_pairs={{0,1},{1,2},{2,3},{4,5},{5,6},{6,7},{8,9},{9,10},{10,11},{12,13},{... | collective-permute-start | bytes 27656 | tf_op jit(solution)/shard_map/ppermute | solution.py:18
  49.3 7.8 %collective-permute-start.4 = (f32[5,1,32,128]{3,0,2,1:T(8,128)S(1)}, f32[5,1,32,128]{3,0,2,1:T(8,128)S(1)}, u32[]{:S(2)}, u32[]{:S(2)}) collective-permute-start(f32[5,1,32,128]{3,0,2,1:T(8,128)S(1)} %get-tuple-element.57), channel_id=1, source_target_pairs={{4,0},{8,4},{12,8},{16,12},{20,16},{24,20},{28,24},{5,1},{9,5},{13... | collective-permute-start | bytes 245768 | tf_op jit(solution)/shard_map/ppermute | solution.py:21
  50.6 10.8 %collective-permute-start.5 = (f32[5,1,32,128]{3,0,2,1:T(8,128)S(1)}, f32[5,1,32,128]{3,0,2,1:T(8,128)S(1)}, u32[]{:S(2)}, u32[]{:S(2)}) collective-permute-start(f32[5,1,32,128]{3,0,2,1:T(8,128)S(1)} %get-tuple-element.56), channel_id=1, source_target_pairs={{0,4},{4,8},{8,12},{12,16},{16,20},{20,24},{24,28},{1,5},{5,9},{9,... | collective-permute-start | bytes 245768 | tf_op jit(solution)/shard_map/ppermute | solution.py:18
  61.4 4.4 %collective-permute-start.6 = (f32[5,10,1,128]{3,0,2,1:T(8,128)S(1)}, f32[5,10,1,128]{3,0,2,1:T(8,128)S(1)}, u32[]{:S(2)}, u32[]{:S(2)}) collective-permute-start(f32[5,10,1,128]{3,0,2,1:T(8,128)S(1)} %get-tuple-element.47), channel_id=1, source_target_pairs={{1,0},{2,1},{3,2},{5,4},{6,5},{7,6},{9,8},{10,9},{11,10},{13,12},{... | collective-permute-start | bytes 76808 | tf_op jit(solution)/shard_map/ppermute | solution.py:21
  62.7 3.9 %collective-permute-start.7 = (f32[5,10,1,128]{3,0,2,1:T(8,128)S(1)}, f32[5,10,1,128]{3,0,2,1:T(8,128)S(1)}, u32[]{:S(2)}, u32[]{:S(2)}) collective-permute-start(f32[5,10,1,128]{3,0,2,1:T(8,128)S(1)} %get-tuple-element.46), channel_id=1, source_target_pairs={{0,1},{1,2},{2,3},{4,5},{5,6},{6,7},{8,9},{9,10},{10,11},{12,13},{... | collective-permute-start | bytes 76808 | tf_op jit(solution)/shard_map/ppermute | solution.py:18
  69.6 7.9 %collective-permute-start.8 = (f32[5,1,32,128]{3,0,2,1:T(8,128)S(1)}, f32[5,1,32,128]{3,0,2,1:T(8,128)S(1)}, u32[]{:S(2)}, u32[]{:S(2)}) collective-permute-start(f32[5,1,32,128]{3,0,2,1:T(8,128)S(1)} %get-tuple-element.55), channel_id=1, source_target_pairs={{4,0},{8,4},{12,8},{16,12},{20,16},{24,20},{28,24},{5,1},{9,5},{13... | collective-permute-start | bytes 245768 | tf_op jit(solution)/shard_map/ppermute | solution.py:21
  70.9 10.6 %collective-permute-start.9 = (f32[5,1,32,128]{3,0,2,1:T(8,128)S(1)}, f32[5,1,32,128]{3,0,2,1:T(8,128)S(1)}, u32[]{:S(2)}, u32[]{:S(2)}) collective-permute-start(f32[5,1,32,128]{3,0,2,1:T(8,128)S(1)} %get-tuple-element.54), channel_id=1, source_target_pairs={{0,4},{4,8},{8,12},{12,16},{16,20},{20,24},{24,28},{1,5},{5,9},{9,... | collective-permute-start | bytes 245768 | tf_op jit(solution)/shard_map/ppermute | solution.py:18
  81.5 5.7 %collective-permute-start.10 = (f32[5,10,1,128]{3,0,2,1:T(8,128)S(1)}, f32[5,10,1,128]{3,0,2,1:T(8,128)S(1)}, u32[]{:S(2)}, u32[]{:S(2)}) collective-permute-start(f32[5,10,1,128]{3,0,2,1:T(8,128)S(1)} %get-tuple-element.45), channel_id=1, source_target_pairs={{1,0},{2,1},{3,2},{5,4},{6,5},{7,6},{9,8},{10,9},{11,10},{13,12},{... | collective-permute-start | bytes 76808 | tf_op jit(solution)/shard_map/ppermute | solution.py:21
  82.8 8.6 %collective-permute-start.11 = (f32[5,10,1,128]{3,0,2,1:T(8,128)S(1)}, f32[5,10,1,128]{3,0,2,1:T(8,128)S(1)}, u32[]{:S(2)}, u32[]{:S(2)}) collective-permute-start(f32[5,10,1,128]{3,0,2,1:T(8,128)S(1)} %get-tuple-element.44), channel_id=1, source_target_pairs={{0,1},{1,2},{2,3},{4,5},{5,6},{6,7},{8,9},{9,10},{10,11},{12,13},{... | collective-permute-start | bytes 76808 | tf_op jit(solution)/shard_map/ppermute | solution.py:18
  85.9 24.9 %collective-permute-start.22 = (f32[18,1,128]{2,1,0:T(1,128)S(1)}, f32[18,1,128]{2,1,0:T(1,128)S(1)}, u32[]{:S(2)}, u32[]{:S(2)}) collective-permute-start(f32[18,1,128]{2,1,0:T(1,128)S(1)} %get-tuple-element.73), channel_id=1, source_target_pairs={{1,0},{2,1},{3,2},{5,4},{6,5},{7,6},{9,8},{10,9},{11,10},{13,12},{... | collective-permute-start | bytes 27656 | tf_op jit(solution)/shard_map/ppermute | solution.py:21
  87.2 23.6 %collective-permute-start.23 = (f32[18,1,128]{2,1,0:T(1,128)S(1)}, f32[18,1,128]{2,1,0:T(1,128)S(1)}, u32[]{:S(2)}, u32[]{:S(2)}) collective-permute-start(f32[18,1,128]{2,1,0:T(1,128)S(1)} %get-tuple-element.72), channel_id=1, source_target_pairs={{0,1},{1,2},{2,3},{4,5},{5,6},{6,7},{8,9},{9,10},{10,11},{12,13},{... | collective-permute-start | bytes 27656 | tf_op jit(solution)/shard_map/ppermute | solution.py:18
  94.4 7.6 %collective-permute-start.12 = (f32[5,1,32,128]{3,0,2,1:T(8,128)S(1)}, f32[5,1,32,128]{3,0,2,1:T(8,128)S(1)}, u32[]{:S(2)}, u32[]{:S(2)}) collective-permute-start(f32[5,1,32,128]{3,0,2,1:T(8,128)S(1)} %get-tuple-element.53), channel_id=1, source_target_pairs={{4,0},{8,4},{12,8},{16,12},{20,16},{24,20},{28,24},{5,1},{9,5},{13... | collective-permute-start | bytes 245768 | tf_op jit(solution)/shard_map/ppermute | solution.py:21
  95.7 10.5 %collective-permute-start.13 = (f32[5,1,32,128]{3,0,2,1:T(8,128)S(1)}, f32[5,1,32,128]{3,0,2,1:T(8,128)S(1)}, u32[]{:S(2)}, u32[]{:S(2)}) collective-permute-start(f32[5,1,32,128]{3,0,2,1:T(8,128)S(1)} %get-tuple-element.52), channel_id=1, source_target_pairs={{0,4},{4,8},{8,12},{12,16},{16,20},{20,24},{24,28},{1,5},{5,9},{9,... | collective-permute-start | bytes 245768 | tf_op jit(solution)/shard_map/ppermute | solution.py:18
  106.3 4.8 %collective-permute-start.14 = (f32[5,10,1,128]{3,0,2,1:T(8,128)S(1)}, f32[5,10,1,128]{3,0,2,1:T(8,128)S(1)}, u32[]{:S(2)}, u32[]{:S(2)}) collective-permute-start(f32[5,10,1,128]{3,0,2,1:T(8,128)S(1)} %get-tuple-element.43), channel_id=1, source_target_pairs={{1,0},{2,1},{3,2},{5,4},{6,5},{7,6},{9,8},{10,9},{11,10},{13,12},{... | collective-permute-start | bytes 76808 | tf_op jit(solution)/shard_map/ppermute | solution.py:21
  107.7 3.9 %collective-permute-start.15 = (f32[5,10,1,128]{3,0,2,1:T(8,128)S(1)}, f32[5,10,1,128]{3,0,2,1:T(8,128)S(1)}, u32[]{:S(2)}, u32[]{:S(2)}) collective-permute-start(f32[5,10,1,128]{3,0,2,1:T(8,128)S(1)} %get-tuple-element.42), channel_id=1, source_target_pairs={{0,1},{1,2},{2,3},{4,5},{5,6},{6,7},{8,9},{9,10},{10,11},{12,13},{... | collective-permute-start | bytes 76808 | tf_op jit(solution)/shard_map/ppermute | solution.py:18
  112.4 34.0 %copy-start.2 = (f32[16,32,128]{2,1,0:T(8,128)S(1)}, f32[16,32,128]{2,1,0:T(8,128)}, u32[]{:S(2)}) copy-start(f32[16,32,128]{2,1,0:T(8,128)} %param.23) | copy-start | bytes 786436
  147.4 5.9 %collective-permute-start.24 = (f32[1,32,128]{2,1,0:T(8,128)S(1)}, f32[1,32,128]{2,1,0:T(8,128)S(1)}, u32[]{:S(2)}, u32[]{:S(2)}) collective-permute-start(f32[1,32,128]{2,1,0:T(8,128)S(1)} %get-tuple-element.79), channel_id=1, source_target_pairs={{4,0},{8,4},{12,8},{16,12},{20,16},{24,20},{28,24},{5,1},{9,5},{13... | collective-permute-start | bytes 49160 | tf_op jit(solution)/shard_map/ppermute | solution.py:21
  148.7 6.0 %collective-permute-start.25 = (f32[1,32,128]{2,1,0:T(8,128)S(1)}, f32[1,32,128]{2,1,0:T(8,128)S(1)}, u32[]{:S(2)}, u32[]{:S(2)}) collective-permute-start(f32[1,32,128]{2,1,0:T(8,128)S(1)} %get-tuple-element.78), channel_id=1, source_target_pairs={{0,4},{4,8},{8,12},{12,16},{16,20},{20,24},{24,28},{1,5},{5,9},{9,... | collective-permute-start | bytes 49160 | tf_op jit(solution)/shard_map/ppermute | solution.py:18
  154.7 4.3 %collective-permute-start.26 = (f32[18,1,128]{2,1,0:T(1,128)S(1)}, f32[18,1,128]{2,1,0:T(1,128)S(1)}, u32[]{:S(2)}, u32[]{:S(2)}) collective-permute-start(f32[18,1,128]{2,1,0:T(1,128)S(1)} %get-tuple-element.69), channel_id=1, source_target_pairs={{1,0},{2,1},{3,2},{5,4},{6,5},{7,6},{9,8},{10,9},{11,10},{13,12},{... | collective-permute-start | bytes 27656 | tf_op jit(solution)/shard_map/ppermute | solution.py:21
  156.0 3.9 %collective-permute-start.27 = (f32[18,1,128]{2,1,0:T(1,128)S(1)}, f32[18,1,128]{2,1,0:T(1,128)S(1)}, u32[]{:S(2)}, u32[]{:S(2)}) collective-permute-start(f32[18,1,128]{2,1,0:T(1,128)S(1)} %get-tuple-element.68), channel_id=1, source_target_pairs={{0,1},{1,2},{2,3},{4,5},{5,6},{6,7},{8,9},{9,10},{10,11},{12,13},{... | collective-permute-start | bytes 27656 | tf_op jit(solution)/shard_map/ppermute | solution.py:18
  160.5 6.2 %collective-permute-start.28 = (f32[1,32,128]{2,1,0:T(8,128)S(1)}, f32[1,32,128]{2,1,0:T(8,128)S(1)}, u32[]{:S(2)}, u32[]{:S(2)}) collective-permute-start(f32[1,32,128]{2,1,0:T(8,128)S(1)} %get-tuple-element.77), channel_id=1, source_target_pairs={{4,0},{8,4},{12,8},{16,12},{20,16},{24,20},{28,24},{5,1},{9,5},{13... | collective-permute-start | bytes 49160 | tf_op jit(solution)/shard_map/ppermute | solution.py:21
  161.8 6.3 %collective-permute-start.29 = (f32[1,32,128]{2,1,0:T(8,128)S(1)}, f32[1,32,128]{2,1,0:T(8,128)S(1)}, u32[]{:S(2)}, u32[]{:S(2)}) collective-permute-start(f32[1,32,128]{2,1,0:T(8,128)S(1)} %get-tuple-element.76), channel_id=1, source_target_pairs={{0,4},{4,8},{8,12},{12,16},{16,20},{20,24},{24,28},{1,5},{5,9},{9,... | collective-permute-start | bytes 49160 | tf_op jit(solution)/shard_map/ppermute | solution.py:18
  168.1 6.7 %collective-permute-start.30 = (f32[18,1,128]{2,1,0:T(1,128)S(1)}, f32[18,1,128]{2,1,0:T(1,128)S(1)}, u32[]{:S(2)}, u32[]{:S(2)}) collective-permute-start(f32[18,1,128]{2,1,0:T(1,128)S(1)} %get-tuple-element.67), channel_id=1, source_target_pairs={{1,0},{2,1},{3,2},{5,4},{6,5},{7,6},{9,8},{10,9},{11,10},{13,12},{... | collective-permute-start | bytes 27656 | tf_op jit(solution)/shard_map/ppermute | solution.py:21
  169.4 6.2 %collective-permute-start.31 = (f32[18,1,128]{2,1,0:T(1,128)S(1)}, f32[18,1,128]{2,1,0:T(1,128)S(1)}, u32[]{:S(2)}, u32[]{:S(2)}) collective-permute-start(f32[18,1,128]{2,1,0:T(1,128)S(1)} %get-tuple-element.66), channel_id=1, source_target_pairs={{0,1},{1,2},{2,3},{4,5},{5,6},{6,7},{8,9},{9,10},{10,11},{12,13},{... | collective-permute-start | bytes 27656 | tf_op jit(solution)/shard_map/ppermute | solution.py:18
  176.4 6.7 %collective-permute-start.32 = (f32[1,32,128]{2,1,0:T(8,128)S(1)}, f32[1,32,128]{2,1,0:T(8,128)S(1)}, u32[]{:S(2)}, u32[]{:S(2)}) collective-permute-start(f32[1,32,128]{2,1,0:T(8,128)S(1)} %get-tuple-element.75), channel_id=1, source_target_pairs={{4,0},{8,4},{12,8},{16,12},{20,16},{24,20},{28,24},{5,1},{9,5},{13... | collective-permute-start | bytes 49160 | tf_op jit(solution)/shard_map/ppermute | solution.py:21
  177.7 6.8 %collective-permute-start.33 = (f32[1,32,128]{2,1,0:T(8,128)S(1)}, f32[1,32,128]{2,1,0:T(8,128)S(1)}, u32[]{:S(2)}, u32[]{:S(2)}) collective-permute-start(f32[1,32,128]{2,1,0:T(8,128)S(1)} %get-tuple-element.74), channel_id=1, source_target_pairs={{0,4},{4,8},{8,12},{12,16},{16,20},{20,24},{24,28},{1,5},{5,9},{9,... | collective-permute-start | bytes 49160 | tf_op jit(solution)/shard_map/ppermute | solution.py:18
  184.6 6.2 %collective-permute-start.34 = (f32[18,1,128]{2,1,0:T(1,128)S(1)}, f32[18,1,128]{2,1,0:T(1,128)S(1)}, u32[]{:S(2)}, u32[]{:S(2)}) collective-permute-start(f32[18,1,128]{2,1,0:T(1,128)S(1)} %get-tuple-element.65), channel_id=1, source_target_pairs={{1,0},{2,1},{3,2},{5,4},{6,5},{7,6},{9,8},{10,9},{11,10},{13,12},{... | collective-permute-start | bytes 27656 | tf_op jit(solution)/shard_map/ppermute | solution.py:21
  185.9 5.7 %collective-permute-start.35 = (f32[18,1,128]{2,1,0:T(1,128)S(1)}, f32[18,1,128]{2,1,0:T(1,128)S(1)}, u32[]{:S(2)}, u32[]{:S(2)}) collective-permute-start(f32[18,1,128]{2,1,0:T(1,128)S(1)} %get-tuple-element.64), channel_id=1, source_target_pairs={{0,1},{1,2},{2,3},{4,5},{5,6},{6,7},{8,9},{9,10},{10,11},{12,13},{... | collective-permute-start | bytes 27656 | tf_op jit(solution)/shard_map/ppermute | solution.py:18
  192.8 80.4 %copy-start.18 = (f32[6]{0:T(128)S(1)}, f32[6]{0:T(128)}, u32[]{:S(2)}) copy-start(f32[6]{0:T(128)} %constant.124) | copy-start | bytes 76
  240.8 32.9 %copy-start.6 = (f32[16,32,128]{2,1,0:T(8,128)}, f32[16,32,128]{2,1,0:T(8,128)S(1)}, u32[]{:S(2)}) copy-start(f32[16,32,128]{2,1,0:T(8,128)S(1)} %divide_add_fusion) | copy-start | bytes 786436
  (8 other events, 87.0 us)
where the time goes:
time: 275 us; the launch traced here: 274 us
  blocking collectives  121 us (44%)
  starting transfers between devices  101 us (37%)
  waiting for transfers between devices  24.3 us (9%)
  matrix products  9.88 us (4%)
  other arithmetic  8.88 us (3%)
  local copies, waits for them, and re-layouts  6.8 us (2%)
    ppermute x18, starting transfers between devices, padded(): lax.ppermute(lax.slice_in_dim(block, block.shape[dim] - width, None, axis...  77.5 us
    psum x1, blocking collectives, shards(): lax.psum(jnp.concatenate([fluid_squares, solid_squares]), ('blk', 'span'))  47.1 us
    all_gather x1, blocking collectives, shards(): arrived = lax.all_gather(wall_flux, 'blk', axis=0, tiled=True)  31.4 us
    all_gather x1, blocking collectives, shards(): lax.all_gather(interface_heat_level, 'blk', axis=0, tiled=True)  30.6 us
    ppermute x18, starting transfers between devices, padded(): lax.ppermute(lax.slice_in_dim(block, 0, width, axis=dim), axis, backward)  23.4 us
    ppermute x18, waiting for transfers between devices, padded(): lax.ppermute(lax.slice_in_dim(block, block.shape[dim] - width, None, axis...  20.4 us
    unnamed x1, blocking collectives  11.5 us
    dot_general x4, matrix products, fluid_operator(): jnp.einsum('fg,gxyz->fxyz', jacobian, centre, precision=lax.Precision.HIG...  9.52 us
  transfers between devices with their start and end apart: 36, of which 14 were waited for; matrix products, arithmetic and copies ran while one was open for 5% of the time, Pallas kernels for 0%

commit v1 on v0

v1 whole, which is shorter than its diff:
```python
import functools

import jax
import jax.numpy as jnp
from jax import lax
from jax.experimental import pallas as pl
from jax.experimental.pallas import tpu as pltpu
from jax.sharding import PartitionSpec as P

SWEEPS = 4
DAMPING = 0.8
HIGHEST = lax.Precision.HIGHEST
F32 = jnp.float32
VMEM = pl.BlockSpec(memory_space=pltpu.VMEM)
SMEM = pl.BlockSpec(memory_space=pltpu.SMEM)
LIMIT = 40 * 1024 * 1024
G = 8
W = 4
GD = 12


def call(kernel, outs, scratch, specs, *args):
    return pl.pallas_call(
        kernel,
        out_shape=[jax.ShapeDtypeStruct(s, F32) for s in outs],
        in_specs=specs,
        out_specs=[VMEM] * len(outs),
        scratch_shapes=[pltpu.VMEM(s, F32) for s in scratch],
        compiler_params=pltpu.CompilerParams(vmem_limit_bytes=LIMIT),
    )(*args)


def beside(x):
    lane = lax.broadcasted_iota(jnp.int32, x.shape, 1)
    last = x.shape[1] - 1
    before = jnp.where(lane == 0, 0.0, pltpu.roll(x, 1, 1))
    after = jnp.where(lane == last, 0.0, pltpu.roll(x, last, 1))
    return before, after


def unless(flag, x):
    return jnp.where(flag, 0.0, x)


def pack_first_kernel(p, t, k, xf, xb, yf, yb):
    fields, depth, rows = p.shape[0], p.shape[1], p.shape[2]
    thick = t.shape[0]
    for f in range(fields):
        xf[f * rows : (f + 1) * rows] = p[f, depth - 1]
        xb[f * rows : (f + 1) * rows] = p[f, 0]
    for j, q in enumerate((t, k)):
        n = fields + j
        xf[n * rows : (n + 1) * rows] = q[thick - 1]
        xb[n * rows : (n + 1) * rows] = q[0]
    for f in range(fields):
        for i in range(depth):
            n = f * depth + i
            yf[n : n + 1] = p[f, i, rows - 1 :]
            yb[n : n + 1] = p[f, i, :1]
    base = fields * depth
    for i in range(thick):
        yf[base + i : base + i + 1] = t[i, rows - 1 :]
        yb[base + i : base + i + 1] = t[i, :1]
    base = base + thick
    for i in range(thick):
        yf[base + W * i : base + W * (i + 1)] = k[i, rows - W :]
        yb[base + W * i : base + W * (i + 1)] = k[i, :W]


def sweep_kernel(level, blocks, spans, *refs):
    first, last = level == 0, level == SWEEPS - 1
    names = ["spread", "jacobian", "p", "src", "vel", "t", "heat", "xl", "xr", "yl", "yr"]
    names += ["k"] if first else ["w", "he", "hx", "ws"]
    names += ["coef", "idx"] if last else []
    names += ["pn", "tn"]
    names += ["wo", "heo", "hxo", "wso"] if first else []
    names += ["rb", "sq", "parts"] if last else ["xf", "xb", "yf", "yb"]
    names += ["pe", "te", "hq"]
    r = dict(zip(names, refs, strict=True))
    p, src, vel, t, heat = r["p"], r["src"], r["vel"], r["t"], r["heat"]
    xl, xr, yl, yr = r["xl"], r["xr"], r["yl"], r["yr"]
    pe, te, hq = r["pe"], r["te"], r["hq"]
    pn, tn = r["pn"], r["tn"]
    fields, depth, rows = p.shape[0], p.shape[1], p.shape[2]
    thick = t.shape[0]
    b, s = lax.axis_index("blk"), lax.axis_index("span")
    no_left, no_right = b == 0, b == blocks - 1
    no_low, no_high = s == 0, s == spans - 1
    own = slice(G, G + rows)
    low = slice(G - 1, G - 1 + rows)
    high = slice(G + 1, G + 1 + rows)
    for f in range(fields):
        for i in range(depth):
            n = f * depth + i
            pe[f, i, own] = p[f, i]
            pe[f, i, G - 1 : G] = unless(no_low, yl[n : n + 1])
            pe[f, i, G + rows : G + rows + 1] = unless(no_high, yr[n : n + 1])
    d = [r["spread"][f] for f in range(fields)]
    jac = [[r["jacobian"][f, g] for g in range(fields)] for f in range(fields)]
    total = [None] * fields
    for i in range(depth):
        u0, u1, u2 = vel[0, i], vel[1, i], vel[2, i]
        us = u0 + u1 + u2
        centre = [pe[f, i, own] for f in range(fields)]
        for f in range(fields):
            side = slice(f * rows, (f + 1) * rows)
            diagonal = us + (6.0 * d[f] + jac[f][f])
            if first:
                w = DAMPING / diagonal
                r["wo"][f, i] = w
            else:
                w = r["w"][f, i]
            xm = pe[f, i - 1, own] if i > 0 else unless(no_left, xl[side])
            xp = pe[f, i + 1, own] if i < depth - 1 else unless(no_right, xr[side])
            ym, yp = pe[f, i, low], pe[f, i, high]
            zm, zp = beside(centre[f])
            res = src[f, i] - diagonal * centre[f]
            res = res + d[f] * ((xm + xp) + (ym + yp) + (zm + zp))
            res = res + u0 * xp + u1 * yp + u2 * zp
            for g in range(fields):
                if g != f:
                    res = res - jac[f][g] * centre[g]
            new = centre[f] + w * res
            pn[f, i] = new
            if last:
                square = res * res
                total[f] = square if total[f] is None else total[f] + square
            else:
                if i == depth - 1:
                    r["xf"][side] = new
                if i == 0:
                    r["xb"][side] = new
                n = f * depth + i
                r["yf"][n : n + 1] = new[rows - 1 :]
                r["yb"][n : n + 1] = new[:1]
    base = fields * depth
    side = slice(fields * rows, (fields + 1) * rows)
    tl, tr = unless(no_left, xl[side]), unless(no_right, xr[side])
    if first:
        he, hx = r["heo"], r["hxo"]
        side = slice((fields + 1) * rows, (fields + 2) * rows)
        hx[0] = unless(no_left, 0.5 * xl[side])
        hx[1] = unless(no_right, 0.5 * xr[side])
        he[...] = jnp.zeros_like(he)
        kbase = base + thick
        for i in range(thick):
            he[i, own] = 0.5 * r["k"][i]
            n = kbase + W * i
            he[i, G - W : G] = unless(no_low, 0.5 * yl[n : n + W])
            he[i, G + rows : G + rows + W] = unless(no_high, 0.5 * yr[n : n + W])
    else:
        he, hx = r["he"], r["hx"]
    for i in range(thick):
        te[i, own] = t[i]
        te[i, G - 1 : G] = unless(no_low, yl[base + i : base + i + 1])
        te[i, G + rows : G + rows + 1] = unless(no_high, yr[base + i : base + i + 1])
        hq[i] = he[i] * te[i]
    hl, hr = hx[0], hx[1]
    hql, hqr = hl * tl, hr * tr
    middle = None

    def around(buf, i, left, right):
        centre = buf[i, own]
        zm, zp = beside(centre)
        xm = buf[i - 1, own] if i > 0 else left
        xp = buf[i + 1, own] if i < thick - 1 else right
        return (xm + xp) + (buf[i, low] + buf[i, high]) + (zm + zp)

    kept = 0
    for i in range(thick):
        h, q = he[i, own], te[i, own]
        diagonal = 6.0 * h + around(he, i, hl, hr)
        if first:
            w = DAMPING / diagonal
            r["wso"][i] = w
        else:
            w = r["ws"][i]
        res = heat[i] - diagonal * q + h * around(te, i, tl, tr) + around(hq, i, hql, hqr)
        new = q + w * res
        tn[i] = new
        if last:
            if i < 3 or i >= thick - 4:
                r["rb"][kept] = res
                kept = kept + 1
            else:
                square = res * res
                middle = square if middle is None else middle + square
        else:
            if i == thick - 1:
                r["xf"][fields * rows : (fields + 1) * rows] = new
            if i == 0:
                r["xb"][fields * rows : (fields + 1) * rows] = new
            r["yf"][base + i : base + i + 1] = new[rows - 1 :]
            r["yb"][base + i : base + i + 1] = new[:1]
    if first:
        tall = rows + 2 * W
        n = (fields + 1) * rows
        for j in range(3):
            r["xf"][n + j * tall : n + (j + 1) * tall] = he[thick - 3 + j, G - W : G + rows + W]
        for j in range(2):
            r["xb"][n + j * tall : n + (j + 1) * tall] = he[j, G - W : G + rows + W]
    if last:
        sq, parts = r["sq"], r["parts"]
        sq[...] = jnp.zeros_like(sq)
        for f in range(fields):
            sq[f : f + 1] = jnp.sum(total[f], axis=0, keepdims=True)
        sq[fields : fields + 1] = jnp.sum(middle, axis=0, keepdims=True)
        flux = r["coef"][0] * pn[fields - 1, 0]
        n = lax.broadcasted_iota(jnp.int32, (blocks * 2 * rows, rows), 0)
        key = n // (2 * rows) * rows + n % (2 * rows) - rows
        hot = jnp.where(key == r["idx"][...], 1.0, 0.0)
        parts[...] = jnp.dot(hot, flux, precision=HIGHEST, preferred_element_type=F32)


def surface_kernel(blocks, arrived, surface, yf, yb):
    rows = surface.shape[0] // 2
    whole = arrived[0]
    for j in range(1, blocks):
        whole = whole + arrived[j]
    surface[...] = whole
    yf[:W] = whole[rows - W : rows]
    yf[W:] = whole[2 * rows - W :]
    yb[:W] = whole[:W]
    yb[W:] = whole[rows : rows + W]


def response_kernel(
    blocks, spans, surface, yl, yr, he, kl, kr, tb, rb, sqb, tn, out, hk, w, da, db, hd, so
):
    thick, rows = tb.shape[0], tb.shape[1]
    b, s = lax.axis_index("blk"), lax.axis_index("span")
    no_left, no_right = b == 0, b == blocks - 1
    no_low, no_high = s == 0, s == spans - 1
    tall = rows + 2 * W
    low_of = GD - W
    whole = slice(low_of, low_of + tall)
    below = slice(low_of - 1, low_of - 1 + tall)
    above = slice(low_of + 1, low_of + 1 + tall)
    own = slice(GD, GD + rows)
    ext = slice(G - W, G + rows + W)
    for buf in (hk, da, db, hd, so):
        buf[...] = jnp.zeros_like(buf)
    sq = sqb[...]
    gained = jnp.zeros((rows, tb.shape[2]), F32)
    for j in range(3):
        hk[0, j, whole] = unless(no_left, kl[j * tall : (j + 1) * tall])
    for j in range(4):
        hk[0, 3 + j, whole] = he[j, ext]
    for j in range(5):
        hk[1, j, whole] = he[thick - 5 + j, ext]
    for j in range(2):
        hk[1, 5 + j, whole] = unless(no_right, kr[j * tall : (j + 1) * tall])
    for region in range(2):
        edge = slice(region * W, (region + 1) * W)
        so[region, own] = surface[region * rows : (region + 1) * rows]
        so[region, GD - W : GD] = unless(no_low, yl[edge])
        so[region, GD + rows : GD + rows + W] = unless(no_high, yr[edge])

    def around(buf, region, j):
        centre = buf[region, j, whole]
        zm, zp = beside(centre)
        return (
            (buf[region, j - 1, whole] + buf[region, j + 1, whole])
            + (buf[region, j, below] + buf[region, j, above])
            + (zm + zp)
        )

    needed = (((2,), (1, 2, 3), (1, 2, 3, 4), (3, 4, 5)), ((4,), (3, 4, 5), (2, 3, 4, 5), (1, 2, 3, 4)))
    diagonals = {}
    for region in range(2):
        for j in range(1, 6):
            h = hk[region, j, whole]
            diagonal = 6.0 * h + around(hk, region, j)
            w[region, j, whole] = jnp.where(h > 0.0, DAMPING / jnp.where(h > 0.0, diagonal, 1.0), 0.0)
            diagonals[region, j] = diagonal
    for i in range(3, thick - 4):
        tn[i] = tb[i]
    for region in range(2):
        old, new = da, db
        at = 2 if region == 0 else 4
        for sweep in range(SWEEPS):
            final = sweep == SWEEPS - 1
            for j in needed[region][sweep]:
                res = so[region, whole] if j == at else None
                if sweep > 0:
                    q = old[region, j, whole]
                    flow = (
                        hk[region, j, whole] * around(old, region, j)
                        + around(hd, region, j)
                        - diagonals[region, j] * q
                    )
                    res = flow if res is None else res + flow
                    change = q + w[region, j, whole] * res
                else:
                    change = w[region, j, whole] * res
                if final:
                    i = j - 3 if region == 0 else thick - 5 + j
                    kept = i if region == 0 else 2 + j
                    mine = slice(W, W + rows)
                    tn[i] = tb[i] + change[mine]
                    full = rb[kept] + res[mine]
                    gained = gained + full * full
                else:
                    new[region, j, whole] = change
            if not final:
                for j in needed[region][sweep]:
                    hd[region, j, whole] = hk[region, j, whole] * new[region, j, whole]
                old, new = new, old
    extra = jnp.sum(gained, axis=0, keepdims=True)
    row = lax.broadcasted_iota(jnp.int32, sq.shape, 0)
    sq = sq + jnp.where(row == 5, extra, 0.0)
    for j in range(blocks):
        out[j, :rows] = tn[thick - 1]
        out[j, rows:] = sq


def return_kernel(blocks, arrived, column, coef, added, sq):
    rows = added.shape[0]
    lane = lax.broadcasted_iota(jnp.int32, (rows, rows), 1)
    taken, squares = None, None
    for j in range(blocks):
        hot = jnp.where(column[...] - j * rows == lane, 1.0, 0.0)
        got = jnp.dot(hot, arrived[j, :rows], precision=HIGHEST, preferred_element_type=F32)
        taken = got if taken is None else taken + got
        squares = arrived[j, rows:] if squares is None else squares + arrived[j, rows:]
    added[...] = coef[0] * taken
    sq[...] = squares


def shards(
    blocks,
    spans,
    fluid_adjoint_in,
    fluid_source,
    velocity,
    diffusion,
    jacobian,
    wall_coefficient,
    metal_costate_prior,
    solid_source,
    conductivity,
    tile_owner,
    tile_target,
):
    fields, depth, rows, z = fluid_adjoint_in.shape
    thick = metal_costate_prior.shape[0]
    tall = rows + 2 * W
    forward = {
        "blk": [(i, (i + 1) % blocks) for i in range(blocks)],
        "span": [(i, (i + 1) % spans) for i in range(spans)],
    }
    backward = {axis: [(j, i) for i, j in pairs] for axis, pairs in forward.items()}

    def exchange(xf, xb, yf, yb):
        return (
            lax.ppermute(xf, "blk", forward["blk"]),
            lax.ppermute(xb, "blk", backward["blk"]),
            lax.ppermute(yf, "span", forward["span"]),
            lax.ppermute(yb, "span", backward["span"]),
        )

    idx = tile_owner[0, :, 0] * rows + tile_target[0]
    row_idx, column_idx = idx[None, :], idx[:, None]
    xrows = (fields + 1) * rows
    yrows = fields * depth + thick
    p, t = fluid_adjoint_in, metal_costate_prior
    sends = call(
        pack_first_kernel,
        [(xrows + rows, z)] * 2 + [(yrows + W * thick, z)] * 2,
        [],
        [VMEM] * 3,
        p,
        t,
        conductivity,
    )
    scratch = [(fields, depth, rows + 2 * G, z), (thick, rows + 2 * G, z), (thick, rows + 2 * G, z)]
    for level in range(SWEEPS):
        first, last = level == 0, level == SWEEPS - 1
        halos = exchange(*sends)
        xl, xr, yl, yr = halos
        if level == 1:
            kl, kr = xl[xrows:], xr[xrows:]
        args = [diffusion, jacobian, p, fluid_source, velocity, t, solid_source, xl, xr, yl, yr]
        args += [conductivity] if first else list(held)
        args += [wall_coefficient, row_idx] if last else []
        outs = [p.shape, t.shape]
        if first:
            outs += [p.shape, (thick, rows + 2 * G, z), (2, rows, z), t.shape]
        if last:
            outs += [(7, rows, z), (8, z), (blocks * 2 * rows, z)]
        else:
            outs += [(xrows + (3 * tall if first else 0), z), (xrows + (2 * tall if first else 0), z)]
            outs += [(yrows, z)] * 2
        got = call(
            functools.partial(sweep_kernel, level, blocks, spans),
            outs,
            scratch,
            [SMEM] * 2 + [VMEM] * (len(args) - 2),
            *args,
        )
        p, t = got[:2]
        if first:
            held = got[2:6]
        if last:
            rb, sq, parts = got[2:]
        else:
            sends = got[-4:]
    arrived = lax.all_to_all(parts.reshape(blocks, 2 * rows, z), "blk", 0, 0)
    surface, yf, yb = call(
        functools.partial(surface_kernel, blocks),
        [(2 * rows, z), (2 * W, z), (2 * W, z)],
        [],
        [VMEM],
        arrived,
    )
    yl = lax.ppermute(yf, "span", forward["span"])
    yr = lax.ppermute(yb, "span", backward["span"])
    region = (2, 7, rows + 2 * GD, z)
    t, out = call(
        functools.partial(response_kernel, blocks, spans),
        [t.shape, (blocks, rows + 8, z)],
        [region] * 5 + [(2, rows + 2 * GD, z)],
        [VMEM] * 9,
        surface,
        yl,
        yr,
        held[1],
        kl,
        kr,
        t,
        rb,
        sq,
    )
    arrived = lax.all_to_all(out, "blk", 0, 0)
    added, sq = call(
        functools.partial(return_kernel, blocks),
        [(rows, z), (8, z)],
        [],
        [VMEM] * 3,
        arrived,
        column_idx,
        wall_coefficient,
    )
    step = 1
    while step < spans:
        sq = sq + lax.ppermute(sq, "span", [(i, i ^ step) for i in range(spans)])
        step = step * 2
    gas = p.at[fields - 1, 0].add(added)
    everyone = blocks * spans
    counts = [float(depth * rows * z * everyone)] * fields + [float(thick * rows * z * everyone)]
    totals = jnp.sum(sq[: fields + 1], axis=1)
    norms = jnp.sqrt(totals / jnp.array(counts, F32))
    return gas, t, norms


def solution(mesh):
    placed = (
        P(None, "blk", "span", None),
        P(None, "blk", "span", None),
        P(None, "blk", "span", None),
        P(),
        P(),
        P("blk", "span", None),
        P("blk", "span", None),
        P("blk", "span", None),
        P("blk", "span", None),
        P("span", "blk", None),
        P("span", "blk"),
    )
    return jax.shard_map(
        functools.partial(shards, mesh.shape["blk"], mesh.shape["span"]),
        mesh=mesh,
        in_specs=placed,
        out_specs=(P(None, "blk", "span", None), P("blk", "span", None), P()),
        check_vma=False,
    )
```

time: 275 us -> 88.7 us (0.32)
  blocking collectives: 121 us -> 14 us
  starting transfers between devices: 101 us -> 33 us
  Pallas kernels: 0 us -> 10.5 us
  matrix products: 9.88 us -> 0 us
  other arithmetic: 8.88 us -> 1.97 us
    ppermute x36 -> x20, starting transfers between devices: 101 us -> 29.6 us  [the longest x4 17.1 us: exchange(): lax.ppermute(xb, 'blk', backward['blk'])]
    all_gather x2 -> x0, blocking collectives: 62 us -> none  [the longest x1 31.4 us: shards(): arrived = lax.all_gather(wall_flux, 'blk', axis=0, tiled=True)]
    psum x1 -> x0, blocking collectives: 47.1 us -> none  [shards(): lax.psum(jnp.concatenate([fluid_squares, solid_squares]), ('blk', 'span'))]
    all_to_all x0 -> x1, blocking collectives: none -> 14 us  [shards(): arrived = lax.all_to_all(parts.reshape(blocks, 2 * rows, z), 'blk', 0, 0)]
    unnamed x1 -> x0, blocking collectives: 11.5 us -> none
    pallas_call x0 -> x8, Pallas kernels: none -> 10.5 us  [call(): pl.pallas_call(kernel, out_shape=[jax.ShapeDtypeStruct(s, F32) for s in o...]
    dot_general x5 -> x0, matrix products: 9.88 us -> none  [the longest x4 9.52 us: fluid_operator(): jnp.einsum('fg,gxyz->fxyz', jacobian, centre, precision=lax.Precision.HIG...]
    ppermute x36 -> x20, waiting for transfers between devices: 24.3 us -> 14.8 us  [the longest x4 5 us: exchange(): lax.ppermute(yf, 'span', forward['span'])]
  transfers between devices with their start and end apart: 36 -> 21, of which waited for: 14 -> 10; matrix products, arithmetic and copies ran while one was open for 5% -> 2% of each run, Pallas kernels for 0% -> 0%
where the time goes in v1:
time: 88.7 us; the launch traced here: 88.3 us
  starting transfers between devices  33 us (37%)
  waiting for transfers between devices  23.3 us (26%)
  blocking collectives  14 us (16%)
  Pallas kernels  10.5 us (12%)
  local copies, waits for them, and re-layouts  4.68 us (5%)
  other arithmetic  1.97 us (2%)
    ppermute x4, starting transfers between devices, exchange(): lax.ppermute(xb, 'blk', backward['blk'])  17.1 us
    all_to_all x1, blocking collectives, shards(): arrived = lax.all_to_all(parts.reshape(blocks, 2 * rows, z), 'blk', 0, 0)  14 us
    pallas_call x8, Pallas kernels, call(): pl.pallas_call(kernel, out_shape=[jax.ShapeDtypeStruct(s, F32) for s in o...  10.5 us
    all_to_all x1, waiting for transfers between devices, shards(): arrived = lax.all_to_all(out, 'blk', 0, 0)  8.49 us
    ppermute x4, starting transfers between devices, exchange(): lax.ppermute(yb, 'span', backward['span'])  5.5 us
    ppermute x4, waiting for transfers between devices, exchange(): lax.ppermute(yf, 'span', forward['span'])  5 us
    unnamed x26, local copies, waits for them, and re-layouts  4.58 us
    all_to_all x1, starting transfers between devices, shards(): arrived = lax.all_to_all(out, 'blk', 0, 0)  3.38 us
  transfers between devices with their start and end apart: 21, of which 10 were waited for; matrix products, arithmetic and copies ran while one was open for 2% of the time, Pallas kernels for 0%

profile of v1, /device:TPU:0, one launch (start us, length us, event | category | flops | bytes accessed | tf_op | source)
XLA Modules:
  0.0 88.3 jit_solution(9065523679525234282)
XLA Ops:
  0.7 1.2 %copy-done.4 = f32[5,8,32,128]{3,2,1,0:T(8,128)S(1)} copy-done((f32[5,8,32,128]{3,2,1,0:T(8,128)S(1)}, f32[5,8,32,128]{3,2,1,0:T(8,128)}, u32[]{:S(2)}) %copy-start.4) | copy-done | bytes 655384
  1.8 0.9 %copy-done.5 = f32[16,32,128]{2,1,0:T(8,128)S(1)} copy-done((f32[16,32,128]{2,1,0:T(8,128)S(1)}, f32[16,32,128]{2,1,0:T(8,128)}, u32[]{:S(2)}) %copy-start.5) | copy-done | bytes 262168
  2.8 0.9 %copy-done.6 = f32[16,32,128]{2,1,0:T(8,128)S(1)} copy-done((f32[16,32,128]{2,1,0:T(8,128)S(1)}, f32[16,32,128]{2,1,0:T(8,128)}, u32[]{:S(2)}) %copy-start.6) | copy-done | bytes 262168
  3.7 0.1 shard_map.139
  3.8 0.0 copy-start.8
  3.8 3.0 %collective-permute-start = (f32[224,128]{1,0:T(8,128)S(1)}, f32[224,128]{1,0:T(8,128)S(1)}, u32[]{:S(2)}, u32[]{:S(2)}) collective-permute-start(f32[224,128]{1,0:T(8,128)S(1)} %get-tuple-element.53), channel_id=1, source_target_pairs={{0,4},{4,8},{8,12},{12,16},{16,20},{20,24},{24,28},{28,0},{1,5},{5... | collective-permute-start | bytes 344072 | tf_op jit(solution)/shard_map/ppermute | solution.py:356
  6.8 3.1 %collective-permute-start.1 = (f32[224,128]{1,0:T(8,128)S(1)}, f32[224,128]{1,0:T(8,128)S(1)}, u32[]{:S(2)}, u32[]{:S(2)}) collective-permute-start(f32[224,128]{1,0:T(8,128)S(1)} %get-tuple-element.54), channel_id=1, source_target_pairs={{4,0},{8,4},{12,8},{16,12},{20,16},{24,20},{28,24},{0,28},{5,1},{9... | collective-permute-start | bytes 344072 | tf_op jit(solution)/shard_map/ppermute | solution.py:357
  9.9 1.7 %collective-permute-start.3 = (f32[120,128]{1,0:T(8,128)S(1)}, f32[120,128]{1,0:T(8,128)S(1)}, u32[]{:S(2)}, u32[]{:S(2)}) collective-permute-start(f32[120,128]{1,0:T(8,128)S(1)} %get-tuple-element.56), channel_id=1, source_target_pairs={{1,0},{2,1},{3,2},{0,3},{5,4},{6,5},{7,6},{4,7},{9,8},{10,9},{11,1... | collective-permute-start | bytes 184328 | tf_op jit(solution)/shard_map/ppermute | solution.py:359
  11.7 1.9 %collective-permute-done.2.refs_9_ = f32[120,128]{1,0:T(8,128)S(1)} collective-permute-done((f32[120,128]{1,0:T(8,128)S(1)}, f32[120,128]{1,0:T(8,128)S(1)}, u32[]{:S(2)}, u32[]{:S(2)}) %collective-permute-start.2) | collective-permute-done | bytes 61472 | tf_op jit(solution)/shard_map/ppermute | solution.py:358
  13.6 0.5 collective-permute-done.1.refs_8_
  14.1 0.9 %copy-done.2 = f32[16,32,128]{2,1,0:T(8,128)S(1)} copy-done((f32[16,32,128]{2,1,0:T(8,128)S(1)}, f32[16,32,128]{2,1,0:T(8,128)}, u32[]{:S(2)}) %copy-start.2) | copy-done | bytes 262168
  15.0 2.0 %shard_map.140 = (f32[5,8,32,128]{3,2,1,0:T(8,128)S(1)}, f32[16,32,128]{2,1,0:T(8,128)S(1)}, f32[5,8,32,128]{3,2,1,0:T(8,128)S(1)}, f32[16,48,128]{2,1,0:T(8,128...) custom-call(f32[5]{0:T(128)S(1)} %copy-done.9, ...), custom_call_target="tpu_custom_call" | custom-call | tf_op jit(solution)/shard_map/pallas_call | solution.py:23
  17.0 0.2 collective-permute-start.4
  17.2 4.6 %collective-permute-start.5 = (f32[272,128]{1,0:T(8,128)S(1)}, f32[272,128]{1,0:T(8,128)S(1)}, u32[]{:S(2)}, u32[]{:S(2)}) collective-permute-start(f32[272,128]{1,0:T(8,128)S(1)} %get-tuple-element.60), channel_id=1, source_target_pairs={{4,0},{8,4},{12,8},{16,12},{20,16},{24,20},{28,24},{0,28},{5,1},{9... | collective-permute-start | bytes 417800 | tf_op jit(solution)/shard_map/ppermute | solution.py:357
  21.8 0.7 collective-permute-start.6
  22.6 1.0 %collective-permute-start.7 = (f32[56,128]{1,0:T(8,128)S(1)}, f32[56,128]{1,0:T(8,128)S(1)}, u32[]{:S(2)}, u32[]{:S(2)}) collective-permute-start(f32[56,128]{1,0:T(8,128)S(1)} %get-tuple-element.62), channel_id=1, source_target_pairs={{1,0},{2,1},{3,2},{0,3},{5,4},{6,5},{7,6},{4,7},{9,8},{10,9},{11,1... | collective-permute-start | bytes 86024 | tf_op jit(solution)/shard_map/ppermute | solution.py:359
  23.6 1.5 %collective-permute-done.6.refs_9_ = f32[56,128]{1,0:T(8,128)S(1)} collective-permute-done((f32[56,128]{1,0:T(8,128)S(1)}, f32[56,128]{1,0:T(8,128)S(1)}, u32[]{:S(2)}, u32[]{:S(2)}) %collective-permute-start.6) | collective-permute-done | bytes 28704 | tf_op jit(solution)/shard_map/ppermute | solution.py:358
  25.1 0.0 collective-permute-done.7.refs_10_
  25.1 2.3 %collective-permute-done.5.refs_8_ = f32[272,128]{1,0:T(8,128)S(1)} collective-permute-done((f32[272,128]{1,0:T(8,128)S(1)}, f32[272,128]{1,0:T(8,128)S(1)}, u32[]{:S(2)}, u32[]{:S(2)}) %collective-permute-start.5) | collective-permute-done | bytes 139296 | tf_op jit(solution)/shard_map/ppermute | solution.py:357
  27.5 2.0 %shard_map.141 = (f32[5,8,32,128]{3,2,1,0:T(8,128)S(1)}, f32[16,32,128]{2,1,0:T(8,128)S(1)}, f32[192,128]{1,0:T(8,128)S(1)}, f32[192,128]{1,0:T(8,128)S(1)}, f32...) custom-call(f32[5]{0:T(128)S(1)} %copy-done.9, f32[5,5]{1,0:T(8,128)S(1)} %copy-done.8, ...), custom_call_target="tpu_custom_call" | custom-call | tf_op jit(solution)/shard_map/pallas_call | solution.py:23
  29.5 0.1 collective-permute-start.8
  29.5 4.7 %collective-permute-start.9 = (f32[192,128]{1,0:T(8,128)S(1)}, f32[192,128]{1,0:T(8,128)S(1)}, u32[]{:S(2)}, u32[]{:S(2)}) collective-permute-start(f32[192,128]{1,0:T(8,128)S(1)} %get-tuple-element.70), channel_id=1, source_target_pairs={{4,0},{8,4},{12,8},{16,12},{20,16},{24,20},{28,24},{0,28},{5,1},{9... | collective-permute-start | bytes 294920 | tf_op jit(solution)/shard_map/ppermute | solution.py:357
  34.2 1.7 %collective-permute-start.11 = (f32[56,128]{1,0:T(8,128)S(1)}, f32[56,128]{1,0:T(8,128)S(1)}, u32[]{:S(2)}, u32[]{:S(2)}) collective-permute-start(f32[56,128]{1,0:T(8,128)S(1)} %get-tuple-element.72), channel_id=1, source_target_pairs={{1,0},{2,1},{3,2},{0,3},{5,4},{6,5},{7,6},{4,7},{9,8},{10,9},{11,1... | collective-permute-start | bytes 86024 | tf_op jit(solution)/shard_map/ppermute | solution.py:359
  36.0 1.5 %collective-permute-done.10.refs_9_ = f32[56,128]{1,0:T(8,128)S(1)} collective-permute-done((f32[56,128]{1,0:T(8,128)S(1)}, f32[56,128]{1,0:T(8,128)S(1)}, u32[]{:S(2)}, u32[]{:S(2)}) %collective-permute-start.10) | collective-permute-done | bytes 28704 | tf_op jit(solution)/shard_map/ppermute | solution.py:358
  37.5 0.0 collective-permute-done.11.refs_10_
  37.6 2.0 %shard_map.142 = (f32[5,8,32,128]{3,2,1,0:T(8,128)S(1)}, f32[16,32,128]{2,1,0:T(8,128)S(1)}, f32[192,128]{1,0:T(8,128)S(1)}, f32[192,128]{1,0:T(8,128)S(1)}, f32...) custom-call(f32[5]{0:T(128)S(1)} %copy-done.9, f32[5,5]{1,0:T(8,128)S(1)} %copy-done.8, ...), custom_call_target="tpu_custom_call" | custom-call | tf_op jit(solution)/shard_map/pallas_call | solution.py:23
  39.6 0.9 collective-permute-start.14
  40.4 1.0 %collective-permute-start.15 = (f32[56,128]{1,0:T(8,128)S(1)}, f32[56,128]{1,0:T(8,128)S(1)}, u32[]{:S(2)}, u32[]{:S(2)}) collective-permute-start(f32[56,128]{1,0:T(8,128)S(1)} %get-tuple-element.78), channel_id=1, source_target_pairs={{1,0},{2,1},{3,2},{0,3},{5,4},{6,5},{7,6},{4,7},{9,8},{10,9},{11,1... | collective-permute-start | bytes 86024 | tf_op jit(solution)/shard_map/ppermute | solution.py:359
  41.4 4.7 %collective-permute-start.13 = (f32[192,128]{1,0:T(8,128)S(1)}, f32[192,128]{1,0:T(8,128)S(1)}, u32[]{:S(2)}, u32[]{:S(2)}) collective-permute-start(f32[192,128]{1,0:T(8,128)S(1)} %get-tuple-element.76), channel_id=1, source_target_pairs={{4,0},{8,4},{12,8},{16,12},{20,16},{24,20},{28,24},{0,28},{5,1},{9... | collective-permute-start | bytes 294920 | tf_op jit(solution)/shard_map/ppermute | solution.py:357
  46.2 2.6 %collective-permute-done.12.refs_7_ = f32[192,128]{1,0:T(8,128)S(1)} collective-permute-done((f32[192,128]{1,0:T(8,128)S(1)}, f32[192,128]{1,0:T(8,128)S(1)}, u32[]{:S(2)}, u32[]{:S(2)}) %collective-permute-start.12) | collective-permute-done | bytes 98336 | tf_op jit(solution)/shard_map/ppermute | solution.py:356
  48.7 2.5 %shard_map.143 = (f32[5,8,32,128]{3,2,1,0:T(8,128)}, f32[16,32,128]{2,1,0:T(8,128)S(1)}, f32[7,32,128]{2,1,0:T(8,128)S(1)}, f32[8,128]{1,0:T(8,128)S(1)}, f32[512,128]{1,0:T(8,128)S(1)}) custom-call(f32[5]{0:T(128)S(1)} %copy-done.9, f32[5,5]{1,0:T(8,128)S(1)} %copy-done.8, f32[5,8,32,128]{3,2,1,0:T(8,128)S(1)} %get-tuple-element.73.refs_2_, ...), custom_call_target="tpu_custom_call" | custom-call | tf_op jit(solution)/shard_map/pallas_call | solution.py:23
  51.3 14.0 %all_to_all.10.arrived = f32[8,64,128]{2,1,0:T(8,128)S(1)} all-to-all(f32[8,64,128]{2,1,0:T(8,128)S(1)} %bitcast.11), channel_id=1, replica_groups=mesh['blk'=8,'span'=4] {'blk'}, dimensions={0} | all-to-all | bytes 524288 | tf_op jit(solution)/shard_map/all_to_all | solution.py:408
  65.3 0.1 collective-permute-start.16
  65.4 1.7 %collective-permute-start.17 = (f32[8,128]{1,0:T(8,128)S(1)}, f32[8,128]{1,0:T(8,128)S(1)}, u32[]{:S(2)}, u32[]{:S(2)}) collective-permute-start(f32[8,128]{1,0:T(8,128)S(1)} %get-tuple-element.83), channel_id=1, source_target_pairs={{1,0},{2,1},{3,2},{0,3},{5,4},{6,5},{7,6},{4,7},{9,8},{10,9},{11,1... | collective-permute-start | bytes 12296 | tf_op jit(solution)/shard_map/ppermute | solution.py:417
  67.1 1.3 %collective-permute-done.16.yl = f32[8,128]{1,0:T(8,128)S(1)} collective-permute-done((f32[8,128]{1,0:T(8,128)S(1)}, f32[8,128]{1,0:T(8,128)S(1)}, u32[]{:S(2)}, u32[]{:S(2)}) %collective-permute-start.16) | collective-permute-done | bytes 4128 | tf_op jit(solution)/shard_map/ppermute | solution.py:416
  68.4 0.0 collective-permute-done.17.yr
  68.4 1.6 %shard_map.145 = (f32[16,32,128]{2,1,0:T(8,128)}, f32[8,40,128]{2,1,0:T(8,128)}) custom-call(f32[64,128]{1,0:T(8,128)S(1)} %get-tuple-element.81.surface, f32[8,128]{1,0:T(8,128)S(1)} %collective-permute-done.16.yl, f32[8,128]{1,0:T(8,128)S(1)} %collective-permute-done.17.yr, f32[16,48,128]{2,1,0:T(8,128)S(1)} %get-tuple-element.64.refs_12_.he, ...), custom_call_target="tpu_custom_call" | custom-call | tf_op jit(solution)/shard_map/pallas_call | solution.py:23
  70.0 3.4 %all-to-all-start.1 = ((f32[8,40,128]{2,1,0:T(8,128)}), f32[8,40,128]{2,1,0:T(8,128)S(1)}, u32[]{:S(2)}, u32[]{:S(2)}) async-start(f32[8,40,128]{2,1,0:T(8,128)} %get-tuple-element.87), calls=%async_computation.1 | async-start | bytes 327680 | tf_op jit(solution)/shard_map/all_to_all | solution.py:434
  73.4 0.1 copy.17.column
  73.5 8.5 %all-to-all-done.1.arrived = f32[8,40,128]{2,1,0:T(8,128)S(1)} async-done(((f32[8,40,128]{2,1,0:T(8,128)}), f32[8,40,128]{2,1,0:T(8,128)S(1)}, u32[]{:S(2)}, u32[]{:S(2)}) %all-to-all-start.1) | async-done | bytes 163872 | tf_op jit(solution)/shard_map/all_to_all | solution.py:434
  82.0 0.4 shard_map.146
  82.3 1.2 %collective-permute-done.18 = f32[8,128]{1,0:T(8,128)S(1)} collective-permute-done((f32[8,128]{1,0:T(8,128)S(1)}, f32[8,128]{1,0:T(8,128)S(1)}, u32[]{:S(2)}, u32[]{:S(2)}) %collective-permute-start.18) | collective-permute-done | bytes 4128 | tf_op jit(solution)/shard_map/ppermute | solution.py:446
  83.5 0.4 collective-permute-start.19
  83.9 1.3 %fusion = f32[5,8,32,128]{3,2,1,0:T(8,128)} fusion(f32[5,8,32,128]{3,2,1,0:T(8,128)} %get-tuple-element.79, f32[32,128]{1,0:T(8,128)S(1)} %get-tuple-element.88), kind=kLoop, calls=%fused_computation.1 | loop fusion | flops 4096 | bytes 49152 | tf_op jit(solution)/shard_map/scatter-add | solution.py:448
  85.2 1.9 %collective-permute-done.19 = f32[8,128]{1,0:T(8,128)S(1)} collective-permute-done((f32[8,128]{1,0:T(8,128)S(1)}, f32[8,128]{1,0:T(8,128)S(1)}, u32[]{:S(2)}, u32[]{:S(2)}) %collective-permute-start.19) | collective-permute-done | bytes 4128 | tf_op jit(solution)/shard_map/ppermute | solution.py:446
  87.1 0.1 slice_reduce_fusion
  87.2 0.5 copy-done.12
  87.8 0.5 multiply_sqrt_fusion
  (39 shorter events, 0.1 us)
Async XLA Ops:
  0.6 13.4 %copy-start.1 = (f32[3,8,32,128]{3,2,1,0:T(8,128)S(1)}, f32[3,8,32,128]{3,2,1,0:T(8,128)}, u32[]{:S(2)}) copy-start(f32[3,8,32,128]{3,2,1,0:T(8,128)} %refs_4_.7) | copy-start | bytes 1179652
  0.6 13.4 %copy-start = (f32[5,8,32,128]{3,2,1,0:T(8,128)S(1)}, f32[5,8,32,128]{3,2,1,0:T(8,128)}, u32[]{:S(2)}) copy-start(f32[5,8,32,128]{3,2,1,0:T(8,128)} %refs_3_.7) | copy-start | bytes 1966084
  0.7 1.2 %copy-start.4 = (f32[5,8,32,128]{3,2,1,0:T(8,128)S(1)}, f32[5,8,32,128]{3,2,1,0:T(8,128)}, u32[]{:S(2)}) copy-start(f32[5,8,32,128]{3,2,1,0:T(8,128)} %refs_2_.1) | copy-start | bytes 1966084
  1.8 0.9 %copy-start.5 = (f32[16,32,128]{2,1,0:T(8,128)S(1)}, f32[16,32,128]{2,1,0:T(8,128)}, u32[]{:S(2)}) copy-start(f32[16,32,128]{2,1,0:T(8,128)} %refs_5_.1) | copy-start | bytes 786436
  2.8 0.9 %copy-start.6 = (f32[16,32,128]{2,1,0:T(8,128)S(1)}, f32[16,32,128]{2,1,0:T(8,128)}, u32[]{:S(2)}) copy-start(f32[16,32,128]{2,1,0:T(8,128)} %refs_11_.1) | copy-start | bytes 786436
  3.8 10.3 %copy-start.8 = (f32[5,5]{1,0:T(8,128)S(1)}, f32[5,5]{1,0:T(8,128)}, u32[]{:S(2)}) copy-start(f32[5,5]{1,0:T(8,128)} %refs_1_.7) | copy-start | bytes 304
  3.8 9.8 %collective-permute-start = (f32[224,128]{1,0:T(8,128)S(1)}, f32[224,128]{1,0:T(8,128)S(1)}, u32[]{:S(2)}, u32[]{:S(2)}) collective-permute-start(f32[224,128]{1,0:T(8,128)S(1)} %get-tuple-element.53), channel_id=1, source_target_pairs={{0,4},{4,8},{8,12},{12,16},{16,20},{20,24},{24,28},{28,0},{1,5},{5... | collective-permute-start | bytes 344072 | tf_op jit(solution)/shard_map/ppermute | solution.py:356
  6.8 7.2 %collective-permute-start.1 = (f32[224,128]{1,0:T(8,128)S(1)}, f32[224,128]{1,0:T(8,128)S(1)}, u32[]{:S(2)}, u32[]{:S(2)}) collective-permute-start(f32[224,128]{1,0:T(8,128)S(1)} %get-tuple-element.54), channel_id=1, source_target_pairs={{4,0},{8,4},{12,8},{16,12},{20,16},{24,20},{28,24},{0,28},{5,1},{9... | collective-permute-start | bytes 344072 | tf_op jit(solution)/shard_map/ppermute | solution.py:357
  9.9 4.2 %copy-start.9 = (f32[5]{0:T(128)S(1)}, f32[5]{0:T(128)}, u32[]{:S(2)}) copy-start(f32[5]{0:T(128)} %refs_0_.7) | copy-start | bytes 64
  9.9 3.6 %collective-permute-start.2 = (f32[120,128]{1,0:T(8,128)S(1)}, f32[120,128]{1,0:T(8,128)S(1)}, u32[]{:S(2)}, u32[]{:S(2)}) collective-permute-start(f32[120,128]{1,0:T(8,128)S(1)} %get-tuple-element.55), channel_id=1, source_target_pairs={{0,1},{1,2},{2,3},{3,0},{4,5},{5,6},{6,7},{7,4},{8,9},{9,10},{10,1... | collective-permute-start | bytes 184328 | tf_op jit(solution)/shard_map/ppermute | solution.py:358
  9.9 3.6 %collective-permute-start.3 = (f32[120,128]{1,0:T(8,128)S(1)}, f32[120,128]{1,0:T(8,128)S(1)}, u32[]{:S(2)}, u32[]{:S(2)}) collective-permute-start(f32[120,128]{1,0:T(8,128)S(1)} %get-tuple-element.56), channel_id=1, source_target_pairs={{1,0},{2,1},{3,2},{0,3},{5,4},{6,5},{7,6},{4,7},{9,8},{10,9},{11,1... | collective-permute-start | bytes 184328 | tf_op jit(solution)/shard_map/ppermute | solution.py:359
  14.1 1.0 %copy-start.2 = (f32[16,32,128]{2,1,0:T(8,128)S(1)}, f32[16,32,128]{2,1,0:T(8,128)}, u32[]{:S(2)}) copy-start(f32[16,32,128]{2,1,0:T(8,128)} %refs_6_.7) | copy-start | bytes 786436
  15.0 12.4 %copy-start.3 = (f32[16,32,128]{2,1,0:T(8,128)S(1)}, f32[16,32,128]{2,1,0:T(8,128)}, u32[]{:S(2)}) copy-start(f32[16,32,128]{2,1,0:T(8,128)} %refs_6_.7) | copy-start | bytes 786436
  17.0 10.4 %collective-permute-start.4 = (f32[312,128]{1,0:T(8,128)S(1)}, f32[312,128]{1,0:T(8,128)S(1)}, u32[]{:S(2)}, u32[]{:S(2)}) collective-permute-start(f32[312,128]{1,0:T(8,128)S(1)} %get-tuple-element.59), channel_id=1, source_target_pairs={{0,4},{4,8},{8,12},{12,16},{16,20},{20,24},{24,28},{28,0},{1,5},{5... | collective-permute-start | bytes 479240 | tf_op jit(solution)/shard_map/ppermute | solution.py:356
  17.2 10.2 %collective-permute-start.5 = (f32[272,128]{1,0:T(8,128)S(1)}, f32[272,128]{1,0:T(8,128)S(1)}, u32[]{:S(2)}, u32[]{:S(2)}) collective-permute-start(f32[272,128]{1,0:T(8,128)S(1)} %get-tuple-element.60), channel_id=1, source_target_pairs={{4,0},{8,4},{12,8},{16,12},{20,16},{24,20},{28,24},{0,28},{5,1},{9... | collective-permute-start | bytes 417800 | tf_op jit(solution)/shard_map/ppermute | solution.py:357
  21.8 3.3 %collective-permute-start.6 = (f32[56,128]{1,0:T(8,128)S(1)}, f32[56,128]{1,0:T(8,128)S(1)}, u32[]{:S(2)}, u32[]{:S(2)}) collective-permute-start(f32[56,128]{1,0:T(8,128)S(1)} %get-tuple-element.61), channel_id=1, source_target_pairs={{0,1},{1,2},{2,3},{3,0},{4,5},{5,6},{6,7},{7,4},{8,9},{9,10},{10,1... | collective-permute-start | bytes 86024 | tf_op jit(solution)/shard_map/ppermute | solution.py:358
  22.6 2.6 %collective-permute-start.7 = (f32[56,128]{1,0:T(8,128)S(1)}, f32[56,128]{1,0:T(8,128)S(1)}, u32[]{:S(2)}, u32[]{:S(2)}) collective-permute-start(f32[56,128]{1,0:T(8,128)S(1)} %get-tuple-element.62), channel_id=1, source_target_pairs={{1,0},{2,1},{3,2},{0,3},{5,4},{6,5},{7,6},{4,7},{9,8},{10,9},{11,1... | collective-permute-start | bytes 86024 | tf_op jit(solution)/shard_map/ppermute | solution.py:359
  29.5 8.1 %collective-permute-start.8 = (f32[192,128]{1,0:T(8,128)S(1)}, f32[192,128]{1,0:T(8,128)S(1)}, u32[]{:S(2)}, u32[]{:S(2)}) collective-permute-start(f32[192,128]{1,0:T(8,128)S(1)} %get-tuple-element.69), channel_id=1, source_target_pairs={{0,4},{4,8},{8,12},{12,16},{16,20},{20,24},{24,28},{28,0},{1,5},{5... | collective-permute-start | bytes 294920 | tf_op jit(solution)/shard_map/ppermute | solution.py:356
  29.5 8.0 %collective-permute-start.9 = (f32[192,128]{1,0:T(8,128)S(1)}, f32[192,128]{1,0:T(8,128)S(1)}, u32[]{:S(2)}, u32[]{:S(2)}) collective-permute-start(f32[192,128]{1,0:T(8,128)S(1)} %get-tuple-element.70), channel_id=1, source_target_pairs={{4,0},{8,4},{12,8},{16,12},{20,16},{24,20},{28,24},{0,28},{5,1},{9... | collective-permute-start | bytes 294920 | tf_op jit(solution)/shard_map/ppermute | solution.py:357
  34.2 3.3 %collective-permute-start.10 = (f32[56,128]{1,0:T(8,128)S(1)}, f32[56,128]{1,0:T(8,128)S(1)}, u32[]{:S(2)}, u32[]{:S(2)}) collective-permute-start(f32[56,128]{1,0:T(8,128)S(1)} %get-tuple-element.71), channel_id=1, source_target_pairs={{0,1},{1,2},{2,3},{3,0},{4,5},{5,6},{6,7},{7,4},{8,9},{9,10},{10,1... | collective-permute-start | bytes 86024 | tf_op jit(solution)/shard_map/ppermute | solution.py:358
  34.2 3.3 %collective-permute-start.11 = (f32[56,128]{1,0:T(8,128)S(1)}, f32[56,128]{1,0:T(8,128)S(1)}, u32[]{:S(2)}, u32[]{:S(2)}) collective-permute-start(f32[56,128]{1,0:T(8,128)S(1)} %get-tuple-element.72), channel_id=1, source_target_pairs={{1,0},{2,1},{3,2},{0,3},{5,4},{6,5},{7,6},{4,7},{9,8},{10,9},{11,1... | collective-permute-start | bytes 86024 | tf_op jit(solution)/shard_map/ppermute | solution.py:359
  37.5 11.2 %copy-start.7 = (f32[1,32,128]{2,1,0:T(8,128)S(1)}, f32[1,32,128]{2,1,0:T(8,128)}, u32[]{:S(2)}) copy-start(f32[1,32,128]{2,1,0:T(8,128)} %coef.1) | copy-start | bytes 49156
  39.6 6.6 %collective-permute-start.14 = (f32[56,128]{1,0:T(8,128)S(1)}, f32[56,128]{1,0:T(8,128)S(1)}, u32[]{:S(2)}, u32[]{:S(2)}) collective-permute-start(f32[56,128]{1,0:T(8,128)S(1)} %get-tuple-element.77), channel_id=1, source_target_pairs={{0,1},{1,2},{2,3},{3,0},{4,5},{5,6},{6,7},{7,4},{8,9},{9,10},{10,1... | collective-permute-start | bytes 86024 | tf_op jit(solution)/shard_map/ppermute | solution.py:358
  40.4 5.7 %collective-permute-start.15 = (f32[56,128]{1,0:T(8,128)S(1)}, f32[56,128]{1,0:T(8,128)S(1)}, u32[]{:S(2)}, u32[]{:S(2)}) collective-permute-start(f32[56,128]{1,0:T(8,128)S(1)} %get-tuple-element.78), channel_id=1, source_target_pairs={{1,0},{2,1},{3,2},{0,3},{5,4},{6,5},{7,6},{4,7},{9,8},{10,9},{11,1... | collective-permute-start | bytes 86024 | tf_op jit(solution)/shard_map/ppermute | solution.py:359
  41.4 4.7 %copy-start.10 = (s32[1,32]{1,0:T(1,128)S(1)}, s32[1,32]{1,0:T(1,128)}, u32[]{:S(2)}) copy-start(s32[1,32]{1,0:T(1,128)} %param.24) | copy-start | bytes 388
  41.4 4.7 %copy-start.11 = (s32[1,32,1]{1,2,0:T(1,128)S(1)}, s32[1,32,1]{1,2,0:T(1,128)}, u32[]{:S(2)}) copy-start(s32[1,32,1]{1,2,0:T(1,128)} %param.23) | copy-start | bytes 388
  41.4 7.3 %collective-permute-start.12 = (f32[192,128]{1,0:T(8,128)S(1)}, f32[192,128]{1,0:T(8,128)S(1)}, u32[]{:S(2)}, u32[]{:S(2)}) collective-permute-start(f32[192,128]{1,0:T(8,128)S(1)} %get-tuple-element.75), channel_id=1, source_target_pairs={{0,4},{4,8},{8,12},{12,16},{16,20},{20,24},{24,28},{28,0},{1,5},{5... | collective-permute-start | bytes 294920 | tf_op jit(solution)/shard_map/ppermute | solution.py:356
  41.4 7.3 %collective-permute-start.13 = (f32[192,128]{1,0:T(8,128)S(1)}, f32[192,128]{1,0:T(8,128)S(1)}, u32[]{:S(2)}, u32[]{:S(2)}) collective-permute-start(f32[192,128]{1,0:T(8,128)S(1)} %get-tuple-element.76), channel_id=1, source_target_pairs={{4,0},{8,4},{12,8},{16,12},{20,16},{24,20},{28,24},{0,28},{5,1},{9... | collective-permute-start | bytes 294920 | tf_op jit(solution)/shard_map/ppermute | solution.py:357
  65.3 3.1 %collective-permute-start.16 = (f32[8,128]{1,0:T(8,128)S(1)}, f32[8,128]{1,0:T(8,128)S(1)}, u32[]{:S(2)}, u32[]{:S(2)}) collective-permute-start(f32[8,128]{1,0:T(8,128)S(1)} %get-tuple-element.82), channel_id=1, source_target_pairs={{0,1},{1,2},{2,3},{3,0},{4,5},{5,6},{6,7},{7,4},{8,9},{9,10},{10,1... | collective-permute-start | bytes 12296 | tf_op jit(solution)/shard_map/ppermute | solution.py:416
  65.4 3.1 %collective-permute-start.17 = (f32[8,128]{1,0:T(8,128)S(1)}, f32[8,128]{1,0:T(8,128)S(1)}, u32[]{:S(2)}, u32[]{:S(2)}) collective-permute-start(f32[8,128]{1,0:T(8,128)S(1)} %get-tuple-element.83), channel_id=1, source_target_pairs={{1,0},{2,1},{3,2},{0,3},{5,4},{6,5},{7,6},{4,7},{9,8},{10,9},{11,1... | collective-permute-start | bytes 12296 | tf_op jit(solution)/shard_map/ppermute | solution.py:417
  70.0 12.0 %all-to-all-start.1 = ((f32[8,40,128]{2,1,0:T(8,128)}), f32[8,40,128]{2,1,0:T(8,128)S(1)}, u32[]{:S(2)}, u32[]{:S(2)}) async-start(f32[8,40,128]{2,1,0:T(8,128)} %get-tuple-element.87), calls=%async_computation.1 | async-start | bytes 327680 | tf_op jit(solution)/shard_map/all_to_all | solution.py:434
  82.3 1.2 %collective-permute-start.18 = (f32[8,128]{1,0:T(8,128)S(1)}, f32[8,128]{1,0:T(8,128)S(1)}, u32[]{:S(2)}, u32[]{:S(2)}) collective-permute-start(f32[8,128]{1,0:T(8,128)S(1)} %get-tuple-element.90), channel_id=1, source_target_pairs={{0,1},{1,0},{2,3},{3,2},{4,5},{5,4},{6,7},{7,6},{8,9},{9,8},{10,11... | collective-permute-start | bytes 12296 | tf_op jit(solution)/shard_map/ppermute | solution.py:446
  83.5 3.6 %collective-permute-start.19 = (f32[8,128]{1,0:T(8,128)S(1)}, f32[8,128]{1,0:T(8,128)S(1)}, u32[]{:S(2)}, u32[]{:S(2)}) collective-permute-start(f32[8,128]{1,0:T(8,128)S(1)} %add.29), channel_id=1, source_target_pairs={{0,2},{1,3},{2,0},{3,1},{4,6},{5,7},{6,4},{7,5},{8,10},{9,11},{10,... | collective-permute-start | bytes 12296 | tf_op jit(solution)/shard_map/ppermute | solution.py:446
  87.1 0.7 copy-start.12

commit v2 on v0

v2 whole, which is shorter than its diff:
```python
import functools

import jax
import jax.numpy as jnp
from jax import lax
from jax.experimental import pallas as pl
from jax.experimental.pallas import tpu as pltpu
from jax.sharding import PartitionSpec as P

SWEEPS = 4
DAMPING = 0.8
HIGHEST = lax.Precision.HIGHEST
F32 = jnp.float32
VMEM = pl.BlockSpec(memory_space=pltpu.VMEM)
SMEM = pl.BlockSpec(memory_space=pltpu.SMEM)
HBM = pl.BlockSpec(memory_space=pltpu.HBM)
COSTS = (1.0, 30.0, 0.01, 2.0, 3.0, 3.0)
LIMIT = 12 * 1024 * 1024
W = 4
B = 8


def held(*shapes):
    return [pltpu.VMEM(s, F32) for s in shapes]


def call(kernel, outs, scratch, specs, *args, cost=1.0):
    return pl.pallas_call(
        kernel,
        out_shape=[jax.ShapeDtypeStruct(s, F32) if isinstance(s, tuple) else s for s in outs],
        in_specs=specs,
        out_specs=[VMEM] * len(outs),
        scratch_shapes=[pltpu.VMEM(s, F32) if isinstance(s, tuple) else s for s in scratch],
        compiler_params=pltpu.CompilerParams(vmem_limit_bytes=LIMIT),
        cost_estimate=pl.CostEstimate(
            flops=int(cost * 1e6), bytes_accessed=int(cost * 3e6), transcendentals=0
        ),
    )(*args)


def beside(x):
    lane = lax.broadcasted_iota(jnp.int32, x.shape, 1)
    last = x.shape[1] - 1
    before = jnp.where(lane == 0, 0.0, pltpu.roll(x, 1, 1))
    after = jnp.where(lane == last, 0.0, pltpu.roll(x, last, 1))
    return before, after


def unless(flag, x):
    return jnp.where(flag, 0.0, x)


class Place:
    def __init__(self, rows, blocks, spans):
        b, s = lax.axis_index("blk"), lax.axis_index("span")
        self.rows, self.tall = rows, rows + 2 * W
        self.no_left, self.no_right = b == 0, b == blocks - 1
        self.no_low, self.no_high = s == 0, s == spans - 1
        self.ext = slice(B, B + self.tall)
        self.own = slice(B + W, B + W + rows)
        self.low = slice(B, B + W)
        self.high = slice(B + W + rows, B + self.tall)

    def reach(self, by):
        return slice(B + W - by, B + W + self.rows + by)

    def fill(self, store, own, low, high, hide=None):
        no_low, no_high = self.no_low, self.no_high
        if hide is not None:
            own, no_low, no_high = unless(hide, own), no_low | hide, no_high | hide
        store(self.own, own)
        store(self.low, unless(no_low, low))
        store(self.high, unless(no_high, high))

    def inside(self, z):
        row = lax.broadcasted_iota(jnp.int32, (self.tall, z), 0)
        out = ((row < W) & self.no_low) | ((row >= W + self.rows) & self.no_high)
        return jnp.logical_not(out)


def beyond(sl, by):
    return slice(sl.start + by, sl.stop + by)


def rows_at(ref, n, count):
    return ref[n : n + count]


class Arrivals:
    def __init__(self, first, rows, fields, reaches):
        self.first, self.rows, self.fields, self.reaches = first, rows, fields, reaches

    def window(self, level, f, ext=True):
        n = self.first
        for reach in self.reaches[:level]:
            n = n + self.fields * (self.rows + 2 * reach)
        reach = self.reaches[level]
        n = n + f * (self.rows + 2 * reach)
        if ext:
            return slice(n + reach - W, n + reach + W + self.rows)
        return slice(n + reach, n + reach + self.rows)

    def size(self):
        return self.first + sum(self.fields * (self.rows + 2 * reach) for reach in self.reaches)


class Fluid:
    def __init__(self, spread, jacobian, fields):
        self.n = fields
        self.d = [spread[f] for f in range(fields)]
        self.jac = [[jacobian[f, g] for g in range(fields)] for f in range(fields)]

    def diagonal(self, f, us):
        return us + (6.0 * self.d[f] + self.jac[f][f])

    def advance(self, cur, left, right, vel, w, src, sl, which=None):
        u0, u1, u2 = vel
        us = u0 + u1 + u2
        centre = [cur(f, sl) for f in range(self.n)]
        out = {}
        for f in range(self.n) if which is None else which:
            c = centre[f]
            zm, zp = beside(c)
            yp = cur(f, beyond(sl, 1))
            near = (cur(f, beyond(sl, -1)) + yp) + (zm + zp)
            if left is not None:
                near = near + left(f)
            res = u1 * yp + u2 * zp - self.diagonal(f, us) * c
            if right is not None:
                xp = right(f)
                near = near + xp
                res = res + u0 * xp
            res = res + self.d[f] * near
            for g in range(self.n):
                if g != f:
                    res = res - self.jac[f][g] * centre[g]
            if src is not None:
                res = res + src(f)
            out[f] = (res, c + w(f) * res)
        return out


def at(ref, i):
    return lambda f, sl: ref[f, i, sl]


def at_rows(ref, i, sl):
    return lambda f: ref[f, i, sl]


def early_kernel(*refs):
    bufs = refs[6:12]
    yf, yb, xf, sems = refs[12:]
    copies = [
        pltpu.make_async_copy(ref, buf, sems.at[j])
        for j, (ref, buf) in enumerate(zip(refs[:6], bufs, strict=True))
    ]
    for copy in copies:
        copy.start()
    for copy in copies:
        copy.wait()
    p, src, vel, t, heat, k = bufs
    fields, depth, rows = p.shape[0], p.shape[1], p.shape[2]
    thick = t.shape[0]
    n = 0
    for ref in (p, src, vel):
        for f in range(ref.shape[0]):
            for i in range(depth):
                yf[n : n + W] = ref[f, i, rows - W :]
                yb[n : n + W] = ref[f, i, :W]
                n = n + W
    for ref in (t, k, heat):
        for i in range(thick):
            yf[n : n + W] = ref[i, rows - W :]
            yb[n : n + W] = ref[i, :W]
            n = n + W
    planes = [p[f, depth - 1] for f in range(fields)]
    planes += [vel[f, depth - 1] for f in range(3)]
    planes += [vel[0, depth - 2], vel[0, depth - 2] + vel[1, depth - 2] + vel[2, depth - 2]]
    planes += [t[thick - 4 + j] for j in range(4)]
    planes += [k[thick - 4 + j] for j in range(4)]
    planes += [heat[thick - 3 + j] for j in range(3)]
    for j, plane in enumerate(planes):
        xf[j * rows : (j + 1) * rows] = plane


def ahead_kernel(blocks, spans, spread, jacobian, p, src, vel, yl, yr, _, out, a0, a1, a2, sa, va, wa):
    fields, depth, rows, z = p.shape
    thick = (yl.shape[0] // W - (2 * fields + 3) * depth) // 3
    at_place = Place(rows, blocks, spans)
    ext, own = at_place.ext, at_place.own
    fluid = Fluid(spread, jacobian, fields)
    inside = at_place.inside(z)

    def fill(buf, f, j, ref, first, i):
        def store(sl, x):
            buf[f, j, sl] = x

        n = ((first + f) * depth + i) * W
        at_place.fill(store, ref[f, i], rows_at(yl, n, W), rows_at(yr, n, W))

    for f in range(fields):
        for j in range(4):
            fill(a0, f, j, p, 0, depth - 4 + j)
        for j in range(3):
            fill(sa, f, j, src, fields, depth - 3 + j)
    for f in range(3):
        for j in range(3):
            fill(va, f, j, vel, 2 * fields, depth - 3 + j)
    for j in range(3):
        us = va[0, j, ext] + va[1, j, ext] + va[2, j, ext]
        for f in range(fields):
            wa[f, j, ext] = jnp.where(inside, DAMPING / fluid.diagonal(f, us), 0.0)

    def step(old, i, new, j, shift):
        last = j == 2
        got = fluid.advance(
            at(old, i),
            at_rows(old, i - 1, ext),
            None if last else at_rows(old, i + 1, ext),
            [va[c, j, ext] for c in range(3)],
            at_rows(wa, j, ext),
            at_rows(sa, j, ext),
            ext,
        )
        for f in range(fields):
            new(f, got[f][1])

    def into(buf, j):
        def store(f, x):
            buf[f, j, ext] = x

        return store

    for j in range(3):
        step(a0, j + 1, into(a1, j), j, 0)
    for j in range(1, 3):
        step(a1, j, into(a2, j - 1), j, 0)
    corners = [(f * depth + depth - 1) * W for f in range(fields)]
    corners += [((2 * fields + c) * depth + depth - 1) * W for c in range(3)]
    base = (2 * fields + 3) * depth
    corners += [(base + thick - 3 + j) * W for j in range(3)]
    corners += [(base + thick + thick - 3 + j) * W for j in range(3)]
    corners += [(base + 2 * thick + thick - 2 + j) * W for j in range(2)]
    n = 0
    for m in corners:
        out[n : n + W] = yl[m : m + W]
        out[n + W : n + 2 * W] = yr[m : m + W]
        n = n + 2 * W
    for reach, buf, j in ((2, a1, 2), (1, a2, 1)):
        size = rows + 2 * reach
        for f in range(fields):
            out[n : n + size] = buf[f, j, at_place.reach(reach)]
            n = n + size

    def last(f, x):
        out[n + f * rows : n + (f + 1) * rows] = x[W : W + rows]

    step(a2, 1, last, 2, 0)


def around(buf, j, sl):
    zm, zp = beside(buf[j, sl])
    return (
        (buf[j - 1, sl] + buf[j + 1, sl])
        + (buf[j, beyond(sl, -1)] + buf[j, beyond(sl, 1)])
        + (zm + zp)
    )


def solid_weight(h, diagonal):
    return jnp.where(h > 0.0, DAMPING / jnp.where(h > 0.0, diagonal, 1.0), 0.0)


def inner_kernel(
    blocks, spans, spread, jacobian, p, src, vel, t, heat, k, yl, yr, *outs
):
    p0, s0, v0, w0, p1, p2, p3, te, he, so, ti, tb, sqi, dg, ws, ta, tc, qa, qc = outs
    fields, depth, rows, z = p.shape
    thick = t.shape[0]
    here = Place(rows, blocks, spans)
    ext = here.ext
    fluid = Fluid(spread, jacobian, fields)
    inside = here.inside(z)
    first = 0
    for buf, ref in ((p0, p), (s0, src), (v0, vel)):
        for f in range(ref.shape[0]):
            for i in range(depth):

                def store(sl, x, buf=buf, f=f, i=i):
                    buf[f, i, sl] = x

                n = ((first + f) * depth + i) * W
                here.fill(store, ref[f, i], rows_at(yl, n, W), rows_at(yr, n, W))
        first = first + ref.shape[0]
    for i in range(depth):
        us = v0[0, i, ext] + v0[1, i, ext] + v0[2, i, ext]
        for f in range(fields):
            w0[f, i, ext] = jnp.where(inside, DAMPING / fluid.diagonal(f, us), 0.0)
    for level, (old, new) in enumerate(((p0, p1), (p1, p2), (p2, p3))):
        for i in range(level + 1, depth - 1 - level):
            got = fluid.advance(
                at(old, i - level),
                at_rows(old, i - level - 1, ext),
                at_rows(old, i - level + 1, ext),
                [v0[c, i, ext] for c in range(3)],
                at_rows(w0, i, ext),
                at_rows(s0, i, ext),
                ext,
            )
            for f in range(fields):
                new[f, i - level - 1, ext] = got[f][1]
    base = (2 * fields + 3) * depth
    for j, (buf, ref, scale) in enumerate(((te, t, 1.0), (he, k, 0.5), (so, heat, 1.0))):
        for i in range(thick):

            def store(sl, x, buf=buf, i=i, scale=scale):
                buf[i, sl] = scale * x

            n = (base + j * thick + i) * W
            here.fill(store, ref[i], yl[n : n + W], yr[n : n + W])
    for i in range(1, thick - 1):
        h = he[i, ext]
        diagonal = 6.0 * h + around(he, i, ext)
        dg[i, ext] = diagonal
        ws[i, ext] = solid_weight(h, diagonal)
    for i in range(thick):
        qa[i, ext] = he[i, ext] * te[i, ext]
    old, oldq, new, newq = te, qa, ta, qc
    total = None
    for level in range(SWEEPS):
        last = level == SWEEPS - 1
        sl = here.own if last else ext
        for i in range(level + 1, thick - 1 - level):
            h, q = he[i, sl], old[i, sl]
            res = so[i, sl] - dg[i, sl] * q + h * around(old, i, sl) + around(oldq, i, sl)
            value = q + ws[i, sl] * res
            if last:
                tb[i - SWEEPS] = value
                square = res * res
                total = square if total is None else total + square
            else:
                new[i, sl] = value
                newq[i, sl] = h * value
        if not last:
            one = level + 1
            for j, i in enumerate((one, one + 1, thick - 2 - one, thick - 1 - one)):
                ti[level, j] = new[i]
            old, new = new, (tc if new is ta else ta)
            oldq, newq = newq, oldq
    sqi[...] = jnp.zeros_like(sqi)
    sqi[fields : fields + 1] = jnp.sum(total, axis=0, keepdims=True)


def cone_kernel(blocks, spans, sent, spread, jacobian, *refs):
    p0, s0, v0, w0, p1, p2, _, te, he, so, xe, xn, coef, idx = refs[:14]
    back, parts, first, sq, c2, c3, sl_ = refs[14:21]
    l0, d1, d2, vm, wm, n1, n2 = refs[21:]
    fields = p0.shape[0]
    rows, z = coef.shape[1], coef.shape[2]
    here = Place(rows, blocks, spans)
    ext, own, tall = here.ext, here.own, here.tall
    fluid = Fluid(spread, jacobian, fields)
    inside = jnp.logical_and(here.inside(z), jnp.logical_not(here.no_left))
    mine = slice(W, W + rows)
    corner = 0
    for f in range(fields):

        def store(sl, x, f=f):
            l0[f, sl] = x

        n = corner + f * 2 * W
        here.fill(
            store, xe[f * rows : (f + 1) * rows], xn[n : n + W], xn[n + W : n + 2 * W], here.no_left
        )
    for c in range(3):

        def store(sl, x, c=c):
            vm[c, sl] = x

        n = corner + (fields + c) * 2 * W
        m = (fields + c) * rows
        here.fill(store, xe[m : m + rows], xn[n : n + W], xn[n + W : n + 2 * W])
    um = [vm[c, ext] for c in range(3)]
    usm = um[0] + um[1] + um[2]
    for f in range(fields):
        wm[f] = jnp.where(inside, DAMPING / fluid.diagonal(f, usm), 0.0)
    m = (fields + 3) * rows
    u0mm, usmm = xe[m : m + rows], xe[m + rows : m + 2 * rows]

    def arrived(level, f):
        return unless(here.no_left, xn[sent.window(level - 1, f, level < 3)])

    def plane(cur, i, left, right, sl=ext):
        return fluid.advance(
            cur,
            left,
            right,
            [v0[c, i, sl] for c in range(3)],
            at_rows(w0, i, sl),
            at_rows(s0, i, sl),
            sl,
        )

    def put(new, got):
        for f in range(fields):
            new(f, got[f][1])

    def flat(ref):
        return lambda f, sl: ref[f, sl]

    def flat_rows(ref, sl):
        return lambda f: ref[f, sl]

    def into(ref):
        def store(f, x):
            ref[f, ext] = x

        return store

    def into_plane(ref, i):
        def store(f, x):
            ref[f, i, ext] = x

        return store

    put(into(n1), plane(at(p0, 0), 0, flat_rows(l0, ext), at_rows(p0, 1, ext)))
    for f in range(fields):
        d1[f, ext] = wm[f] * (fluid.d[f] + um[0]) * p0[f, 0, ext]
    put(into(n2), plane(flat(n1), 0, lambda f: arrived(1, f) + d1[f, ext], at_rows(p1, 0, ext)))
    put(into(c2), plane(at(p1, 0), 1, flat_rows(n1, ext), at_rows(p1, 1, ext)))
    got = fluid.advance(
        flat(d1), None, flat_rows(n1, ext), um, lambda f: wm[f], None, ext
    )
    for f in range(fields):
        d2[f, ext] = got[f][1]
    put(
        into_plane(c3, 0),
        plane(flat(n2), 0, lambda f: arrived(2, f) + d2[f, ext], flat_rows(c2, ext)),
    )
    put(into_plane(c3, 1), plane(flat(c2), 1, flat_rows(n2, ext), at_rows(p2, 0, ext)))

    def farther(f):
        w = unless(here.no_left, DAMPING / fluid.diagonal(f, usmm))
        return w * (fluid.d[f] + u0mm) * d1[f, own]

    got = fluid.advance(
        flat(d2),
        farther,
        flat_rows(n2, own),
        [u[mine] for u in um],
        lambda f: wm[f, mine],
        None,
        own,
    )
    third = [got[f][1] for f in range(fields)]
    got = plane(at(c3, 0), 0, lambda f: arrived(3, f) + third[f], at_rows(c3, 1, own), own)
    sq[...] = jnp.zeros_like(sq)
    for f in range(fields):
        res, new = got[f]
        first[f] = new
        sq[f : f + 1] = jnp.sum(res * res, axis=0, keepdims=True)
    flux = coef[0] * first[fields - 1]
    n = lax.broadcasted_iota(jnp.int32, (blocks * 2 * rows, rows), 0)
    key = n // (2 * rows) * rows + n % (2 * rows) - rows
    hot = jnp.where(key == idx[...], 1.0, 0.0)
    parts[...] = jnp.dot(hot, flux, precision=HIGHEST, preferred_element_type=F32)
    n = 0
    for buf, count in ((te, 4), (he, 4), (so, 3)):
        for i in range(count):
            back[n : n + tall] = buf[i, ext]
            n = n + tall
    for reach, read in (
        (3, at(p0, 0)),
        (2, flat(n1)),
        (1, flat(n2)),
        (0, at(c3, 0)),
    ):
        size = rows + 2 * reach
        for f in range(fields):
            back[n : n + size] = read(f, here.reach(reach))
            n = n + size
    corner = corner + (fields + 3) * 2 * W
    early = (fields + 5) * rows
    zero = jnp.zeros((W, z), F32)
    j = 0
    for near, scale in ((4, 1.0), (4, 0.5), (3, 1.0)):
        for i in range(near):

            def store(sl, x, j=j, scale=scale):
                sl_[j, sl.start - B : sl.stop - B] = scale * x

            if i > 0:
                low, high = xn[corner : corner + W], xn[corner + W : corner + 2 * W]
                corner = corner + 2 * W
            else:
                low, high = zero, zero
            here.fill(store, xe[early : early + rows], low, high, here.no_left)
            early = early + rows
            j = j + 1


def rest_kernel(blocks, spans, sent, spread, jacobian, *refs):
    p0, s0, v0, w0, p1, p2, p3, c2, c3, first, sqb, xn, _, gas, sq, n1, n2, n3 = refs
    fields, depth = gas.shape[0], gas.shape[1]
    rows = gas.shape[2]
    here = Place(rows, blocks, spans)
    ext, own, tall = here.ext, here.own, here.tall
    fluid = Fluid(spread, jacobian, fields)
    def arrived(level):
        return lambda f: unless(here.no_right, xn[sent.window(level, f, level < 3)])

    known = [{i: (p0, i) for i in range(depth)}, {}, {}, {}]
    for level, buf in enumerate((p1, p2, p3)):
        for i in range(level + 1, depth - 1 - level):
            known[level + 1][i] = (buf, i - level - 1)
    known[2][1], known[3][0], known[3][1] = (c2, None), (c3, 0), (c3, 1)

    def read(level, i):
        ref, j = known[level][i]
        return (lambda f, sl: ref[f, sl]) if j is None else (lambda f, sl: ref[f, j, sl])

    def plane(level, i, sl=ext):
        right = arrived(level)
        if i < depth - 1:
            right = functools.partial(read(level, i + 1), sl=sl)
        return fluid.advance(
            read(level, i),
            functools.partial(read(level, i - 1), sl=sl),
            right,
            [v0[c, i, sl] for c in range(3)],
            at_rows(w0, i, sl),
            at_rows(s0, i, sl),
            sl,
        )

    todo = ((depth - 1,), (depth - 2, depth - 1), (2, depth - 3, depth - 2, depth - 1))
    for level, new in enumerate((n1, n2, n3)):
        for j, i in enumerate(todo[level]):
            got = plane(level, i)
            for f in range(fields):
                new[f, j, ext] = got[f][1]
            known[level + 1][i] = (new, j)
    total = [None] * fields
    for f in range(fields):
        gas[f, 0] = first[f]
    for i in range(1, depth):
        got = plane(3, i, own)
        for f in range(fields):
            res, new = got[f]
            gas[f, i] = new
            square = res * res
            total[f] = square if total[f] is None else total[f] + square
    sq[...] = sqb[...]
    for f in range(fields):
        sq[f : f + 1] = sq[f : f + 1] + jnp.sum(total[f], axis=0, keepdims=True)


def solid_kernel(blocks, spans, te, he, so, ti, tbi, sqi, dg, ws, sl_, xb, _, *refs):
    tb, rb, sq, rh, rd, rw = refs[:6]
    to, ho, do, wo, heat, t0, q0, t1, q1 = refs[6:]
    thick, rows, z = tb.shape
    here = Place(rows, blocks, spans)
    ext, own, tall = here.ext, here.own, here.tall
    left, right = 0, 0
    for buf, near in ((to, 4), (ho, 4), (heat, 3)):
        for i in range(near):
            buf[4 - near + i, ext] = sl_[left]
            buf[4 + i, ext] = unless(here.no_right, xb[right : right + tall])
            left, right = left + 1, right + tall

    def place(inside, outside, i):
        if 0 <= i < thick:
            return inside, i
        return outside, (i + 4 if i < 0 else i - thick + 4)

    def h_of(i, sl):
        ref, j = place(he, ho, i)
        return ref[j, sl]

    for i in (-3, -2, -1, 0, thick - 1, thick, thick + 1, thick + 2):
        zm, zp = beside(h_of(i, ext))
        h = h_of(i, ext)
        near = (h_of(i - 1, ext) + h_of(i + 1, ext)) + (zm + zp)
        near = near + (h_of(i, beyond(ext, -1)) + h_of(i, beyond(ext, 1)))
        diagonal = 6.0 * h + near
        j = i + 3 if i <= 0 else i - (thick - 1) + 4
        do[j, ext] = diagonal
        wo[j, ext] = solid_weight(h, diagonal)

    def d_of(ref, outer, i, sl):
        if 0 < i < thick - 1:
            return ref[i, sl]
        return outer[i + 3 if i <= 0 else i - (thick - 1) + 4, sl]

    def first(side, level):
        return level - 4 if side == 0 else thick - 2 - level

    sums = None
    for side in range(2):
        old, oldq, new, newq = t0, q0, t1, q1
        for j in range(6):
            i = first(side, 0) + j
            ref, m = place(te, to, i)
            old[j] = ref[m]
            oldq[j, ext] = h_of(i, ext) * ref[m, ext]
        for level in range(SWEEPS):
            last = level == SWEEPS - 1
            sl = own if last else ext
            for j in range(1, 5):
                i = first(side, level) + j
                ref, m = place(so, heat, i)
                h, q = h_of(i, sl), old[j, sl]
                res = ref[m, sl] - d_of(dg, do, i, sl) * q
                res = res + h * around(old, j, sl) + around(oldq, j, sl)
                value = q + d_of(ws, wo, i, sl) * res
                if last:
                    tb[i] = value
                    if i < 3:
                        rb[i] = res
                    elif i >= thick - 4:
                        rb[i - (thick - 7)] = res
                    else:
                        sums = res * res
                else:
                    m = j - 1 if side == 0 else j + 1
                    new[m, ext] = value
                    newq[m, ext] = h * value
            if not last:
                for m in range(2):
                    j = m + 4 if side == 0 else m
                    i = first(side, level + 1) + j
                    new[j] = ti[level, m + 2 * side]
                    newq[j, ext] = h_of(i, ext) * new[j, ext]
            old, oldq, new, newq = new, newq, old, oldq
    for i in range(SWEEPS, thick - SWEEPS):
        tb[i] = tbi[i - SWEEPS]
    sq[...] = sqi[...]
    n = refs[2].shape[0] - 3
    sq[n : n + 1] = sq[n : n + 1] + jnp.sum(sums, axis=0, keepdims=True)
    for region in range(2):
        for j in range(5):
            i = j - 2 if region == 0 else thick - 4 + j
            rh[region, j, ext] = h_of(i, ext)
            rd[region, j, ext] = d_of(dg, do, i, ext)
            rw[region, j, ext] = d_of(ws, wo, i, ext)


def surface_kernel(blocks, arrived, surface, yf, yb):
    rows = surface.shape[0] // 2
    whole = arrived[0]
    for j in range(1, blocks):
        whole = whole + arrived[j]
    surface[...] = whole
    yf[:W] = whole[rows - W : rows]
    yf[W:] = whole[2 * rows - W :]
    yb[:W] = whole[:W]
    yb[W:] = whole[rows : rows + W]


def response_kernel(
    blocks, spans, fields, surface, yl, yr, rh, rd, rw, tb, rb, sqf, sqs, tn, out, da, db, hd, so
):
    thick, rows, z = tb.shape
    here = Place(rows, blocks, spans)
    ext, own = here.ext, here.own
    for buf in (da, db, hd):
        buf[...] = jnp.zeros_like(buf)
    sq = sqf[...] + sqs[...]
    gained = jnp.zeros((rows, z), F32)
    for region in range(2):

        def store(sl, x, region=region):
            so[region, sl] = x

        edge = slice(region * W, (region + 1) * W)
        here.fill(store, surface[region * rows : (region + 1) * rows], yl[edge], yr[edge])

    needed = (((2,), (1, 2, 3), (1, 2, 3, 4), (3, 4, 5)), ((4,), (3, 4, 5), (2, 3, 4, 5), (1, 2, 3, 4)))
    for i in range(3, thick - 4):
        tn[i] = tb[i]
    for region in range(2):
        old, new = da, db
        source = 2 if region == 0 else 4
        for sweep in range(SWEEPS):
            final = sweep == SWEEPS - 1
            for j in needed[region][sweep]:
                res = so[region, ext] if j == source else None
                h, w = rh[region, j - 1, ext], rw[region, j - 1, ext]
                if sweep > 0:
                    q = old[region, j, ext]
                    flow = h * around(old.at[region], j, ext) + around(hd.at[region], j, ext) - rd[region, j - 1, ext] * q
                    res = flow if res is None else res + flow
                    change = q + w * res
                else:
                    change = w * res
                if final:
                    i = j - 3 if region == 0 else thick - 5 + j
                    kept = i if region == 0 else 2 + j
                    mine = slice(W, W + rows)
                    tn[i] = tb[i] + change[mine]
                    full = rb[kept] + res[mine]
                    gained = gained + full * full
                else:
                    new[region, j, ext] = change
            if not final:
                for j in needed[region][sweep]:
                    hd[region, j, ext] = rh[region, j - 1, ext] * new[region, j, ext]
                old, new = new, old
    extra = jnp.sum(gained, axis=0, keepdims=True)
    row = lax.broadcasted_iota(jnp.int32, sq.shape, 0)
    sq = sq + jnp.where(row == fields, extra, 0.0)
    for j in range(blocks):
        out[j, :rows] = tn[thick - 1]
        out[j, rows:] = sq


def return_kernel(blocks, arrived, idx, coef, added, sq):
    rows = added.shape[0]
    row = lax.broadcasted_iota(jnp.int32, (rows, rows), 0)
    taken, squares = None, None
    for j in range(blocks):
        hot = jnp.where(idx[...] - j * rows == row, 1.0, 0.0)
        got = lax.dot_general(
            hot,
            arrived[j, :rows],
            (((0,), (0,)), ((), ())),
            precision=HIGHEST,
            preferred_element_type=F32,
        )
        taken = got if taken is None else taken + got
        squares = arrived[j, rows:] if squares is None else squares + arrived[j, rows:]
    added[...] = coef[0] * taken
    sq[...] = squares


def shards(
    blocks,
    spans,
    fluid_adjoint_in,
    fluid_source,
    velocity,
    diffusion,
    jacobian,
    wall_coefficient,
    metal_costate_prior,
    solid_source,
    conductivity,
    tile_owner,
    tile_target,
):
    p, src, vel = fluid_adjoint_in, fluid_source, velocity
    t, heat, k = metal_costate_prior, solid_source, conductivity
    fields, depth, rows, z = p.shape
    thick = t.shape[0]
    tall = rows + 2 * W
    buf = tall + 2 * B
    forward = {
        "blk": [(i, (i + 1) % blocks) for i in range(blocks)],
        "span": [(i, (i + 1) % spans) for i in range(spans)],
    }
    backward = {axis: [(j, i) for i, j in pairs] for axis, pairs in forward.items()}

    def ahead(x, axis):
        return lax.ppermute(x, axis, forward[axis])

    def behind(x, axis):
        return lax.ppermute(x, axis, backward[axis])

    idx = tile_owner[0, :, 0] * rows + tile_target[0]
    row_idx = idx[None, :]
    yrows = ((2 * fields + 3) * depth + 3 * thick) * W
    inputs = [p, src, vel, t, heat, k]
    p, src, vel, t, heat, k, yf, yb, xf = call(
        early_kernel,
        held(*[x.shape for x in inputs])
        + [(yrows, z), (yrows, z), ((fields + 16) * rows, z)],
        [pltpu.SemaphoreType.DMA((6,))],
        [HBM] * 6,
        *[pltpu.with_memory_space_constraint(x, pltpu.HBM) for x in inputs],
    )
    yl, yr = ahead(yf, "span"), behind(yb, "span")
    xe = ahead(xf, "blk")
    sent_ahead = Arrivals((fields + 11) * 2 * W, rows, fields, (2, 1, 0))
    (out,) = call(
        functools.partial(ahead_kernel, blocks, spans),
        [(sent_ahead.size(), z)],
        [(fields, 4, buf, z), (fields, 3, buf, z), (fields, 2, buf, z), (fields, 3, buf, z)]
        + [(3, 3, buf, z), (fields, 3, buf, z)],
        [SMEM] * 2 + [VMEM] * 6,
        diffusion,
        jacobian,
        p,
        src,
        vel,
        yl,
        yr,
        xe,
        cost=COSTS[1],
    )
    xn = ahead(out, "blk")
    full = (fields, depth, buf, z)
    part = [(fields, depth - 2 * (level + 1), buf, z) for level in range(3)]
    solid = (thick, buf, z)
    p0, s0, v0, w0, p1, p2, p3, te, he, so, ti, tb, sqi, dg, ws = call(
        functools.partial(inner_kernel, blocks, spans),
        held(full, full, (3, depth, buf, z), full, *part, solid, solid, solid)
        + held((3, 4, buf, z), (thick - 2 * SWEEPS, rows, z), (8, z), solid, solid),
        [solid] * 4,
        [SMEM] * 2 + [VMEM] * 8,
        diffusion,
        jacobian,
        p,
        src,
        vel,
        t,
        heat,
        k,
        yl,
        yr,
        cost=COSTS[2],
    )
    sent_back = Arrivals(11 * tall, rows, fields, (3, 2, 1, 0))
    flat = (fields, buf, z)
    back, parts, first, sq, c2, c3, sl_ = call(
        functools.partial(cone_kernel, blocks, spans, sent_ahead),
        [(sent_back.size(), z), (blocks * 2 * rows, z)]
        + held((fields, rows, z), (8, z), flat, (fields, 2, buf, z), (11, tall, z)),
        [flat] * 3 + [(3, buf, z), (fields, tall, z)] + [flat] * 2,
        [SMEM] * 2 + [VMEM] * 14,
        diffusion,
        jacobian,
        p0,
        s0,
        v0,
        w0,
        p1,
        p2,
        p3,
        te,
        he,
        so,
        xe,
        xn,
        wall_coefficient,
        row_idx,
        cost=COSTS[3],
    )
    xr = behind(back, "blk")
    arrived = lax.all_to_all(parts.reshape(blocks, 2 * rows, z), "blk", 0, 0)
    surface, yf, yb = call(
        functools.partial(surface_kernel, blocks),
        [(2 * rows, z), (2 * W, z), (2 * W, z)],
        [],
        [VMEM],
        arrived,
    )
    yl, yr = ahead(yf, "span"), behind(yb, "span")
    gas, sqf = call(
        functools.partial(rest_kernel, blocks, spans, sent_back),
        [p.shape, (8, z)],
        [(fields, 1, buf, z), (fields, 2, buf, z), (fields, 4, buf, z)],
        [SMEM] * 2 + [VMEM] * 13,
        diffusion,
        jacobian,
        p0,
        s0,
        v0,
        w0,
        p1,
        p2,
        p3,
        c2,
        c3,
        first,
        sq,
        xr,
        yf,
        cost=COSTS[4],
    )
    outer, edge = (8, buf, z), (2, 5, buf, z)
    tb, rb, sqs, rh, rd, rw = call(
        functools.partial(solid_kernel, blocks, spans),
        held(t.shape, (7, rows, z), (8, z), edge, edge, edge),
        [outer] * 5 + [(6, buf, z)] * 4,
        [VMEM] * 11,
        te,
        he,
        so,
        ti,
        tb,
        sqi,
        dg,
        ws,
        sl_,
        xr,
        yf,
        cost=COSTS[5],
    )
    region = (2, 7, buf, z)
    t, out = call(
        functools.partial(response_kernel, blocks, spans, fields),
        [t.shape, (blocks, rows + 8, z)],
        [region] * 3 + [(2, buf, z)],
        [VMEM] * 10,
        surface,
        yl,
        yr,
        rh,
        rd,
        rw,
        tb,
        rb,
        sqf,
        sqs,
    )
    arrived = lax.all_to_all(out, "blk", 0, 0)
    added, sq = call(
        functools.partial(return_kernel, blocks),
        [(rows, z), (8, z)],
        [],
        [VMEM] * 3,
        arrived,
        row_idx,
        wall_coefficient,
    )
    step = 1
    while step < spans:
        sq = sq + lax.ppermute(sq, "span", [(i, i ^ step) for i in range(spans)])
        step = step * 2
    gas = gas.at[fields - 1, 0].add(added)
    everyone = blocks * spans
    counts = [float(depth * rows * z * everyone)] * fields + [float(thick * rows * z * everyone)]
    totals = jnp.sum(sq[: fields + 1], axis=1)
    norms = jnp.sqrt(totals / jnp.array(counts, F32))
    return gas, t, norms


def solution(mesh):
    placed = (
        P(None, "blk", "span", None),
        P(None, "blk", "span", None),
        P(None, "blk", "span", None),
        P(),
        P(),
        P("blk", "span", None),
        P("blk", "span", None),
        P("blk", "span", None),
        P("blk", "span", None),
        P("span", "blk", None),
        P("span", "blk"),
    )
    return jax.shard_map(
        functools.partial(shards, mesh.shape["blk"], mesh.shape["span"]),
        mesh=mesh,
        in_specs=placed,
        out_specs=(P(None, "blk", "span", None), P("blk", "span", None), P()),
        check_vma=False,
    )
```

time: 275 us -> 75.7 us (0.28)
  starting transfers between devices: 101 us -> 8.2 us
  blocking collectives: 121 us -> 30.6 us
  Pallas kernels: 0 us -> 14.7 us
  matrix products: 9.88 us -> 0 us
  other arithmetic: 8.88 us -> 1.98 us
  local copies, waits for them, and re-layouts: 6.8 us -> 0.03 us
  waiting for transfers between devices: 24.3 us -> 19.1 us
    ppermute x36 -> x9, starting transfers between devices: 101 us -> 8.2 us  [the longest x3 3.53 us: behind(): return lax.ppermute(x, axis, backward[axis])]
    all_gather x2 -> x0, blocking collectives: 62 us -> none  [the longest x1 31.4 us: shards(): arrived = lax.all_gather(wall_flux, 'blk', axis=0, tiled=True)]
    psum x1 -> x0, blocking collectives: 47.1 us -> none  [shards(): lax.psum(jnp.concatenate([fluid_squares, solid_squares]), ('blk', 'span'))]
    all_to_all x0 -> x2, blocking collectives: none -> 30.6 us  [the longest x1 19.2 us: shards(): arrived = lax.all_to_all(parts.reshape(blocks, 2 * rows, z), 'blk', 0, 0)]
    pallas_call x0 -> x9, Pallas kernels: none -> 14.7 us  [call(): pl.pallas_call(kernel, out_shape=[jax.ShapeDtypeStruct(s, F32) if isinsta...]
    unnamed x1 -> x0, blocking collectives: 11.5 us -> none
    dot_general x5 -> x0, matrix products: 9.88 us -> none  [the longest x4 9.52 us: fluid_operator(): jnp.einsum('fg,gxyz->fxyz', jacobian, centre, precision=lax.Precision.HIG...]
    concatenate x17 -> x0, other arithmetic: 5.7 us -> none  [the longest x15 4.97 us: padded(): block = jnp.concatenate([low, block, high], axis=dim)]
  transfers between devices with their start and end apart: 36 -> 9, of which waited for: 14 -> 6; matrix products, arithmetic and copies ran while one was open for 5% -> 2% of each run, Pallas kernels for 0% -> 10%
where the time goes in v2:
time: 75.7 us; the launch traced here: 75.4 us
  blocking collectives  30.6 us (40%)
  waiting for transfers between devices  19.1 us (25%)
  Pallas kernels  14.7 us (19%)
  starting transfers between devices  8.2 us (11%)
  other arithmetic  1.98 us (3%)
  between operations  0.79 us (1%)
    all_to_all x1, blocking collectives, shards(): arrived = lax.all_to_all(parts.reshape(blocks, 2 * rows, z), 'blk', 0, 0)  19.2 us
    ppermute x4, waiting for transfers between devices, ahead(): return lax.ppermute(x, axis, forward[axis])  16.3 us
    pallas_call x9, Pallas kernels, call(): pl.pallas_call(kernel, out_shape=[jax.ShapeDtypeStruct(s, F32) if isinsta...  14.7 us
    all_to_all x1, blocking collectives, shards(): arrived = lax.all_to_all(out, 'blk', 0, 0)  11.4 us
    ppermute x3, starting transfers between devices, behind(): return lax.ppermute(x, axis, backward[axis])  3.53 us
    ppermute x4, starting transfers between devices, ahead(): return lax.ppermute(x, axis, forward[axis])  3.11 us
    ppermute x2, waiting for transfers between devices, shards(): sq = sq + lax.ppermute(sq, 'span', [(i, i ^ step) for i in range(spans)])  1.9 us
    ppermute x2, starting transfers between devices, shards(): sq = sq + lax.ppermute(sq, 'span', [(i, i ^ step) for i in range(spans)])  1.56 us
  transfers between devices with their start and end apart: 9, of which 6 were waited for; matrix products, arithmetic and copies ran while one was open for 2% of the time, Pallas kernels for 10%

profile of v2, /device:TPU:0, one launch (start us, length us, event | category | flops | bytes accessed | tf_op | source)
XLA Modules:
  0.0 75.4 jit_solution(16872297164359784690)
XLA Ops:
  0.6 0.0 copy-start.2
  0.6 0.0 copy-start
  0.7 1.8 %shard_map.139 = (f32[5,8,32,128]{3,2,1,0:T(8,128)S(1)}, f32[5,8,32,128]{3,2,1,0:T(8,128)S(1)}, f32[3,8,32,128]{3,2,1,0:T(8,128)S(1)}, f32[16,32,128]{2,1,0:T(8,...) custom-call(f32[5,8,32,128]{3,2,1,0:T(8,128)} %refs_0_.1, ...), custom_call_target="tpu_custom_call" | custom-call | flops 1000000 | bytes 3000000 | tf_op jit(solution)/shard_map/pallas_call | solution.py:28
  2.5 3.0 %collective-permute-start.2 = (f32[672,128]{1,0:T(8,128)S(1)}, f32[672,128]{1,0:T(8,128)S(1)}, u32[]{:S(2)}, u32[]{:S(2)}) collective-permute-start(f32[672,128]{1,0:T(8,128)S(1)} %get-tuple-element.79), channel_id=1, source_target_pairs={{0,4},{4,8},{8,12},{12,16},{16,20},{20,24},{24,28},{28,0},{1,5},{5... | collective-permute-start | bytes 1032200 | tf_op jit(solution)/shard_map/ppermute | solution.py:765
  5.5 0.0 collective-permute-start
  5.5 1.7 %collective-permute-start.1 = (f32[608,128]{1,0:T(8,128)S(1)}, f32[608,128]{1,0:T(8,128)S(1)}, u32[]{:S(2)}, u32[]{:S(2)}) collective-permute-start(f32[608,128]{1,0:T(8,128)S(1)} %get-tuple-element.68), channel_id=1, source_target_pairs={{1,0},{2,1},{3,2},{0,3},{5,4},{6,5},{7,6},{4,7},{9,8},{10,9},{11,1... | collective-permute-start | bytes 933896 | tf_op jit(solution)/shard_map/ppermute | solution.py:768
  7.2 6.0 %collective-permute-done.yl = f32[608,128]{1,0:T(8,128)S(1)} collective-permute-done((f32[608,128]{1,0:T(8,128)S(1)}, f32[608,128]{1,0:T(8,128)S(1)}, u32[]{:S(2)}, u32[]{:S(2)}) %collective-permute-start) | collective-permute-done | bytes 311328 | tf_op jit(solution)/shard_map/ppermute | solution.py:765
  13.2 0.9 %collective-permute-done.1.yr = f32[608,128]{1,0:T(8,128)S(1)} collective-permute-done((f32[608,128]{1,0:T(8,128)S(1)}, f32[608,128]{1,0:T(8,128)S(1)}, u32[]{:S(2)}, u32[]{:S(2)}) %collective-permute-start.1) | collective-permute-done | bytes 311328 | tf_op jit(solution)/shard_map/ppermute | solution.py:768
  14.2 2.4 %collective-permute-done.2._.refs_10_ = f32[672,128]{1,0:T(8,128)S(1)} collective-permute-done((f32[672,128]{1,0:T(8,128)S(1)}, f32[672,128]{1,0:T(8,128)S(1)}, u32[]{:S(2)}, u32[]{:S(2)}) %collective-permute-start.2) | collective-permute-done | bytes 344096 | tf_op jit(solution)/shard_map/ppermute | solution.py:765
  16.6 0.0 copy-done.2
  16.6 0.0 copy-done
  16.6 0.0 copy-start.3
  16.6 0.0 copy-start.4
  16.6 1.3 %shard_map.141 = f32[638,128]{1,0:T(8,128)S(1)} custom-call(f32[5]{0:T(128)S(1)} %copy-done.2, f32[5,5]{1,0:T(8,128)S(1)} %copy-done, f32[5,8,32,128]{3,2,1,0:T(8,128)S(1)} %get-tuple-element.61.p, f32[5,8,32,128]{3,2,1,0:T(8,128)S(1)} %get-tuple-element.62.src, f32[3,8,32,128]{3,2,1,0:T(8,128)S(1)} %get-tuple-element.63.vel, ...), custom_call_target="tpu_custom_call" | custom-call | flops 30000000 | bytes 90000000 | tf_op jit(solution)/shard_map/pallas_call | solution.py:28
  17.9 0.1 collective-permute-start.3
  18.0 0.0 copy-done.3
  18.0 0.0 copy-done.4
  18.0 0.0 copy-start.1
  18.0 3.7 %shard_map.140 = (f32[5,8,56,128]{3,2,1,0:T(8,128)S(1)}, f32[5,8,56,128]{3,2,1,0:T(8,128)S(1)}, f32[3,8,56,128]{3,2,1,0:T(8,128)S(1)}, f32[5,8,56,128]{3,2,1,0:T...) custom-call(f32[5]{0:T(128)S(1)} %copy-done.2, ...), custom_call_target="tpu_custom_call" | custom-call | flops 10000 | bytes 30000 | tf_op jit(solution)/shard_map/pallas_call | solution.py:28
  21.7 7.9 %collective-permute-done.3.refs_11_ = f32[638,128]{1,0:T(8,128)S(1)} collective-permute-done((f32[638,128]{1,0:T(8,128)S(1)}, f32[638,128]{1,0:T(8,128)S(1)}, u32[]{:S(2)}, u32[]{:S(2)}) %collective-permute-start.3) | collective-permute-done | bytes 326688 | tf_op jit(solution)/shard_map/ppermute | solution.py:765
  29.6 0.0 copy-done.1
  29.6 2.0 %shard_map.142 = (f32[1140,128]{1,0:T(8,128)S(1)}, f32[512,128]{1,0:T(8,128)S(1)}, f32[5,32,128]{2,1,0:T(8,128)S(1)}, f32[8,128]{1,0:T(8,128)S(1)}, f32[5,56,128...) custom-call(f32[5]{0:T(128)S(1)} %copy-done.2, f32[5,5]{1,0:T(8,128)S(1)} %copy-done, ...), custom_call_target="tpu_custom_call" | custom-call | flops 2000000 | bytes 6000000 | tf_op jit(solution)/shard_map/pallas_call | solution.py:28
  31.6 0.1 collective-permute-start.4
  31.7 19.2 %all_to_all.10.arrived = f32[8,64,128]{2,1,0:T(8,128)S(1)} all-to-all(f32[8,64,128]{2,1,0:T(8,128)S(1)} %bitcast.7), channel_id=1, replica_groups=mesh['blk'=8,'span'=4] {'blk'}, dimensions={0} | all-to-all | bytes 524288 | tf_op jit(solution)/shard_map/all_to_all | solution.py:850
  50.9 0.1 collective-permute-start.5
  50.9 1.7 %collective-permute-start.6 = (f32[8,128]{1,0:T(8,128)S(1)}, f32[8,128]{1,0:T(8,128)S(1)}, u32[]{:S(2)}, u32[]{:S(2)}) collective-permute-start(f32[8,128]{1,0:T(8,128)S(1)} %get-tuple-element.89), channel_id=1, source_target_pairs={{1,0},{2,1},{3,2},{0,3},{5,4},{6,5},{7,6},{4,7},{9,8},{10,9},{11,1... | collective-permute-start | bytes 12296 | tf_op jit(solution)/shard_map/ppermute | solution.py:768
  52.7 0.0 collective-permute-done.4.refs_11_.xb
  52.7 3.0 %shard_map.144 = (f32[5,8,32,128]{3,2,1,0:T(8,128)}, f32[8,128]{1,0:T(8,128)S(1)}) custom-call(f32[5]{0:T(128)S(1)} %copy-done.2, f32[5,5]{1,0:T(8,128)S(1)} %copy-done, f32[5,8,56,128]{3,2,1,0:T(8,128)S(1)} %get-tuple-element.69.refs_0_, f32[5,8,56,128]{3,2,1,0:T(8,128)S(1)} %get-tuple-element.70.refs_1_, f32[3,8,56,128]{3,2,1,0:T(8,128)S(1)} %get-tuple-element.71.refs_2_, ...), custom_call_target="tpu_custom_call" | custom-call | flops 3000000 | bytes 9000000 | tf_op jit(solution)/shard_map/pallas_call | solution.py:28
  55.7 1.1 %shard_map.145 = (f32[16,32,128]{2,1,0:T(8,128)S(1)}, f32[7,32,128]{2,1,0:T(8,128)S(1)}, f32[8,128]{1,0:T(8,128)S(1)}, f32[2,5,56,128]{3,2,1,0:T(8,128)S(1)}, f3...) custom-call(f32[16,56,128]{2,1,0:T(8,128)S(1)} %get-tuple-element.76.refs_7_.te, ...), custom_call_target="tpu_custom_call" | custom-call | flops 3000000 | bytes 9000000 | tf_op jit(solution)/shard_map/pallas_call | solution.py:28
  56.8 0.0 copy-start.5
  56.8 0.0 collective-permute-done.5.yl
  56.8 0.0 collective-permute-done.6.yr
  56.8 1.4 %shard_map.146 = (f32[16,32,128]{2,1,0:T(8,128)}, f32[8,40,128]{2,1,0:T(8,128)S(1)}) custom-call(f32[64,128]{1,0:T(8,128)S(1)} %get-tuple-element.88.surface, f32[8,128]{1,0:T(8,128)S(1)} %collective-permute-done.5.yl, f32[8,128]{1,0:T(8,128)S(1)} %collective-permute-done.6.yr, f32[2,5,56,128]{3,2,1,0:T(8,128)S(1)} %get-tuple-element.96.rh, ...), custom_call_target="tpu_custom_call" | custom-call | flops 1000000 | bytes 3000000 | tf_op jit(solution)/shard_map/pallas_call | solution.py:28
  58.2 11.4 %all_to_all.11.arrived = f32[8,40,128]{2,1,0:T(8,128)S(1)} all-to-all(f32[8,40,128]{2,1,0:T(8,128)S(1)} %get-tuple-element.103), channel_id=1, replica_groups=mesh['blk'=8,'span'=4] {'blk'}, dimensions={0} | all-to-all | bytes 327680 | tf_op jit(solution)/shard_map/all_to_all | solution.py:917
  69.6 0.4 shard_map.147
  70.0 0.0 collective-permute-start.7
  70.0 1.2 %collective-permute-done.7 = f32[8,128]{1,0:T(8,128)S(1)} collective-permute-done((f32[8,128]{1,0:T(8,128)S(1)}, f32[8,128]{1,0:T(8,128)S(1)}, u32[]{:S(2)}, u32[]{:S(2)}) %collective-permute-start.7) | collective-permute-done | bytes 4128 | tf_op jit(solution)/shard_map/ppermute | solution.py:929
  71.2 1.6 %collective-permute-start.8 = (f32[8,128]{1,0:T(8,128)S(1)}, f32[8,128]{1,0:T(8,128)S(1)}, u32[]{:S(2)}, u32[]{:S(2)}) collective-permute-start(f32[8,128]{1,0:T(8,128)S(1)} %add.19), channel_id=1, source_target_pairs={{0,2},{1,3},{2,0},{3,1},{4,6},{5,7},{6,4},{7,5},{8,10},{9,11},{10,... | collective-permute-start | bytes 12296 | tf_op jit(solution)/shard_map/ppermute | solution.py:929
  72.7 1.3 %fusion = f32[5,8,32,128]{3,2,1,0:T(8,128)} fusion(f32[5,8,32,128]{3,2,1,0:T(8,128)} %get-tuple-element.87, f32[32,128]{1,0:T(8,128)S(1)} %get-tuple-element.104), kind=kLoop, calls=%fused_computation.1 | loop fusion | flops 4096 | bytes 49152 | tf_op jit(solution)/shard_map/scatter-add | solution.py:931
  74.1 0.7 collective-permute-done.8
  74.8 0.1 slice_reduce_fusion
  74.9 0.0 copy-done.5
  74.9 0.5 multiply_sqrt_fusion
  (4 shorter events, 0.0 us)
Async XLA Ops:
  0.6 15.9 %copy-start.2 = (f32[5]{0:T(128)S(1)}, f32[5]{0:T(128)}, u32[]{:S(2)}) copy-start(f32[5]{0:T(128)} %spread.7) | copy-start | bytes 64
  0.6 15.9 %copy-start = (f32[5,5]{1,0:T(8,128)S(1)}, f32[5,5]{1,0:T(8,128)}, u32[]{:S(2)}) copy-start(f32[5,5]{1,0:T(8,128)} %jacobian.7) | copy-start | bytes 304
  2.5 14.1 %collective-permute-start.2 = (f32[672,128]{1,0:T(8,128)S(1)}, f32[672,128]{1,0:T(8,128)S(1)}, u32[]{:S(2)}, u32[]{:S(2)}) collective-permute-start(f32[672,128]{1,0:T(8,128)S(1)} %get-tuple-element.79), channel_id=1, source_target_pairs={{0,4},{4,8},{8,12},{12,16},{16,20},{20,24},{24,28},{28,0},{1,5},{5... | collective-permute-start | bytes 1032200 | tf_op jit(solution)/shard_map/ppermute | solution.py:765
  5.5 7.8 %collective-permute-start = (f32[608,128]{1,0:T(8,128)S(1)}, f32[608,128]{1,0:T(8,128)S(1)}, u32[]{:S(2)}, u32[]{:S(2)}) collective-permute-start(f32[608,128]{1,0:T(8,128)S(1)} %get-tuple-element.67), channel_id=1, source_target_pairs={{0,1},{1,2},{2,3},{3,0},{4,5},{5,6},{6,7},{7,4},{8,9},{9,10},{10,1... | collective-permute-start | bytes 933896 | tf_op jit(solution)/shard_map/ppermute | solution.py:765
  5.5 8.7 %collective-permute-start.1 = (f32[608,128]{1,0:T(8,128)S(1)}, f32[608,128]{1,0:T(8,128)S(1)}, u32[]{:S(2)}, u32[]{:S(2)}) collective-permute-start(f32[608,128]{1,0:T(8,128)S(1)} %get-tuple-element.68), channel_id=1, source_target_pairs={{1,0},{2,1},{3,2},{0,3},{5,4},{6,5},{7,6},{4,7},{9,8},{10,9},{11,1... | collective-permute-start | bytes 933896 | tf_op jit(solution)/shard_map/ppermute | solution.py:768
  16.6 1.4 %copy-start.3 = (s32[1,32]{1,0:T(1,128)S(1)}, s32[1,32]{1,0:T(1,128)}, u32[]{:S(2)}) copy-start(s32[1,32]{1,0:T(1,128)} %param.24) | copy-start | bytes 388
  16.6 1.4 %copy-start.4 = (s32[1,32,1]{1,2,0:T(1,128)S(1)}, s32[1,32,1]{1,2,0:T(1,128)}, u32[]{:S(2)}) copy-start(s32[1,32,1]{1,2,0:T(1,128)} %param.23) | copy-start | bytes 388
  17.9 11.6 %collective-permute-start.3 = (f32[638,128]{1,0:T(8,128)S(1)}, f32[638,128]{1,0:T(8,128)S(1)}, u32[]{:S(2)}, u32[]{:S(2)}) collective-permute-start(f32[638,128]{1,0:T(8,128)S(1)} %shard_map.141), channel_id=1, source_target_pairs={{0,4},{4,8},{8,12},{12,16},{16,20},{20,24},{24,28},{28,0},{1,5},{5... | collective-permute-start | bytes 979976 | tf_op jit(solution)/shard_map/ppermute | solution.py:765
  18.0 11.6 %copy-start.1 = (f32[1,32,128]{2,1,0:T(8,128)S(1)}, f32[1,32,128]{2,1,0:T(8,128)}, u32[]{:S(2)}) copy-start(f32[1,32,128]{2,1,0:T(8,128)} %coef.1) | copy-start | bytes 49156
  31.6 21.0 %collective-permute-start.4 = (f32[1140,128]{1,0:T(8,128)S(1)}, f32[1140,128]{1,0:T(8,128)S(1)}, u32[]{:S(2)}, u32[]{:S(2)}) collective-permute-start(f32[1140,128]{1,0:T(8,128)S(1)} %get-tuple-element.84), channel_id=1, source_target_pairs={{4,0},{8,4},{12,8},{16,12},{20,16},{24,20},{28,24},{0,28},{5,1},{9... | collective-permute-start | bytes 1751048 | tf_op jit(solution)/shard_map/ppermute | solution.py:768
  50.9 5.9 %collective-permute-start.5 = (f32[8,128]{1,0:T(8,128)S(1)}, f32[8,128]{1,0:T(8,128)S(1)}, u32[]{:S(2)}, u32[]{:S(2)}) collective-permute-start(f32[8,128]{1,0:T(8,128)S(1)} %get-tuple-element.86.refs_12_._), channel_id=1, source_target_pairs={{0,1},{1,2},{2,3},{3,0},{4,5},{5,6},{6,7},{7,4},{8,9},{9,10},{10,1... | collective-permute-start | bytes 12296 | tf_op jit(solution)/shard_map/ppermute | solution.py:765
  50.9 5.9 %collective-permute-start.6 = (f32[8,128]{1,0:T(8,128)S(1)}, f32[8,128]{1,0:T(8,128)S(1)}, u32[]{:S(2)}, u32[]{:S(2)}) collective-permute-start(f32[8,128]{1,0:T(8,128)S(1)} %get-tuple-element.89), channel_id=1, source_target_pairs={{1,0},{2,1},{3,2},{0,3},{5,4},{6,5},{7,6},{4,7},{9,8},{10,9},{11,1... | collective-permute-start | bytes 12296 | tf_op jit(solution)/shard_map/ppermute | solution.py:768
  56.8 18.1 %copy-start.5 = (f32[6]{0:T(128)S(1)}, f32[6]{0:T(128)}, u32[]{:S(2)}) copy-start(f32[6]{0:T(128)} %constant.43) | copy-start | bytes 76
  70.0 1.2 %collective-permute-start.7 = (f32[8,128]{1,0:T(8,128)S(1)}, f32[8,128]{1,0:T(8,128)S(1)}, u32[]{:S(2)}, u32[]{:S(2)}) collective-permute-start(f32[8,128]{1,0:T(8,128)S(1)} %get-tuple-element.106), channel_id=1, source_target_pairs={{0,1},{1,0},{2,3},{3,2},{4,5},{5,4},{6,7},{7,6},{8,9},{9,8},{10,11... | collective-permute-start | bytes 12296 | tf_op jit(solution)/shard_map/ppermute | solution.py:929
  71.2 3.6 %collective-permute-start.8 = (f32[8,128]{1,0:T(8,128)S(1)}, f32[8,128]{1,0:T(8,128)S(1)}, u32[]{:S(2)}, u32[]{:S(2)}) collective-permute-start(f32[8,128]{1,0:T(8,128)S(1)} %add.19), channel_id=1, source_target_pairs={{0,2},{1,3},{2,0},{3,1},{4,6},{5,7},{6,4},{7,5},{8,10},{9,11},{10,... | collective-permute-start | bytes 12296 | tf_op jit(solution)/shard_map/ppermute | solution.py:929

commit v3 on v2

--- a/solution.py
+++ b/solution.py
@@ -17,6 +17,8 @@
 COSTS = (1.0, 30.0, 0.01, 2.0, 3.0, 3.0)
 LIMIT = 12 * 1024 * 1024
 W = 4
+CAP = 12
+CHUNK = 32
 B = 8
 
 
@@ -69,8 +71,8 @@
         if hide is not None:
             own, no_low, no_high = unless(hide, own), no_low | hide, no_high | hide
         store(self.own, own)
-        store(self.low, unless(no_low, low))
-        store(self.high, unless(no_high, high))
+        store(slice(self.low.stop - low.shape[0], self.low.stop), unless(no_low, low))
+        store(slice(self.high.start, self.high.start + high.shape[0]), unless(no_high, high))
 
     def inside(self, z):
         row = lax.broadcasted_iota(jnp.int32, (self.tall, z), 0)
@@ -102,6 +104,28 @@
 
     def size(self):
         return self.first + sum(self.fields * (self.rows + 2 * reach) for reach in self.reaches)
+
+
+class Edges:
+    def __init__(self, fields, depth, thick):
+        n = 0
+        self.fluid, self.outer, self.solid = {}, {}, {}
+        for name, count, reach in (("p", fields, W), ("src", fields, W - 1), ("vel", 3, W - 1)):
+            for f in range(count):
+                for i in range(depth):
+                    self.fluid[name, f, i] = slice(n, n + reach)
+                    n = n + reach
+        for name, near, reach in (("t", 3, W), ("k", 3, W), ("heat", 2, W - 1)):
+            for i in range(thick - near, thick):
+                self.outer[name, i] = slice(n, n + reach)
+                n = n + reach
+        self.size = (n + 7) // 8 * 8
+        n = 0
+        for name, reach in (("t", W), ("k", W), ("heat", W - 1)):
+            for i in range(thick):
+                self.solid[name, i] = slice(n, n + reach)
+                n = n + reach
+        self.solid_size = (n + 7) // 8 * 8
 
 
 class Fluid:
@@ -148,9 +172,9 @@
     return lambda f: ref[f, i, sl]
 
 
-def early_kernel(*refs):
+def early_kernel(edges, *refs):
     bufs = refs[6:12]
-    yf, yb, xf, sems = refs[12:]
+    yf, yb, xf, zf, zb, sems = refs[12:]
     copies = [
         pltpu.make_async_copy(ref, buf, sems.at[j])
         for j, (ref, buf) in enumerate(zip(refs[:6], bufs, strict=True))
@@ -162,18 +186,7 @@
     p, src, vel, t, heat, k = bufs
     fields, depth, rows = p.shape[0], p.shape[1], p.shape[2]
     thick = t.shape[0]
-    n = 0
-    for ref in (p, src, vel):
-        for f in range(ref.shape[0]):
-            for i in range(depth):
-                yf[n : n + W] = ref[f, i, rows - W :]
-                yb[n : n + W] = ref[f, i, :W]
-                n = n + W
-    for ref in (t, k, heat):
-        for i in range(thick):
-            yf[n : n + W] = ref[i, rows - W :]
-            yb[n : n + W] = ref[i, :W]
-            n = n + W
+    named = {"p": p, "src": src, "vel": vel, "t": t, "heat": heat, "k": k}
     planes = [p[f, depth - 1] for f in range(fields)]
     planes += [vel[f, depth - 1] for f in range(3)]
     planes += [vel[0, depth - 2], vel[0, depth - 2] + vel[1, depth - 2] + vel[2, depth - 2]]
@@ -182,31 +195,35 @@
     planes += [heat[thick - 3 + j] for j in range(3)]
     for j, plane in enumerate(planes):
         xf[j * rows : (j + 1) * rows] = plane
-
-
-def ahead_kernel(blocks, spans, spread, jacobian, p, src, vel, yl, yr, _, out, a0, a1, a2, sa, va, wa):
+    for up, down, places in ((yf, yb, edges.fluid), (yf, yb, edges.outer), (zf, zb, edges.solid)):
+        for (name, *at_plane), sl in places.items():
+            ref, reach = named[name], sl.stop - sl.start
+            up[sl] = ref[*at_plane, rows - reach :]
+            down[sl] = ref[*at_plane, :reach]
+
+
+def ahead_kernel(blocks, spans, edges, spread, jacobian, p, src, vel, yl, yr, out, a0, a1, a2, sa, va, wa):
     fields, depth, rows, z = p.shape
-    thick = (yl.shape[0] // W - (2 * fields + 3) * depth) // 3
     at_place = Place(rows, blocks, spans)
     ext, own = at_place.ext, at_place.own
     fluid = Fluid(spread, jacobian, fields)
     inside = at_place.inside(z)
 
-    def fill(buf, f, j, ref, first, i):
+    def fill(buf, f, j, ref, name, i):
         def store(sl, x):
             buf[f, j, sl] = x
 
-        n = ((first + f) * depth + i) * W
-        at_place.fill(store, ref[f, i], rows_at(yl, n, W), rows_at(yr, n, W))
+        sl = edges.fluid[name, f, i]
+        at_place.fill(store, ref[f, i], yl[sl], yr[sl])
 
     for f in range(fields):
         for j in range(4):
-            fill(a0, f, j, p, 0, depth - 4 + j)
+            fill(a0, f, j, p, "p", depth - 4 + j)
         for j in range(3):
-            fill(sa, f, j, src, fields, depth - 3 + j)
+            fill(sa, f, j, src, "src", depth - 3 + j)
     for f in range(3):
         for j in range(3):
-            fill(va, f, j, vel, 2 * fields, depth - 3 + j)
+            fill(va, f, j, vel, "vel", depth - 3 + j)
     for j in range(3):
         us = va[0, j, ext] + va[1, j, ext] + va[2, j, ext]
         for f in range(fields):
@@ -236,16 +253,14 @@
         step(a0, j + 1, into(a1, j), j, 0)
     for j in range(1, 3):
         step(a1, j, into(a2, j - 1), j, 0)
-    corners = [(f * depth + depth - 1) * W for f in range(fields)]
-    corners += [((2 * fields + c) * depth + depth - 1) * W for c in range(3)]
-    base = (2 * fields + 3) * depth
-    corners += [(base + thick - 3 + j) * W for j in range(3)]
-    corners += [(base + thick + thick - 3 + j) * W for j in range(3)]
-    corners += [(base + 2 * thick + thick - 2 + j) * W for j in range(2)]
+    corners = [edges.fluid["p", f, depth - 1] for f in range(fields)]
+    corners += [edges.fluid["vel", c, depth - 1] for c in range(3)]
+    corners += list(edges.outer.values())
     n = 0
-    for m in corners:
-        out[n : n + W] = yl[m : m + W]
-        out[n + W : n + 2 * W] = yr[m : m + W]
+    for sl in corners:
+        reach = sl.stop - sl.start
+        out[n + W - reach : n + W] = yl[sl]
+        out[n + W : n + W + reach] = yr[sl]
         n = n + 2 * W
     for reach, buf, j in ((2, a1, 2), (1, a2, 1)):
         size = rows + 2 * reach
@@ -272,27 +287,57 @@
     return jnp.where(h > 0.0, DAMPING / jnp.where(h > 0.0, diagonal, 1.0), 0.0)
 
 
+def plan(blocks, owner, target, place, meta, idx):
+    rows = target.shape[1]
+    me = lax.axis_index("blk")
+    row = lax.broadcasted_iota(jnp.int32, (rows, rows), 0)
+    lane = lax.broadcasted_iota(jnp.int32, (rows, rows), 1)
+    owner = owner[...].astype(F32)
+    column = jnp.where(row == lane, jnp.broadcast_to(owner, (rows, rows)), 0.0)
+    column = jnp.sum(column, axis=1, keepdims=True)
+    idx[...] = owner * rows + target[...].astype(F32)
+    before = jnp.where((column == owner) & (row < lane), 1.0, 0.0)
+    rank = jnp.sum(before, axis=0, keepdims=True)
+    n = lax.broadcasted_iota(jnp.int32, (blocks * CHUNK, rows), 0)
+    slot = n % CHUNK
+    second = slot >= CAP
+    named = n // CHUNK - jnp.where(second, 0, 1)
+    at_rank = (slot - jnp.where(second, CAP, 0)).astype(F32)
+    hot = jnp.where((owner == named.astype(F32)) & (rank == at_rank), 1.0, 0.0)
+    hot = jnp.where(slot < 2 * CAP, hot, 0.0)
+    place[...] = hot
+    targets = jnp.broadcast_to((target[...] + 1).astype(F32), (8, rows))
+    lanes = lax.dot_general(
+        targets, hot, (((1,), (1,)), ((), ())), precision=HIGHEST, preferred_element_type=F32
+    )
+    row = lax.broadcasted_iota(jnp.int32, (8, 4 * CHUNK), 0)
+    lane = lax.broadcasted_iota(jnp.int32, (8, 4 * CHUNK), 1)
+    for j in range(blocks):
+        group = lanes[:, j // 4 * 4 * CHUNK : (j // 4 + 1) * 4 * CHUNK]
+        group = jnp.where(lane // CHUNK == j % 4, group, 0.0)
+        group = pltpu.roll(group, lax.rem(me - j + 4 * blocks, 4) * CHUNK, 1)
+        meta[j] = jnp.where(row == me // 4, group, 0.0)
+
+
 def inner_kernel(
-    blocks, spans, spread, jacobian, p, src, vel, t, heat, k, yl, yr, *outs
+    blocks, spans, edges, spread, jacobian, owner, target, p, src, vel, yl, yr, *outs
 ):
-    p0, s0, v0, w0, p1, p2, p3, te, he, so, ti, tb, sqi, dg, ws, ta, tc, qa, qc = outs
+    p0, s0, v0, w0, p1, p2, p3, place, meta, idx = outs
+    plan(blocks, owner, target, place, meta, idx)
     fields, depth, rows, z = p.shape
-    thick = t.shape[0]
     here = Place(rows, blocks, spans)
     ext = here.ext
     fluid = Fluid(spread, jacobian, fields)
     inside = here.inside(z)
-    first = 0
-    for buf, ref in ((p0, p), (s0, src), (v0, vel)):
+    for name, buf, ref in (("p", p0, p), ("src", s0, src), ("vel", v0, vel)):
         for f in range(ref.shape[0]):
             for i in range(depth):
 
                 def store(sl, x, buf=buf, f=f, i=i):
                     buf[f, i, sl] = x
 
-                n = ((first + f) * depth + i) * W
-                here.fill(store, ref[f, i], rows_at(yl, n, W), rows_at(yr, n, W))
-        first = first + ref.shape[0]
+                sl = edges.fluid[name, f, i]
+                here.fill(store, ref[f, i], yl[sl], yr[sl])
     for i in range(depth):
         us = v0[0, i, ext] + v0[1, i, ext] + v0[2, i, ext]
         for f in range(fields):
@@ -310,15 +355,21 @@
             )
             for f in range(fields):
                 new[f, i - level - 1, ext] = got[f][1]
-    base = (2 * fields + 3) * depth
-    for j, (buf, ref, scale) in enumerate(((te, t, 1.0), (he, k, 0.5), (so, heat, 1.0))):
+
+
+def inner_solid_kernel(blocks, spans, edges, fields, t, heat, k, yl, yr, *refs):
+    te, he, so, ti, tb, sqi, dg, ws, ta, tc, qa, qc = refs
+    thick, rows, z = t.shape
+    here = Place(rows, blocks, spans)
+    ext = here.ext
+    for name, buf, ref, scale in (("t", te, t, 1.0), ("k", he, k, 0.5), ("heat", so, heat, 1.0)):
         for i in range(thick):
 
             def store(sl, x, buf=buf, i=i, scale=scale):
                 buf[i, sl] = scale * x
 
-            n = (base + j * thick + i) * W
-            here.fill(store, ref[i], yl[n : n + W], yr[n : n + W])
+            sl = edges.solid[name, i]
+            here.fill(store, ref[i], yl[sl], yr[sl])
     for i in range(1, thick - 1):
         h = he[i, ext]
         diagonal = 6.0 * h + around(he, i, ext)
@@ -353,9 +404,9 @@
 
 
 def cone_kernel(blocks, spans, sent, spread, jacobian, *refs):
-    p0, s0, v0, w0, p1, p2, _, te, he, so, xe, xn, coef, idx = refs[:14]
-    back, parts, first, sq, c2, c3, sl_ = refs[14:21]
-    l0, d1, d2, vm, wm, n1, n2 = refs[21:]
+    p0, s0, v0, w0, p1, p2, _, te, he, so, xe, xn, coef, hot, meta = refs[:15]
+    back, parts, first, sq, c2, c3, sl_ = refs[15:22]
+    l0, d1, d2, vm, wm, n1, n2 = refs[22:]
     fields = p0.shape[0]
     rows, z = coef.shape[1], coef.shape[2]
     here = Place(rows, blocks, spans)
@@ -461,10 +512,9 @@
         first[f] = new
         sq[f : f + 1] = jnp.sum(res * res, axis=0, keepdims=True)
     flux = coef[0] * first[fields - 1]
-    n = lax.broadcasted_iota(jnp.int32, (blocks * 2 * rows, rows), 0)
-    key = n // (2 * rows) * rows + n % (2 * rows) - rows
-    hot = jnp.where(key == idx[...], 1.0, 0.0)
-    parts[...] = jnp.dot(hot, flux, precision=HIGHEST, preferred_element_type=F32)
+    parts[...] = jnp.dot(hot[...], flux, precision=HIGHEST, preferred_element_type=F32)
+    for j in range(blocks):
+        parts[j * CHUNK + 2 * CAP : (j + 1) * CHUNK] = meta[j]
     n = 0
     for buf, count in ((te, 4), (he, 4), (so, 3)):
         for i in range(count):
@@ -648,9 +698,19 @@
 
 def surface_kernel(blocks, arrived, surface, yf, yb):
     rows = surface.shape[0] // 2
-    whole = arrived[0]
+    meta = arrived[0, 2 * CAP :]
     for j in range(1, blocks):
-        whole = whole + arrived[j]
+        meta = meta + arrived[j, 2 * CAP :]
+    row = lax.broadcasted_iota(jnp.int32, (2 * rows, 4 * CHUNK), 0)
+    slot = lax.broadcasted_iota(jnp.int32, (2 * rows, 4 * CHUNK), 1) % CHUNK
+    row = row + 1 - jnp.where(slot < CAP, 0, rows)
+    row = jnp.where((row >= 1) & (row <= rows), row, -1).astype(F32)
+    whole = None
+    for j in range(0, blocks, 4):
+        sent = jnp.concatenate([arrived[j + m] for m in range(4)], axis=0)
+        hot = jnp.where(row == meta[j // 4 : j // 4 + 1], 1.0, 0.0)
+        got = jnp.dot(hot, sent, precision=HIGHEST, preferred_element_type=F32)
+        whole = got if whole is None else whole + got
     surface[...] = whole
     yf[:W] = whole[rows - W : rows]
     yf[W:] = whole[2 * rows - W :]
@@ -717,10 +777,10 @@
 
 def return_kernel(blocks, arrived, idx, coef, added, sq):
     rows = added.shape[0]
-    row = lax.broadcasted_iota(jnp.int32, (rows, rows), 0)
+    row = lax.broadcasted_iota(jnp.int32, (rows, rows), 0).astype(F32)
     taken, squares = None, None
     for j in range(blocks):
-        hot = jnp.where(idx[...] - j * rows == row, 1.0, 0.0)
+        hot = jnp.where(idx[...] - float(j * rows) == row, 1.0, 0.0)
         got = lax.dot_general(
             hot,
             arrived[j, :rows],
@@ -767,14 +827,14 @@
     def behind(x, axis):
         return lax.ppermute(x, axis, backward[axis])
 
-    idx = tile_owner[0, :, 0] * rows + tile_target[0]
-    row_idx = idx[None, :]
-    yrows = ((2 * fields + 3) * depth + 3 * thick) * W
+    edges = Edges(fields, depth, thick)
     inputs = [p, src, vel, t, heat, k]
-    p, src, vel, t, heat, k, yf, yb, xf = call(
-        early_kernel,
+    p, src, vel, t, heat, k, yf, yb, xf, zf, zb = call(
+        functools.partial(early_kernel, edges),
         held(*[x.shape for x in inputs])
-        + [(yrows, z), (yrows, z), ((fields + 16) * rows, z)],
+        + [(edges.size, z)] * 2
+        + [((fields + 16) * rows, z)]
+        + [(edges.solid_size, z)] * 2,
         [pltpu.SemaphoreType.DMA((6,))],
         [HBM] * 6,
         *[pltpu.with_memory_space_constraint(x, pltpu.HBM) for x in inputs],
@@ -783,11 +843,11 @@
     xe = ahead(xf, "blk")
     sent_ahead = Arrivals((fields + 11) * 2 * W, rows, fields, (2, 1, 0))
     (out,) = call(
-        functools.partial(ahead_kernel, blocks, spans),
+        functools.partial(ahead_kernel, blocks, spans, edges),
         [(sent_ahead.size(), z)],
         [(fields, 4, buf, z), (fields, 3, buf, z), (fields, 2, buf, z), (fields, 3, buf, z)]
         + [(3, 3, buf, z), (fields, 3, buf, z)],
-        [SMEM] * 2 + [VMEM] * 6,
+        [SMEM] * 2 + [VMEM] * 5,
         diffusion,
         jacobian,
         p,
@@ -795,39 +855,50 @@
         vel,
         yl,
         yr,
-        xe,
         cost=COSTS[1],
     )
     xn = ahead(out, "blk")
     full = (fields, depth, buf, z)
     part = [(fields, depth - 2 * (level + 1), buf, z) for level in range(3)]
     solid = (thick, buf, z)
-    p0, s0, v0, w0, p1, p2, p3, te, he, so, ti, tb, sqi, dg, ws = call(
-        functools.partial(inner_kernel, blocks, spans),
-        held(full, full, (3, depth, buf, z), full, *part, solid, solid, solid)
-        + held((3, 4, buf, z), (thick - 2 * SWEEPS, rows, z), (8, z), solid, solid),
-        [solid] * 4,
-        [SMEM] * 2 + [VMEM] * 8,
+    p0, s0, v0, w0, p1, p2, p3, place, meta, idx = call(
+        functools.partial(inner_kernel, blocks, spans, edges),
+        held(full, full, (3, depth, buf, z), full, *part)
+        + held((blocks * CHUNK, rows), (blocks, 8, z), (1, rows)),
+        [],
+        [SMEM] * 2 + [VMEM] * 7,
         diffusion,
         jacobian,
+        tile_owner.reshape(1, rows),
+        tile_target,
         p,
         src,
         vel,
+        yl,
+        yr,
+        cost=COSTS[2],
+    )
+    zl, zr = ahead(zf, "span"), behind(zb, "span")
+    te, he, so, ti, tb, sqi, dg, ws = call(
+        functools.partial(inner_solid_kernel, blocks, spans, edges, fields),
+        held(solid, solid, solid, (3, 4, buf, z), (thick - 2 * SWEEPS, rows, z), (8, z), solid, solid),
+        [solid] * 4,
+        [VMEM] * 5,
         t,
         heat,
         k,
-        yl,
-        yr,
+        zl,
+        zr,
         cost=COSTS[2],
     )
     sent_back = Arrivals(11 * tall, rows, fields, (3, 2, 1, 0))
     flat = (fields, buf, z)
     back, parts, first, sq, c2, c3, sl_ = call(
         functools.partial(cone_kernel, blocks, spans, sent_ahead),
-        [(sent_back.size(), z), (blocks * 2 * rows, z)]
+        [(sent_back.size(), z), (blocks * CHUNK, z)]
         + held((fields, rows, z), (8, z), flat, (fields, 2, buf, z), (11, tall, z)),
         [flat] * 3 + [(3, buf, z), (fields, tall, z)] + [flat] * 2,
-        [SMEM] * 2 + [VMEM] * 14,
+        [SMEM] * 2 + [VMEM] * 15,
         diffusion,
         jacobian,
         p0,
@@ -843,11 +914,12 @@
         xe,
         xn,
         wall_coefficient,
-        row_idx,
+        place,
+        meta,
         cost=COSTS[3],
     )
     xr = behind(back, "blk")
-    arrived = lax.all_to_all(parts.reshape(blocks, 2 * rows, z), "blk", 0, 0)
+    arrived = lax.all_to_all(parts.reshape(blocks, CHUNK, z), "blk", 0, 0)
     surface, yf, yb = call(
         functools.partial(surface_kernel, blocks),
         [(2 * rows, z), (2 * W, z), (2 * W, z)],
@@ -921,7 +993,7 @@
         [],
         [VMEM] * 3,
         arrived,
-        row_idx,
+        idx,
         wall_coefficient,
     )
     step = 1

time: 75.7 us -> 71.6 us (0.946)
  waiting for transfers between devices: 19.1 us -> 11.7 us
  starting transfers between devices: 8.2 us -> 11.7 us
    ppermute x4 -> x5, waiting for transfers between devices: 16.3 us -> 7.43 us  [ahead(): return lax.ppermute(x, axis, forward[axis])]
    all_to_all x1, blocking collectives: 19.2 us -> 16.1 us  [shards(): arrived = lax.all_to_all(parts.reshape(blocks, CHUNK, z), 'blk', 0, 0)]
    all_to_all x1, blocking collectives: 11.4 us -> 14.1 us  [shards(): arrived = lax.all_to_all(out, 'blk', 0, 0)]
    ppermute x4 -> x5, starting transfers between devices: 3.11 us -> 5.56 us  [ahead(): return lax.ppermute(x, axis, forward[axis])]
    ppermute x3 -> x4, starting transfers between devices: 3.53 us -> 5.01 us  [behind(): return lax.ppermute(x, axis, backward[axis])]
    ppermute x3 -> x4, waiting for transfers between devices: 0.92 us -> 1.96 us  [behind(): return lax.ppermute(x, axis, backward[axis])]
    pallas_call x9 -> x10, Pallas kernels: 14.7 us -> 14.9 us  [call(): pl.pallas_call(kernel, out_shape=[jax.ShapeDtypeStruct(s, F32) if isinsta...]
  transfers between devices with their start and end apart: 9 -> 11, of which waited for: 6 -> 6; matrix products, arithmetic and copies ran while one was open for 2% -> 2% of each run, Pallas kernels for 10% -> 13%
where the time goes in v3:
time: 71.6 us; the launch traced here: 71.3 us
  blocking collectives  30.2 us (42%)
  Pallas kernels  14.9 us (21%)
  starting transfers between devices  11.7 us (16%)
  waiting for transfers between devices  11.7 us (16%)
  other arithmetic  1.97 us (3%)
  between operations  0.78 us (1%)
    all_to_all x1, blocking collectives, shards(): arrived = lax.all_to_all(parts.reshape(blocks, CHUNK, z), 'blk', 0, 0)  16.1 us
    pallas_call x10, Pallas kernels, call(): pl.pallas_call(kernel, out_shape=[jax.ShapeDtypeStruct(s, F32) if isinsta...  14.9 us
    all_to_all x1, blocking collectives, shards(): arrived = lax.all_to_all(out, 'blk', 0, 0)  14.1 us
    ppermute x5, waiting for transfers between devices, ahead(): return lax.ppermute(x, axis, forward[axis])  7.43 us
    ppermute x5, starting transfers between devices, ahead(): return lax.ppermute(x, axis, forward[axis])  5.56 us
    ppermute x4, starting transfers between devices, behind(): return lax.ppermute(x, axis, backward[axis])  5.01 us
    ppermute x2, waiting for transfers between devices, shards(): sq = sq + lax.ppermute(sq, 'span', [(i, i ^ step) for i in range(spans)])  2.3 us
    ppermute x4, waiting for transfers between devices, behind(): return lax.ppermute(x, axis, backward[axis])  1.96 us
  transfers between devices with their start and end apart: 11, of which 6 were waited for; matrix products, arithmetic and copies ran while one was open for 2% of the time, Pallas kernels for 13%

profile of v3, /device:TPU:0, one launch (start us, length us, event | category | flops | bytes accessed | tf_op | source)
XLA Modules:
  0.0 71.3 jit_solution(17692013125645114719)
XLA Ops:
  0.6 0.0 copy-start
  0.6 0.0 copy-start.2
  0.7 1.8 %shard_map.139 = (f32[5,8,32,128]{3,2,1,0:T(8,128)S(1)}, f32[5,8,32,128]{3,2,1,0:T(8,128)S(1)}, f32[3,8,32,128]{3,2,1,0:T(8,128)S(1)}, f32[16,32,128]{2,1,0:T(8,...) custom-call(f32[5,8,32,128]{3,2,1,0:T(8,128)} %refs_0_.1, ...), custom_call_target="tpu_custom_call" | custom-call | flops 1000000 | bytes 3000000 | tf_op jit(solution)/shard_map/pallas_call | solution.py:30
  2.5 0.5 collective-permute-start
  3.0 2.0 %collective-permute-start.1 = (f32[384,128]{1,0:T(8,128)S(1)}, f32[384,128]{1,0:T(8,128)S(1)}, u32[]{:S(2)}, u32[]{:S(2)}) collective-permute-start(f32[384,128]{1,0:T(8,128)S(1)} %get-tuple-element.70), channel_id=1, source_target_pairs={{1,0},{2,1},{3,2},{0,3},{5,4},{6,5},{7,6},{4,7},{9,8},{10,9},{11,1... | collective-permute-start | bytes 589832 | tf_op jit(solution)/shard_map/ppermute | solution.py:828
  5.0 2.2 %collective-permute-start.4 = (f32[672,128]{1,0:T(8,128)S(1)}, f32[672,128]{1,0:T(8,128)S(1)}, u32[]{:S(2)}, u32[]{:S(2)}) collective-permute-start(f32[672,128]{1,0:T(8,128)S(1)} %get-tuple-element.86), channel_id=1, source_target_pairs={{0,4},{4,8},{8,12},{12,16},{16,20},{20,24},{24,28},{28,0},{1,5},{5... | collective-permute-start | bytes 1032200 | tf_op jit(solution)/shard_map/ppermute | solution.py:825
  7.2 1.1 %collective-permute-done.yl = f32[384,128]{1,0:T(8,128)S(1)} collective-permute-done((f32[384,128]{1,0:T(8,128)S(1)}, f32[384,128]{1,0:T(8,128)S(1)}, u32[]{:S(2)}, u32[]{:S(2)}) %collective-permute-start) | collective-permute-done | bytes 196640 | tf_op jit(solution)/shard_map/ppermute | solution.py:825
  8.3 1.9 %collective-permute-done.1.yr = f32[384,128]{1,0:T(8,128)S(1)} collective-permute-done((f32[384,128]{1,0:T(8,128)S(1)}, f32[384,128]{1,0:T(8,128)S(1)}, u32[]{:S(2)}, u32[]{:S(2)}) %collective-permute-start.1) | collective-permute-done | bytes 196640 | tf_op jit(solution)/shard_map/ppermute | solution.py:828
  10.2 0.0 copy-done
  10.2 0.0 copy-done.2
  10.2 0.0 copy-start.3
  10.2 1.4 %shard_map.142 = f32[638,128]{1,0:T(8,128)S(1)} custom-call(f32[5]{0:T(128)S(1)} %copy-done.2, f32[5,5]{1,0:T(8,128)S(1)} %copy-done, f32[5,8,32,128]{3,2,1,0:T(8,128)S(1)} %get-tuple-element.66.p, f32[5,8,32,128]{3,2,1,0:T(8,128)S(1)} %get-tuple-element.67.src, f32[3,8,32,128]{3,2,1,0:T(8,128)S(1)} %get-tuple-element.68.vel, ...), custom_call_target="tpu_custom_call" | custom-call | flops 30000000 | bytes 90000000 | tf_op jit(solution)/shard_map/pallas_call | solution.py:30
  11.6 1.5 %collective-permute-start.5 = (f32[638,128]{1,0:T(8,128)S(1)}, f32[638,128]{1,0:T(8,128)S(1)}, u32[]{:S(2)}, u32[]{:S(2)}) collective-permute-start(f32[638,128]{1,0:T(8,128)S(1)} %shard_map.142), channel_id=1, source_target_pairs={{0,4},{4,8},{8,12},{12,16},{16,20},{20,24},{24,28},{28,0},{1,5},{5... | collective-permute-start | bytes 979976 | tf_op jit(solution)/shard_map/ppermute | solution.py:825
  13.1 0.8 %collective-permute-start.2 = (f32[176,128]{1,0:T(8,128)S(1)}, f32[176,128]{1,0:T(8,128)S(1)}, u32[]{:S(2)}, u32[]{:S(2)}) collective-permute-start(f32[176,128]{1,0:T(8,128)S(1)} %get-tuple-element.81), channel_id=1, source_target_pairs={{0,1},{1,2},{2,3},{3,0},{4,5},{5,6},{6,7},{7,4},{8,9},{9,10},{10,1... | collective-permute-start | bytes 270344 | tf_op jit(solution)/shard_map/ppermute | solution.py:825
  13.9 1.1 %collective-permute-start.3 = (f32[176,128]{1,0:T(8,128)S(1)}, f32[176,128]{1,0:T(8,128)S(1)}, u32[]{:S(2)}, u32[]{:S(2)}) collective-permute-start(f32[176,128]{1,0:T(8,128)S(1)} %get-tuple-element.82), channel_id=1, source_target_pairs={{1,0},{2,1},{3,2},{0,3},{5,4},{6,5},{7,6},{4,7},{9,8},{10,9},{11,1... | collective-permute-start | bytes 270344 | tf_op jit(solution)/shard_map/ppermute | solution.py:828
  15.1 2.2 %collective-permute-done.2.yl = f32[176,128]{1,0:T(8,128)S(1)} collective-permute-done((f32[176,128]{1,0:T(8,128)S(1)}, f32[176,128]{1,0:T(8,128)S(1)}, u32[]{:S(2)}, u32[]{:S(2)}) %collective-permute-start.2) | collective-permute-done | bytes 90144 | tf_op jit(solution)/shard_map/ppermute | solution.py:825
  17.3 0.0 collective-permute-done.3.yr
  17.3 1.4 %shard_map.141 = (f32[16,56,128]{2,1,0:T(8,128)S(1)}, f32[16,56,128]{2,1,0:T(8,128)S(1)}, f32[16,56,128]{2,1,0:T(8,128)S(1)}, f32[3,4,56,128]{3,2,1,0:T(8,128)S(...) custom-call(f32[16,32,128]{2,1,0:T(8,128)S(1)} %get-tuple-element.78, ...), custom_call_target="tpu_custom_call" | custom-call | flops 10000 | bytes 30000 | tf_op jit(solution)/shard_map/pallas_call | solution.py:30
  18.7 0.0 copy-start.1
  18.7 0.0 copy-done.3
  18.8 0.0 copy-done.4
  18.8 2.5 %shard_map.140 = (f32[5,8,56,128]{3,2,1,0:T(8,128)S(1)}, f32[5,8,56,128]{3,2,1,0:T(8,128)S(1)}, f32[3,8,56,128]{3,2,1,0:T(8,128)S(1)}, f32[5,8,56,128]{3,2,1,0:T...) custom-call(f32[5]{0:T(128)S(1)} %copy-done.2, ...), custom_call_target="tpu_custom_call" | custom-call | flops 10000 | bytes 30000 | tf_op jit(solution)/shard_map/pallas_call | solution.py:30
  21.2 0.0 collective-permute-done.4.refs_10_
  21.2 4.1 %collective-permute-done.5.refs_11_ = f32[638,128]{1,0:T(8,128)S(1)} collective-permute-done((f32[638,128]{1,0:T(8,128)S(1)}, f32[638,128]{1,0:T(8,128)S(1)}, u32[]{:S(2)}, u32[]{:S(2)}) %collective-permute-start.5) | collective-permute-done | bytes 326688 | tf_op jit(solution)/shard_map/ppermute | solution.py:825
  25.4 0.0 copy-done.1
  25.4 1.8 %shard_map.143 = (f32[1140,128]{1,0:T(8,128)S(1)}, f32[256,128]{1,0:T(8,128)S(1)}, f32[5,32,128]{2,1,0:T(8,128)S(1)}, f32[8,128]{1,0:T(8,128)S(1)}, f32[5,56,128...) custom-call(f32[5]{0:T(128)S(1)} %copy-done.2, f32[5,5]{1,0:T(8,128)S(1)} %copy-done, ...), custom_call_target="tpu_custom_call" | custom-call | flops 2000000 | bytes 6000000 | tf_op jit(solution)/shard_map/pallas_call | solution.py:30
  27.2 1.8 %collective-permute-start.6 = (f32[1140,128]{1,0:T(8,128)S(1)}, f32[1140,128]{1,0:T(8,128)S(1)}, u32[]{:S(2)}, u32[]{:S(2)}) collective-permute-start(f32[1140,128]{1,0:T(8,128)S(1)} %get-tuple-element.93), channel_id=1, source_target_pairs={{4,0},{8,4},{12,8},{16,12},{20,16},{24,20},{28,24},{0,28},{5,1},{9... | collective-permute-start | bytes 1751048 | tf_op jit(solution)/shard_map/ppermute | solution.py:828
  29.0 16.1 %all_to_all.10.arrived = f32[8,32,128]{2,1,0:T(8,128)S(1)} all-to-all(f32[8,32,128]{2,1,0:T(8,128)S(1)} %bitcast.6), channel_id=1, replica_groups=mesh['blk'=8,'span'=4] {'blk'}, dimensions={0} | all-to-all | bytes 262144 | tf_op jit(solution)/shard_map/all_to_all | solution.py:922
  45.1 0.2 shard_map.144
  45.3 0.1 collective-permute-start.8
  45.4 0.5 collective-permute-start.7
  45.9 0.0 collective-permute-done.6.refs_11_.xb
  45.9 3.0 %shard_map.145 = (f32[5,8,32,128]{3,2,1,0:T(8,128)}, f32[8,128]{1,0:T(8,128)S(1)}) custom-call(f32[5]{0:T(128)S(1)} %copy-done.2, f32[5,5]{1,0:T(8,128)S(1)} %copy-done, f32[5,8,56,128]{3,2,1,0:T(8,128)S(1)} %get-tuple-element.71.refs_0_, f32[5,8,56,128]{3,2,1,0:T(8,128)S(1)} %get-tuple-element.72.refs_1_, f32[3,8,56,128]{3,2,1,0:T(8,128)S(1)} %get-tuple-element.73.refs_2_, ...), custom_call_target="tpu_custom_call" | custom-call | flops 3000000 | bytes 9000000 | tf_op jit(solution)/shard_map/pallas_call | solution.py:30
  48.9 1.1 %shard_map.146 = (f32[16,32,128]{2,1,0:T(8,128)S(1)}, f32[7,32,128]{2,1,0:T(8,128)S(1)}, f32[8,128]{1,0:T(8,128)S(1)}, f32[2,5,56,128]{3,2,1,0:T(8,128)S(1)}, f3...) custom-call(f32[16,56,128]{2,1,0:T(8,128)S(1)} %get-tuple-element.83.refs_7_.te, ...), custom_call_target="tpu_custom_call" | custom-call | flops 3000000 | bytes 9000000 | tf_op jit(solution)/shard_map/pallas_call | solution.py:30
  50.0 0.0 copy-start.5
  50.0 0.0 collective-permute-done.8.yr
  50.0 0.0 collective-permute-done.7.yl
  50.0 1.4 %shard_map.147 = (f32[16,32,128]{2,1,0:T(8,128)}, f32[8,40,128]{2,1,0:T(8,128)S(1)}) custom-call(f32[64,128]{1,0:T(8,128)S(1)} %get-tuple-element.97.surface, f32[8,128]{1,0:T(8,128)S(1)} %collective-permute-done.7.yl, f32[8,128]{1,0:T(8,128)S(1)} %collective-permute-done.8.yr, f32[2,5,56,128]{3,2,1,0:T(8,128)S(1)} %get-tuple-element.105.rh, ...), custom_call_target="tpu_custom_call" | custom-call | flops 1000000 | bytes 3000000 | tf_op jit(solution)/shard_map/pallas_call | solution.py:30
  51.4 14.1 %all_to_all.11.arrived = f32[8,40,128]{2,1,0:T(8,128)S(1)} all-to-all(f32[8,40,128]{2,1,0:T(8,128)S(1)} %get-tuple-element.112), channel_id=1, replica_groups=mesh['blk'=8,'span'=4] {'blk'}, dimensions={0} | all-to-all | bytes 327680 | tf_op jit(solution)/shard_map/all_to_all | solution.py:989
  65.6 0.4 shard_map.148
  65.9 0.0 collective-permute-start.9
  65.9 1.2 %collective-permute-done.9 = f32[8,128]{1,0:T(8,128)S(1)} collective-permute-done((f32[8,128]{1,0:T(8,128)S(1)}, f32[8,128]{1,0:T(8,128)S(1)}, u32[]{:S(2)}, u32[]{:S(2)}) %collective-permute-start.9) | collective-permute-done | bytes 4128 | tf_op jit(solution)/shard_map/ppermute | solution.py:1001
  67.1 1.2 %collective-permute-start.10 = (f32[8,128]{1,0:T(8,128)S(1)}, f32[8,128]{1,0:T(8,128)S(1)}, u32[]{:S(2)}, u32[]{:S(2)}) collective-permute-start(f32[8,128]{1,0:T(8,128)S(1)} %add.14), channel_id=1, source_target_pairs={{0,2},{1,3},{2,0},{3,1},{4,6},{5,7},{6,4},{7,5},{8,10},{9,11},{10,... | collective-permute-start | bytes 12296 | tf_op jit(solution)/shard_map/ppermute | solution.py:1001
  68.2 1.3 %fusion = f32[5,8,32,128]{3,2,1,0:T(8,128)} fusion(f32[5,8,32,128]{3,2,1,0:T(8,128)} %get-tuple-element.96, f32[32,128]{1,0:T(8,128)S(1)} %get-tuple-element.114), kind=kLoop, calls=%fused_computation.1 | loop fusion | flops 4096 | bytes 49152 | tf_op jit(solution)/shard_map/scatter-add | solution.py:1003
  69.6 1.1 %collective-permute-done.10 = f32[8,128]{1,0:T(8,128)S(1)} collective-permute-done((f32[8,128]{1,0:T(8,128)S(1)}, f32[8,128]{1,0:T(8,128)S(1)}, u32[]{:S(2)}, u32[]{:S(2)}) %collective-permute-start.10) | collective-permute-done | bytes 4128 | tf_op jit(solution)/shard_map/ppermute | solution.py:1001
  70.7 0.1 slice_reduce_fusion
  70.8 0.0 copy-done.5
  70.8 0.5 multiply_sqrt_fusion
  (3 shorter events, 0.0 us)
Async XLA Ops:
  0.6 9.6 %copy-start = (f32[5,5]{1,0:T(8,128)S(1)}, f32[5,5]{1,0:T(8,128)}, u32[]{:S(2)}) copy-start(f32[5,5]{1,0:T(8,128)} %jacobian.7) | copy-start | bytes 304
  0.6 9.6 %copy-start.2 = (f32[5]{0:T(128)S(1)}, f32[5]{0:T(128)}, u32[]{:S(2)}) copy-start(f32[5]{0:T(128)} %spread.7) | copy-start | bytes 64
  2.5 5.8 %collective-permute-start = (f32[384,128]{1,0:T(8,128)S(1)}, f32[384,128]{1,0:T(8,128)S(1)}, u32[]{:S(2)}, u32[]{:S(2)}) collective-permute-start(f32[384,128]{1,0:T(8,128)S(1)} %get-tuple-element.69), channel_id=1, source_target_pairs={{0,1},{1,2},{2,3},{3,0},{4,5},{5,6},{6,7},{7,4},{8,9},{9,10},{10,1... | collective-permute-start | bytes 589832 | tf_op jit(solution)/shard_map/ppermute | solution.py:825
  3.0 7.2 %collective-permute-start.1 = (f32[384,128]{1,0:T(8,128)S(1)}, f32[384,128]{1,0:T(8,128)S(1)}, u32[]{:S(2)}, u32[]{:S(2)}) collective-permute-start(f32[384,128]{1,0:T(8,128)S(1)} %get-tuple-element.70), channel_id=1, source_target_pairs={{1,0},{2,1},{3,2},{0,3},{5,4},{6,5},{7,6},{4,7},{9,8},{10,9},{11,1... | collective-permute-start | bytes 589832 | tf_op jit(solution)/shard_map/ppermute | solution.py:828
  5.0 16.2 %collective-permute-start.4 = (f32[672,128]{1,0:T(8,128)S(1)}, f32[672,128]{1,0:T(8,128)S(1)}, u32[]{:S(2)}, u32[]{:S(2)}) collective-permute-start(f32[672,128]{1,0:T(8,128)S(1)} %get-tuple-element.86), channel_id=1, source_target_pairs={{0,4},{4,8},{8,12},{12,16},{16,20},{20,24},{24,28},{28,0},{1,5},{5... | collective-permute-start | bytes 1032200 | tf_op jit(solution)/shard_map/ppermute | solution.py:825
  10.2 8.5 %copy-start.3 = (s32[1,32,1]{1,2,0:T(1,128)S(1)}, s32[1,32,1]{1,2,0:T(1,128)}, u32[]{:S(2)}) copy-start(s32[1,32,1]{1,2,0:T(1,128)} %param.23) | copy-start | bytes 388
  10.2 8.5 %copy-start.4 = (s32[1,32]{1,0:T(1,128)S(1)}, s32[1,32]{1,0:T(1,128)}, u32[]{:S(2)}) copy-start(s32[1,32]{1,0:T(1,128)} %target.1) | copy-start | bytes 388
  11.6 13.8 %collective-permute-start.5 = (f32[638,128]{1,0:T(8,128)S(1)}, f32[638,128]{1,0:T(8,128)S(1)}, u32[]{:S(2)}, u32[]{:S(2)}) collective-permute-start(f32[638,128]{1,0:T(8,128)S(1)} %shard_map.142), channel_id=1, source_target_pairs={{0,4},{4,8},{8,12},{12,16},{16,20},{20,24},{24,28},{28,0},{1,5},{5... | collective-permute-start | bytes 979976 | tf_op jit(solution)/shard_map/ppermute | solution.py:825
  13.1 4.1 %collective-permute-start.2 = (f32[176,128]{1,0:T(8,128)S(1)}, f32[176,128]{1,0:T(8,128)S(1)}, u32[]{:S(2)}, u32[]{:S(2)}) collective-permute-start(f32[176,128]{1,0:T(8,128)S(1)} %get-tuple-element.81), channel_id=1, source_target_pairs={{0,1},{1,2},{2,3},{3,0},{4,5},{5,6},{6,7},{7,4},{8,9},{9,10},{10,1... | collective-permute-start | bytes 270344 | tf_op jit(solution)/shard_map/ppermute | solution.py:825
  13.9 3.4 %collective-permute-start.3 = (f32[176,128]{1,0:T(8,128)S(1)}, f32[176,128]{1,0:T(8,128)S(1)}, u32[]{:S(2)}, u32[]{:S(2)}) collective-permute-start(f32[176,128]{1,0:T(8,128)S(1)} %get-tuple-element.82), channel_id=1, source_target_pairs={{1,0},{2,1},{3,2},{0,3},{5,4},{6,5},{7,6},{4,7},{9,8},{10,9},{11,1... | collective-permute-start | bytes 270344 | tf_op jit(solution)/shard_map/ppermute | solution.py:828
  18.7 6.7 %copy-start.1 = (f32[1,32,128]{2,1,0:T(8,128)S(1)}, f32[1,32,128]{2,1,0:T(8,128)}, u32[]{:S(2)}) copy-start(f32[1,32,128]{2,1,0:T(8,128)} %coef.1) | copy-start | bytes 49156
  27.2 18.7 %collective-permute-start.6 = (f32[1140,128]{1,0:T(8,128)S(1)}, f32[1140,128]{1,0:T(8,128)S(1)}, u32[]{:S(2)}, u32[]{:S(2)}) collective-permute-start(f32[1140,128]{1,0:T(8,128)S(1)} %get-tuple-element.93), channel_id=1, source_target_pairs={{4,0},{8,4},{12,8},{16,12},{20,16},{24,20},{28,24},{0,28},{5,1},{9... | collective-permute-start | bytes 1751048 | tf_op jit(solution)/shard_map/ppermute | solution.py:828
  45.3 4.6 %collective-permute-start.8 = (f32[8,128]{1,0:T(8,128)S(1)}, f32[8,128]{1,0:T(8,128)S(1)}, u32[]{:S(2)}, u32[]{:S(2)}) collective-permute-start(f32[8,128]{1,0:T(8,128)S(1)} %get-tuple-element.98), channel_id=1, source_target_pairs={{1,0},{2,1},{3,2},{0,3},{5,4},{6,5},{7,6},{4,7},{9,8},{10,9},{11,1... | collective-permute-start | bytes 12296 | tf_op jit(solution)/shard_map/ppermute | solution.py:828
  45.4 4.6 %collective-permute-start.7 = (f32[8,128]{1,0:T(8,128)S(1)}, f32[8,128]{1,0:T(8,128)S(1)}, u32[]{:S(2)}, u32[]{:S(2)}) collective-permute-start(f32[8,128]{1,0:T(8,128)S(1)} %get-tuple-element.95.refs_12_._), channel_id=1, source_target_pairs={{0,1},{1,2},{2,3},{3,0},{4,5},{5,6},{6,7},{7,4},{8,9},{9,10},{10,1... | collective-permute-start | bytes 12296 | tf_op jit(solution)/shard_map/ppermute | solution.py:825
  50.0 20.9 %copy-start.5 = (f32[6]{0:T(128)S(1)}, f32[6]{0:T(128)}, u32[]{:S(2)}) copy-start(f32[6]{0:T(128)} %constant.41) | copy-start | bytes 76
  65.9 1.2 %collective-permute-start.9 = (f32[8,128]{1,0:T(8,128)S(1)}, f32[8,128]{1,0:T(8,128)S(1)}, u32[]{:S(2)}, u32[]{:S(2)}) collective-permute-start(f32[8,128]{1,0:T(8,128)S(1)} %get-tuple-element.116), channel_id=1, source_target_pairs={{0,1},{1,0},{2,3},{3,2},{4,5},{5,4},{6,7},{7,6},{8,9},{9,8},{10,11... | collective-permute-start | bytes 12296 | tf_op jit(solution)/shard_map/ppermute | solution.py:1001
  67.1 3.6 %collective-permute-start.10 = (f32[8,128]{1,0:T(8,128)S(1)}, f32[8,128]{1,0:T(8,128)S(1)}, u32[]{:S(2)}, u32[]{:S(2)}) collective-permute-start(f32[8,128]{1,0:T(8,128)S(1)} %add.14), channel_id=1, source_target_pairs={{0,2},{1,3},{2,0},{3,1},{4,6},{5,7},{6,4},{7,5},{8,10},{9,11},{10,... | collective-permute-start | bytes 12296 | tf_op jit(solution)/shard_map/ppermute | solution.py:1001

commit v4 on v3

--- a/solution.py
+++ b/solution.py
@@ -137,39 +137,57 @@
     def diagonal(self, f, us):
         return us + (6.0 * self.d[f] + self.jac[f][f])
 
-    def advance(self, cur, left, right, vel, w, src, sl, which=None):
-        u0, u1, u2 = vel
-        us = u0 + u1 + u2
-        centre = [cur(f, sl) for f in range(self.n)]
-        out = {}
-        for f in range(self.n) if which is None else which:
-            c = centre[f]
-            zm, zp = beside(c)
-            yp = cur(f, beyond(sl, 1))
-            near = (cur(f, beyond(sl, -1)) + yp) + (zm + zp)
-            if left is not None:
-                near = near + left(f)
-            res = u1 * yp + u2 * zp - self.diagonal(f, us) * c
-            if right is not None:
-                xp = right(f)
-                near = near + xp
-                res = res + u0 * xp
-            res = res + self.d[f] * near
-            for g in range(self.n):
-                if g != f:
-                    res = res - self.jac[f][g] * centre[g]
-            if src is not None:
-                res = res + src(f)
-            out[f] = (res, c + w(f) * res)
-        return out
+    def advance(self, cur, left, right, vel, w, src, rows, store):
+        for n in range(rows.start, rows.stop, 8):
+            sl = slice(n, n + 8)
+            u0, u1, u2 = (u(sl) for u in vel)
+            us = u0 + u1 + u2
+            centre = [cur(f, sl) for f in range(self.n)]
+            for f in range(self.n):
+                c = centre[f]
+                zm, zp = beside(c)
+                yp = cur(f, beyond(sl, 1))
+                near = (cur(f, beyond(sl, -1)) + yp) + (zm + zp)
+                if left is not None:
+                    near = near + left(f, sl)
+                res = u1 * yp + u2 * zp - self.diagonal(f, us) * c
+                if right is not None:
+                    xp = right(f, sl)
+                    near = near + xp
+                    res = res + u0 * xp
+                res = res + self.d[f] * near
+                for g in range(self.n):
+                    if g != f:
+                        res = res - self.jac[f][g] * centre[g]
+                if src is not None:
+                    res = res + src(f, sl)
+                store(f, sl, res, c + w(f, sl) * res)
 
 
 def at(ref, i):
     return lambda f, sl: ref[f, i, sl]
 
 
-def at_rows(ref, i, sl):
-    return lambda f: ref[f, i, sl]
+def flat(ref):
+    return lambda f, sl: ref[f, sl]
+
+
+def speeds(ref, i):
+    return [lambda sl, c=c: ref[c, i, sl] for c in range(3)]
+
+
+def into(ref, i):
+    def store(f, sl, _, value):
+        ref[f, i, sl] = value
+
+    return store
+
+
+def into_flat(ref):
+    def store(f, sl, _, value):
+        ref[f, sl] = value
+
+    return store
 
 
 def early_kernel(edges, *refs):
@@ -229,30 +247,22 @@
         for f in range(fields):
             wa[f, j, ext] = jnp.where(inside, DAMPING / fluid.diagonal(f, us), 0.0)
 
-    def step(old, i, new, j, shift):
-        last = j == 2
-        got = fluid.advance(
+    def step(old, i, store, j):
+        fluid.advance(
             at(old, i),
-            at_rows(old, i - 1, ext),
-            None if last else at_rows(old, i + 1, ext),
-            [va[c, j, ext] for c in range(3)],
-            at_rows(wa, j, ext),
-            at_rows(sa, j, ext),
+            at(old, i - 1),
+            None if j == 2 else at(old, i + 1),
+            speeds(va, j),
+            at(wa, j),
+            at(sa, j),
             ext,
+            store,
         )
-        for f in range(fields):
-            new(f, got[f][1])
-
-    def into(buf, j):
-        def store(f, x):
-            buf[f, j, ext] = x
-
-        return store
 
     for j in range(3):
-        step(a0, j + 1, into(a1, j), j, 0)
+        step(a0, j + 1, into(a1, j), j)
     for j in range(1, 3):
-        step(a1, j, into(a2, j - 1), j, 0)
+        step(a1, j, into(a2, j - 1), j)
     corners = [edges.fluid["p", f, depth - 1] for f in range(fields)]
     corners += [edges.fluid["vel", c, depth - 1] for c in range(3)]
     corners += list(edges.outer.values())
@@ -268,10 +278,13 @@
             out[n : n + size] = buf[f, j, at_place.reach(reach)]
             n = n + size
 
-    def last(f, x):
-        out[n + f * rows : n + (f + 1) * rows] = x[W : W + rows]
-
-    step(a2, 1, last, 2, 0)
+    def last(f, sl, _, value):
+        m = n + f * rows + sl.start - own.start
+        out[m : m + 8] = value
+
+    fluid.advance(
+        at(a2, 1), at(a2, 0), None, speeds(va, 2), at(wa, 2), at(sa, 2), own, last
+    )
 
 
 def around(buf, j, sl):
@@ -281,6 +294,13 @@
         + (buf[j, beyond(sl, -1)] + buf[j, beyond(sl, 1)])
         + (zm + zp)
     )
+
+
+def solid_diagonal(h_of, i, sl):
+    zm, zp = beside(h_of(i, sl))
+    near = (h_of(i - 1, sl) + h_of(i + 1, sl)) + (zm + zp)
+    near = near + (h_of(i, beyond(sl, -1)) + h_of(i, beyond(sl, 1)))
+    return 6.0 * h_of(i, sl) + near
 
 
 def solid_weight(h, diagonal):
@@ -344,20 +364,19 @@
             w0[f, i, ext] = jnp.where(inside, DAMPING / fluid.diagonal(f, us), 0.0)
     for level, (old, new) in enumerate(((p0, p1), (p1, p2), (p2, p3))):
         for i in range(level + 1, depth - 1 - level):
-            got = fluid.advance(
+            fluid.advance(
                 at(old, i - level),
-                at_rows(old, i - level - 1, ext),
-                at_rows(old, i - level + 1, ext),
-                [v0[c, i, ext] for c in range(3)],
-                at_rows(w0, i, ext),
-                at_rows(s0, i, ext),
+                at(old, i - level - 1),
+                at(old, i - level + 1),
+                speeds(v0, i),
+                at(w0, i),
+                at(s0, i),
                 ext,
+                into(new, i - level - 1),
             )
-            for f in range(fields):
-                new[f, i - level - 1, ext] = got[f][1]
-
-
-def inner_solid_kernel(blocks, spans, edges, fields, t, heat, k, yl, yr, *refs):
+
+
+def inner_solid_kernel(blocks, spans, edges, fields, t, heat, k, yl, yr, _, *refs):
     te, he, so, ti, tb, sqi, dg, ws, ta, tc, qa, qc = refs
     thick, rows, z = t.shape
     here = Place(rows, blocks, spans)
@@ -404,16 +423,15 @@
 
 
 def cone_kernel(blocks, spans, sent, spread, jacobian, *refs):
-    p0, s0, v0, w0, p1, p2, _, te, he, so, xe, xn, coef, hot, meta = refs[:15]
-    back, parts, first, sq, c2, c3, sl_ = refs[15:22]
-    l0, d1, d2, vm, wm, n1, n2 = refs[22:]
+    p0, s0, v0, w0, p1, p2, _, te, he, so, ti, dg, ws, xe, xn, coef, hot, meta = refs[:18]
+    back, parts, first, sq, c2, c3, sl_, t0, t1, t2, t3, dl, wl = refs[18:31]
+    l0, d1, d2, d3, vm, wm, n1, n2, qa = refs[31:]
     fields = p0.shape[0]
     rows, z = coef.shape[1], coef.shape[2]
     here = Place(rows, blocks, spans)
     ext, own, tall = here.ext, here.own, here.tall
     fluid = Fluid(spread, jacobian, fields)
     inside = jnp.logical_and(here.inside(z), jnp.logical_not(here.no_left))
-    mine = slice(W, W + rows)
     corner = 0
     for f in range(fields):
 
@@ -435,91 +453,52 @@
     um = [vm[c, ext] for c in range(3)]
     usm = um[0] + um[1] + um[2]
     for f in range(fields):
-        wm[f] = jnp.where(inside, DAMPING / fluid.diagonal(f, usm), 0.0)
+        wm[f, ext] = jnp.where(inside, DAMPING / fluid.diagonal(f, usm), 0.0)
     m = (fields + 3) * rows
     u0mm, usmm = xe[m : m + rows], xe[m + rows : m + 2 * rows]
 
-    def arrived(level, f):
-        return unless(here.no_left, xn[sent.window(level - 1, f, level < 3)])
-
-    def plane(cur, i, left, right, sl=ext):
-        return fluid.advance(
-            cur,
-            left,
-            right,
-            [v0[c, i, sl] for c in range(3)],
-            at_rows(w0, i, sl),
-            at_rows(s0, i, sl),
-            sl,
-        )
-
-    def put(new, got):
-        for f in range(fields):
-            new(f, got[f][1])
-
-    def flat(ref):
-        return lambda f, sl: ref[f, sl]
-
-    def flat_rows(ref, sl):
-        return lambda f: ref[f, sl]
-
-    def into(ref):
-        def store(f, x):
-            ref[f, ext] = x
-
-        return store
-
-    def into_plane(ref, i):
-        def store(f, x):
-            ref[f, i, ext] = x
-
-        return store
-
-    put(into(n1), plane(at(p0, 0), 0, flat_rows(l0, ext), at_rows(p0, 1, ext)))
+    def sum_of(level, ref):
+        def read(f, sl):
+            n = sent.window(level - 1, f).start + sl.start - B
+            return unless(here.no_left, xn[n : n + 8]) + ref[f, sl]
+
+        return read
+
+    def plane(cur, i, left, right, store, sl=ext):
+        fluid.advance(cur, left, right, speeds(v0, i), at(w0, i), at(s0, i), sl, store)
+
+    outer = [lambda sl, c=c: vm[c, sl] for c in range(3)]
+    plane(at(p0, 0), 0, flat(l0), at(p0, 1), into_flat(n1))
     for f in range(fields):
-        d1[f, ext] = wm[f] * (fluid.d[f] + um[0]) * p0[f, 0, ext]
-    put(into(n2), plane(flat(n1), 0, lambda f: arrived(1, f) + d1[f, ext], at_rows(p1, 0, ext)))
-    put(into(c2), plane(at(p1, 0), 1, flat_rows(n1, ext), at_rows(p1, 1, ext)))
-    got = fluid.advance(
-        flat(d1), None, flat_rows(n1, ext), um, lambda f: wm[f], None, ext
-    )
+        d1[f, ext] = wm[f, ext] * (fluid.d[f] + um[0]) * p0[f, 0, ext]
+    plane(flat(n1), 0, sum_of(1, d1), at(p1, 0), into_flat(n2))
+    plane(at(p1, 0), 1, flat(n1), at(p1, 1), into_flat(c2))
+    fluid.advance(flat(d1), None, flat(n1), outer, flat(wm), None, ext, into_flat(d2))
+    plane(flat(n2), 0, sum_of(2, d2), flat(c2), into(c3, 0))
+    plane(flat(c2), 1, flat(n2), at(p2, 0), into(c3, 1))
+
+    def farther(f, sl):
+        n = sl.start - own.start
+        w = unless(here.no_left, DAMPING / fluid.diagonal(f, usmm[n : n + 8]))
+        return w * (fluid.d[f] + u0mm[n : n + 8]) * d1[f, sl]
+
+    fluid.advance(flat(d2), farther, flat(n2), outer, flat(wm), None, own, into_flat(d3))
+    sq[...] = jnp.zeros_like(sq)
+    squares = [None] * fields
+
+    def final(f, sl, res, value):
+        first[f, sl.start - own.start : sl.stop - own.start] = value
+        square = res * res
+        squares[f] = square if squares[f] is None else squares[f] + square
+
+    plane(at(c3, 0), 0, sum_of(3, d3), at(c3, 1), final, own)
     for f in range(fields):
-        d2[f, ext] = got[f][1]
-    put(
-        into_plane(c3, 0),
-        plane(flat(n2), 0, lambda f: arrived(2, f) + d2[f, ext], flat_rows(c2, ext)),
-    )
-    put(into_plane(c3, 1), plane(flat(c2), 1, flat_rows(n2, ext), at_rows(p2, 0, ext)))
-
-    def farther(f):
-        w = unless(here.no_left, DAMPING / fluid.diagonal(f, usmm))
-        return w * (fluid.d[f] + u0mm) * d1[f, own]
-
-    got = fluid.advance(
-        flat(d2),
-        farther,
-        flat_rows(n2, own),
-        [u[mine] for u in um],
-        lambda f: wm[f, mine],
-        None,
-        own,
-    )
-    third = [got[f][1] for f in range(fields)]
-    got = plane(at(c3, 0), 0, lambda f: arrived(3, f) + third[f], at_rows(c3, 1, own), own)
-    sq[...] = jnp.zeros_like(sq)
-    for f in range(fields):
-        res, new = got[f]
-        first[f] = new
-        sq[f : f + 1] = jnp.sum(res * res, axis=0, keepdims=True)
+        sq[f : f + 1] = jnp.sum(squares[f], axis=0, keepdims=True)
     flux = coef[0] * first[fields - 1]
     parts[...] = jnp.dot(hot[...], flux, precision=HIGHEST, preferred_element_type=F32)
     for j in range(blocks):
         parts[j * CHUNK + 2 * CAP : (j + 1) * CHUNK] = meta[j]
-    n = 0
-    for buf, count in ((te, 4), (he, 4), (so, 3)):
-        for i in range(count):
-            back[n : n + tall] = buf[i, ext]
-            n = n + tall
+    n = 6 * tall
     for reach, read in (
         (3, at(p0, 0)),
         (2, flat(n1)),
@@ -533,12 +512,12 @@
     corner = corner + (fields + 3) * 2 * W
     early = (fields + 5) * rows
     zero = jnp.zeros((W, z), F32)
-    j = 0
-    for near, scale in ((4, 1.0), (4, 0.5), (3, 1.0)):
+    hl, sl_ = sl_.at[0], sl_.at[1]
+    for buf, near, scale in ((t0, 4, 1.0), (hl, 4, 0.5), (sl_, 3, 1.0)):
         for i in range(near):
 
-            def store(sl, x, j=j, scale=scale):
-                sl_[j, sl.start - B : sl.stop - B] = scale * x
+            def store(sl, x, buf=buf, j=4 - near + i, scale=scale):
+                buf[j, sl] = scale * x
 
             if i > 0:
                 low, high = xn[corner : corner + W], xn[corner + W : corner + 2 * W]
@@ -547,7 +526,36 @@
                 low, high = zero, zero
             here.fill(store, xe[early : early + rows], low, high, here.no_left)
             early = early + rows
-            j = j + 1
+
+    def h_of(i, sl):
+        return hl[i + 4, sl] if i < 0 else he[i, sl]
+
+    for i in range(-3, 1):
+        dl[i + 3, ext] = solid_diagonal(h_of, i, ext)
+        wl[i + 3, ext] = solid_weight(h_of(i, ext), dl[i + 3, ext])
+    for j in range(4, 6):
+        t0[j] = te[j - 4]
+    for level, (old, new) in enumerate(((t0, t1), (t1, t2), (t2, t3))):
+        for j in range(6):
+            qa[j, ext] = h_of(level - 4 + j, ext) * old[j, ext]
+        for j in range(4):
+            i = level - 3 + j
+            q = old[j + 1, ext]
+            res = sl_[i + 4, ext] if i < 0 else so[i, ext]
+            diagonal, w = (dl, wl) if i <= 0 else (dg, ws)
+            m = i + 3 if i <= 0 else i
+            res = res - diagonal[m, ext] * q
+            res = res + h_of(i, ext) * around(old, j + 1, ext) + around(qa, j + 1, ext)
+            new[j, ext] = q + w[m, ext] * res
+        for j in range(4, 6):
+            new[j] = ti[level, j - 4]
+    n = 0
+    for ref, i in ((he, 0), (he, 1), (t0, 4), (t1, 3)):
+        back[n : n + tall] = ref[i, ext]
+        n = n + tall
+    for ref, i in ((t2, 2), (t3, 1)):
+        back[n : n + tall] = ref[i, ext]
+        n = n + tall
 
 
 def rest_kernel(blocks, spans, sent, spread, jacobian, *refs):
@@ -558,7 +566,11 @@
     ext, own, tall = here.ext, here.own, here.tall
     fluid = Fluid(spread, jacobian, fields)
     def arrived(level):
-        return lambda f: unless(here.no_right, xn[sent.window(level, f, level < 3)])
+        def read(f, sl):
+            n = sent.window(level, f).start + sl.start - B
+            return unless(here.no_right, xn[n : n + 8])
+
+        return read
 
     known = [{i: (p0, i) for i in range(depth)}, {}, {}, {}]
     for level, buf in enumerate((p1, p2, p3)):
@@ -570,130 +582,118 @@
         ref, j = known[level][i]
         return (lambda f, sl: ref[f, sl]) if j is None else (lambda f, sl: ref[f, j, sl])
 
-    def plane(level, i, sl=ext):
-        right = arrived(level)
-        if i < depth - 1:
-            right = functools.partial(read(level, i + 1), sl=sl)
-        return fluid.advance(
+    def plane(level, i, store, sl=ext):
+        fluid.advance(
             read(level, i),
-            functools.partial(read(level, i - 1), sl=sl),
-            right,
-            [v0[c, i, sl] for c in range(3)],
-            at_rows(w0, i, sl),
-            at_rows(s0, i, sl),
+            read(level, i - 1),
+            read(level, i + 1) if i < depth - 1 else arrived(level),
+            speeds(v0, i),
+            at(w0, i),
+            at(s0, i),
             sl,
+            store,
         )
 
     todo = ((depth - 1,), (depth - 2, depth - 1), (2, depth - 3, depth - 2, depth - 1))
     for level, new in enumerate((n1, n2, n3)):
         for j, i in enumerate(todo[level]):
-            got = plane(level, i)
-            for f in range(fields):
-                new[f, j, ext] = got[f][1]
+            plane(level, i, into(new, j))
             known[level + 1][i] = (new, j)
     total = [None] * fields
     for f in range(fields):
         gas[f, 0] = first[f]
     for i in range(1, depth):
-        got = plane(3, i, own)
-        for f in range(fields):
-            res, new = got[f]
-            gas[f, i] = new
+
+        def final(f, sl, res, value, i=i):
+            gas[f, i, sl.start - own.start : sl.stop - own.start] = value
             square = res * res
             total[f] = square if total[f] is None else total[f] + square
+
+        plane(3, i, final, own)
     sq[...] = sqb[...]
     for f in range(fields):
         sq[f : f + 1] = sq[f : f + 1] + jnp.sum(total[f], axis=0, keepdims=True)
 
 
-def solid_kernel(blocks, spans, te, he, so, ti, tbi, sqi, dg, ws, sl_, xb, _, *refs):
+def solid_kernel(
+    blocks, spans, te, he, so, ti, tbi, sqi, dg, ws, sl_, tl0, tl1, tl2, tl3, dl, wl, xb, _, *refs
+):
     tb, rb, sq, rh, rd, rw = refs[:6]
-    to, ho, do, wo, heat, t0, q0, t1, q1 = refs[6:]
+    hr, dr, wr, ta, tc, qa = refs[6:]
     thick, rows, z = tb.shape
     here = Place(rows, blocks, spans)
     ext, own, tall = here.ext, here.own, here.tall
-    left, right = 0, 0
-    for buf, near in ((to, 4), (ho, 4), (heat, 3)):
-        for i in range(near):
-            buf[4 - near + i, ext] = sl_[left]
-            buf[4 + i, ext] = unless(here.no_right, xb[right : right + tall])
-            left, right = left + 1, right + tall
-
-    def place(inside, outside, i):
-        if 0 <= i < thick:
-            return inside, i
-        return outside, (i + 4 if i < 0 else i - thick + 4)
+    hl = sl_.at[0]
+
+    def arrived(n):
+        return unless(here.no_right, xb[n * tall : (n + 1) * tall])
+
+    for j in range(2):
+        hr[j, ext] = arrived(j)
 
     def h_of(i, sl):
-        ref, j = place(he, ho, i)
-        return ref[j, sl]
-
-    for i in (-3, -2, -1, 0, thick - 1, thick, thick + 1, thick + 2):
-        zm, zp = beside(h_of(i, ext))
-        h = h_of(i, ext)
-        near = (h_of(i - 1, ext) + h_of(i + 1, ext)) + (zm + zp)
-        near = near + (h_of(i, beyond(ext, -1)) + h_of(i, beyond(ext, 1)))
-        diagonal = 6.0 * h + near
-        j = i + 3 if i <= 0 else i - (thick - 1) + 4
-        do[j, ext] = diagonal
-        wo[j, ext] = solid_weight(h, diagonal)
-
-    def d_of(ref, outer, i, sl):
-        if 0 < i < thick - 1:
-            return ref[i, sl]
-        return outer[i + 3 if i <= 0 else i - (thick - 1) + 4, sl]
-
-    def first(side, level):
-        return level - 4 if side == 0 else thick - 2 - level
+        if i < 0:
+            return hl[i + 4, sl]
+        return he[i, sl] if i < thick else hr[i - thick, sl]
+
+    for j in range(2):
+        i = thick - 1 + j
+        dr[j, ext] = solid_diagonal(h_of, i, ext)
+        wr[j, ext] = solid_weight(h_of(i, ext), dr[j, ext])
+
+    def d_of(left, inside, right, i, sl):
+        if i <= 0:
+            return left[i + 3, sl]
+        return inside[i, sl] if i < thick - 1 else right[i - thick + 1, sl]
+
+    def residual(old, j, i, sl):
+        res = so[i, sl] - d_of(dl, dg, dr, i, sl) * old[j, sl]
+        return res + h_of(i, sl) * around(old, j, sl) + around(qa, j, sl)
 
     sums = None
-    for side in range(2):
-        old, oldq, new, newq = t0, q0, t1, q1
-        for j in range(6):
-            i = first(side, 0) + j
-            ref, m = place(te, to, i)
-            old[j] = ref[m]
-            oldq[j, ext] = h_of(i, ext) * ref[m, ext]
-        for level in range(SWEEPS):
-            last = level == SWEEPS - 1
-            sl = own if last else ext
-            for j in range(1, 5):
-                i = first(side, level) + j
-                ref, m = place(so, heat, i)
-                h, q = h_of(i, sl), old[j, sl]
-                res = ref[m, sl] - d_of(dg, do, i, sl) * q
-                res = res + h * around(old, j, sl) + around(oldq, j, sl)
-                value = q + d_of(ws, wo, i, sl) * res
-                if last:
-                    tb[i] = value
-                    if i < 3:
-                        rb[i] = res
-                    elif i >= thick - 4:
-                        rb[i - (thick - 7)] = res
-                    else:
-                        sums = res * res
-                else:
-                    m = j - 1 if side == 0 else j + 1
-                    new[m, ext] = value
-                    newq[m, ext] = h * value
-            if not last:
-                for m in range(2):
-                    j = m + 4 if side == 0 else m
-                    i = first(side, level + 1) + j
-                    new[j] = ti[level, m + 2 * side]
-                    newq[j, ext] = h_of(i, ext) * new[j, ext]
-            old, oldq, new, newq = new, newq, old, oldq
+    for j in range(6):
+        qa[j, ext] = h_of(j - 1, ext) * tl3[j, ext]
+    for i in range(4):
+        res = residual(tl3, i + 1, i, own)
+        tb[i] = tl3[i + 1, own] + d_of(wl, ws, wr, i, own) * res
+        if i < 3:
+            rb[i] = res
+        else:
+            sums = res * res
+    old, new = ta, tc
+    old[0], old[1] = te[thick - 2], te[thick - 1]
+    old[2, ext] = arrived(2)
+    for level in range(SWEEPS):
+        last = level == SWEEPS - 1
+        sl = own if last else ext
+        low = thick - 2 - level
+        for j in range(level + 3):
+            qa[j, ext] = h_of(low + j, ext) * old[j, ext]
+        for j in range(1, level + 2):
+            i = low + j
+            res = residual(old, j, i, sl)
+            value = old[j, sl] + d_of(wl, ws, wr, i, sl) * res
+            if last:
+                tb[i] = value
+                rb[i - (thick - 7)] = res
+            else:
+                new[j + 1, ext] = value
+        if not last:
+            for j in range(2):
+                new[j] = ti[level, j + 2]
+            new[level + 3, ext] = arrived(3 + level)
+            old, new = new, old
     for i in range(SWEEPS, thick - SWEEPS):
         tb[i] = tbi[i - SWEEPS]
     sq[...] = sqi[...]
-    n = refs[2].shape[0] - 3
+    n = sq.shape[0] - 3
     sq[n : n + 1] = sq[n : n + 1] + jnp.sum(sums, axis=0, keepdims=True)
     for region in range(2):
         for j in range(5):
             i = j - 2 if region == 0 else thick - 4 + j
             rh[region, j, ext] = h_of(i, ext)
-            rd[region, j, ext] = d_of(dg, do, i, ext)
-            rw[region, j, ext] = d_of(ws, wo, i, ext)
+            rd[region, j, ext] = d_of(dl, dg, dr, i, ext)
+            rw[region, j, ext] = d_of(wl, ws, wr, i, ext)
 
 
 def surface_kernel(blocks, arrived, surface, yf, yb):
@@ -883,22 +883,24 @@
         functools.partial(inner_solid_kernel, blocks, spans, edges, fields),
         held(solid, solid, solid, (3, 4, buf, z), (thick - 2 * SWEEPS, rows, z), (8, z), solid, solid),
         [solid] * 4,
-        [VMEM] * 5,
+        [VMEM] * 6,
         t,
         heat,
         k,
         zl,
         zr,
+        idx,
         cost=COSTS[2],
     )
-    sent_back = Arrivals(11 * tall, rows, fields, (3, 2, 1, 0))
-    flat = (fields, buf, z)
-    back, parts, first, sq, c2, c3, sl_ = call(
+    sent_back = Arrivals(6 * tall, rows, fields, (3, 2, 1, 0))
+    one, six = (fields, buf, z), (6, buf, z)
+    back, parts, first, sq, c2, c3, sl_, *lefts = call(
         functools.partial(cone_kernel, blocks, spans, sent_ahead),
         [(sent_back.size(), z), (blocks * CHUNK, z)]
-        + held((fields, rows, z), (8, z), flat, (fields, 2, buf, z), (11, tall, z)),
-        [flat] * 3 + [(3, buf, z), (fields, tall, z)] + [flat] * 2,
-        [SMEM] * 2 + [VMEM] * 15,
+        + held((fields, rows, z), (8, z), one, (fields, 2, buf, z), (2, 4, buf, z))
+        + held(six, six, six, six, (4, buf, z), (4, buf, z)),
+        [one] * 4 + [(3, buf, z)] + [one] * 3 + [six],
+        [SMEM] * 2 + [VMEM] * 18,
         diffusion,
         jacobian,
         p0,
@@ -911,6 +913,9 @@
         te,
         he,
         so,
+        ti,
+        dg,
+        ws,
         xe,
         xn,
         wall_coefficient,
@@ -930,7 +935,7 @@
     yl, yr = ahead(yf, "span"), behind(yb, "span")
     gas, sqf = call(
         functools.partial(rest_kernel, blocks, spans, sent_back),
-        [p.shape, (8, z)],
+        held(p.shape, (8, z)),
         [(fields, 1, buf, z), (fields, 2, buf, z), (fields, 4, buf, z)],
         [SMEM] * 2 + [VMEM] * 13,
         diffusion,
@@ -950,12 +955,12 @@
         yf,
         cost=COSTS[4],
     )
-    outer, edge = (8, buf, z), (2, 5, buf, z)
+    two, edge = (2, buf, z), (2, 5, buf, z)
     tb, rb, sqs, rh, rd, rw = call(
         functools.partial(solid_kernel, blocks, spans),
         held(t.shape, (7, rows, z), (8, z), edge, edge, edge),
-        [outer] * 5 + [(6, buf, z)] * 4,
-        [VMEM] * 11,
+        [two] * 3 + [six] * 3,
+        [VMEM] * 17,
         te,
         he,
         so,
@@ -965,6 +970,7 @@
         dg,
         ws,
         sl_,
+        *lefts,
         xr,
         yf,
         cost=COSTS[5],
@@ -972,7 +978,7 @@
     region = (2, 7, buf, z)
     t, out = call(
         functools.partial(response_kernel, blocks, spans, fields),
-        [t.shape, (blocks, rows + 8, z)],
+        held(t.shape, (blocks, rows + 8, z)),
         [region] * 3 + [(2, buf, z)],
         [VMEM] * 10,
         surface,

time: 71.6 us -> 67.5 us (0.943)
  blocking collectives: 30.2 us -> 28 us
  Pallas kernels: 14.9 us -> 12.8 us
  local copies, waits for them, and re-layouts: 0.03 us -> 1.58 us
  other arithmetic: 1.97 us -> 0.65 us
    all_to_all x1, blocking collectives: 16.1 us -> 13.2 us  [shards(): arrived = lax.all_to_all(parts.reshape(blocks, CHUNK, z), 'blk', 0, 0)]
    pallas_call x10, Pallas kernels: 14.9 us -> 12.8 us  [call(): pl.pallas_call(kernel, out_shape=[jax.ShapeDtypeStruct(s, F32) if isinsta...]
    unnamed x12 -> x14, local copies, waits for them, and re-layouts: 0.03 us -> 1.58 us
    scatter-add x1, other arithmetic: 1.33 us -> 0.01 us  [shards(): gas = gas.at[fields - 1, 0].add(added)]
  transfers between devices with their start and end apart: 11 -> 11, of which waited for: 6 -> 5; matrix products, arithmetic and copies ran while one was open for 2% -> 2% of each run, Pallas kernels for 13% -> 12%
where the time goes in v4:
time: 67.5 us; the launch traced here: 67.3 us
  blocking collectives  28 us (41%)
  Pallas kernels  12.8 us (19%)
  starting transfers between devices  11.8 us (17%)
  waiting for transfers between devices  11.7 us (17%)
  local copies, waits for them, and re-layouts  1.58 us (2%)
  between operations  0.77 us (1%)
    all_to_all x1, blocking collectives, shards(): arrived = lax.all_to_all(out, 'blk', 0, 0)  14.8 us
    all_to_all x1, blocking collectives, shards(): arrived = lax.all_to_all(parts.reshape(blocks, CHUNK, z), 'blk', 0, 0)  13.2 us
    pallas_call x10, Pallas kernels, call(): pl.pallas_call(kernel, out_shape=[jax.ShapeDtypeStruct(s, F32) if isinsta...  12.8 us
    ppermute x5, waiting for transfers between devices, ahead(): return lax.ppermute(x, axis, forward[axis])  7.78 us
    ppermute x5, starting transfers between devices, ahead(): return lax.ppermute(x, axis, forward[axis])  5.56 us
    ppermute x4, starting transfers between devices, behind(): return lax.ppermute(x, axis, backward[axis])  5.01 us
    ppermute x2, waiting for transfers between devices, shards(): sq = sq + lax.ppermute(sq, 'span', [(i, i ^ step) for i in range(spans)])  1.97 us
    ppermute x4, waiting for transfers between devices, behind(): return lax.ppermute(x, axis, backward[axis])  1.93 us
  transfers between devices with their start and end apart: 11, of which 5 were waited for; matrix products, arithmetic and copies ran while one was open for 2% of the time, Pallas kernels for 12%

profile of v4, /device:TPU:0, one launch (start us, length us, event | category | flops | bytes accessed | tf_op | source)
XLA Modules:
  0.0 67.3 jit_solution(15849970925061336282)
XLA Ops:
  0.6 0.0 copy-start.1
  0.6 0.0 copy-start.2
  0.7 1.8 %shard_map.139 = (f32[5,8,32,128]{3,2,1,0:T(8,128)S(1)}, f32[5,8,32,128]{3,2,1,0:T(8,128)S(1)}, f32[3,8,32,128]{3,2,1,0:T(8,128)S(1)}, f32[16,32,128]{2,1,0:T(8,...) custom-call(f32[5,8,32,128]{3,2,1,0:T(8,128)} %refs_0_.1, ...), custom_call_target="tpu_custom_call" | custom-call | flops 1000000 | bytes 3000000 | tf_op jit(solution)/shard_map/pallas_call | solution.py:30
  2.5 0.5 collective-permute-start
  3.0 2.0 %collective-permute-start.1 = (f32[384,128]{1,0:T(8,128)S(1)}, f32[384,128]{1,0:T(8,128)S(1)}, u32[]{:S(2)}, u32[]{:S(2)}) collective-permute-start(f32[384,128]{1,0:T(8,128)S(1)} %get-tuple-element.76), channel_id=1, source_target_pairs={{1,0},{2,1},{3,2},{0,3},{5,4},{6,5},{7,6},{4,7},{9,8},{10,9},{11,1... | collective-permute-start | bytes 589832 | tf_op jit(solution)/shard_map/ppermute | solution.py:828
  5.0 2.2 %collective-permute-start.4 = (f32[672,128]{1,0:T(8,128)S(1)}, f32[672,128]{1,0:T(8,128)S(1)}, u32[]{:S(2)}, u32[]{:S(2)}) collective-permute-start(f32[672,128]{1,0:T(8,128)S(1)} %get-tuple-element.96), channel_id=1, source_target_pairs={{0,4},{4,8},{8,12},{12,16},{16,20},{20,24},{24,28},{28,0},{1,5},{5... | collective-permute-start | bytes 1032200 | tf_op jit(solution)/shard_map/ppermute | solution.py:825
  7.2 1.1 %collective-permute-done.yl = f32[384,128]{1,0:T(8,128)S(1)} collective-permute-done((f32[384,128]{1,0:T(8,128)S(1)}, f32[384,128]{1,0:T(8,128)S(1)}, u32[]{:S(2)}, u32[]{:S(2)}) %collective-permute-start) | collective-permute-done | bytes 196640 | tf_op jit(solution)/shard_map/ppermute | solution.py:825
  8.3 1.9 %collective-permute-done.1.yr = f32[384,128]{1,0:T(8,128)S(1)} collective-permute-done((f32[384,128]{1,0:T(8,128)S(1)}, f32[384,128]{1,0:T(8,128)S(1)}, u32[]{:S(2)}, u32[]{:S(2)}) %collective-permute-start.1) | collective-permute-done | bytes 196640 | tf_op jit(solution)/shard_map/ppermute | solution.py:828
  10.2 0.0 copy-done.1
  10.2 0.0 copy-done.2
  10.2 0.0 copy-start.3
  10.2 1.3 %shard_map.142 = f32[638,128]{1,0:T(8,128)S(1)} custom-call(f32[5]{0:T(128)S(1)} %copy-done.2, f32[5,5]{1,0:T(8,128)S(1)} %copy-done.1, f32[5,8,32,128]{3,2,1,0:T(8,128)S(1)} %get-tuple-element.72.p, f32[5,8,32,128]{3,2,1,0:T(8,128)S(1)} %get-tuple-element.73.src, f32[3,8,32,128]{3,2,1,0:T(8,128)S(1)} %get-tuple-element.74.vel, ...), custom_call_target="tpu_custom_call" | custom-call | flops 30000000 | bytes 90000000 | tf_op jit(solution)/shard_map/pallas_call | solution.py:30
  11.6 1.5 %collective-permute-start.5 = (f32[638,128]{1,0:T(8,128)S(1)}, f32[638,128]{1,0:T(8,128)S(1)}, u32[]{:S(2)}, u32[]{:S(2)}) collective-permute-start(f32[638,128]{1,0:T(8,128)S(1)} %shard_map.142), channel_id=1, source_target_pairs={{0,4},{4,8},{8,12},{12,16},{16,20},{20,24},{24,28},{28,0},{1,5},{5... | collective-permute-start | bytes 979976 | tf_op jit(solution)/shard_map/ppermute | solution.py:825
  13.1 0.8 %collective-permute-start.2 = (f32[176,128]{1,0:T(8,128)S(1)}, f32[176,128]{1,0:T(8,128)S(1)}, u32[]{:S(2)}, u32[]{:S(2)}) collective-permute-start(f32[176,128]{1,0:T(8,128)S(1)} %get-tuple-element.87), channel_id=1, source_target_pairs={{0,1},{1,2},{2,3},{3,0},{4,5},{5,6},{6,7},{7,4},{8,9},{9,10},{10,1... | collective-permute-start | bytes 270344 | tf_op jit(solution)/shard_map/ppermute | solution.py:825
  13.9 1.1 %collective-permute-start.3 = (f32[176,128]{1,0:T(8,128)S(1)}, f32[176,128]{1,0:T(8,128)S(1)}, u32[]{:S(2)}, u32[]{:S(2)}) collective-permute-start(f32[176,128]{1,0:T(8,128)S(1)} %get-tuple-element.88), channel_id=1, source_target_pairs={{1,0},{2,1},{3,2},{0,3},{5,4},{6,5},{7,6},{4,7},{9,8},{10,9},{11,1... | collective-permute-start | bytes 270344 | tf_op jit(solution)/shard_map/ppermute | solution.py:828
  15.0 0.0 copy-done.3
  15.0 0.0 copy-done.4
  15.1 2.3 %shard_map.140 = (f32[5,8,56,128]{3,2,1,0:T(8,128)S(1)}, f32[5,8,56,128]{3,2,1,0:T(8,128)S(1)}, f32[3,8,56,128]{3,2,1,0:T(8,128)S(1)}, f32[5,8,56,128]{3,2,1,0:T...) custom-call(f32[5]{0:T(128)S(1)} %copy-done.2, ...), custom_call_target="tpu_custom_call" | custom-call | flops 10000 | bytes 30000 | tf_op jit(solution)/shard_map/pallas_call | solution.py:30
  17.4 0.0 collective-permute-done.2.yl
  17.4 0.0 collective-permute-done.3.yr
  17.4 1.3 %shard_map.141 = (f32[16,56,128]{2,1,0:T(8,128)S(1)}, f32[16,56,128]{2,1,0:T(8,128)S(1)}, f32[16,56,128]{2,1,0:T(8,128)S(1)}, f32[3,4,56,128]{3,2,1,0:T(8,128)S(...) custom-call(f32[16,32,128]{2,1,0:T(8,128)S(1)} %get-tuple-element.84, ...), custom_call_target="tpu_custom_call" | custom-call | flops 10000 | bytes 30000 | tf_op jit(solution)/shard_map/pallas_call | solution.py:30
  18.7 0.0 collective-permute-done.4.refs_13_
  18.7 6.7 %collective-permute-done.5.refs_14_ = f32[638,128]{1,0:T(8,128)S(1)} collective-permute-done((f32[638,128]{1,0:T(8,128)S(1)}, f32[638,128]{1,0:T(8,128)S(1)}, u32[]{:S(2)}, u32[]{:S(2)}) %collective-permute-start.5) | collective-permute-done | bytes 326688 | tf_op jit(solution)/shard_map/ppermute | solution.py:825
  25.4 0.0 copy-done
  25.4 2.1 %shard_map.143 = (f32[940,128]{1,0:T(8,128)S(1)}, f32[256,128]{1,0:T(8,128)S(1)}, f32[5,32,128]{2,1,0:T(8,128)S(1)}, f32[8,128]{1,0:T(8,128)S(1)}, f32[5,56,128]...) custom-call(f32[5]{0:T(128)S(1)} %copy-done.2, ...), custom_call_target="tpu_custom_call" | custom-call | flops 2000000 | bytes 6000000 | tf_op jit(solution)/shard_map/pallas_call | solution.py:30
  27.5 1.8 %collective-permute-start.6 = (f32[940,128]{1,0:T(8,128)S(1)}, f32[940,128]{1,0:T(8,128)S(1)}, u32[]{:S(2)}, u32[]{:S(2)}) collective-permute-start(f32[940,128]{1,0:T(8,128)S(1)} %get-tuple-element.103), channel_id=1, source_target_pairs={{4,0},{8,4},{12,8},{16,12},{20,16},{24,20},{28,24},{0,28},{5,1},{9... | collective-permute-start | bytes 1443848 | tf_op jit(solution)/shard_map/ppermute | solution.py:828
  29.3 13.2 %all_to_all.10.arrived = f32[8,32,128]{2,1,0:T(8,128)S(1)} all-to-all(f32[8,32,128]{2,1,0:T(8,128)S(1)} %bitcast.6), channel_id=1, replica_groups=mesh['blk'=8,'span'=4] {'blk'}, dimensions={0} | all-to-all | bytes 262144 | tf_op jit(solution)/shard_map/all_to_all | solution.py:927
  42.5 0.2 shard_map.144
  42.7 0.1 collective-permute-start.8
  42.8 0.5 collective-permute-start.7
  43.3 0.0 collective-permute-done.6.refs_11_.xb
  43.3 2.1 %shard_map.145 = (f32[5,8,32,128]{3,2,1,0:T(8,128)S(1)}, f32[8,128]{1,0:T(8,128)S(1)}) custom-call(f32[5]{0:T(128)S(1)} %copy-done.2, f32[5,5]{1,0:T(8,128)S(1)} %copy-done.1, f32[5,8,56,128]{3,2,1,0:T(8,128)S(1)} %get-tuple-element.77.refs_0_, f32[5,8,56,128]{3,2,1,0:T(8,128)S(1)} %get-tuple-element.78.refs_1_, ...), custom_call_target="tpu_custom_call" | custom-call | flops 3000000 | bytes 9000000 | tf_op jit(solution)/shard_map/pallas_call | solution.py:30
  45.4 0.5 shard_map.146
  45.9 0.0 collective-permute-done.8.yr
  45.9 0.0 collective-permute-done.7.yl
  46.0 0.7 %shard_map.147 = (f32[16,32,128]{2,1,0:T(8,128)S(1)}, f32[8,40,128]{2,1,0:T(8,128)S(1)}) custom-call(f32[64,128]{1,0:T(8,128)S(1)} %get-tuple-element.107.surface, f32[8,128]{1,0:T(8,128)S(1)} %collective-permute-done.7.yl, f32[8,128]{1,0:T(8,128)S(1)} %collective-permute-done.8.yr, f32[2,5,56,128]{3,2,1,0:T(8,128)S(1)} %get-tuple-element.118.rh, ...), custom_call_target="tpu_custom_call" | custom-call | flops 1000000 | bytes 3000000 | tf_op jit(solution)/shard_map/pallas_call | solution.py:30
  46.7 0.0 copy-start.5
  46.7 14.8 %all_to_all.11.arrived = f32[8,40,128]{2,1,0:T(8,128)S(1)} all-to-all(f32[8,40,128]{2,1,0:T(8,128)S(1)} %get-tuple-element.125), channel_id=1, replica_groups=mesh['blk'=8,'span'=4] {'blk'}, dimensions={0} | all-to-all | bytes 327680 | tf_op jit(solution)/shard_map/all_to_all | solution.py:995
  61.5 0.4 shard_map.148
  61.8 0.0 collective-permute-start.9
  61.8 0.7 %copy.17 = f32[16,32,128]{2,1,0:T(8,128)} copy(f32[16,32,128]{2,1,0:T(8,128)S(1)} %get-tuple-element.130) | data formatting | bytes 524288
  62.6 0.5 collective-permute-done.9
  63.0 1.3 %collective-permute-start.10 = (f32[8,128]{1,0:T(8,128)S(1)}, f32[8,128]{1,0:T(8,128)S(1)}, u32[]{:S(2)}, u32[]{:S(2)}) collective-permute-start(f32[8,128]{1,0:T(8,128)S(1)} %add.14), channel_id=1, source_target_pairs={{0,2},{1,3},{2,0},{3,1},{4,6},{5,7},{6,4},{7,5},{8,10},{9,11},{10,... | collective-permute-start | bytes 12296 | tf_op jit(solution)/shard_map/ppermute | solution.py:1007
  64.3 0.8 %copy.16 = f32[5,8,32,128]{3,2,1,0:T(8,128)} copy(f32[5,8,32,128]{3,2,1,0:T(8,128)S(1)} %fusion) | data formatting | bytes 1310720
  65.1 1.5 %collective-permute-done.10 = f32[8,128]{1,0:T(8,128)S(1)} collective-permute-done((f32[8,128]{1,0:T(8,128)S(1)}, f32[8,128]{1,0:T(8,128)S(1)}, u32[]{:S(2)}, u32[]{:S(2)}) %collective-permute-start.10) | collective-permute-done | bytes 4128 | tf_op jit(solution)/shard_map/ppermute | solution.py:1007
  66.6 0.1 slice_reduce_fusion
  66.7 0.0 copy-done.5
  66.7 0.5 multiply_sqrt_fusion
  (5 shorter events, 0.0 us)
Async XLA Ops:
  0.6 9.6 %copy-start.1 = (f32[5,5]{1,0:T(8,128)S(1)}, f32[5,5]{1,0:T(8,128)}, u32[]{:S(2)}) copy-start(f32[5,5]{1,0:T(8,128)} %jacobian.7) | copy-start | bytes 304
  0.6 9.6 %copy-start.2 = (f32[5]{0:T(128)S(1)}, f32[5]{0:T(128)}, u32[]{:S(2)}) copy-start(f32[5]{0:T(128)} %spread.7) | copy-start | bytes 64
  2.5 5.8 %collective-permute-start = (f32[384,128]{1,0:T(8,128)S(1)}, f32[384,128]{1,0:T(8,128)S(1)}, u32[]{:S(2)}, u32[]{:S(2)}) collective-permute-start(f32[384,128]{1,0:T(8,128)S(1)} %get-tuple-element.75), channel_id=1, source_target_pairs={{0,1},{1,2},{2,3},{3,0},{4,5},{5,6},{6,7},{7,4},{8,9},{9,10},{10,1... | collective-permute-start | bytes 589832 | tf_op jit(solution)/shard_map/ppermute | solution.py:825
  3.0 7.2 %collective-permute-start.1 = (f32[384,128]{1,0:T(8,128)S(1)}, f32[384,128]{1,0:T(8,128)S(1)}, u32[]{:S(2)}, u32[]{:S(2)}) collective-permute-start(f32[384,128]{1,0:T(8,128)S(1)} %get-tuple-element.76), channel_id=1, source_target_pairs={{1,0},{2,1},{3,2},{0,3},{5,4},{6,5},{7,6},{4,7},{9,8},{10,9},{11,1... | collective-permute-start | bytes 589832 | tf_op jit(solution)/shard_map/ppermute | solution.py:828
  5.0 13.7 %collective-permute-start.4 = (f32[672,128]{1,0:T(8,128)S(1)}, f32[672,128]{1,0:T(8,128)S(1)}, u32[]{:S(2)}, u32[]{:S(2)}) collective-permute-start(f32[672,128]{1,0:T(8,128)S(1)} %get-tuple-element.96), channel_id=1, source_target_pairs={{0,4},{4,8},{8,12},{12,16},{16,20},{20,24},{24,28},{28,0},{1,5},{5... | collective-permute-start | bytes 1032200 | tf_op jit(solution)/shard_map/ppermute | solution.py:825
  10.2 4.8 %copy-start.3 = (s32[1,32,1]{1,2,0:T(1,128)S(1)}, s32[1,32,1]{1,2,0:T(1,128)}, u32[]{:S(2)}) copy-start(s32[1,32,1]{1,2,0:T(1,128)} %param.23) | copy-start | bytes 388
  10.2 4.8 %copy-start.4 = (s32[1,32]{1,0:T(1,128)S(1)}, s32[1,32]{1,0:T(1,128)}, u32[]{:S(2)}) copy-start(s32[1,32]{1,0:T(1,128)} %target.1) | copy-start | bytes 388
  11.6 13.8 %collective-permute-start.5 = (f32[638,128]{1,0:T(8,128)S(1)}, f32[638,128]{1,0:T(8,128)S(1)}, u32[]{:S(2)}, u32[]{:S(2)}) collective-permute-start(f32[638,128]{1,0:T(8,128)S(1)} %shard_map.142), channel_id=1, source_target_pairs={{0,4},{4,8},{8,12},{12,16},{16,20},{20,24},{24,28},{28,0},{1,5},{5... | collective-permute-start | bytes 979976 | tf_op jit(solution)/shard_map/ppermute | solution.py:825
  13.1 4.3 %collective-permute-start.2 = (f32[176,128]{1,0:T(8,128)S(1)}, f32[176,128]{1,0:T(8,128)S(1)}, u32[]{:S(2)}, u32[]{:S(2)}) collective-permute-start(f32[176,128]{1,0:T(8,128)S(1)} %get-tuple-element.87), channel_id=1, source_target_pairs={{0,1},{1,2},{2,3},{3,0},{4,5},{5,6},{6,7},{7,4},{8,9},{9,10},{10,1... | collective-permute-start | bytes 270344 | tf_op jit(solution)/shard_map/ppermute | solution.py:825
  13.9 3.5 %collective-permute-start.3 = (f32[176,128]{1,0:T(8,128)S(1)}, f32[176,128]{1,0:T(8,128)S(1)}, u32[]{:S(2)}, u32[]{:S(2)}) collective-permute-start(f32[176,128]{1,0:T(8,128)S(1)} %get-tuple-element.88), channel_id=1, source_target_pairs={{1,0},{2,1},{3,2},{0,3},{5,4},{6,5},{7,6},{4,7},{9,8},{10,9},{11,1... | collective-permute-start | bytes 270344 | tf_op jit(solution)/shard_map/ppermute | solution.py:828
  15.1 10.3 %copy-start = (f32[1,32,128]{2,1,0:T(8,128)S(1)}, f32[1,32,128]{2,1,0:T(8,128)}, u32[]{:S(2)}) copy-start(f32[1,32,128]{2,1,0:T(8,128)} %coef.1) | copy-start | bytes 49156
  27.5 15.8 %collective-permute-start.6 = (f32[940,128]{1,0:T(8,128)S(1)}, f32[940,128]{1,0:T(8,128)S(1)}, u32[]{:S(2)}, u32[]{:S(2)}) collective-permute-start(f32[940,128]{1,0:T(8,128)S(1)} %get-tuple-element.103), channel_id=1, source_target_pairs={{4,0},{8,4},{12,8},{16,12},{20,16},{24,20},{28,24},{0,28},{5,1},{9... | collective-permute-start | bytes 1443848 | tf_op jit(solution)/shard_map/ppermute | solution.py:828
  42.7 3.2 %collective-permute-start.8 = (f32[8,128]{1,0:T(8,128)S(1)}, f32[8,128]{1,0:T(8,128)S(1)}, u32[]{:S(2)}, u32[]{:S(2)}) collective-permute-start(f32[8,128]{1,0:T(8,128)S(1)} %get-tuple-element.108), channel_id=1, source_target_pairs={{1,0},{2,1},{3,2},{0,3},{5,4},{6,5},{7,6},{4,7},{9,8},{10,9},{11,1... | collective-permute-start | bytes 12296 | tf_op jit(solution)/shard_map/ppermute | solution.py:828
  42.8 3.2 %collective-permute-start.7 = (f32[8,128]{1,0:T(8,128)S(1)}, f32[8,128]{1,0:T(8,128)S(1)}, u32[]{:S(2)}, u32[]{:S(2)}) collective-permute-start(f32[8,128]{1,0:T(8,128)S(1)} %get-tuple-element.105.refs_12_._), channel_id=1, source_target_pairs={{0,1},{1,2},{2,3},{3,0},{4,5},{5,6},{6,7},{7,4},{8,9},{9,10},{10,1... | collective-permute-start | bytes 12296 | tf_op jit(solution)/shard_map/ppermute | solution.py:825
  46.7 20.1 %copy-start.5 = (f32[6]{0:T(128)S(1)}, f32[6]{0:T(128)}, u32[]{:S(2)}) copy-start(f32[6]{0:T(128)} %constant.41) | copy-start | bytes 76
  61.8 1.2 %collective-permute-start.9 = (f32[8,128]{1,0:T(8,128)S(1)}, f32[8,128]{1,0:T(8,128)S(1)}, u32[]{:S(2)}, u32[]{:S(2)}) collective-permute-start(f32[8,128]{1,0:T(8,128)S(1)} %get-tuple-element.128), channel_id=1, source_target_pairs={{0,1},{1,0},{2,3},{3,2},{4,5},{5,4},{6,7},{7,6},{8,9},{9,8},{10,11... | collective-permute-start | bytes 12296 | tf_op jit(solution)/shard_map/ppermute | solution.py:1007
  63.0 3.6 %collective-permute-start.10 = (f32[8,128]{1,0:T(8,128)S(1)}, f32[8,128]{1,0:T(8,128)S(1)}, u32[]{:S(2)}, u32[]{:S(2)}) collective-permute-start(f32[8,128]{1,0:T(8,128)S(1)} %add.14), channel_id=1, source_target_pairs={{0,2},{1,3},{2,0},{3,1},{4,6},{5,7},{6,4},{7,5},{8,10},{9,11},{10,... | collective-permute-start | bytes 12296 | tf_op jit(solution)/shard_map/ppermute | solution.py:1007

commit v5 on v4

--- a/solution.py
+++ b/solution.py
@@ -423,11 +423,11 @@
 
 
 def cone_kernel(blocks, spans, sent, spread, jacobian, *refs):
-    p0, s0, v0, w0, p1, p2, _, te, he, so, ti, dg, ws, xe, xn, coef, hot, meta = refs[:18]
-    back, parts, first, sq, c2, c3, sl_, t0, t1, t2, t3, dl, wl = refs[18:31]
-    l0, d1, d2, d3, vm, wm, n1, n2, qa = refs[31:]
-    fields = p0.shape[0]
-    rows, z = coef.shape[1], coef.shape[2]
+    p0, s0, v0, w0, p1, te, he, so, ti, dg, ws, xe, xn = refs[:13]
+    back, n2, c2, c3, d1, d2, vm, wm, sl_, t0, t1, t2, t3, dl, wl = refs[13:28]
+    l0, n1, qa = refs[28:]
+    fields, z = p0.shape[0], p0.shape[3]
+    rows = p0.shape[2] - 2 * (B + W)
     here = Place(rows, blocks, spans)
     ext, own, tall = here.ext, here.own, here.tall
     fluid = Fluid(spread, jacobian, fields)
@@ -454,9 +454,6 @@
     usm = um[0] + um[1] + um[2]
     for f in range(fields):
         wm[f, ext] = jnp.where(inside, DAMPING / fluid.diagonal(f, usm), 0.0)
-    m = (fields + 3) * rows
-    u0mm, usmm = xe[m : m + rows], xe[m + rows : m + 2 * rows]
-
     def sum_of(level, ref):
         def read(f, sl):
             n = sent.window(level - 1, f).start + sl.start - B
@@ -474,36 +471,13 @@
     plane(flat(n1), 0, sum_of(1, d1), at(p1, 0), into_flat(n2))
     plane(at(p1, 0), 1, flat(n1), at(p1, 1), into_flat(c2))
     fluid.advance(flat(d1), None, flat(n1), outer, flat(wm), None, ext, into_flat(d2))
-    plane(flat(n2), 0, sum_of(2, d2), flat(c2), into(c3, 0))
-    plane(flat(c2), 1, flat(n2), at(p2, 0), into(c3, 1))
-
-    def farther(f, sl):
-        n = sl.start - own.start
-        w = unless(here.no_left, DAMPING / fluid.diagonal(f, usmm[n : n + 8]))
-        return w * (fluid.d[f] + u0mm[n : n + 8]) * d1[f, sl]
-
-    fluid.advance(flat(d2), farther, flat(n2), outer, flat(wm), None, own, into_flat(d3))
-    sq[...] = jnp.zeros_like(sq)
-    squares = [None] * fields
-
-    def final(f, sl, res, value):
-        first[f, sl.start - own.start : sl.stop - own.start] = value
-        square = res * res
-        squares[f] = square if squares[f] is None else squares[f] + square
-
-    plane(at(c3, 0), 0, sum_of(3, d3), at(c3, 1), final, own)
-    for f in range(fields):
-        sq[f : f + 1] = jnp.sum(squares[f], axis=0, keepdims=True)
-    flux = coef[0] * first[fields - 1]
-    parts[...] = jnp.dot(hot[...], flux, precision=HIGHEST, preferred_element_type=F32)
-    for j in range(blocks):
-        parts[j * CHUNK + 2 * CAP : (j + 1) * CHUNK] = meta[j]
+    plane(flat(n2), 0, sum_of(2, d2), flat(c2), into_flat(c3))
     n = 6 * tall
     for reach, read in (
         (3, at(p0, 0)),
         (2, flat(n1)),
         (1, flat(n2)),
-        (0, at(c3, 0)),
+        (0, flat(c3)),
     ):
         size = rows + 2 * reach
         for f in range(fields):
@@ -558,8 +532,53 @@
         n = n + tall
 
 
+def flux_kernel(blocks, spans, sent, spread, jacobian, *refs):
+    s0, v0, w0, p2, p3, n2, c2, c3, d1, d2, vm, wm, xe, xn, coef, hot, meta = refs[:17]
+    parts, left, sq, m3, d3 = refs[17:]
+    fields, rows, z = left.shape[0], left.shape[2], left.shape[3]
+    here = Place(rows, blocks, spans)
+    ext, own = here.ext, here.own
+    fluid = Fluid(spread, jacobian, fields)
+    m = (fields + 3) * rows
+    u0mm, usmm = xe[m : m + rows], xe[m + rows : m + 2 * rows]
+    outer = [lambda sl, c=c: vm[c, sl] for c in range(3)]
+
+    def third(f, sl):
+        n = sent.window(2, f).start + sl.start - B
+        return unless(here.no_left, xn[n : n + 8]) + d3[f, sl]
+
+    def plane(cur, i, before, after, store, sl=ext):
+        fluid.advance(cur, before, after, speeds(v0, i), at(w0, i), at(s0, i), sl, store)
+
+    def farther(f, sl):
+        n = sl.start - own.start
+        w = unless(here.no_left, DAMPING / fluid.diagonal(f, usmm[n : n + 8]))
+        return w * (fluid.d[f] + u0mm[n : n + 8]) * d1[f, sl]
+
+    fluid.advance(flat(d2), farther, flat(n2), outer, flat(wm), None, own, into_flat(d3))
+    plane(flat(c2), 1, flat(n2), at(p2, 0), into(m3, 0))
+    plane(at(p2, 0), 2, flat(c2), at(p2, 1), into(m3, 1))
+    squares = [None] * fields
+    third_of = [flat(c3), at(m3, 0), at(m3, 1), at(p3, 0), at(p3, 1)]
+    for i in range(4):
+
+        def final(f, sl, res, value, i=i):
+            left[f, i, sl.start - own.start : sl.stop - own.start] = value
+            square = res * res
+            squares[f] = square if squares[f] is None else squares[f] + square
+
+        plane(third_of[i], i, third_of[i - 1] if i > 0 else third, third_of[i + 1], final, own)
+    sq[...] = jnp.zeros_like(sq)
+    for f in range(fields):
+        sq[f : f + 1] = jnp.sum(squares[f], axis=0, keepdims=True)
+    flux = coef[0] * left[fields - 1, 0]
+    parts[...] = jnp.dot(hot[...], flux, precision=HIGHEST, preferred_element_type=F32)
+    for j in range(blocks):
+        parts[j * CHUNK + 2 * CAP : (j + 1) * CHUNK] = meta[j]
+
+
 def rest_kernel(blocks, spans, sent, spread, jacobian, *refs):
-    p0, s0, v0, w0, p1, p2, p3, c2, c3, first, sqb, xn, _, gas, sq, n1, n2, n3 = refs
+    p0, s0, v0, w0, p1, p2, p3, left, sqb, xn, _, gas, sq, n1, n2, n3 = refs
     fields, depth = gas.shape[0], gas.shape[1]
     rows = gas.shape[2]
     here = Place(rows, blocks, spans)
@@ -576,11 +595,10 @@
     for level, buf in enumerate((p1, p2, p3)):
         for i in range(level + 1, depth - 1 - level):
             known[level + 1][i] = (buf, i - level - 1)
-    known[2][1], known[3][0], known[3][1] = (c2, None), (c3, 0), (c3, 1)
 
     def read(level, i):
         ref, j = known[level][i]
-        return (lambda f, sl: ref[f, sl]) if j is None else (lambda f, sl: ref[f, j, sl])
+        return at(ref, j)
 
     def plane(level, i, store, sl=ext):
         fluid.advance(
@@ -594,15 +612,16 @@
             store,
         )
 
-    todo = ((depth - 1,), (depth - 2, depth - 1), (2, depth - 3, depth - 2, depth - 1))
+    todo = ((depth - 1,), (depth - 2, depth - 1), (depth - 3, depth - 2, depth - 1))
     for level, new in enumerate((n1, n2, n3)):
         for j, i in enumerate(todo[level]):
             plane(level, i, into(new, j))
             known[level + 1][i] = (new, j)
     total = [None] * fields
     for f in range(fields):
-        gas[f, 0] = first[f]
-    for i in range(1, depth):
+        for i in range(4):
+            gas[f, i] = left[f, i]
+    for i in range(4, depth):
 
         def final(f, sl, res, value, i=i):
             gas[f, i, sl.start - own.start : sl.stop - own.start] = value
@@ -894,13 +913,71 @@
     )
     sent_back = Arrivals(6 * tall, rows, fields, (3, 2, 1, 0))
     one, six = (fields, buf, z), (6, buf, z)
-    back, parts, first, sq, c2, c3, sl_, *lefts = call(
+    back, n2, c2, c3, d1, d2, vm, wm, sl_, *lefts = call(
         functools.partial(cone_kernel, blocks, spans, sent_ahead),
-        [(sent_back.size(), z), (blocks * CHUNK, z)]
-        + held((fields, rows, z), (8, z), one, (fields, 2, buf, z), (2, 4, buf, z))
+        [(sent_back.size(), z)]
+        + held(one, one, one, one, one, (3, buf, z), one, (2, 4, buf, z))
         + held(six, six, six, six, (4, buf, z), (4, buf, z)),
-        [one] * 4 + [(3, buf, z)] + [one] * 3 + [six],
-        [SMEM] * 2 + [VMEM] * 18,
+        [one] * 2 + [six],
+        [SMEM] * 2 + [VMEM] * 13,
+        diffusion,
+        jacobian,
+        p0,
+        s0,
+        v0,
+        w0,
+        p1,
+        te,
+        he,
+        so,
+        ti,
+        dg,
+        ws,
+        xe,
+        xn,
+        cost=COSTS[3],
+    )
+    xr = behind(back, "blk")
+    parts, half, sq = call(
+        functools.partial(flux_kernel, blocks, spans, sent_ahead),
+        [(blocks * CHUNK, z)] + held((fields, 4, rows, z), (8, z)),
+        [(fields, 2, buf, z), one],
+        [SMEM] * 2 + [VMEM] * 17,
+        diffusion,
+        jacobian,
+        s0,
+        v0,
+        w0,
+        p2,
+        p3,
+        n2,
+        c2,
+        c3,
+        d1,
+        d2,
+        vm,
+        wm,
+        xe,
+        xn,
+        wall_coefficient,
+        place,
+        meta,
+        cost=COSTS[2],
+    )
+    arrived = lax.all_to_all(parts.reshape(blocks, CHUNK, z), "blk", 0, 0)
+    surface, yf, yb = call(
+        functools.partial(surface_kernel, blocks),
+        [(2 * rows, z), (2 * W, z), (2 * W, z)],
+        [],
+        [VMEM],
+        arrived,
+    )
+    yl, yr = ahead(yf, "span"), behind(yb, "span")
+    gas, sqf = call(
+        functools.partial(rest_kernel, blocks, spans, sent_back),
+        held(p.shape, (8, z)),
+        [(fields, 1, buf, z), (fields, 2, buf, z), (fields, 3, buf, z)],
+        [SMEM] * 2 + [VMEM] * 11,
         diffusion,
         jacobian,
         p0,
@@ -910,46 +987,7 @@
         p1,
         p2,
         p3,
-        te,
-        he,
-        so,
-        ti,
-        dg,
-        ws,
-        xe,
-        xn,
-        wall_coefficient,
-        place,
-        meta,
-        cost=COSTS[3],
-    )
-    xr = behind(back, "blk")
-    arrived = lax.all_to_all(parts.reshape(blocks, CHUNK, z), "blk", 0, 0)
-    surface, yf, yb = call(
-        functools.partial(surface_kernel, blocks),
-        [(2 * rows, z), (2 * W, z), (2 * W, z)],
-        [],
-        [VMEM],
-        arrived,
-    )
-    yl, yr = ahead(yf, "span"), behind(yb, "span")
-    gas, sqf = call(
-        functools.partial(rest_kernel, blocks, spans, sent_back),
-        held(p.shape, (8, z)),
-        [(fields, 1, buf, z), (fields, 2, buf, z), (fields, 4, buf, z)],
-        [SMEM] * 2 + [VMEM] * 13,
-        diffusion,
-        jacobian,
-        p0,
-        s0,
-        v0,
-        w0,
-        p1,
-        p2,
-        p3,
-        c2,
-        c3,
-        first,
+        half,
         sq,
         xr,
         yf,

time: 67.5 us -> 66.8 us (0.990)
  blocking collectives: 28 us -> 26.3 us
  Pallas kernels: 12.8 us -> 13.6 us
    all_to_all x1, blocking collectives: 13.2 us -> 11.8 us  [shards(): arrived = lax.all_to_all(parts.reshape(blocks, CHUNK, z), 'blk', 0, 0)]
    pallas_call x10 -> x11, Pallas kernels: 12.8 us -> 13.6 us  [call(): pl.pallas_call(kernel, out_shape=[jax.ShapeDtypeStruct(s, F32) if isinsta...]
  transfers between devices with their start and end apart: 11 -> 11, of which waited for: 5 -> 6; matrix products, arithmetic and copies ran while one was open for 2% -> 2% of each run, Pallas kernels for 12% -> 14%
where the time goes in v5:
time: 66.8 us; the launch traced here: 66.6 us
  blocking collectives  26.3 us (39%)
  Pallas kernels  13.6 us (20%)
  starting transfers between devices  11.9 us (18%)
  waiting for transfers between devices  11.7 us (18%)
  local copies, waits for them, and re-layouts  1.58 us (2%)
  between operations  0.77 us (1%)
    all_to_all x1, blocking collectives, shards(): arrived = lax.all_to_all(out, 'blk', 0, 0)  14.5 us
    pallas_call x11, Pallas kernels, call(): pl.pallas_call(kernel, out_shape=[jax.ShapeDtypeStruct(s, F32) if isinsta...  13.6 us
    all_to_all x1, blocking collectives, shards(): arrived = lax.all_to_all(parts.reshape(blocks, CHUNK, z), 'blk', 0, 0)  11.8 us
    ppermute x5, waiting for transfers between devices, ahead(): return lax.ppermute(x, axis, forward[axis])  7.93 us
    ppermute x5, starting transfers between devices, ahead(): return lax.ppermute(x, axis, forward[axis])  5.56 us
    ppermute x4, starting transfers between devices, behind(): return lax.ppermute(x, axis, backward[axis])  5.01 us
    ppermute x4, waiting for transfers between devices, behind(): return lax.ppermute(x, axis, backward[axis])  1.93 us
    ppermute x2, waiting for transfers between devices, shards(): sq = sq + lax.ppermute(sq, 'span', [(i, i ^ step) for i in range(spans)])  1.87 us
  transfers between devices with their start and end apart: 11, of which 6 were waited for; matrix products, arithmetic and copies ran while one was open for 2% of the time, Pallas kernels for 14%

profile of v5, /device:TPU:0, one launch (start us, length us, event | category | flops | bytes accessed | tf_op | source)
XLA Modules:
  0.0 66.6 jit_solution(8043513374522343292)
XLA Ops:
  0.6 0.0 copy-start
  0.6 0.0 copy-start.2
  0.7 1.8 %shard_map.139 = (f32[5,8,32,128]{3,2,1,0:T(8,128)S(1)}, f32[5,8,32,128]{3,2,1,0:T(8,128)S(1)}, f32[3,8,32,128]{3,2,1,0:T(8,128)S(1)}, f32[16,32,128]{2,1,0:T(8,...) custom-call(f32[5,8,32,128]{3,2,1,0:T(8,128)} %refs_0_.1, ...), custom_call_target="tpu_custom_call" | custom-call | flops 1000000 | bytes 3000000 | tf_op jit(solution)/shard_map/pallas_call | solution.py:30
  2.5 0.5 collective-permute-start
  3.0 2.0 %collective-permute-start.1 = (f32[384,128]{1,0:T(8,128)S(1)}, f32[384,128]{1,0:T(8,128)S(1)}, u32[]{:S(2)}, u32[]{:S(2)}) collective-permute-start(f32[384,128]{1,0:T(8,128)S(1)} %get-tuple-element.81), channel_id=1, source_target_pairs={{1,0},{2,1},{3,2},{0,3},{5,4},{6,5},{7,6},{4,7},{9,8},{10,9},{11,1... | collective-permute-start | bytes 589832 | tf_op jit(solution)/shard_map/ppermute | solution.py:847
  5.0 2.2 %collective-permute-start.4 = (f32[672,128]{1,0:T(8,128)S(1)}, f32[672,128]{1,0:T(8,128)S(1)}, u32[]{:S(2)}, u32[]{:S(2)}) collective-permute-start(f32[672,128]{1,0:T(8,128)S(1)} %get-tuple-element.101), channel_id=1, source_target_pairs={{0,4},{4,8},{8,12},{12,16},{16,20},{20,24},{24,28},{28,0},{1,5},{5... | collective-permute-start | bytes 1032200 | tf_op jit(solution)/shard_map/ppermute | solution.py:844
  7.2 1.1 %collective-permute-done.yl = f32[384,128]{1,0:T(8,128)S(1)} collective-permute-done((f32[384,128]{1,0:T(8,128)S(1)}, f32[384,128]{1,0:T(8,128)S(1)}, u32[]{:S(2)}, u32[]{:S(2)}) %collective-permute-start) | collective-permute-done | bytes 196640 | tf_op jit(solution)/shard_map/ppermute | solution.py:844
  8.3 1.9 %collective-permute-done.1.yr = f32[384,128]{1,0:T(8,128)S(1)} collective-permute-done((f32[384,128]{1,0:T(8,128)S(1)}, f32[384,128]{1,0:T(8,128)S(1)}, u32[]{:S(2)}, u32[]{:S(2)}) %collective-permute-start.1) | collective-permute-done | bytes 196640 | tf_op jit(solution)/shard_map/ppermute | solution.py:847
  10.2 0.0 copy-done
  10.2 0.0 copy-done.2
  10.2 1.4 %shard_map.142 = f32[638,128]{1,0:T(8,128)S(1)} custom-call(f32[5]{0:T(128)S(1)} %copy-done.2, f32[5,5]{1,0:T(8,128)S(1)} %copy-done, f32[5,8,32,128]{3,2,1,0:T(8,128)S(1)} %get-tuple-element.77.p, f32[5,8,32,128]{3,2,1,0:T(8,128)S(1)} %get-tuple-element.78.src, f32[3,8,32,128]{3,2,1,0:T(8,128)S(1)} %get-tuple-element.79.vel, ...), custom_call_target="tpu_custom_call" | custom-call | flops 30000000 | bytes 90000000 | tf_op jit(solution)/shard_map/pallas_call | solution.py:30
  11.6 1.5 %collective-permute-start.5 = (f32[638,128]{1,0:T(8,128)S(1)}, f32[638,128]{1,0:T(8,128)S(1)}, u32[]{:S(2)}, u32[]{:S(2)}) collective-permute-start(f32[638,128]{1,0:T(8,128)S(1)} %shard_map.142), channel_id=1, source_target_pairs={{0,4},{4,8},{8,12},{12,16},{16,20},{20,24},{24,28},{28,0},{1,5},{5... | collective-permute-start | bytes 979976 | tf_op jit(solution)/shard_map/ppermute | solution.py:844
  13.1 0.8 %collective-permute-start.2 = (f32[176,128]{1,0:T(8,128)S(1)}, f32[176,128]{1,0:T(8,128)S(1)}, u32[]{:S(2)}, u32[]{:S(2)}) collective-permute-start(f32[176,128]{1,0:T(8,128)S(1)} %get-tuple-element.92), channel_id=1, source_target_pairs={{0,1},{1,2},{2,3},{3,0},{4,5},{5,6},{6,7},{7,4},{8,9},{9,10},{10,1... | collective-permute-start | bytes 270344 | tf_op jit(solution)/shard_map/ppermute | solution.py:844
  13.9 1.1 %collective-permute-start.3 = (f32[176,128]{1,0:T(8,128)S(1)}, f32[176,128]{1,0:T(8,128)S(1)}, u32[]{:S(2)}, u32[]{:S(2)}) collective-permute-start(f32[176,128]{1,0:T(8,128)S(1)} %get-tuple-element.93), channel_id=1, source_target_pairs={{1,0},{2,1},{3,2},{0,3},{5,4},{6,5},{7,6},{4,7},{9,8},{10,9},{11,1... | collective-permute-start | bytes 270344 | tf_op jit(solution)/shard_map/ppermute | solution.py:847
  15.1 0.0 copy-done.3
  15.1 0.0 copy-done.4
  15.1 2.3 %shard_map.140 = (f32[5,8,56,128]{3,2,1,0:T(8,128)S(1)}, f32[5,8,56,128]{3,2,1,0:T(8,128)S(1)}, f32[3,8,56,128]{3,2,1,0:T(8,128)S(1)}, f32[5,8,56,128]{3,2,1,0:T...) custom-call(f32[5]{0:T(128)S(1)} %copy-done.2, ...), custom_call_target="tpu_custom_call" | custom-call | flops 10000 | bytes 30000 | tf_op jit(solution)/shard_map/pallas_call | solution.py:30
  17.4 0.0 collective-permute-done.2.yl
  17.4 0.0 collective-permute-done.3.yr
  17.4 1.4 %shard_map.141 = (f32[16,56,128]{2,1,0:T(8,128)S(1)}, f32[16,56,128]{2,1,0:T(8,128)S(1)}, f32[16,56,128]{2,1,0:T(8,128)S(1)}, f32[3,4,56,128]{3,2,1,0:T(8,128)S(...) custom-call(f32[16,32,128]{2,1,0:T(8,128)S(1)} %get-tuple-element.89, ...), custom_call_target="tpu_custom_call" | custom-call | flops 10000 | bytes 30000 | tf_op jit(solution)/shard_map/pallas_call | solution.py:30
  18.8 0.0 collective-permute-done.4.refs_11_.refs_12_
  18.8 6.6 %collective-permute-done.5.refs_12_.refs_13_ = f32[638,128]{1,0:T(8,128)S(1)} collective-permute-done((f32[638,128]{1,0:T(8,128)S(1)}, f32[638,128]{1,0:T(8,128)S(1)}, u32[]{:S(2)}, u32[]{:S(2)}) %collective-permute-start.5) | collective-permute-done | bytes 326688 | tf_op jit(solution)/shard_map/ppermute | solution.py:844
  25.4 1.7 %shard_map.143 = (f32[940,128]{1,0:T(8,128)S(1)}, f32[5,56,128]{2,1,0:T(8,128)S(1)}, f32[5,56,128]{2,1,0:T(8,128)S(1)}, f32[5,56,128]{2,1,0:T(8,128)S(1)}, f32[5...) custom-call(f32[5]{0:T(128)S(1)} %copy-done.2, ...), custom_call_target="tpu_custom_call" | custom-call | flops 2000000 | bytes 6000000 | tf_op jit(solution)/shard_map/pallas_call | solution.py:30
  27.1 1.8 %collective-permute-start.6 = (f32[940,128]{1,0:T(8,128)S(1)}, f32[940,128]{1,0:T(8,128)S(1)}, u32[]{:S(2)}, u32[]{:S(2)}) collective-permute-start(f32[940,128]{1,0:T(8,128)S(1)} %get-tuple-element.113), channel_id=1, source_target_pairs={{4,0},{8,4},{12,8},{16,12},{20,16},{24,20},{28,24},{0,28},{5,1},{9... | collective-permute-start | bytes 1443848 | tf_op jit(solution)/shard_map/ppermute | solution.py:847
  28.9 0.0 copy-done.1
  28.9 1.4 %shard_map.144 = (f32[256,128]{1,0:T(8,128)S(1)}, f32[5,4,32,128]{3,2,1,0:T(8,128)S(1)}, f32[8,128]{1,0:T(8,128)S(1)}) custom-call(f32[5]{0:T(128)S(1)} %copy-done.2, f32[5,5]{1,0:T(8,128)S(1)} %copy-done, f32[5,8,56,128]{3,2,1,0:T(8,128)S(1)} %get-tuple-element.83.refs_1_.refs_0_, f32[3,8,56,128]{3,2,1,0:T(8,128)S(1)} %get-tuple-element.84.refs_2_.refs_1_, ...), custom_call_target="tpu_custom_call" | custom-call | flops 10000 | bytes 30000 | tf_op jit(solution)/shard_map/pallas_call | solution.py:30
  30.4 11.8 %all_to_all.10.arrived = f32[8,32,128]{2,1,0:T(8,128)S(1)} all-to-all(f32[8,32,128]{2,1,0:T(8,128)S(1)} %bitcast.6), channel_id=1, replica_groups=mesh['blk'=8,'span'=4] {'blk'}, dimensions={0} | all-to-all | bytes 262144 | tf_op jit(solution)/shard_map/all_to_all | solution.py:967
  42.1 0.2 shard_map.145
  42.4 0.1 collective-permute-start.8
  42.4 0.5 collective-permute-start.7
  42.9 0.0 collective-permute-done.6.refs_9_.xb
  42.9 1.7 %shard_map.146 = (f32[5,8,32,128]{3,2,1,0:T(8,128)S(1)}, f32[8,128]{1,0:T(8,128)S(1)}) custom-call(f32[5]{0:T(128)S(1)} %copy-done.2, f32[5,5]{1,0:T(8,128)S(1)} %copy-done, f32[5,8,56,128]{3,2,1,0:T(8,128)S(1)} %get-tuple-element.82.refs_0_, f32[5,8,56,128]{3,2,1,0:T(8,128)S(1)} %get-tuple-element.83.refs_1_.refs_0_, ...), custom_call_target="tpu_custom_call" | custom-call | flops 3000000 | bytes 9000000 | tf_op jit(solution)/shard_map/pallas_call | solution.py:30
  44.7 0.5 shard_map.147
  45.2 0.0 collective-permute-done.8.yr
  45.3 0.3 collective-permute-done.7.yl
  45.5 0.7 %shard_map.148 = (f32[16,32,128]{2,1,0:T(8,128)S(1)}, f32[8,40,128]{2,1,0:T(8,128)S(1)}) custom-call(f32[64,128]{1,0:T(8,128)S(1)} %get-tuple-element.117.surface, f32[8,128]{1,0:T(8,128)S(1)} %collective-permute-done.7.yl, f32[8,128]{1,0:T(8,128)S(1)} %collective-permute-done.8.yr, f32[2,5,56,128]{3,2,1,0:T(8,128)S(1)} %get-tuple-element.128.rh, ...), custom_call_target="tpu_custom_call" | custom-call | flops 1000000 | bytes 3000000 | tf_op jit(solution)/shard_map/pallas_call | solution.py:30
  46.2 0.0 copy-start.5
  46.3 14.5 %all_to_all.11.arrived = f32[8,40,128]{2,1,0:T(8,128)S(1)} all-to-all(f32[8,40,128]{2,1,0:T(8,128)S(1)} %get-tuple-element.135), channel_id=1, replica_groups=mesh['blk'=8,'span'=4] {'blk'}, dimensions={0} | all-to-all | bytes 327680 | tf_op jit(solution)/shard_map/all_to_all | solution.py:1033
  60.8 0.4 shard_map.149
  61.1 0.0 collective-permute-start.9
  61.1 0.7 %copy.17 = f32[16,32,128]{2,1,0:T(8,128)} copy(f32[16,32,128]{2,1,0:T(8,128)S(1)} %get-tuple-element.140) | data formatting | bytes 524288
  61.8 0.5 collective-permute-done.9
  62.3 1.4 %collective-permute-start.10 = (f32[8,128]{1,0:T(8,128)S(1)}, f32[8,128]{1,0:T(8,128)S(1)}, u32[]{:S(2)}, u32[]{:S(2)}) collective-permute-start(f32[8,128]{1,0:T(8,128)S(1)} %add.14), channel_id=1, source_target_pairs={{0,2},{1,3},{2,0},{3,1},{4,6},{5,7},{6,4},{7,5},{8,10},{9,11},{10,... | collective-permute-start | bytes 12296 | tf_op jit(solution)/shard_map/ppermute | solution.py:1045
  63.7 0.8 %copy.16 = f32[5,8,32,128]{3,2,1,0:T(8,128)} copy(f32[5,8,32,128]{3,2,1,0:T(8,128)S(1)} %fusion) | data formatting | bytes 1310720
  64.5 1.4 %collective-permute-done.10 = f32[8,128]{1,0:T(8,128)S(1)} collective-permute-done((f32[8,128]{1,0:T(8,128)S(1)}, f32[8,128]{1,0:T(8,128)S(1)}, u32[]{:S(2)}, u32[]{:S(2)}) %collective-permute-start.10) | collective-permute-done | bytes 4128 | tf_op jit(solution)/shard_map/ppermute | solution.py:1045
  65.9 0.1 slice_reduce_fusion
  66.0 0.0 copy-done.5
  66.0 0.5 multiply_sqrt_fusion
  (6 shorter events, 0.0 us)
Async XLA Ops:
  0.6 9.6 %copy-start = (f32[5,5]{1,0:T(8,128)S(1)}, f32[5,5]{1,0:T(8,128)}, u32[]{:S(2)}) copy-start(f32[5,5]{1,0:T(8,128)} %jacobian.9) | copy-start | bytes 304
  0.6 9.6 %copy-start.2 = (f32[5]{0:T(128)S(1)}, f32[5]{0:T(128)}, u32[]{:S(2)}) copy-start(f32[5]{0:T(128)} %spread.9) | copy-start | bytes 64
  2.5 5.8 %collective-permute-start = (f32[384,128]{1,0:T(8,128)S(1)}, f32[384,128]{1,0:T(8,128)S(1)}, u32[]{:S(2)}, u32[]{:S(2)}) collective-permute-start(f32[384,128]{1,0:T(8,128)S(1)} %get-tuple-element.80), channel_id=1, source_target_pairs={{0,1},{1,2},{2,3},{3,0},{4,5},{5,6},{6,7},{7,4},{8,9},{9,10},{10,1... | collective-permute-start | bytes 589832 | tf_op jit(solution)/shard_map/ppermute | solution.py:844
  3.0 7.2 %collective-permute-start.1 = (f32[384,128]{1,0:T(8,128)S(1)}, f32[384,128]{1,0:T(8,128)S(1)}, u32[]{:S(2)}, u32[]{:S(2)}) collective-permute-start(f32[384,128]{1,0:T(8,128)S(1)} %get-tuple-element.81), channel_id=1, source_target_pairs={{1,0},{2,1},{3,2},{0,3},{5,4},{6,5},{7,6},{4,7},{9,8},{10,9},{11,1... | collective-permute-start | bytes 589832 | tf_op jit(solution)/shard_map/ppermute | solution.py:847
  5.0 13.8 %collective-permute-start.4 = (f32[672,128]{1,0:T(8,128)S(1)}, f32[672,128]{1,0:T(8,128)S(1)}, u32[]{:S(2)}, u32[]{:S(2)}) collective-permute-start(f32[672,128]{1,0:T(8,128)S(1)} %get-tuple-element.101), channel_id=1, source_target_pairs={{0,4},{4,8},{8,12},{12,16},{16,20},{20,24},{24,28},{28,0},{1,5},{5... | collective-permute-start | bytes 1032200 | tf_op jit(solution)/shard_map/ppermute | solution.py:844
  10.2 4.8 %copy-start.3 = (s32[1,32,1]{1,2,0:T(1,128)S(1)}, s32[1,32,1]{1,2,0:T(1,128)}, u32[]{:S(2)}) copy-start(s32[1,32,1]{1,2,0:T(1,128)} %param.23) | copy-start | bytes 388
  10.2 4.8 %copy-start.4 = (s32[1,32]{1,0:T(1,128)S(1)}, s32[1,32]{1,0:T(1,128)}, u32[]{:S(2)}) copy-start(s32[1,32]{1,0:T(1,128)} %target.1) | copy-start | bytes 388
  11.6 13.8 %collective-permute-start.5 = (f32[638,128]{1,0:T(8,128)S(1)}, f32[638,128]{1,0:T(8,128)S(1)}, u32[]{:S(2)}, u32[]{:S(2)}) collective-permute-start(f32[638,128]{1,0:T(8,128)S(1)} %shard_map.142), channel_id=1, source_target_pairs={{0,4},{4,8},{8,12},{12,16},{16,20},{20,24},{24,28},{28,0},{1,5},{5... | collective-permute-start | bytes 979976 | tf_op jit(solution)/shard_map/ppermute | solution.py:844
  13.1 4.3 %collective-permute-start.2 = (f32[176,128]{1,0:T(8,128)S(1)}, f32[176,128]{1,0:T(8,128)S(1)}, u32[]{:S(2)}, u32[]{:S(2)}) collective-permute-start(f32[176,128]{1,0:T(8,128)S(1)} %get-tuple-element.92), channel_id=1, source_target_pairs={{0,1},{1,2},{2,3},{3,0},{4,5},{5,6},{6,7},{7,4},{8,9},{9,10},{10,1... | collective-permute-start | bytes 270344 | tf_op jit(solution)/shard_map/ppermute | solution.py:844
  13.9 3.5 %collective-permute-start.3 = (f32[176,128]{1,0:T(8,128)S(1)}, f32[176,128]{1,0:T(8,128)S(1)}, u32[]{:S(2)}, u32[]{:S(2)}) collective-permute-start(f32[176,128]{1,0:T(8,128)S(1)} %get-tuple-element.93), channel_id=1, source_target_pairs={{1,0},{2,1},{3,2},{0,3},{5,4},{6,5},{7,6},{4,7},{9,8},{10,9},{11,1... | collective-permute-start | bytes 270344 | tf_op jit(solution)/shard_map/ppermute | solution.py:847
  25.4 3.6 %copy-start.1 = (f32[1,32,128]{2,1,0:T(8,128)S(1)}, f32[1,32,128]{2,1,0:T(8,128)}, u32[]{:S(2)}) copy-start(f32[1,32,128]{2,1,0:T(8,128)} %coef.1) | copy-start | bytes 49156
  27.1 15.8 %collective-permute-start.6 = (f32[940,128]{1,0:T(8,128)S(1)}, f32[940,128]{1,0:T(8,128)S(1)}, u32[]{:S(2)}, u32[]{:S(2)}) collective-permute-start(f32[940,128]{1,0:T(8,128)S(1)} %get-tuple-element.113), channel_id=1, source_target_pairs={{4,0},{8,4},{12,8},{16,12},{20,16},{24,20},{28,24},{0,28},{5,1},{9... | collective-permute-start | bytes 1443848 | tf_op jit(solution)/shard_map/ppermute | solution.py:847
  42.4 2.9 %collective-permute-start.8 = (f32[8,128]{1,0:T(8,128)S(1)}, f32[8,128]{1,0:T(8,128)S(1)}, u32[]{:S(2)}, u32[]{:S(2)}) collective-permute-start(f32[8,128]{1,0:T(8,128)S(1)} %get-tuple-element.118), channel_id=1, source_target_pairs={{1,0},{2,1},{3,2},{0,3},{5,4},{6,5},{7,6},{4,7},{9,8},{10,9},{11,1... | collective-permute-start | bytes 12296 | tf_op jit(solution)/shard_map/ppermute | solution.py:847
  42.4 3.1 %collective-permute-start.7 = (f32[8,128]{1,0:T(8,128)S(1)}, f32[8,128]{1,0:T(8,128)S(1)}, u32[]{:S(2)}, u32[]{:S(2)}) collective-permute-start(f32[8,128]{1,0:T(8,128)S(1)} %get-tuple-element.115.refs_10_._), channel_id=1, source_target_pairs={{0,1},{1,2},{2,3},{3,0},{4,5},{5,6},{6,7},{7,4},{8,9},{9,10},{10,1... | collective-permute-start | bytes 12296 | tf_op jit(solution)/shard_map/ppermute | solution.py:844
  46.2 19.8 %copy-start.5 = (f32[6]{0:T(128)S(1)}, f32[6]{0:T(128)}, u32[]{:S(2)}) copy-start(f32[6]{0:T(128)} %constant.41) | copy-start | bytes 76
  61.1 1.2 %collective-permute-start.9 = (f32[8,128]{1,0:T(8,128)S(1)}, f32[8,128]{1,0:T(8,128)S(1)}, u32[]{:S(2)}, u32[]{:S(2)}) collective-permute-start(f32[8,128]{1,0:T(8,128)S(1)} %get-tuple-element.138), channel_id=1, source_target_pairs={{0,1},{1,0},{2,3},{3,2},{4,5},{5,4},{6,7},{7,6},{8,9},{9,8},{10,11... | collective-permute-start | bytes 12296 | tf_op jit(solution)/shard_map/ppermute | solution.py:1045
  62.3 3.6 %collective-permute-start.10 = (f32[8,128]{1,0:T(8,128)S(1)}, f32[8,128]{1,0:T(8,128)S(1)}, u32[]{:S(2)}, u32[]{:S(2)}) collective-permute-start(f32[8,128]{1,0:T(8,128)S(1)} %add.14), channel_id=1, source_target_pairs={{0,2},{1,3},{2,0},{3,1},{4,6},{5,7},{6,4},{7,5},{8,10},{9,11},{10,... | collective-permute-start | bytes 12296 | tf_op jit(solution)/shard_map/ppermute | solution.py:1045

commit v6 on v5

--- a/solution.py
+++ b/solution.py
@@ -26,12 +26,12 @@
     return [pltpu.VMEM(s, F32) for s in shapes]
 
 
-def call(kernel, outs, scratch, specs, *args, cost=1.0):
+def call(kernel, outs, scratch, specs, *args, out_specs=None, cost=1.0):
     return pl.pallas_call(
         kernel,
         out_shape=[jax.ShapeDtypeStruct(s, F32) if isinstance(s, tuple) else s for s in outs],
         in_specs=specs,
-        out_specs=[VMEM] * len(outs),
+        out_specs=out_specs or [VMEM] * len(outs),
         scratch_shapes=[pltpu.VMEM(s, F32) if isinstance(s, tuple) else s for s in scratch],
         compiler_params=pltpu.CompilerParams(vmem_limit_bytes=LIMIT),
         cost_estimate=pl.CostEstimate(
@@ -199,12 +199,22 @@
     ]
     for copy in copies:
         copy.start()
-    for copy in copies:
-        copy.wait()
     p, src, vel, t, heat, k = bufs
     fields, depth, rows = p.shape[0], p.shape[1], p.shape[2]
     thick = t.shape[0]
     named = {"p": p, "src": src, "vel": vel, "t": t, "heat": heat, "k": k}
+
+    def pack(up, down, places, names):
+        for (name, *at_plane), sl in places.items():
+            if name in names:
+                ref, reach = named[name], sl.stop - sl.start
+                up[sl] = ref[*at_plane, rows - reach :]
+                down[sl] = ref[*at_plane, :reach]
+
+    for j, name in enumerate(named):
+        copies[j].wait()
+        if j < 3:
+            pack(yf, yb, edges.fluid, (name,))
     planes = [p[f, depth - 1] for f in range(fields)]
     planes += [vel[f, depth - 1] for f in range(3)]
     planes += [vel[0, depth - 2], vel[0, depth - 2] + vel[1, depth - 2] + vel[2, depth - 2]]
@@ -213,11 +223,8 @@
     planes += [heat[thick - 3 + j] for j in range(3)]
     for j, plane in enumerate(planes):
         xf[j * rows : (j + 1) * rows] = plane
-    for up, down, places in ((yf, yb, edges.fluid), (yf, yb, edges.outer), (zf, zb, edges.solid)):
-        for (name, *at_plane), sl in places.items():
-            ref, reach = named[name], sl.stop - sl.start
-            up[sl] = ref[*at_plane, rows - reach :]
-            down[sl] = ref[*at_plane, :reach]
+    for up, down, places in ((yf, yb, edges.outer), (zf, zb, edges.solid)):
+        pack(up, down, places, named)
 
 
 def ahead_kernel(blocks, spans, edges, spread, jacobian, p, src, vel, yl, yr, out, a0, a1, a2, sa, va, wa):
@@ -422,7 +429,7 @@
     sqi[fields : fields + 1] = jnp.sum(total, axis=0, keepdims=True)
 
 
-def cone_kernel(blocks, spans, sent, spread, jacobian, *refs):
+def cone_kernel(blocks, spans, sent, solid, spread, jacobian, *refs):
     p0, s0, v0, w0, p1, te, he, so, ti, dg, ws, xe, xn = refs[:13]
     back, n2, c2, c3, d1, d2, vm, wm, sl_, t0, t1, t2, t3, dl, wl = refs[13:28]
     l0, n1, qa = refs[28:]
@@ -472,7 +479,7 @@
     plane(at(p1, 0), 1, flat(n1), at(p1, 1), into_flat(c2))
     fluid.advance(flat(d1), None, flat(n1), outer, flat(wm), None, ext, into_flat(d2))
     plane(flat(n2), 0, sum_of(2, d2), flat(c2), into_flat(c3))
-    n = 6 * tall
+    n = solid.size()
     for reach, read in (
         (3, at(p0, 0)),
         (2, flat(n1)),
@@ -523,13 +530,10 @@
             new[j, ext] = q + w[m, ext] * res
         for j in range(4, 6):
             new[j] = ti[level, j - 4]
-    n = 0
-    for ref, i in ((he, 0), (he, 1), (t0, 4), (t1, 3)):
-        back[n : n + tall] = ref[i, ext]
-        n = n + tall
-    for ref, i in ((t2, 2), (t3, 1)):
-        back[n : n + tall] = ref[i, ext]
-        n = n + tall
+    for level, (ref, i) in enumerate(((he, 0), (he, 1), (t0, 4), (t1, 3), (t2, 2), (t3, 1))):
+        sl = solid.window(level, 0)
+        reach = solid.reaches[level]
+        back[sl.start + W - reach : sl.stop - W + reach] = ref[i, here.reach(reach)]
 
 
 def flux_kernel(blocks, spans, sent, spread, jacobian, *refs):
@@ -635,7 +639,7 @@
 
 
 def solid_kernel(
-    blocks, spans, te, he, so, ti, tbi, sqi, dg, ws, sl_, tl0, tl1, tl2, tl3, dl, wl, xb, _, *refs
+    blocks, spans, sent, te, he, so, ti, tbi, sqi, dg, ws, sl_, tl0, tl1, tl2, tl3, dl, wl, xb, _, *refs
 ):
     tb, rb, sq, rh, rd, rw = refs[:6]
     hr, dr, wr, ta, tc, qa = refs[6:]
@@ -645,7 +649,7 @@
     hl = sl_.at[0]
 
     def arrived(n):
-        return unless(here.no_right, xb[n * tall : (n + 1) * tall])
+        return unless(here.no_right, xb[sent.window(n, 0)])
 
     for j in range(2):
         hr[j, ext] = arrived(j)
@@ -794,10 +798,29 @@
         out[j, rows:] = sq
 
 
-def return_kernel(blocks, arrived, idx, coef, added, sq):
-    rows = added.shape[0]
+def squares_kernel(blocks, rows, arrived, sq):
+    whole = arrived[0, rows:]
+    for j in range(1, blocks):
+        whole = whole + arrived[j, rows:]
+    sq[...] = whole
+
+
+def return_kernel(blocks, arrived, idx, coef, gas, t, gas_out, t_out, plane, sems):
+    fields, rows = gas.shape[0], gas.shape[2]
+    last = fields - 1
+    copies = [
+        pltpu.make_async_copy(gas.at[pl.ds(0, last)], gas_out.at[pl.ds(0, last)], sems.at[0]),
+        pltpu.make_async_copy(
+            gas.at[last, pl.ds(1, gas.shape[1] - 1)],
+            gas_out.at[last, pl.ds(1, gas.shape[1] - 1)],
+            sems.at[1],
+        ),
+        pltpu.make_async_copy(t, t_out, sems.at[2]),
+    ]
+    for copy in copies:
+        copy.start()
     row = lax.broadcasted_iota(jnp.int32, (rows, rows), 0).astype(F32)
-    taken, squares = None, None
+    taken = None
     for j in range(blocks):
         hot = jnp.where(idx[...] - float(j * rows) == row, 1.0, 0.0)
         got = lax.dot_general(
@@ -808,9 +831,12 @@
             preferred_element_type=F32,
         )
         taken = got if taken is None else taken + got
-        squares = arrived[j, rows:] if squares is None else squares + arrived[j, rows:]
-    added[...] = coef[0] * taken
-    sq[...] = squares
+    plane[...] = gas[last, 0] + coef[0] * taken
+    copy = pltpu.make_async_copy(plane, gas_out.at[last, 0], sems.at[3])
+    copy.start()
+    for other in copies:
+        other.wait()
+    copy.wait()
 
 
 def shards(
@@ -911,10 +937,11 @@
         idx,
         cost=COSTS[2],
     )
-    sent_back = Arrivals(6 * tall, rows, fields, (3, 2, 1, 0))
+    solid_back = Arrivals(8, rows, 1, (3, 1, 3, 2, 1, 0))
+    sent_back = Arrivals(solid_back.size(), rows, fields, (3, 2, 1, 0))
     one, six = (fields, buf, z), (6, buf, z)
     back, n2, c2, c3, d1, d2, vm, wm, sl_, *lefts = call(
-        functools.partial(cone_kernel, blocks, spans, sent_ahead),
+        functools.partial(cone_kernel, blocks, spans, sent_ahead, solid_back),
         [(sent_back.size(), z)]
         + held(one, one, one, one, one, (3, buf, z), one, (2, 4, buf, z))
         + held(six, six, six, six, (4, buf, z), (4, buf, z)),
@@ -937,7 +964,7 @@
         xn,
         cost=COSTS[3],
     )
-    xr = behind(back, "blk")
+    xr = lax.ppermute(back, "blk", backward["blk"][: blocks - 1])
     parts, half, sq = call(
         functools.partial(flux_kernel, blocks, spans, sent_ahead),
         [(blocks * CHUNK, z)] + held((fields, 4, rows, z), (8, z)),
@@ -995,7 +1022,7 @@
     )
     two, edge = (2, buf, z), (2, 5, buf, z)
     tb, rb, sqs, rh, rd, rw = call(
-        functools.partial(solid_kernel, blocks, spans),
+        functools.partial(solid_kernel, blocks, spans, solid_back),
         held(t.shape, (7, rows, z), (8, z), edge, edge, edge),
         [two] * 3 + [six] * 3,
         [VMEM] * 17,
@@ -1031,20 +1058,26 @@
         sqs,
     )
     arrived = lax.all_to_all(out, "blk", 0, 0)
-    added, sq = call(
+    (sq,) = call(
+        functools.partial(squares_kernel, blocks, rows), held((8, z)), [], [VMEM], arrived
+    )
+    others = [
+        lax.ppermute(sq, "span", [(i, i ^ step) for i in range(spans)]) for step in range(1, spans)
+    ]
+    gas, t = call(
         functools.partial(return_kernel, blocks),
-        [(rows, z), (8, z)],
-        [],
-        [VMEM] * 3,
+        [gas.shape, t.shape],
+        [(rows, z), pltpu.SemaphoreType.DMA((4,))],
+        [VMEM] * 5,
         arrived,
         idx,
         wall_coefficient,
-    )
-    step = 1
-    while step < spans:
-        sq = sq + lax.ppermute(sq, "span", [(i, i ^ step) for i in range(spans)])
-        step = step * 2
-    gas = gas.at[fields - 1, 0].add(added)
+        gas,
+        t,
+        out_specs=[pl.BlockSpec(memory_space=pl.ANY)] * 2,
+        cost=2.0,
+    )
+    sq = functools.reduce(jnp.add, others, sq)
     everyone = blocks * spans
     counts = [float(depth * rows * z * everyone)] * fields + [float(thick * rows * z * everyone)]
     totals = jnp.sum(sq[: fields + 1], axis=1)

time: 66.8 us -> 64 us (0.958)
  local copies, waits for them, and re-layouts: 1.58 us -> 0.02 us
  blocking collectives: 26.3 us -> 25.5 us
  waiting for transfers between devices: 11.7 us -> 10.9 us
    all_to_all x1, blocking collectives: 14.5 us -> 11.1 us  [shards(): arrived = lax.all_to_all(out, 'blk', 0, 0)]
    all_to_all x1, blocking collectives: 11.8 us -> 14.4 us  [shards(): arrived = lax.all_to_all(parts.reshape(blocks, CHUNK, z), 'blk', 0, 0)]
    ppermute x4 -> x3, starting transfers between devices: 5.01 us -> 3.2 us  [behind(): return lax.ppermute(x, axis, backward[axis])]
    ppermute x2 -> x4, starting transfers between devices: 1.35 us -> 3.15 us  [the longest x3 1.86 us: shards(): lax.ppermute(sq, 'span', [(i, i ^ step) for i in range(spans)])]
    unnamed x14 -> x12, local copies, waits for them, and re-layouts: 1.58 us -> 0.02 us
    ppermute x2 -> x4, waiting for transfers between devices: 1.87 us -> 0.81 us  [the longest x3 0.8 us: shards(): lax.ppermute(sq, 'span', [(i, i ^ step) for i in range(spans)])]
    pallas_call x11 -> x12, Pallas kernels: 13.6 us -> 14 us  [call(): pl.pallas_call(kernel, out_shape=[jax.ShapeDtypeStruct(s, F32) if isinsta...]
    ppermute x4 -> x3, waiting for transfers between devices: 1.93 us -> 1.93 us  [behind(): return lax.ppermute(x, axis, backward[axis])]
  transfers between devices with their start and end apart: 11 -> 12, of which waited for: 6 -> 6; matrix products, arithmetic and copies ran while one was open for 2% -> 0% of each run, Pallas kernels for 14% -> 15%
where the time goes in v6:
time: 64 us; the launch traced here: 63.8 us
  blocking collectives  25.5 us (40%)
  Pallas kernels  14 us (22%)
  starting transfers between devices  11.9 us (19%)
  waiting for transfers between devices  10.9 us (17%)
  between operations  0.79 us (1%)
  other arithmetic  0.64 us (1%)
    all_to_all x1, blocking collectives, shards(): arrived = lax.all_to_all(parts.reshape(blocks, CHUNK, z), 'blk', 0, 0)  14.4 us
    pallas_call x12, Pallas kernels, call(): pl.pallas_call(kernel, out_shape=[jax.ShapeDtypeStruct(s, F32) if isinsta...  14 us
    all_to_all x1, blocking collectives, shards(): arrived = lax.all_to_all(out, 'blk', 0, 0)  11.1 us
    ppermute x5, waiting for transfers between devices, ahead(): return lax.ppermute(x, axis, forward[axis])  8.16 us
    ppermute x5, starting transfers between devices, ahead(): return lax.ppermute(x, axis, forward[axis])  5.56 us
    ppermute x3, starting transfers between devices, behind(): return lax.ppermute(x, axis, backward[axis])  3.2 us
    ppermute x3, waiting for transfers between devices, behind(): return lax.ppermute(x, axis, backward[axis])  1.93 us
    ppermute x3, starting transfers between devices, shards(): lax.ppermute(sq, 'span', [(i, i ^ step) for i in range(spans)])  1.86 us
  transfers between devices with their start and end apart: 12, of which 6 were waited for; matrix products, arithmetic and copies ran while one was open for 0% of the time, Pallas kernels for 15%

profile of v6, /device:TPU:0, one launch (start us, length us, event | category | flops | bytes accessed | tf_op | source)
XLA Modules:
  0.0 63.8 jit_solution(5023265076236319994)
XLA Ops:
  0.6 0.0 copy-start
  0.6 0.0 copy-start.2
  0.7 1.7 %shard_map.139 = (f32[5,8,32,128]{3,2,1,0:T(8,128)S(1)}, f32[5,8,32,128]{3,2,1,0:T(8,128)S(1)}, f32[3,8,32,128]{3,2,1,0:T(8,128)S(1)}, f32[16,32,128]{2,1,0:T(8,...) custom-call(f32[5,8,32,128]{3,2,1,0:T(8,128)} %refs_0_.1, ...), custom_call_target="tpu_custom_call" | custom-call | flops 1000000 | bytes 3000000 | tf_op jit(solution)/shard_map/pallas_call | solution.py:30
  2.4 0.5 collective-permute-start
  2.9 2.0 %collective-permute-start.1 = (f32[384,128]{1,0:T(8,128)S(1)}, f32[384,128]{1,0:T(8,128)S(1)}, u32[]{:S(2)}, u32[]{:S(2)}) collective-permute-start(f32[384,128]{1,0:T(8,128)S(1)} %get-tuple-element.69), channel_id=1, source_target_pairs={{1,0},{2,1},{3,2},{0,3},{5,4},{6,5},{7,6},{4,7},{9,8},{10,9},{11,1... | collective-permute-start | bytes 589832 | tf_op jit(solution)/shard_map/ppermute | solution.py:873
  4.9 2.2 %collective-permute-start.4 = (f32[672,128]{1,0:T(8,128)S(1)}, f32[672,128]{1,0:T(8,128)S(1)}, u32[]{:S(2)}, u32[]{:S(2)}) collective-permute-start(f32[672,128]{1,0:T(8,128)S(1)} %get-tuple-element.89), channel_id=1, source_target_pairs={{0,4},{4,8},{8,12},{12,16},{16,20},{20,24},{24,28},{28,0},{1,5},{5... | collective-permute-start | bytes 1032200 | tf_op jit(solution)/shard_map/ppermute | solution.py:870
  7.1 1.1 %collective-permute-done.yl = f32[384,128]{1,0:T(8,128)S(1)} collective-permute-done((f32[384,128]{1,0:T(8,128)S(1)}, f32[384,128]{1,0:T(8,128)S(1)}, u32[]{:S(2)}, u32[]{:S(2)}) %collective-permute-start) | collective-permute-done | bytes 196640 | tf_op jit(solution)/shard_map/ppermute | solution.py:870
  8.2 1.9 %collective-permute-done.1.yr = f32[384,128]{1,0:T(8,128)S(1)} collective-permute-done((f32[384,128]{1,0:T(8,128)S(1)}, f32[384,128]{1,0:T(8,128)S(1)}, u32[]{:S(2)}, u32[]{:S(2)}) %collective-permute-start.1) | collective-permute-done | bytes 196640 | tf_op jit(solution)/shard_map/ppermute | solution.py:873
  10.1 0.0 copy-done
  10.1 0.0 copy-done.2
  10.2 0.0 copy-start.3
  10.2 1.4 %shard_map.142 = f32[638,128]{1,0:T(8,128)S(1)} custom-call(f32[5]{0:T(128)S(1)} %copy-done.2, f32[5,5]{1,0:T(8,128)S(1)} %copy-done, f32[5,8,32,128]{3,2,1,0:T(8,128)S(1)} %get-tuple-element.65.p, f32[5,8,32,128]{3,2,1,0:T(8,128)S(1)} %get-tuple-element.66.src, f32[3,8,32,128]{3,2,1,0:T(8,128)S(1)} %get-tuple-element.67.vel, ...), custom_call_target="tpu_custom_call" | custom-call | flops 30000000 | bytes 90000000 | tf_op jit(solution)/shard_map/pallas_call | solution.py:30
  11.5 1.5 %collective-permute-start.5 = (f32[638,128]{1,0:T(8,128)S(1)}, f32[638,128]{1,0:T(8,128)S(1)}, u32[]{:S(2)}, u32[]{:S(2)}) collective-permute-start(f32[638,128]{1,0:T(8,128)S(1)} %shard_map.142), channel_id=1, source_target_pairs={{0,4},{4,8},{8,12},{12,16},{16,20},{20,24},{24,28},{28,0},{1,5},{5... | collective-permute-start | bytes 979976 | tf_op jit(solution)/shard_map/ppermute | solution.py:870
  13.1 0.8 %collective-permute-start.2 = (f32[176,128]{1,0:T(8,128)S(1)}, f32[176,128]{1,0:T(8,128)S(1)}, u32[]{:S(2)}, u32[]{:S(2)}) collective-permute-start(f32[176,128]{1,0:T(8,128)S(1)} %get-tuple-element.80), channel_id=1, source_target_pairs={{0,1},{1,2},{2,3},{3,0},{4,5},{5,6},{6,7},{7,4},{8,9},{9,10},{10,1... | collective-permute-start | bytes 270344 | tf_op jit(solution)/shard_map/ppermute | solution.py:870
  13.9 1.1 %collective-permute-start.3 = (f32[176,128]{1,0:T(8,128)S(1)}, f32[176,128]{1,0:T(8,128)S(1)}, u32[]{:S(2)}, u32[]{:S(2)}) collective-permute-start(f32[176,128]{1,0:T(8,128)S(1)} %get-tuple-element.81), channel_id=1, source_target_pairs={{1,0},{2,1},{3,2},{0,3},{5,4},{6,5},{7,6},{4,7},{9,8},{10,9},{11,1... | collective-permute-start | bytes 270344 | tf_op jit(solution)/shard_map/ppermute | solution.py:873
  15.0 0.0 copy-done.3
  15.0 0.0 copy-done.4
  15.0 2.3 %shard_map.140 = (f32[5,8,56,128]{3,2,1,0:T(8,128)S(1)}, f32[5,8,56,128]{3,2,1,0:T(8,128)S(1)}, f32[3,8,56,128]{3,2,1,0:T(8,128)S(1)}, f32[5,8,56,128]{3,2,1,0:T...) custom-call(f32[5]{0:T(128)S(1)} %copy-done.2, ...), custom_call_target="tpu_custom_call" | custom-call | flops 10000 | bytes 30000 | tf_op jit(solution)/shard_map/pallas_call | solution.py:30
  17.3 0.0 collective-permute-done.2.yl
  17.3 0.0 collective-permute-done.3.yr
  17.4 1.2 %shard_map.141 = (f32[16,56,128]{2,1,0:T(8,128)S(1)}, f32[16,56,128]{2,1,0:T(8,128)S(1)}, f32[16,56,128]{2,1,0:T(8,128)S(1)}, f32[3,4,56,128]{3,2,1,0:T(8,128)S(...) custom-call(f32[16,32,128]{2,1,0:T(8,128)S(1)} %get-tuple-element.77, ...), custom_call_target="tpu_custom_call" | custom-call | flops 10000 | bytes 30000 | tf_op jit(solution)/shard_map/pallas_call | solution.py:30
  18.5 0.0 collective-permute-done.4.refs_11_.refs_12_
  18.6 6.8 %collective-permute-done.5.refs_12_.refs_13_ = f32[638,128]{1,0:T(8,128)S(1)} collective-permute-done((f32[638,128]{1,0:T(8,128)S(1)}, f32[638,128]{1,0:T(8,128)S(1)}, u32[]{:S(2)}, u32[]{:S(2)}) %collective-permute-start.5) | collective-permute-done | bytes 326688 | tf_op jit(solution)/shard_map/ppermute | solution.py:870
  25.3 1.7 %shard_map.143 = (f32[920,128]{1,0:T(8,128)S(1)}, f32[5,56,128]{2,1,0:T(8,128)S(1)}, f32[5,56,128]{2,1,0:T(8,128)S(1)}, f32[5,56,128]{2,1,0:T(8,128)S(1)}, f32[5...) custom-call(f32[5]{0:T(128)S(1)} %copy-done.2, ...), custom_call_target="tpu_custom_call" | custom-call | flops 2000000 | bytes 6000000 | tf_op jit(solution)/shard_map/pallas_call | solution.py:30
  27.1 1.3 %collective-permute-start.8 = (f32[920,128]{1,0:T(8,128)S(1)}, f32[920,128]{1,0:T(8,128)S(1)}, u32[]{:S(2)}, u32[]{:S(2)}) collective-permute-start(f32[920,128]{1,0:T(8,128)S(1)} %get-tuple-element.112), channel_id=1, source_target_pairs={{4,0},{8,4},{12,8},{16,12},{20,16},{24,20},{28,24},{5,1},{9,5},{13... | collective-permute-start | bytes 1413128 | tf_op jit(solution)/shard_map/ppermute | solution.py:967
  28.4 0.0 copy-done.1
  28.4 1.4 %shard_map.144 = (f32[256,128]{1,0:T(8,128)S(1)}, f32[5,4,32,128]{3,2,1,0:T(8,128)S(1)}, f32[8,128]{1,0:T(8,128)S(1)}) custom-call(f32[5]{0:T(128)S(1)} %copy-done.2, f32[5,5]{1,0:T(8,128)S(1)} %copy-done, f32[5,8,56,128]{3,2,1,0:T(8,128)S(1)} %get-tuple-element.70.refs_1_.refs_0_, f32[3,8,56,128]{3,2,1,0:T(8,128)S(1)} %get-tuple-element.71.refs_2_.refs_1_, ...), custom_call_target="tpu_custom_call" | custom-call | flops 10000 | bytes 30000 | tf_op jit(solution)/shard_map/pallas_call | solution.py:30
  29.8 14.4 %all_to_all.10.arrived = f32[8,32,128]{2,1,0:T(8,128)S(1)} all-to-all(f32[8,32,128]{2,1,0:T(8,128)S(1)} %bitcast.2), channel_id=1, replica_groups=mesh['blk'=8,'span'=4] {'blk'}, dimensions={0} | all-to-all | bytes 262144 | tf_op jit(solution)/shard_map/all_to_all | solution.py:994
  44.2 0.2 shard_map.145
  44.5 0.1 collective-permute-start.7
  44.5 0.5 collective-permute-start.6
  45.0 0.0 collective-permute-done.8.xb.refs_9_
  45.0 1.7 %shard_map.147 = (f32[5,8,32,128]{3,2,1,0:T(8,128)S(1)}, f32[8,128]{1,0:T(8,128)S(1)}) custom-call(f32[5]{0:T(128)S(1)} %copy-done.2, f32[5,5]{1,0:T(8,128)S(1)} %copy-done, f32[5,8,56,128]{3,2,1,0:T(8,128)S(1)} %get-tuple-element.75.refs_0_, f32[5,8,56,128]{3,2,1,0:T(8,128)S(1)} %get-tuple-element.70.refs_1_.refs_0_, ...), custom_call_target="tpu_custom_call" | custom-call | flops 3000000 | bytes 9000000 | tf_op jit(solution)/shard_map/pallas_call | solution.py:30
  46.8 0.5 shard_map.146
  47.3 0.0 collective-permute-done.7.yr
  47.3 0.3 collective-permute-done.6.yl
  47.6 0.7 %shard_map.148 = (f32[16,32,128]{2,1,0:T(8,128)S(1)}, f32[8,40,128]{2,1,0:T(8,128)S(1)}) custom-call(f32[64,128]{1,0:T(8,128)S(1)} %get-tuple-element.100.surface, f32[8,128]{1,0:T(8,128)S(1)} %collective-permute-done.6.yl, f32[8,128]{1,0:T(8,128)S(1)} %collective-permute-done.7.yr, f32[2,5,56,128]{3,2,1,0:T(8,128)S(1)} %get-tuple-element.113.rh, ...), custom_call_target="tpu_custom_call" | custom-call | flops 1000000 | bytes 3000000 | tf_op jit(solution)/shard_map/pallas_call | solution.py:30
  48.3 11.1 %all_to_all.11.arrived = f32[8,40,128]{2,1,0:T(8,128)S(1)} all-to-all(f32[8,40,128]{2,1,0:T(8,128)S(1)} %get-tuple-element.122), channel_id=1, replica_groups=mesh['blk'=8,'span'=4] {'blk'}, dimensions={0} | all-to-all | bytes 327680 | tf_op jit(solution)/shard_map/all_to_all | solution.py:1060
  59.4 0.0 collective-permute-start.11
  59.4 0.8 %collective-permute-start.10 = (f32[8,128]{1,0:T(8,128)S(1)}, f32[8,128]{1,0:T(8,128)S(1)}, u32[]{:S(2)}, u32[]{:S(2)}) collective-permute-start(f32[8,128]{1,0:T(8,128)S(1)} %shard_map.150), channel_id=1, source_target_pairs={{0,2},{1,3},{2,0},{3,1},{4,6},{5,7},{6,4},{7,5},{8,10},{9,11},{10,... | collective-permute-start | bytes 12296 | tf_op jit(solution)/shard_map/ppermute | solution.py:1065
  60.2 1.1 %collective-permute-start.9 = (f32[8,128]{1,0:T(8,128)S(1)}, f32[8,128]{1,0:T(8,128)S(1)}, u32[]{:S(2)}, u32[]{:S(2)}) collective-permute-start(f32[8,128]{1,0:T(8,128)S(1)} %shard_map.150), channel_id=1, source_target_pairs={{0,1},{1,0},{2,3},{3,2},{4,5},{5,4},{6,7},{7,6},{8,9},{9,8},{10,11... | collective-permute-start | bytes 12296 | tf_op jit(solution)/shard_map/ppermute | solution.py:1065
  61.3 1.0 %shard_map.149 = (f32[5,8,32,128]{3,2,1,0:T(8,128)}, f32[16,32,128]{2,1,0:T(8,128)}) custom-call(f32[8,40,128]{2,1,0:T(8,128)S(1)} %all_to_all.11.arrived, f32[1,32]{1,0:T(1,128)S(1)} %get-tuple-element.82._.idx, f32[1,32,128]{2,1,0:T(8,128)S(1)} %copy-done.1, f32[5,8,32,128]{3,2,1,0:T(8,128)S(1)} %get-tuple-element.123.gas, ...), custom_call_target="tpu_custom_call" | custom-call | flops 2000000 | bytes 6000000 | tf_op jit(solution)/shard_map/pallas_call | solution.py:30
  62.3 0.2 collective-permute-done.11
  62.5 0.6 %collective-permute-done.10 = f32[8,128]{1,0:T(8,128)S(1)} collective-permute-done((f32[8,128]{1,0:T(8,128)S(1)}, f32[8,128]{1,0:T(8,128)S(1)}, u32[]{:S(2)}, u32[]{:S(2)}) %collective-permute-start.10) | collective-permute-done | bytes 4128 | tf_op jit(solution)/shard_map/ppermute | solution.py:1065
  63.1 0.0 collective-permute-done.9
  63.1 0.1 slice_reduce_fusion
  63.2 0.0 copy-done.5
  63.2 0.5 multiply_sqrt_fusion
  (5 shorter events, 0.0 us)
Async XLA Ops:
  0.6 9.5 %copy-start = (f32[5,5]{1,0:T(8,128)S(1)}, f32[5,5]{1,0:T(8,128)}, u32[]{:S(2)}) copy-start(f32[5,5]{1,0:T(8,128)} %jacobian.9) | copy-start | bytes 304
  0.6 9.5 %copy-start.2 = (f32[5]{0:T(128)S(1)}, f32[5]{0:T(128)}, u32[]{:S(2)}) copy-start(f32[5]{0:T(128)} %spread.9) | copy-start | bytes 64
  2.4 5.8 %collective-permute-start = (f32[384,128]{1,0:T(8,128)S(1)}, f32[384,128]{1,0:T(8,128)S(1)}, u32[]{:S(2)}, u32[]{:S(2)}) collective-permute-start(f32[384,128]{1,0:T(8,128)S(1)} %get-tuple-element.68), channel_id=1, source_target_pairs={{0,1},{1,2},{2,3},{3,0},{4,5},{5,6},{6,7},{7,4},{8,9},{9,10},{10,1... | collective-permute-start | bytes 589832 | tf_op jit(solution)/shard_map/ppermute | solution.py:870
  2.9 7.2 %collective-permute-start.1 = (f32[384,128]{1,0:T(8,128)S(1)}, f32[384,128]{1,0:T(8,128)S(1)}, u32[]{:S(2)}, u32[]{:S(2)}) collective-permute-start(f32[384,128]{1,0:T(8,128)S(1)} %get-tuple-element.69), channel_id=1, source_target_pairs={{1,0},{2,1},{3,2},{0,3},{5,4},{6,5},{7,6},{4,7},{9,8},{10,9},{11,1... | collective-permute-start | bytes 589832 | tf_op jit(solution)/shard_map/ppermute | solution.py:873
  4.9 13.6 %collective-permute-start.4 = (f32[672,128]{1,0:T(8,128)S(1)}, f32[672,128]{1,0:T(8,128)S(1)}, u32[]{:S(2)}, u32[]{:S(2)}) collective-permute-start(f32[672,128]{1,0:T(8,128)S(1)} %get-tuple-element.89), channel_id=1, source_target_pairs={{0,4},{4,8},{8,12},{12,16},{16,20},{20,24},{24,28},{28,0},{1,5},{5... | collective-permute-start | bytes 1032200 | tf_op jit(solution)/shard_map/ppermute | solution.py:870
  10.2 4.8 %copy-start.3 = (s32[1,32,1]{1,2,0:T(1,128)S(1)}, s32[1,32,1]{1,2,0:T(1,128)}, u32[]{:S(2)}) copy-start(s32[1,32,1]{1,2,0:T(1,128)} %param.21) | copy-start | bytes 388
  10.2 4.8 %copy-start.4 = (s32[1,32]{1,0:T(1,128)S(1)}, s32[1,32]{1,0:T(1,128)}, u32[]{:S(2)}) copy-start(s32[1,32]{1,0:T(1,128)} %target.1) | copy-start | bytes 388
  11.5 13.8 %collective-permute-start.5 = (f32[638,128]{1,0:T(8,128)S(1)}, f32[638,128]{1,0:T(8,128)S(1)}, u32[]{:S(2)}, u32[]{:S(2)}) collective-permute-start(f32[638,128]{1,0:T(8,128)S(1)} %shard_map.142), channel_id=1, source_target_pairs={{0,4},{4,8},{8,12},{12,16},{16,20},{20,24},{24,28},{28,0},{1,5},{5... | collective-permute-start | bytes 979976 | tf_op jit(solution)/shard_map/ppermute | solution.py:870
  13.1 4.3 %collective-permute-start.2 = (f32[176,128]{1,0:T(8,128)S(1)}, f32[176,128]{1,0:T(8,128)S(1)}, u32[]{:S(2)}, u32[]{:S(2)}) collective-permute-start(f32[176,128]{1,0:T(8,128)S(1)} %get-tuple-element.80), channel_id=1, source_target_pairs={{0,1},{1,2},{2,3},{3,0},{4,5},{5,6},{6,7},{7,4},{8,9},{9,10},{10,1... | collective-permute-start | bytes 270344 | tf_op jit(solution)/shard_map/ppermute | solution.py:870
  13.9 3.5 %collective-permute-start.3 = (f32[176,128]{1,0:T(8,128)S(1)}, f32[176,128]{1,0:T(8,128)S(1)}, u32[]{:S(2)}, u32[]{:S(2)}) collective-permute-start(f32[176,128]{1,0:T(8,128)S(1)} %get-tuple-element.81), channel_id=1, source_target_pairs={{1,0},{2,1},{3,2},{0,3},{5,4},{6,5},{7,6},{4,7},{9,8},{10,9},{11,1... | collective-permute-start | bytes 270344 | tf_op jit(solution)/shard_map/ppermute | solution.py:873
  25.3 3.0 %copy-start.1 = (f32[1,32,128]{2,1,0:T(8,128)S(1)}, f32[1,32,128]{2,1,0:T(8,128)}, u32[]{:S(2)}) copy-start(f32[1,32,128]{2,1,0:T(8,128)} %coef.1) | copy-start | bytes 49156
  27.1 18.0 %collective-permute-start.8 = (f32[920,128]{1,0:T(8,128)S(1)}, f32[920,128]{1,0:T(8,128)S(1)}, u32[]{:S(2)}, u32[]{:S(2)}) collective-permute-start(f32[920,128]{1,0:T(8,128)S(1)} %get-tuple-element.112), channel_id=1, source_target_pairs={{4,0},{8,4},{12,8},{16,12},{20,16},{24,20},{28,24},{5,1},{9,5},{13... | collective-permute-start | bytes 1413128 | tf_op jit(solution)/shard_map/ppermute | solution.py:967
  44.5 2.8 %collective-permute-start.7 = (f32[8,128]{1,0:T(8,128)S(1)}, f32[8,128]{1,0:T(8,128)S(1)}, u32[]{:S(2)}, u32[]{:S(2)}) collective-permute-start(f32[8,128]{1,0:T(8,128)S(1)} %get-tuple-element.102), channel_id=1, source_target_pairs={{1,0},{2,1},{3,2},{0,3},{5,4},{6,5},{7,6},{4,7},{9,8},{10,9},{11,1... | collective-permute-start | bytes 12296 | tf_op jit(solution)/shard_map/ppermute | solution.py:873
  44.5 3.1 %collective-permute-start.6 = (f32[8,128]{1,0:T(8,128)S(1)}, f32[8,128]{1,0:T(8,128)S(1)}, u32[]{:S(2)}, u32[]{:S(2)}) collective-permute-start(f32[8,128]{1,0:T(8,128)S(1)} %get-tuple-element.101._.refs_10_), channel_id=1, source_target_pairs={{0,1},{1,2},{2,3},{3,0},{4,5},{5,6},{6,7},{7,4},{8,9},{9,10},{10,1... | collective-permute-start | bytes 12296 | tf_op jit(solution)/shard_map/ppermute | solution.py:870
  47.6 15.6 %copy-start.5 = (f32[6]{0:T(128)S(1)}, f32[6]{0:T(128)}, u32[]{:S(2)}) copy-start(f32[6]{0:T(128)} %constant.8) | copy-start | bytes 76
  59.4 3.0 %collective-permute-start.11 = (f32[8,128]{1,0:T(8,128)S(1)}, f32[8,128]{1,0:T(8,128)S(1)}, u32[]{:S(2)}, u32[]{:S(2)}) collective-permute-start(f32[8,128]{1,0:T(8,128)S(1)} %shard_map.150), channel_id=1, source_target_pairs={{0,3},{1,2},{2,1},{3,0},{4,7},{5,6},{6,5},{7,4},{8,11},{9,10},{10,... | collective-permute-start | bytes 12296 | tf_op jit(solution)/shard_map/ppermute | solution.py:1065
  59.4 3.7 %collective-permute-start.10 = (f32[8,128]{1,0:T(8,128)S(1)}, f32[8,128]{1,0:T(8,128)S(1)}, u32[]{:S(2)}, u32[]{:S(2)}) collective-permute-start(f32[8,128]{1,0:T(8,128)S(1)} %shard_map.150), channel_id=1, source_target_pairs={{0,2},{1,3},{2,0},{3,1},{4,6},{5,7},{6,4},{7,5},{8,10},{9,11},{10,... | collective-permute-start | bytes 12296 | tf_op jit(solution)/shard_map/ppermute | solution.py:1065
  60.2 2.9 %collective-permute-start.9 = (f32[8,128]{1,0:T(8,128)S(1)}, f32[8,128]{1,0:T(8,128)S(1)}, u32[]{:S(2)}, u32[]{:S(2)}) collective-permute-start(f32[8,128]{1,0:T(8,128)S(1)} %shard_map.150), channel_id=1, source_target_pairs={{0,1},{1,0},{2,3},{3,2},{4,5},{5,4},{6,7},{7,6},{8,9},{9,8},{10,11... | collective-permute-start | bytes 12296 | tf_op jit(solution)/shard_map/ppermute | solution.py:1065

commit v7 on v6

--- a/solution.py
+++ b/solution.py
@@ -108,24 +108,31 @@
 
 class Edges:
     def __init__(self, fields, depth, thick):
-        n = 0
-        self.fluid, self.outer, self.solid = {}, {}, {}
-        for name, count, reach in (("p", fields, W), ("src", fields, W - 1), ("vel", 3, W - 1)):
+        n, later = 0, 0
+        self.fluid, self.late, self.outer, self.solid = {}, {}, {}, {}
+        for name, count, reach, near in (
+            ("p", fields, W, 4),
+            ("src", fields, W - 1, 3),
+            ("vel", 3, W - 1, 3),
+        ):
             for f in range(count):
                 for i in range(depth):
-                    self.fluid[name, f, i] = slice(n, n + reach)
-                    n = n + reach
-        for name, near, reach in (("t", 3, W), ("k", 3, W), ("heat", 2, W - 1)):
+                    if i < depth - near:
+                        self.late[name, f, i] = slice(later, later + reach)
+                        later = later + reach
+                    else:
+                        self.fluid[name, f, i] = slice(n, n + reach)
+                        n = n + reach
+        for name, near, reach in (("t", 4, W), ("k", 4, W), ("heat", 3, W - 1)):
             for i in range(thick - near, thick):
                 self.outer[name, i] = slice(n, n + reach)
                 n = n + reach
         self.size = (n + 7) // 8 * 8
-        n = 0
         for name, reach in (("t", W), ("k", W), ("heat", W - 1)):
             for i in range(thick):
-                self.solid[name, i] = slice(n, n + reach)
-                n = n + reach
-        self.solid_size = (n + 7) // 8 * 8
+                self.solid[name, i] = slice(later, later + reach)
+                later = later + reach
+        self.late_size = (later + 7) // 8 * 8
 
 
 class Fluid:
@@ -215,19 +222,21 @@
         copies[j].wait()
         if j < 3:
             pack(yf, yb, edges.fluid, (name,))
+            pack(zf, zb, edges.late, (name,))
     planes = [p[f, depth - 1] for f in range(fields)]
     planes += [vel[f, depth - 1] for f in range(3)]
     planes += [vel[0, depth - 2], vel[0, depth - 2] + vel[1, depth - 2] + vel[2, depth - 2]]
-    planes += [t[thick - 4 + j] for j in range(4)]
-    planes += [k[thick - 4 + j] for j in range(4)]
-    planes += [heat[thick - 3 + j] for j in range(3)]
+    planes += [t[thick - 1], t[thick - 2], k[thick - 1], k[thick - 2], k[thick - 3]]
+    planes += [heat[thick - 1]]
     for j, plane in enumerate(planes):
         xf[j * rows : (j + 1) * rows] = plane
     for up, down, places in ((yf, yb, edges.outer), (zf, zb, edges.solid)):
         pack(up, down, places, named)
 
 
-def ahead_kernel(blocks, spans, edges, spread, jacobian, p, src, vel, yl, yr, out, a0, a1, a2, sa, va, wa):
+def ahead_kernel(blocks, spans, edges, solid, third, spread, jacobian, *refs):
+    p, src, vel, t, heat, k, yl, yr, out, later = refs[:10]
+    a0, a1, a2, sa, va, wa, ta, ha, so, qa, tb, qb = refs[10:]
     fields, depth, rows, z = p.shape
     at_place = Place(rows, blocks, spans)
     ext, own = at_place.ext, at_place.own
@@ -272,7 +281,10 @@
         step(a1, j, into(a2, j - 1), j)
     corners = [edges.fluid["p", f, depth - 1] for f in range(fields)]
     corners += [edges.fluid["vel", c, depth - 1] for c in range(3)]
-    corners += list(edges.outer.values())
+    thick = t.shape[0]
+    corners += [edges.outer["t", thick - 1], edges.outer["t", thick - 2]]
+    corners += [edges.outer["k", thick - 1], edges.outer["k", thick - 2]]
+    corners += [edges.outer["heat", thick - 1]]
     n = 0
     for sl in corners:
         reach = sl.stop - sl.start
@@ -286,12 +298,49 @@
             n = n + size
 
     def last(f, sl, _, value):
-        m = n + f * rows + sl.start - own.start
-        out[m : m + 8] = value
+        m = third.window(0, f).start + sl.start - B
+        later[m : m + 8] = value
 
     fluid.advance(
         at(a2, 1), at(a2, 0), None, speeds(va, 2), at(wa, 2), at(sa, 2), own, last
     )
+    for name, buf, ref, near, scale in (
+        ("t", ta, t, 4, 1.0),
+        ("k", ha, k, 4, 0.5),
+        ("heat", so, heat, 3, 1.0),
+    ):
+        for j in range(4 - near, 4):
+            i = thick - 4 + j
+
+            def store(sl, x, buf=buf, j=j, scale=scale):
+                buf[j, sl] = scale * x
+
+            sl = edges.outer[name, i]
+            at_place.fill(store, ref[i], yl[sl], yr[sl])
+    for j in range(4):
+        qa[j, ext] = ha[j, ext] * ta[j, ext]
+
+    def h_of(j, sl):
+        return ha[j, sl]
+
+    kept = {}
+    for j in (1, 2):
+        h = ha[j, ext]
+        diagonal = solid_diagonal(h_of, j, ext)
+        w = solid_weight(h, diagonal)
+        res = so[j, ext] - diagonal * ta[j, ext] + h * around(ta, j, ext) + around(qa, j, ext)
+        tb[j, ext] = ta[j, ext] + w * res
+        qb[j, ext] = h * tb[j, ext]
+        kept[j] = (h, diagonal, w)
+    tb[3] = jnp.zeros_like(tb[3])
+    qb[3] = jnp.zeros_like(qb[3])
+    h, diagonal, w = kept[2]
+    res = so[2, ext] - diagonal * tb[2, ext] + h * around(tb, 2, ext) + around(qb, 2, ext)
+    value = tb[2, ext] + w * res
+    m = solid.window(0, 0).start + W - 1
+    later[m : m + rows + 2] = tb[2, at_place.reach(1)]
+    m = solid.window(1, 0).start + W
+    later[m : m + rows] = value[W : W + rows]
 
 
 def around(buf, j, sl):
@@ -347,9 +396,9 @@
 
 
 def inner_kernel(
-    blocks, spans, edges, spread, jacobian, owner, target, p, src, vel, yl, yr, *outs
+    blocks, spans, edges, spread, jacobian, owner, target, p, src, vel, yl, yr, zl, zr, *outs
 ):
-    p0, s0, v0, w0, p1, p2, p3, place, meta, idx = outs
+    p0, s0, v0, w0, p1, place, meta, idx = outs
     plan(blocks, owner, target, place, meta, idx)
     fields, depth, rows, z = p.shape
     here = Place(rows, blocks, spans)
@@ -363,24 +412,27 @@
                 def store(sl, x, buf=buf, f=f, i=i):
                     buf[f, i, sl] = x
 
-                sl = edges.fluid[name, f, i]
-                here.fill(store, ref[f, i], yl[sl], yr[sl])
+                if (name, f, i) in edges.late:
+                    sl = edges.late[name, f, i]
+                    here.fill(store, ref[f, i], zl[sl], zr[sl])
+                else:
+                    sl = edges.fluid[name, f, i]
+                    here.fill(store, ref[f, i], yl[sl], yr[sl])
     for i in range(depth):
         us = v0[0, i, ext] + v0[1, i, ext] + v0[2, i, ext]
         for f in range(fields):
             w0[f, i, ext] = jnp.where(inside, DAMPING / fluid.diagonal(f, us), 0.0)
-    for level, (old, new) in enumerate(((p0, p1), (p1, p2), (p2, p3))):
-        for i in range(level + 1, depth - 1 - level):
-            fluid.advance(
-                at(old, i - level),
-                at(old, i - level - 1),
-                at(old, i - level + 1),
-                speeds(v0, i),
-                at(w0, i),
-                at(s0, i),
-                ext,
-                into(new, i - level - 1),
-            )
+    for i in (1, 2):
+        fluid.advance(
+            at(p0, i),
+            at(p0, i - 1),
+            at(p0, i + 1),
+            speeds(v0, i),
+            at(w0, i),
+            at(s0, i),
+            ext,
+            into(p1, i - 1),
+        )
 
 
 def inner_solid_kernel(blocks, spans, edges, fields, t, heat, k, yl, yr, _, *refs):
@@ -429,10 +481,10 @@
     sqi[fields : fields + 1] = jnp.sum(total, axis=0, keepdims=True)
 
 
-def cone_kernel(blocks, spans, sent, solid, spread, jacobian, *refs):
-    p0, s0, v0, w0, p1, te, he, so, ti, dg, ws, xe, xn = refs[:13]
-    back, n2, c2, c3, d1, d2, vm, wm, sl_, t0, t1, t2, t3, dl, wl = refs[13:28]
-    l0, n1, qa = refs[28:]
+def cone_kernel(blocks, spans, sent, sent_solid, solid, spread, jacobian, *refs):
+    p0, s0, v0, w0, p1, te, he, so, ti, dg, ws, xe, xn, xl = refs[:14]
+    back, n2, c2, c3, d1, d2, vm, wm, sl_, t0, t1, t2, t3, dl, wl = refs[14:29]
+    l0, n1, qa = refs[29:]
     fields, z = p0.shape[0], p0.shape[3]
     rows = p0.shape[2] - 2 * (B + W)
     here = Place(rows, blocks, spans)
@@ -494,51 +546,62 @@
     early = (fields + 5) * rows
     zero = jnp.zeros((W, z), F32)
     hl, sl_ = sl_.at[0], sl_.at[1]
-    for buf, near, scale in ((t0, 4, 1.0), (hl, 4, 0.5), (sl_, 3, 1.0)):
-        for i in range(near):
-
-            def store(sl, x, buf=buf, j=4 - near + i, scale=scale):
-                buf[j, sl] = scale * x
-
-            if i > 0:
-                low, high = xn[corner : corner + W], xn[corner + W : corner + 2 * W]
-                corner = corner + 2 * W
-            else:
-                low, high = zero, zero
-            here.fill(store, xe[early : early + rows], low, high, here.no_left)
-            early = early + rows
+    for buf, j, scale in ((t0, 1, 1.0), (t0, 0, 1.0), (hl, 3, 0.5), (hl, 2, 0.5), (hl, 1, 0.5), (sl_, 3, 1.0)):
+
+        def store(sl, x, buf=buf, j=j, scale=scale):
+            buf[j, sl] = scale * x
+
+        low, high = zero, zero
+        if buf is not hl or j > 1:
+            low, high = xn[corner : corner + W], xn[corner + W : corner + 2 * W]
+            corner = corner + 2 * W
+        here.fill(store, xe[early : early + rows], low, high, here.no_left)
+        early = early + rows
 
     def h_of(i, sl):
         return hl[i + 4, sl] if i < 0 else he[i, sl]
 
-    for i in range(-3, 1):
+    for i in range(-2, 1):
         dl[i + 3, ext] = solid_diagonal(h_of, i, ext)
         wl[i + 3, ext] = solid_weight(h_of(i, ext), dl[i + 3, ext])
-    for j in range(4, 6):
-        t0[j] = te[j - 4]
-    for level, (old, new) in enumerate(((t0, t1), (t1, t2), (t2, t3))):
-        for j in range(6):
-            qa[j, ext] = h_of(level - 4 + j, ext) * old[j, ext]
-        for j in range(4):
-            i = level - 3 + j
-            q = old[j + 1, ext]
-            res = sl_[i + 4, ext] if i < 0 else so[i, ext]
-            diagonal, w = (dl, wl) if i <= 0 else (dg, ws)
-            m = i + 3 if i <= 0 else i
-            res = res - diagonal[m, ext] * q
-            res = res + h_of(i, ext) * around(old, j + 1, ext) + around(qa, j + 1, ext)
-            new[j, ext] = q + w[m, ext] * res
-        for j in range(4, 6):
-            new[j] = ti[level, j - 4]
-    for level, (ref, i) in enumerate(((he, 0), (he, 1), (t0, 4), (t1, 3), (t2, 2), (t3, 1))):
+
+    def sweep(old, shift, new, i, j):
+        q = old[i + shift, ext]
+        diagonal, w, m = (dl, wl, i + 3) if i <= 0 else (dg, ws, i)
+        res = (sl_[3, ext] if i < 0 else so[i, ext]) - diagonal[m, ext] * q
+        res = res + h_of(i, ext) * around(old, i + shift, ext) + around(qa, i + shift, ext)
+        new[j, ext] = q + w[m, ext] * res
+
+    def weigh(old, count):
+        for j in range(count):
+            qa[j, ext] = h_of(j - 2, ext) * old[j, ext]
+
+    t0[2], t0[3] = te[0], te[1]
+    weigh(t0, 4)
+    for i in (-1, 0):
+        sweep(t0, 2, t1, i, i + 2)
+    t1[0, ext] = unless(here.no_left, xl[sent_solid.window(0, 0)])
+    t1[3], t1[4] = ti[0, 0], ti[0, 1]
+    weigh(t1, 5)
+    for i in (-1, 0, 1):
+        sweep(t1, 2, t2, i, i + 2)
+    t2[0, ext] = unless(here.no_left, xl[sent_solid.window(1, 0)])
+    t2[0, ext] = t2[0, ext] + wl[1, ext] * (hl[2, ext] + hl[3, ext]) * t1[1, ext]
+    t2[4], t2[5] = ti[1, 0], ti[1, 1]
+    weigh(t2, 6)
+    for i in (-1, 0, 1, 2):
+        sweep(t2, 2, t3, i, i + 1)
+    t3[4], t3[5] = ti[2, 0], ti[2, 1]
+    for level, (ref, i) in enumerate(((he, 0), (he, 1), (t0, 2), (t1, 2), (t2, 2), (t3, 1))):
         sl = solid.window(level, 0)
         reach = solid.reaches[level]
         back[sl.start + W - reach : sl.stop - W + reach] = ref[i, here.reach(reach)]
 
 
-def flux_kernel(blocks, spans, sent, spread, jacobian, *refs):
-    s0, v0, w0, p2, p3, n2, c2, c3, d1, d2, vm, wm, xe, xn, coef, hot, meta = refs[:17]
-    parts, left, sq, m3, d3 = refs[17:]
+def flux_kernel(blocks, spans, third_at, spread, jacobian, *refs):
+    p0, s0, v0, w0, p1, n2, c2, c3, d1, d2, vm, wm, xe, xl, coef, hot, meta = refs[:17]
+    parts, left, sq, q1, p2, p3, m3, d3 = refs[17:]
+    depth = p0.shape[1]
     fields, rows, z = left.shape[0], left.shape[2], left.shape[3]
     here = Place(rows, blocks, spans)
     ext, own = here.ext, here.own
@@ -548,8 +611,8 @@
     outer = [lambda sl, c=c: vm[c, sl] for c in range(3)]
 
     def third(f, sl):
-        n = sent.window(2, f).start + sl.start - B
-        return unless(here.no_left, xn[n : n + 8]) + d3[f, sl]
+        n = third_at.window(0, f).start + sl.start - B
+        return unless(here.no_left, xl[n : n + 8]) + d3[f, sl]
 
     def plane(cur, i, before, after, store, sl=ext):
         fluid.advance(cur, before, after, speeds(v0, i), at(w0, i), at(s0, i), sl, store)
@@ -559,6 +622,15 @@
         w = unless(here.no_left, DAMPING / fluid.diagonal(f, usmm[n : n + 8]))
         return w * (fluid.d[f] + u0mm[n : n + 8]) * d1[f, sl]
 
+    def first(i):
+        return at(p1, i - 1) if i < 3 else at(q1, i - 3)
+
+    for i in range(3, depth - 1):
+        plane(at(p0, i), i, at(p0, i - 1), at(p0, i + 1), into(q1, i - 3))
+    for i in range(2, depth - 2):
+        plane(first(i), i, first(i - 1), first(i + 1), into(p2, i - 2))
+    for i in range(3, depth - 3):
+        plane(at(p2, i - 2), i, at(p2, i - 3), at(p2, i - 1), into(p3, i - 3))
     fluid.advance(flat(d2), farther, flat(n2), outer, flat(wm), None, own, into_flat(d3))
     plane(flat(c2), 1, flat(n2), at(p2, 0), into(m3, 0))
     plane(at(p2, 0), 2, flat(c2), at(p2, 1), into(m3, 1))
@@ -596,9 +668,9 @@
         return read
 
     known = [{i: (p0, i) for i in range(depth)}, {}, {}, {}]
-    for level, buf in enumerate((p1, p2, p3)):
-        for i in range(level + 1, depth - 1 - level):
-            known[level + 1][i] = (buf, i - level - 1)
+    for level, (buf, low) in enumerate(((p1, 3), (p2, 2), (p3, 3))):
+        for i in range(low, depth - 1 - level):
+            known[level + 1][i] = (buf, i - low)
 
     def read(level, i):
         ref, j = known[level][i]
@@ -878,40 +950,48 @@
         functools.partial(early_kernel, edges),
         held(*[x.shape for x in inputs])
         + [(edges.size, z)] * 2
-        + [((fields + 16) * rows, z)]
-        + [(edges.solid_size, z)] * 2,
+        + [((fields + 11) * rows, z)]
+        + [(edges.late_size, z)] * 2,
         [pltpu.SemaphoreType.DMA((6,))],
         [HBM] * 6,
         *[pltpu.with_memory_space_constraint(x, pltpu.HBM) for x in inputs],
     )
     yl, yr = ahead(yf, "span"), behind(yb, "span")
     xe = ahead(xf, "blk")
-    sent_ahead = Arrivals((fields + 11) * 2 * W, rows, fields, (2, 1, 0))
-    (out,) = call(
-        functools.partial(ahead_kernel, blocks, spans, edges),
-        [(sent_ahead.size(), z)],
+    sent_ahead = Arrivals((fields + 8) * 2 * W, rows, fields, (2, 1))
+    solid_ahead = Arrivals(8, rows, 1, (1, 0))
+    third_ahead = Arrivals((solid_ahead.size() + 7) // 8 * 8, rows, fields, (0,))
+    four = (4, buf, z)
+    out, later = call(
+        functools.partial(ahead_kernel, blocks, spans, edges, solid_ahead, third_ahead),
+        [((sent_ahead.size() + W + 7) // 8 * 8, z), (third_ahead.size(), z)],
         [(fields, 4, buf, z), (fields, 3, buf, z), (fields, 2, buf, z), (fields, 3, buf, z)]
-        + [(3, 3, buf, z), (fields, 3, buf, z)],
-        [SMEM] * 2 + [VMEM] * 5,
+        + [(3, 3, buf, z), (fields, 3, buf, z)]
+        + [four] * 6,
+        [SMEM] * 2 + [VMEM] * 8,
         diffusion,
         jacobian,
         p,
         src,
         vel,
+        t,
+        heat,
+        k,
         yl,
         yr,
         cost=COSTS[1],
     )
-    xn = ahead(out, "blk")
+    xn, xl = ahead(out, "blk"), ahead(later, "blk")
     full = (fields, depth, buf, z)
     part = [(fields, depth - 2 * (level + 1), buf, z) for level in range(3)]
     solid = (thick, buf, z)
-    p0, s0, v0, w0, p1, p2, p3, place, meta, idx = call(
+    zl, zr = ahead(zf, "span"), behind(zb, "span")
+    p0, s0, v0, w0, p1, place, meta, idx = call(
         functools.partial(inner_kernel, blocks, spans, edges),
-        held(full, full, (3, depth, buf, z), full, *part)
+        held(full, full, (3, depth, buf, z), full, (fields, 2, buf, z))
         + held((blocks * CHUNK, rows), (blocks, 8, z), (1, rows)),
         [],
-        [SMEM] * 2 + [VMEM] * 7,
+        [SMEM] * 2 + [VMEM] * 9,
         diffusion,
         jacobian,
         tile_owner.reshape(1, rows),
@@ -921,9 +1001,10 @@
         vel,
         yl,
         yr,
+        zl,
+        zr,
         cost=COSTS[2],
     )
-    zl, zr = ahead(zf, "span"), behind(zb, "span")
     te, he, so, ti, tb, sqi, dg, ws = call(
         functools.partial(inner_solid_kernel, blocks, spans, edges, fields),
         held(solid, solid, solid, (3, 4, buf, z), (thick - 2 * SWEEPS, rows, z), (8, z), solid, solid),
@@ -941,12 +1022,12 @@
     sent_back = Arrivals(solid_back.size(), rows, fields, (3, 2, 1, 0))
     one, six = (fields, buf, z), (6, buf, z)
     back, n2, c2, c3, d1, d2, vm, wm, sl_, *lefts = call(
-        functools.partial(cone_kernel, blocks, spans, sent_ahead, solid_back),
+        functools.partial(cone_kernel, blocks, spans, sent_ahead, solid_ahead, solid_back),
         [(sent_back.size(), z)]
         + held(one, one, one, one, one, (3, buf, z), one, (2, 4, buf, z))
         + held(six, six, six, six, (4, buf, z), (4, buf, z)),
         [one] * 2 + [six],
-        [SMEM] * 2 + [VMEM] * 13,
+        [SMEM] * 2 + [VMEM] * 14,
         diffusion,
         jacobian,
         p0,
@@ -962,21 +1043,23 @@
         ws,
         xe,
         xn,
+        xl,
         cost=COSTS[3],
     )
     xr = lax.ppermute(back, "blk", backward["blk"][: blocks - 1])
-    parts, half, sq = call(
-        functools.partial(flux_kernel, blocks, spans, sent_ahead),
-        [(blocks * CHUNK, z)] + held((fields, 4, rows, z), (8, z)),
+    parts, half, sq, q1, p2, p3 = call(
+        functools.partial(flux_kernel, blocks, spans, third_ahead),
+        [(blocks * CHUNK, z)]
+        + held((fields, 4, rows, z), (8, z), (fields, depth - 4, buf, z), *part[1:]),
         [(fields, 2, buf, z), one],
         [SMEM] * 2 + [VMEM] * 17,
         diffusion,
         jacobian,
+        p0,
         s0,
         v0,
         w0,
-        p2,
-        p3,
+        p1,
         n2,
         c2,
         c3,
@@ -985,7 +1068,7 @@
         vm,
         wm,
         xe,
-        xn,
+        xl,
         wall_coefficient,
         place,
         meta,
@@ -1011,7 +1094,7 @@
         s0,
         v0,
         w0,
-        p1,
+        q1,
         p2,
         p3,
         half,

time: 64 us -> 63.1 us (0.986)
  waiting for transfers between devices: 10.9 us -> 9.34 us
  starting transfers between devices: 11.9 us -> 13.3 us
  blocking collectives: 25.5 us -> 24.4 us
    ppermute x5 -> x6, waiting for transfers between devices: 8.16 us -> 6.29 us  [ahead(): return lax.ppermute(x, axis, forward[axis])]
    ppermute x5 -> x6, starting transfers between devices: 5.56 us -> 7.34 us  [ahead(): return lax.ppermute(x, axis, forward[axis])]
    all_to_all x1, blocking collectives: 14.4 us -> 13.3 us  [shards(): arrived = lax.all_to_all(parts.reshape(blocks, CHUNK, z), 'blk', 0, 0)]
  transfers between devices with their start and end apart: 12 -> 13, of which waited for: 6 -> 8; matrix products, arithmetic and copies ran while one was open for 0% -> 0% of each run, Pallas kernels for 15% -> 16%
where the time goes in v7:
time: 63.1 us; the launch traced here: 62.8 us
  blocking collectives  24.4 us (39%)
  Pallas kernels  14.4 us (23%)
  starting transfers between devices  13.3 us (21%)
  waiting for transfers between devices  9.34 us (15%)
  between operations  0.77 us (1%)
  other arithmetic  0.64 us (1%)
    pallas_call x12, Pallas kernels, call(): pl.pallas_call(kernel, out_shape=[jax.ShapeDtypeStruct(s, F32) if isinsta...  14.4 us
    all_to_all x1, blocking collectives, shards(): arrived = lax.all_to_all(parts.reshape(blocks, CHUNK, z), 'blk', 0, 0)  13.3 us
    all_to_all x1, blocking collectives, shards(): arrived = lax.all_to_all(out, 'blk', 0, 0)  11.1 us
    ppermute x6, starting transfers between devices, ahead(): return lax.ppermute(x, axis, forward[axis])  7.34 us
    ppermute x6, waiting for transfers between devices, ahead(): return lax.ppermute(x, axis, forward[axis])  6.29 us
    ppermute x3, starting transfers between devices, behind(): return lax.ppermute(x, axis, backward[axis])  2.81 us
    ppermute x3, waiting for transfers between devices, behind(): return lax.ppermute(x, axis, backward[axis])  2.23 us
    ppermute x3, starting transfers between devices, shards(): lax.ppermute(sq, 'span', [(i, i ^ step) for i in range(spans)])  1.86 us
  transfers between devices with their start and end apart: 13, of which 8 were waited for; matrix products, arithmetic and copies ran while one was open for 0% of the time, Pallas kernels for 16%

profile of v7, /device:TPU:0, one launch (start us, length us, event | category | flops | bytes accessed | tf_op | source)
XLA Modules:
  0.0 62.8 jit_solution(1261803005803735282)
XLA Ops:
  0.6 0.0 copy-start
  0.6 0.0 copy-start.2
  0.7 1.7 %shard_map.139 = (f32[5,8,32,128]{3,2,1,0:T(8,128)S(1)}, f32[5,8,32,128]{3,2,1,0:T(8,128)S(1)}, f32[3,8,32,128]{3,2,1,0:T(8,128)S(1)}, f32[16,32,128]{2,1,0:T(8,...) custom-call(f32[5,8,32,128]{3,2,1,0:T(8,128)} %refs_0_.1, ...), custom_call_target="tpu_custom_call" | custom-call | flops 1000000 | bytes 3000000 | tf_op jit(solution)/shard_map/pallas_call | solution.py:30
  2.4 0.5 collective-permute-start
  2.9 2.0 %collective-permute-start.1 = (f32[200,128]{1,0:T(8,128)S(1)}, f32[200,128]{1,0:T(8,128)S(1)}, u32[]{:S(2)}, u32[]{:S(2)}) collective-permute-start(f32[200,128]{1,0:T(8,128)S(1)} %get-tuple-element.72), channel_id=1, source_target_pairs={{1,0},{2,1},{3,2},{0,3},{5,4},{6,5},{7,6},{4,7},{9,8},{10,9},{11,1... | collective-permute-start | bytes 307208 | tf_op jit(solution)/shard_map/ppermute | solution.py:945
  4.9 2.2 %collective-permute-start.4 = (f32[512,128]{1,0:T(8,128)S(1)}, f32[512,128]{1,0:T(8,128)S(1)}, u32[]{:S(2)}, u32[]{:S(2)}) collective-permute-start(f32[512,128]{1,0:T(8,128)S(1)} %get-tuple-element.90), channel_id=1, source_target_pairs={{0,4},{4,8},{8,12},{12,16},{16,20},{20,24},{24,28},{28,0},{1,5},{5... | collective-permute-start | bytes 786440 | tf_op jit(solution)/shard_map/ppermute | solution.py:942
  7.1 0.1 collective-permute-done.yl.refs_6_
  7.2 0.9 %collective-permute-done.1.yr.refs_7_ = f32[200,128]{1,0:T(8,128)S(1)} collective-permute-done((f32[200,128]{1,0:T(8,128)S(1)}, f32[200,128]{1,0:T(8,128)S(1)}, u32[]{:S(2)}, u32[]{:S(2)}) %collective-permute-start.1) | collective-permute-done | bytes 102432 | tf_op jit(solution)/shard_map/ppermute | solution.py:945
  8.1 0.0 copy-done
  8.1 0.0 copy-done.2
  8.1 1.4 %shard_map.142 = (f32[464,128]{1,0:T(8,128)S(1)}, f32[240,128]{1,0:T(8,128)S(1)}) custom-call(f32[5]{0:T(128)S(1)} %copy-done.2, f32[5,5]{1,0:T(8,128)S(1)} %copy-done, f32[5,8,32,128]{3,2,1,0:T(8,128)S(1)} %get-tuple-element.68.p.refs_0_, f32[5,8,32,128]{3,2,1,0:T(8,128)S(1)} %get-tuple-element.69.src.refs_1_, ...), custom_call_target="tpu_custom_call" | custom-call | flops 30000000 | bytes 90000000 | tf_op jit(solution)/shard_map/pallas_call | solution.py:30
  9.6 1.5 %collective-permute-start.5 = (f32[464,128]{1,0:T(8,128)S(1)}, f32[464,128]{1,0:T(8,128)S(1)}, u32[]{:S(2)}, u32[]{:S(2)}) collective-permute-start(f32[464,128]{1,0:T(8,128)S(1)} %get-tuple-element.91), channel_id=1, source_target_pairs={{0,4},{4,8},{8,12},{12,16},{16,20},{20,24},{24,28},{28,0},{1,5},{5... | collective-permute-start | bytes 712712 | tf_op jit(solution)/shard_map/ppermute | solution.py:942
  11.1 1.5 %collective-permute-start.2 = (f32[376,128]{1,0:T(8,128)S(1)}, f32[376,128]{1,0:T(8,128)S(1)}, u32[]{:S(2)}, u32[]{:S(2)}) collective-permute-start(f32[376,128]{1,0:T(8,128)S(1)} %get-tuple-element.73), channel_id=1, source_target_pairs={{0,1},{1,2},{2,3},{3,0},{4,5},{5,6},{6,7},{7,4},{8,9},{9,10},{10,1... | collective-permute-start | bytes 577544 | tf_op jit(solution)/shard_map/ppermute | solution.py:942
  12.6 0.2 collective-permute-start.3
  12.9 1.5 %collective-permute-start.6 = (f32[240,128]{1,0:T(8,128)S(1)}, f32[240,128]{1,0:T(8,128)S(1)}, u32[]{:S(2)}, u32[]{:S(2)}) collective-permute-start(f32[240,128]{1,0:T(8,128)S(1)} %get-tuple-element.92), channel_id=1, source_target_pairs={{0,4},{4,8},{8,12},{12,16},{16,20},{20,24},{24,28},{28,0},{1,5},{5... | collective-permute-start | bytes 368648 | tf_op jit(solution)/shard_map/ppermute | solution.py:942
  14.4 1.7 %collective-permute-done.2.zl.yl = f32[376,128]{1,0:T(8,128)S(1)} collective-permute-done((f32[376,128]{1,0:T(8,128)S(1)}, f32[376,128]{1,0:T(8,128)S(1)}, u32[]{:S(2)}, u32[]{:S(2)}) %collective-permute-start.2) | collective-permute-done | bytes 192544 | tf_op jit(solution)/shard_map/ppermute | solution.py:942
  16.2 1.3 %collective-permute-done.3.zr.yr = f32[376,128]{1,0:T(8,128)S(1)} collective-permute-done((f32[376,128]{1,0:T(8,128)S(1)}, f32[376,128]{1,0:T(8,128)S(1)}, u32[]{:S(2)}, u32[]{:S(2)}) %collective-permute-start.3) | collective-permute-done | bytes 192544 | tf_op jit(solution)/shard_map/ppermute | solution.py:945
  17.5 0.0 copy-done.3
  17.5 0.0 copy-done.4
  17.5 1.3 %shard_map.140 = (f32[5,8,56,128]{3,2,1,0:T(8,128)S(1)}, f32[5,8,56,128]{3,2,1,0:T(8,128)S(1)}, f32[3,8,56,128]{3,2,1,0:T(8,128)S(1)}, f32[5,8,56,128]{3,2,1,0:T...) custom-call(f32[5]{0:T(128)S(1)} %copy-done.2, ...), custom_call_target="tpu_custom_call" | custom-call | flops 10000 | bytes 30000 | tf_op jit(solution)/shard_map/pallas_call | solution.py:30
  18.8 1.4 %shard_map.141 = (f32[16,56,128]{2,1,0:T(8,128)S(1)}, f32[16,56,128]{2,1,0:T(8,128)S(1)}, f32[16,56,128]{2,1,0:T(8,128)S(1)}, f32[3,4,56,128]{3,2,1,0:T(8,128)S(...) custom-call(f32[16,32,128]{2,1,0:T(8,128)S(1)} %get-tuple-element.80, ...), custom_call_target="tpu_custom_call" | custom-call | flops 10000 | bytes 30000 | tf_op jit(solution)/shard_map/pallas_call | solution.py:30
  20.1 3.8 %collective-permute-done.6.refs_13_ = f32[240,128]{1,0:T(8,128)S(1)} collective-permute-done((f32[240,128]{1,0:T(8,128)S(1)}, f32[240,128]{1,0:T(8,128)S(1)}, u32[]{:S(2)}, u32[]{:S(2)}) %collective-permute-start.6) | collective-permute-done | bytes 122912 | tf_op jit(solution)/shard_map/ppermute | solution.py:942
  23.9 0.0 collective-permute-done.4.refs_11_.refs_12_
  23.9 0.0 collective-permute-done.5.refs_12_
  23.9 1.7 %shard_map.143 = (f32[920,128]{1,0:T(8,128)S(1)}, f32[5,56,128]{2,1,0:T(8,128)S(1)}, f32[5,56,128]{2,1,0:T(8,128)S(1)}, f32[5,56,128]{2,1,0:T(8,128)S(1)}, f32[5...) custom-call(f32[5]{0:T(128)S(1)} %copy-done.2, ...), custom_call_target="tpu_custom_call" | custom-call | flops 2000000 | bytes 6000000 | tf_op jit(solution)/shard_map/pallas_call | solution.py:30
  25.6 1.3 %collective-permute-start.9 = (f32[920,128]{1,0:T(8,128)S(1)}, f32[920,128]{1,0:T(8,128)S(1)}, u32[]{:S(2)}, u32[]{:S(2)}) collective-permute-start(f32[920,128]{1,0:T(8,128)S(1)} %get-tuple-element.115), channel_id=1, source_target_pairs={{4,0},{8,4},{12,8},{16,12},{20,16},{24,20},{28,24},{5,1},{9,5},{13... | collective-permute-start | bytes 1413128 | tf_op jit(solution)/shard_map/ppermute | solution.py:1049
  26.9 2.6 %shard_map.144 = (f32[256,128]{1,0:T(8,128)S(1)}, f32[5,4,32,128]{3,2,1,0:T(8,128)S(1)}, f32[8,128]{1,0:T(8,128)S(1)}, f32[5,4,56,128]{3,2,1,0:T(8,128)S(1)}, f3...) custom-call(f32[5]{0:T(128)S(1)} %copy-done.2, f32[5,5]{1,0:T(8,128)S(1)} %copy-done, ...), custom_call_target="tpu_custom_call" | custom-call | flops 10000 | bytes 30000 | tf_op jit(solution)/shard_map/pallas_call | solution.py:30
  29.5 13.3 %all_to_all.10.arrived = f32[8,32,128]{2,1,0:T(8,128)S(1)} all-to-all(f32[8,32,128]{2,1,0:T(8,128)S(1)} %bitcast.2), channel_id=1, replica_groups=mesh['blk'=8,'span'=4] {'blk'}, dimensions={0} | all-to-all | bytes 262144 | tf_op jit(solution)/shard_map/all_to_all | solution.py:1077
  42.9 0.2 shard_map.145
  43.1 0.5 collective-permute-start.8
  43.7 0.0 collective-permute-start.7
  43.7 0.0 collective-permute-done.9.xb.refs_9_
  43.7 1.7 %shard_map.147 = (f32[5,8,32,128]{3,2,1,0:T(8,128)S(1)}, f32[8,128]{1,0:T(8,128)S(1)}) custom-call(f32[5]{0:T(128)S(1)} %copy-done.2, f32[5,5]{1,0:T(8,128)S(1)} %copy-done, f32[5,8,56,128]{3,2,1,0:T(8,128)S(1)} %get-tuple-element.75.refs_0_, f32[5,8,56,128]{3,2,1,0:T(8,128)S(1)} %get-tuple-element.76.refs_1_, ...), custom_call_target="tpu_custom_call" | custom-call | flops 3000000 | bytes 9000000 | tf_op jit(solution)/shard_map/pallas_call | solution.py:30
  45.4 0.5 shard_map.146
  46.0 0.0 collective-permute-done.8.yr
  46.0 0.7 %collective-permute-done.7.yl = f32[8,128]{1,0:T(8,128)S(1)} collective-permute-done((f32[8,128]{1,0:T(8,128)S(1)}, f32[8,128]{1,0:T(8,128)S(1)}, u32[]{:S(2)}, u32[]{:S(2)}) %collective-permute-start.7) | collective-permute-done | bytes 4128 | tf_op jit(solution)/shard_map/ppermute | solution.py:942
  46.7 0.7 %shard_map.148 = (f32[16,32,128]{2,1,0:T(8,128)S(1)}, f32[8,40,128]{2,1,0:T(8,128)S(1)}) custom-call(f32[64,128]{1,0:T(8,128)S(1)} %get-tuple-element.103.surface, f32[8,128]{1,0:T(8,128)S(1)} %collective-permute-done.7.yl, f32[8,128]{1,0:T(8,128)S(1)} %collective-permute-done.8.yr, f32[2,5,56,128]{3,2,1,0:T(8,128)S(1)} %get-tuple-element.116.rh, ...), custom_call_target="tpu_custom_call" | custom-call | flops 1000000 | bytes 3000000 | tf_op jit(solution)/shard_map/pallas_call | solution.py:30
  47.4 11.1 %all_to_all.11.arrived = f32[8,40,128]{2,1,0:T(8,128)S(1)} all-to-all(f32[8,40,128]{2,1,0:T(8,128)S(1)} %get-tuple-element.128), channel_id=1, replica_groups=mesh['blk'=8,'span'=4] {'blk'}, dimensions={0} | all-to-all | bytes 327680 | tf_op jit(solution)/shard_map/all_to_all | solution.py:1143
  58.5 0.0 collective-permute-start.12
  58.5 1.0 %collective-permute-start.11 = (f32[8,128]{1,0:T(8,128)S(1)}, f32[8,128]{1,0:T(8,128)S(1)}, u32[]{:S(2)}, u32[]{:S(2)}) collective-permute-start(f32[8,128]{1,0:T(8,128)S(1)} %shard_map.150), channel_id=1, source_target_pairs={{0,2},{1,3},{2,0},{3,1},{4,6},{5,7},{6,4},{7,5},{8,10},{9,11},{10,... | collective-permute-start | bytes 12296 | tf_op jit(solution)/shard_map/ppermute | solution.py:1148
  59.5 0.9 %collective-permute-start.10 = (f32[8,128]{1,0:T(8,128)S(1)}, f32[8,128]{1,0:T(8,128)S(1)}, u32[]{:S(2)}, u32[]{:S(2)}) collective-permute-start(f32[8,128]{1,0:T(8,128)S(1)} %shard_map.150), channel_id=1, source_target_pairs={{0,1},{1,0},{2,3},{3,2},{4,5},{5,4},{6,7},{7,6},{8,9},{9,8},{10,11... | collective-permute-start | bytes 12296 | tf_op jit(solution)/shard_map/ppermute | solution.py:1148
  60.3 1.0 %shard_map.149 = (f32[5,8,32,128]{3,2,1,0:T(8,128)}, f32[16,32,128]{2,1,0:T(8,128)}) custom-call(f32[8,40,128]{2,1,0:T(8,128)S(1)} %all_to_all.11.arrived, f32[1,32]{1,0:T(1,128)S(1)} %get-tuple-element.83._.idx, f32[1,32,128]{2,1,0:T(8,128)S(1)} %copy-done.1, f32[5,8,32,128]{3,2,1,0:T(8,128)S(1)} %get-tuple-element.129.gas, ...), custom_call_target="tpu_custom_call" | custom-call | flops 2000000 | bytes 6000000 | tf_op jit(solution)/shard_map/pallas_call | solution.py:30
  61.4 0.2 collective-permute-done.12
  61.5 0.7 %collective-permute-done.11 = f32[8,128]{1,0:T(8,128)S(1)} collective-permute-done((f32[8,128]{1,0:T(8,128)S(1)}, f32[8,128]{1,0:T(8,128)S(1)}, u32[]{:S(2)}, u32[]{:S(2)}) %collective-permute-start.11) | collective-permute-done | bytes 4128 | tf_op jit(solution)/shard_map/ppermute | solution.py:1148
  62.2 0.0 collective-permute-done.10
  62.2 0.1 slice_reduce_fusion
  62.3 0.0 copy-done.5
  62.3 0.5 multiply_sqrt_fusion
  (7 shorter events, 0.0 us)
Async XLA Ops:
  0.6 7.5 %copy-start = (f32[5,5]{1,0:T(8,128)S(1)}, f32[5,5]{1,0:T(8,128)}, u32[]{:S(2)}) copy-start(f32[5,5]{1,0:T(8,128)} %jacobian.9) | copy-start | bytes 304
  0.6 7.5 %copy-start.2 = (f32[5]{0:T(128)S(1)}, f32[5]{0:T(128)}, u32[]{:S(2)}) copy-start(f32[5]{0:T(128)} %spread.9) | copy-start | bytes 64
  2.4 4.8 %collective-permute-start = (f32[200,128]{1,0:T(8,128)S(1)}, f32[200,128]{1,0:T(8,128)S(1)}, u32[]{:S(2)}, u32[]{:S(2)}) collective-permute-start(f32[200,128]{1,0:T(8,128)S(1)} %get-tuple-element.71), channel_id=1, source_target_pairs={{0,1},{1,2},{2,3},{3,0},{4,5},{5,6},{6,7},{7,4},{8,9},{9,10},{10,1... | collective-permute-start | bytes 307208 | tf_op jit(solution)/shard_map/ppermute | solution.py:942
  2.9 5.2 %collective-permute-start.1 = (f32[200,128]{1,0:T(8,128)S(1)}, f32[200,128]{1,0:T(8,128)S(1)}, u32[]{:S(2)}, u32[]{:S(2)}) collective-permute-start(f32[200,128]{1,0:T(8,128)S(1)} %get-tuple-element.72), channel_id=1, source_target_pairs={{1,0},{2,1},{3,2},{0,3},{5,4},{6,5},{7,6},{4,7},{9,8},{10,9},{11,1... | collective-permute-start | bytes 307208 | tf_op jit(solution)/shard_map/ppermute | solution.py:945
  4.9 19.0 %collective-permute-start.4 = (f32[512,128]{1,0:T(8,128)S(1)}, f32[512,128]{1,0:T(8,128)S(1)}, u32[]{:S(2)}, u32[]{:S(2)}) collective-permute-start(f32[512,128]{1,0:T(8,128)S(1)} %get-tuple-element.90), channel_id=1, source_target_pairs={{0,4},{4,8},{8,12},{12,16},{16,20},{20,24},{24,28},{28,0},{1,5},{5... | collective-permute-start | bytes 786440 | tf_op jit(solution)/shard_map/ppermute | solution.py:942
  8.1 9.4 %copy-start.3 = (s32[1,32,1]{1,2,0:T(1,128)S(1)}, s32[1,32,1]{1,2,0:T(1,128)}, u32[]{:S(2)}) copy-start(s32[1,32,1]{1,2,0:T(1,128)} %param.21) | copy-start | bytes 388
  8.1 9.4 %copy-start.4 = (s32[1,32]{1,0:T(1,128)S(1)}, s32[1,32]{1,0:T(1,128)}, u32[]{:S(2)}) copy-start(s32[1,32]{1,0:T(1,128)} %target.1) | copy-start | bytes 388
  9.6 14.3 %collective-permute-start.5 = (f32[464,128]{1,0:T(8,128)S(1)}, f32[464,128]{1,0:T(8,128)S(1)}, u32[]{:S(2)}, u32[]{:S(2)}) collective-permute-start(f32[464,128]{1,0:T(8,128)S(1)} %get-tuple-element.91), channel_id=1, source_target_pairs={{0,4},{4,8},{8,12},{12,16},{16,20},{20,24},{24,28},{28,0},{1,5},{5... | collective-permute-start | bytes 712712 | tf_op jit(solution)/shard_map/ppermute | solution.py:942
  11.1 5.1 %collective-permute-start.2 = (f32[376,128]{1,0:T(8,128)S(1)}, f32[376,128]{1,0:T(8,128)S(1)}, u32[]{:S(2)}, u32[]{:S(2)}) collective-permute-start(f32[376,128]{1,0:T(8,128)S(1)} %get-tuple-element.73), channel_id=1, source_target_pairs={{0,1},{1,2},{2,3},{3,0},{4,5},{5,6},{6,7},{7,4},{8,9},{9,10},{10,1... | collective-permute-start | bytes 577544 | tf_op jit(solution)/shard_map/ppermute | solution.py:942
  12.6 4.8 %collective-permute-start.3 = (f32[376,128]{1,0:T(8,128)S(1)}, f32[376,128]{1,0:T(8,128)S(1)}, u32[]{:S(2)}, u32[]{:S(2)}) collective-permute-start(f32[376,128]{1,0:T(8,128)S(1)} %get-tuple-element.74), channel_id=1, source_target_pairs={{1,0},{2,1},{3,2},{0,3},{5,4},{6,5},{7,6},{4,7},{9,8},{10,9},{11,1... | collective-permute-start | bytes 577544 | tf_op jit(solution)/shard_map/ppermute | solution.py:945
  12.9 11.0 %collective-permute-start.6 = (f32[240,128]{1,0:T(8,128)S(1)}, f32[240,128]{1,0:T(8,128)S(1)}, u32[]{:S(2)}, u32[]{:S(2)}) collective-permute-start(f32[240,128]{1,0:T(8,128)S(1)} %get-tuple-element.92), channel_id=1, source_target_pairs={{0,4},{4,8},{8,12},{12,16},{16,20},{20,24},{24,28},{28,0},{1,5},{5... | collective-permute-start | bytes 368648 | tf_op jit(solution)/shard_map/ppermute | solution.py:942
  23.9 3.0 %copy-start.1 = (f32[1,32,128]{2,1,0:T(8,128)S(1)}, f32[1,32,128]{2,1,0:T(8,128)}, u32[]{:S(2)}) copy-start(f32[1,32,128]{2,1,0:T(8,128)} %coef.1) | copy-start | bytes 49156
  25.6 18.0 %collective-permute-start.9 = (f32[920,128]{1,0:T(8,128)S(1)}, f32[920,128]{1,0:T(8,128)S(1)}, u32[]{:S(2)}, u32[]{:S(2)}) collective-permute-start(f32[920,128]{1,0:T(8,128)S(1)} %get-tuple-element.115), channel_id=1, source_target_pairs={{4,0},{8,4},{12,8},{16,12},{20,16},{24,20},{28,24},{5,1},{9,5},{13... | collective-permute-start | bytes 1413128 | tf_op jit(solution)/shard_map/ppermute | solution.py:1049
  43.1 2.9 %collective-permute-start.8 = (f32[8,128]{1,0:T(8,128)S(1)}, f32[8,128]{1,0:T(8,128)S(1)}, u32[]{:S(2)}, u32[]{:S(2)}) collective-permute-start(f32[8,128]{1,0:T(8,128)S(1)} %get-tuple-element.105), channel_id=1, source_target_pairs={{1,0},{2,1},{3,2},{0,3},{5,4},{6,5},{7,6},{4,7},{9,8},{10,9},{11,1... | collective-permute-start | bytes 12296 | tf_op jit(solution)/shard_map/ppermute | solution.py:945
  43.7 3.0 %collective-permute-start.7 = (f32[8,128]{1,0:T(8,128)S(1)}, f32[8,128]{1,0:T(8,128)S(1)}, u32[]{:S(2)}, u32[]{:S(2)}) collective-permute-start(f32[8,128]{1,0:T(8,128)S(1)} %get-tuple-element.104._.refs_10_), channel_id=1, source_target_pairs={{0,1},{1,2},{2,3},{3,0},{4,5},{5,6},{6,7},{7,4},{8,9},{9,10},{10,1... | collective-permute-start | bytes 12296 | tf_op jit(solution)/shard_map/ppermute | solution.py:942
  46.7 15.6 %copy-start.5 = (f32[6]{0:T(128)S(1)}, f32[6]{0:T(128)}, u32[]{:S(2)}) copy-start(f32[6]{0:T(128)} %constant.8) | copy-start | bytes 76
  58.5 3.0 %collective-permute-start.12 = (f32[8,128]{1,0:T(8,128)S(1)}, f32[8,128]{1,0:T(8,128)S(1)}, u32[]{:S(2)}, u32[]{:S(2)}) collective-permute-start(f32[8,128]{1,0:T(8,128)S(1)} %shard_map.150), channel_id=1, source_target_pairs={{0,3},{1,2},{2,1},{3,0},{4,7},{5,6},{6,5},{7,4},{8,11},{9,10},{10,... | collective-permute-start | bytes 12296 | tf_op jit(solution)/shard_map/ppermute | solution.py:1148
  58.5 3.7 %collective-permute-start.11 = (f32[8,128]{1,0:T(8,128)S(1)}, f32[8,128]{1,0:T(8,128)S(1)}, u32[]{:S(2)}, u32[]{:S(2)}) collective-permute-start(f32[8,128]{1,0:T(8,128)S(1)} %shard_map.150), channel_id=1, source_target_pairs={{0,2},{1,3},{2,0},{3,1},{4,6},{5,7},{6,4},{7,5},{8,10},{9,11},{10,... | collective-permute-start | bytes 12296 | tf_op jit(solution)/shard_map/ppermute | solution.py:1148
  59.5 2.7 %collective-permute-start.10 = (f32[8,128]{1,0:T(8,128)S(1)}, f32[8,128]{1,0:T(8,128)S(1)}, u32[]{:S(2)}, u32[]{:S(2)}) collective-permute-start(f32[8,128]{1,0:T(8,128)S(1)} %shard_map.150), channel_id=1, source_target_pairs={{0,1},{1,0},{2,3},{3,2},{4,5},{5,4},{6,7},{7,6},{8,9},{9,8},{10,11... | collective-permute-start | bytes 12296 | tf_op jit(solution)/shard_map/ppermute | solution.py:1148

commit v8 on v7

--- a/solution.py
+++ b/solution.py
@@ -26,7 +26,7 @@
     return [pltpu.VMEM(s, F32) for s in shapes]
 
 
-def call(kernel, outs, scratch, specs, *args, out_specs=None, cost=1.0):
+def call(kernel, outs, scratch, specs, *args, out_specs=None, cost=0.01):
     return pl.pallas_call(
         kernel,
         out_shape=[jax.ShapeDtypeStruct(s, F32) if isinstance(s, tuple) else s for s in outs],
@@ -1162,9 +1162,11 @@
     )
     sq = functools.reduce(jnp.add, others, sq)
     everyone = blocks * spans
-    counts = [float(depth * rows * z * everyone)] * fields + [float(thick * rows * z * everyone)]
+    fluid_cells = float(depth * rows * z * everyone)
+    solid_cells = float(thick * rows * z * everyone)
+    counts = jnp.where(jnp.arange(fields + 1) < fields, fluid_cells, solid_cells)
     totals = jnp.sum(sq[: fields + 1], axis=1)
-    norms = jnp.sqrt(totals / jnp.array(counts, F32))
+    norms = jnp.sqrt(totals / counts)
     return gas, t, norms
 
 

time: 63.1 us -> 63.1 us (level)
  no operation moved by 1% of the time
where the time goes in v8:
time: 63.1 us; the launch traced here: 62.8 us
  blocking collectives  24.4 us (39%)
  Pallas kernels  14.4 us (23%)
  starting transfers between devices  13.3 us (21%)
  waiting for transfers between devices  9.34 us (15%)
  between operations  0.76 us (1%)
  other arithmetic  0.65 us (1%)
    pallas_call x12, Pallas kernels, call(): pl.pallas_call(kernel, out_shape=[jax.ShapeDtypeStruct(s, F32) if isinsta...  14.4 us
    all_to_all x1, blocking collectives, shards(): arrived = lax.all_to_all(parts.reshape(blocks, CHUNK, z), 'blk', 0, 0)  13.3 us
    all_to_all x1, blocking collectives, shards(): arrived = lax.all_to_all(out, 'blk', 0, 0)  11.1 us
    ppermute x6, starting transfers between devices, ahead(): return lax.ppermute(x, axis, forward[axis])  7.34 us
    ppermute x6, waiting for transfers between devices, ahead(): return lax.ppermute(x, axis, forward[axis])  6.29 us
    ppermute x3, starting transfers between devices, behind(): return lax.ppermute(x, axis, backward[axis])  2.81 us
    ppermute x3, waiting for transfers between devices, behind(): return lax.ppermute(x, axis, backward[axis])  2.23 us
    ppermute x3, starting transfers between devices, shards(): lax.ppermute(sq, 'span', [(i, i ^ step) for i in range(spans)])  1.86 us
  transfers between devices with their start and end apart: 13, of which 8 were waited for; matrix products, arithmetic and copies ran while one was open for 0% of the time, Pallas kernels for 16%

profile of v8, /device:TPU:0, one launch (start us, length us, event | category | flops | bytes accessed | tf_op | source)
XLA Modules:
  0.0 62.8 jit_solution(8546335173155124573)
XLA Ops:
  0.6 0.0 copy-start
  0.6 0.0 copy-start.2
  0.7 1.7 %shard_map.130 = (f32[5,8,32,128]{3,2,1,0:T(8,128)S(1)}, f32[5,8,32,128]{3,2,1,0:T(8,128)S(1)}, f32[3,8,32,128]{3,2,1,0:T(8,128)S(1)}, f32[16,32,128]{2,1,0:T(8,...) custom-call(f32[5,8,32,128]{3,2,1,0:T(8,128)} %refs_0_.1, ...), custom_call_target="tpu_custom_call" | custom-call | flops 10000 | bytes 30000 | tf_op jit(solution)/shard_map/pallas_call | solution.py:30
  2.4 0.5 collective-permute-start
  2.9 2.0 %collective-permute-start.1 = (f32[200,128]{1,0:T(8,128)S(1)}, f32[200,128]{1,0:T(8,128)S(1)}, u32[]{:S(2)}, u32[]{:S(2)}) collective-permute-start(f32[200,128]{1,0:T(8,128)S(1)} %get-tuple-element.72), channel_id=1, source_target_pairs={{1,0},{2,1},{3,2},{0,3},{5,4},{6,5},{7,6},{4,7},{9,8},{10,9},{11,1... | collective-permute-start | bytes 307208 | tf_op jit(solution)/shard_map/ppermute | solution.py:945
  4.9 2.2 %collective-permute-start.4 = (f32[512,128]{1,0:T(8,128)S(1)}, f32[512,128]{1,0:T(8,128)S(1)}, u32[]{:S(2)}, u32[]{:S(2)}) collective-permute-start(f32[512,128]{1,0:T(8,128)S(1)} %get-tuple-element.90), channel_id=1, source_target_pairs={{0,4},{4,8},{8,12},{12,16},{16,20},{20,24},{24,28},{28,0},{1,5},{5... | collective-permute-start | bytes 786440 | tf_op jit(solution)/shard_map/ppermute | solution.py:942
  7.1 0.1 collective-permute-done.yl.refs_6_
  7.2 0.9 %collective-permute-done.1.yr.refs_7_ = f32[200,128]{1,0:T(8,128)S(1)} collective-permute-done((f32[200,128]{1,0:T(8,128)S(1)}, f32[200,128]{1,0:T(8,128)S(1)}, u32[]{:S(2)}, u32[]{:S(2)}) %collective-permute-start.1) | collective-permute-done | bytes 102432 | tf_op jit(solution)/shard_map/ppermute | solution.py:945
  8.1 0.0 copy-done
  8.1 0.0 copy-done.2
  8.1 1.4 %shard_map.133 = (f32[464,128]{1,0:T(8,128)S(1)}, f32[240,128]{1,0:T(8,128)S(1)}) custom-call(f32[5]{0:T(128)S(1)} %copy-done.2, f32[5,5]{1,0:T(8,128)S(1)} %copy-done, f32[5,8,32,128]{3,2,1,0:T(8,128)S(1)} %get-tuple-element.68.p.refs_0_, f32[5,8,32,128]{3,2,1,0:T(8,128)S(1)} %get-tuple-element.69.src.refs_1_, ...), custom_call_target="tpu_custom_call" | custom-call | flops 30000000 | bytes 90000000 | tf_op jit(solution)/shard_map/pallas_call | solution.py:30
  9.6 1.5 %collective-permute-start.5 = (f32[464,128]{1,0:T(8,128)S(1)}, f32[464,128]{1,0:T(8,128)S(1)}, u32[]{:S(2)}, u32[]{:S(2)}) collective-permute-start(f32[464,128]{1,0:T(8,128)S(1)} %get-tuple-element.91), channel_id=1, source_target_pairs={{0,4},{4,8},{8,12},{12,16},{16,20},{20,24},{24,28},{28,0},{1,5},{5... | collective-permute-start | bytes 712712 | tf_op jit(solution)/shard_map/ppermute | solution.py:942
  11.1 1.5 %collective-permute-start.2 = (f32[376,128]{1,0:T(8,128)S(1)}, f32[376,128]{1,0:T(8,128)S(1)}, u32[]{:S(2)}, u32[]{:S(2)}) collective-permute-start(f32[376,128]{1,0:T(8,128)S(1)} %get-tuple-element.73), channel_id=1, source_target_pairs={{0,1},{1,2},{2,3},{3,0},{4,5},{5,6},{6,7},{7,4},{8,9},{9,10},{10,1... | collective-permute-start | bytes 577544 | tf_op jit(solution)/shard_map/ppermute | solution.py:942
  12.6 0.2 collective-permute-start.3
  12.9 1.5 %collective-permute-start.6 = (f32[240,128]{1,0:T(8,128)S(1)}, f32[240,128]{1,0:T(8,128)S(1)}, u32[]{:S(2)}, u32[]{:S(2)}) collective-permute-start(f32[240,128]{1,0:T(8,128)S(1)} %get-tuple-element.92), channel_id=1, source_target_pairs={{0,4},{4,8},{8,12},{12,16},{16,20},{20,24},{24,28},{28,0},{1,5},{5... | collective-permute-start | bytes 368648 | tf_op jit(solution)/shard_map/ppermute | solution.py:942
  14.4 1.7 %collective-permute-done.2.zl.yl = f32[376,128]{1,0:T(8,128)S(1)} collective-permute-done((f32[376,128]{1,0:T(8,128)S(1)}, f32[376,128]{1,0:T(8,128)S(1)}, u32[]{:S(2)}, u32[]{:S(2)}) %collective-permute-start.2) | collective-permute-done | bytes 192544 | tf_op jit(solution)/shard_map/ppermute | solution.py:942
  16.2 1.3 %collective-permute-done.3.zr.yr = f32[376,128]{1,0:T(8,128)S(1)} collective-permute-done((f32[376,128]{1,0:T(8,128)S(1)}, f32[376,128]{1,0:T(8,128)S(1)}, u32[]{:S(2)}, u32[]{:S(2)}) %collective-permute-start.3) | collective-permute-done | bytes 192544 | tf_op jit(solution)/shard_map/ppermute | solution.py:945
  17.5 0.0 copy-done.3
  17.5 0.0 copy-done.4
  17.5 1.3 %shard_map.131 = (f32[5,8,56,128]{3,2,1,0:T(8,128)S(1)}, f32[5,8,56,128]{3,2,1,0:T(8,128)S(1)}, f32[3,8,56,128]{3,2,1,0:T(8,128)S(1)}, f32[5,8,56,128]{3,2,1,0:T...) custom-call(f32[5]{0:T(128)S(1)} %copy-done.2, ...), custom_call_target="tpu_custom_call" | custom-call | flops 10000 | bytes 30000 | tf_op jit(solution)/shard_map/pallas_call | solution.py:30
  18.8 1.4 %shard_map.132 = (f32[16,56,128]{2,1,0:T(8,128)S(1)}, f32[16,56,128]{2,1,0:T(8,128)S(1)}, f32[16,56,128]{2,1,0:T(8,128)S(1)}, f32[3,4,56,128]{3,2,1,0:T(8,128)S(...) custom-call(f32[16,32,128]{2,1,0:T(8,128)S(1)} %get-tuple-element.80, ...), custom_call_target="tpu_custom_call" | custom-call | flops 10000 | bytes 30000 | tf_op jit(solution)/shard_map/pallas_call | solution.py:30
  20.1 3.8 %collective-permute-done.6.refs_13_ = f32[240,128]{1,0:T(8,128)S(1)} collective-permute-done((f32[240,128]{1,0:T(8,128)S(1)}, f32[240,128]{1,0:T(8,128)S(1)}, u32[]{:S(2)}, u32[]{:S(2)}) %collective-permute-start.6) | collective-permute-done | bytes 122912 | tf_op jit(solution)/shard_map/ppermute | solution.py:942
  23.9 0.0 collective-permute-done.4.refs_11_.refs_12_
  23.9 0.0 collective-permute-done.5.refs_12_
  23.9 1.7 %shard_map.134 = (f32[920,128]{1,0:T(8,128)S(1)}, f32[5,56,128]{2,1,0:T(8,128)S(1)}, f32[5,56,128]{2,1,0:T(8,128)S(1)}, f32[5,56,128]{2,1,0:T(8,128)S(1)}, f32[5...) custom-call(f32[5]{0:T(128)S(1)} %copy-done.2, ...), custom_call_target="tpu_custom_call" | custom-call | flops 2000000 | bytes 6000000 | tf_op jit(solution)/shard_map/pallas_call | solution.py:30
  25.6 1.3 %collective-permute-start.9 = (f32[920,128]{1,0:T(8,128)S(1)}, f32[920,128]{1,0:T(8,128)S(1)}, u32[]{:S(2)}, u32[]{:S(2)}) collective-permute-start(f32[920,128]{1,0:T(8,128)S(1)} %get-tuple-element.115), channel_id=1, source_target_pairs={{4,0},{8,4},{12,8},{16,12},{20,16},{24,20},{28,24},{5,1},{9,5},{13... | collective-permute-start | bytes 1413128 | tf_op jit(solution)/shard_map/ppermute | solution.py:1049
  26.9 0.0 copy-done.1
  26.9 2.6 %shard_map.135 = (f32[256,128]{1,0:T(8,128)S(1)}, f32[5,4,32,128]{3,2,1,0:T(8,128)S(1)}, f32[8,128]{1,0:T(8,128)S(1)}, f32[5,4,56,128]{3,2,1,0:T(8,128)S(1)}, f3...) custom-call(f32[5]{0:T(128)S(1)} %copy-done.2, f32[5,5]{1,0:T(8,128)S(1)} %copy-done, ...), custom_call_target="tpu_custom_call" | custom-call | flops 10000 | bytes 30000 | tf_op jit(solution)/shard_map/pallas_call | solution.py:30
  29.5 13.3 %all_to_all.10.arrived = f32[8,32,128]{2,1,0:T(8,128)S(1)} all-to-all(f32[8,32,128]{2,1,0:T(8,128)S(1)} %bitcast.2), channel_id=1, replica_groups=mesh['blk'=8,'span'=4] {'blk'}, dimensions={0} | all-to-all | bytes 262144 | tf_op jit(solution)/shard_map/all_to_all | solution.py:1077
  42.9 0.2 shard_map.136
  43.1 0.5 collective-permute-start.8
  43.7 0.0 collective-permute-start.7
  43.7 0.0 collective-permute-done.9.xb.refs_9_
  43.7 1.7 %shard_map.138 = (f32[5,8,32,128]{3,2,1,0:T(8,128)S(1)}, f32[8,128]{1,0:T(8,128)S(1)}) custom-call(f32[5]{0:T(128)S(1)} %copy-done.2, f32[5,5]{1,0:T(8,128)S(1)} %copy-done, f32[5,8,56,128]{3,2,1,0:T(8,128)S(1)} %get-tuple-element.75.refs_0_, f32[5,8,56,128]{3,2,1,0:T(8,128)S(1)} %get-tuple-element.76.refs_1_, ...), custom_call_target="tpu_custom_call" | custom-call | flops 3000000 | bytes 9000000 | tf_op jit(solution)/shard_map/pallas_call | solution.py:30
  45.4 0.5 shard_map.137
  46.0 0.0 collective-permute-done.8.yr
  46.0 0.7 %collective-permute-done.7.yl = f32[8,128]{1,0:T(8,128)S(1)} collective-permute-done((f32[8,128]{1,0:T(8,128)S(1)}, f32[8,128]{1,0:T(8,128)S(1)}, u32[]{:S(2)}, u32[]{:S(2)}) %collective-permute-start.7) | collective-permute-done | bytes 4128 | tf_op jit(solution)/shard_map/ppermute | solution.py:942
  46.7 0.7 %shard_map.139 = (f32[16,32,128]{2,1,0:T(8,128)S(1)}, f32[8,40,128]{2,1,0:T(8,128)S(1)}) custom-call(f32[64,128]{1,0:T(8,128)S(1)} %get-tuple-element.103.surface, f32[8,128]{1,0:T(8,128)S(1)} %collective-permute-done.7.yl, f32[8,128]{1,0:T(8,128)S(1)} %collective-permute-done.8.yr, f32[2,5,56,128]{3,2,1,0:T(8,128)S(1)} %get-tuple-element.116.rh, ...), custom_call_target="tpu_custom_call" | custom-call | flops 10000 | bytes 30000 | tf_op jit(solution)/shard_map/pallas_call | solution.py:30
  47.4 11.1 %all_to_all.11.arrived = f32[8,40,128]{2,1,0:T(8,128)S(1)} all-to-all(f32[8,40,128]{2,1,0:T(8,128)S(1)} %get-tuple-element.128), channel_id=1, replica_groups=mesh['blk'=8,'span'=4] {'blk'}, dimensions={0} | all-to-all | bytes 327680 | tf_op jit(solution)/shard_map/all_to_all | solution.py:1143
  58.5 0.0 collective-permute-start.12
  58.5 1.0 %collective-permute-start.11 = (f32[8,128]{1,0:T(8,128)S(1)}, f32[8,128]{1,0:T(8,128)S(1)}, u32[]{:S(2)}, u32[]{:S(2)}) collective-permute-start(f32[8,128]{1,0:T(8,128)S(1)} %shard_map.141), channel_id=1, source_target_pairs={{0,2},{1,3},{2,0},{3,1},{4,6},{5,7},{6,4},{7,5},{8,10},{9,11},{10,... | collective-permute-start | bytes 12296 | tf_op jit(solution)/shard_map/ppermute | solution.py:1148
  59.4 0.9 %collective-permute-start.10 = (f32[8,128]{1,0:T(8,128)S(1)}, f32[8,128]{1,0:T(8,128)S(1)}, u32[]{:S(2)}, u32[]{:S(2)}) collective-permute-start(f32[8,128]{1,0:T(8,128)S(1)} %shard_map.141), channel_id=1, source_target_pairs={{0,1},{1,0},{2,3},{3,2},{4,5},{5,4},{6,7},{7,6},{8,9},{9,8},{10,11... | collective-permute-start | bytes 12296 | tf_op jit(solution)/shard_map/ppermute | solution.py:1148
  60.3 1.0 %shard_map.140 = (f32[5,8,32,128]{3,2,1,0:T(8,128)}, f32[16,32,128]{2,1,0:T(8,128)}) custom-call(f32[8,40,128]{2,1,0:T(8,128)S(1)} %all_to_all.11.arrived, f32[1,32]{1,0:T(1,128)S(1)} %get-tuple-element.83._.idx, f32[1,32,128]{2,1,0:T(8,128)S(1)} %copy-done.1, f32[5,8,32,128]{3,2,1,0:T(8,128)S(1)} %get-tuple-element.129.gas, ...), custom_call_target="tpu_custom_call" | custom-call | flops 2000000 | bytes 6000000 | tf_op jit(solution)/shard_map/pallas_call | solution.py:30
  61.3 0.2 collective-permute-done.12
  61.5 0.7 %collective-permute-done.11 = f32[8,128]{1,0:T(8,128)S(1)} collective-permute-done((f32[8,128]{1,0:T(8,128)S(1)}, f32[8,128]{1,0:T(8,128)S(1)}, u32[]{:S(2)}, u32[]{:S(2)}) %collective-permute-start.11) | collective-permute-done | bytes 4128 | tf_op jit(solution)/shard_map/ppermute | solution.py:1148
  62.2 0.0 collective-permute-done.10
  62.2 0.1 slice_reduce_fusion
  62.3 0.5 fusion.1
  (5 shorter events, 0.0 us)
Async XLA Ops:
  0.6 7.5 %copy-start = (f32[5,5]{1,0:T(8,128)S(1)}, f32[5,5]{1,0:T(8,128)}, u32[]{:S(2)}) copy-start(f32[5,5]{1,0:T(8,128)} %jacobian.9) | copy-start | bytes 304
  0.6 7.5 %copy-start.2 = (f32[5]{0:T(128)S(1)}, f32[5]{0:T(128)}, u32[]{:S(2)}) copy-start(f32[5]{0:T(128)} %spread.9) | copy-start | bytes 64
  2.4 4.8 %collective-permute-start = (f32[200,128]{1,0:T(8,128)S(1)}, f32[200,128]{1,0:T(8,128)S(1)}, u32[]{:S(2)}, u32[]{:S(2)}) collective-permute-start(f32[200,128]{1,0:T(8,128)S(1)} %get-tuple-element.71), channel_id=1, source_target_pairs={{0,1},{1,2},{2,3},{3,0},{4,5},{5,6},{6,7},{7,4},{8,9},{9,10},{10,1... | collective-permute-start | bytes 307208 | tf_op jit(solution)/shard_map/ppermute | solution.py:942
  2.9 5.2 %collective-permute-start.1 = (f32[200,128]{1,0:T(8,128)S(1)}, f32[200,128]{1,0:T(8,128)S(1)}, u32[]{:S(2)}, u32[]{:S(2)}) collective-permute-start(f32[200,128]{1,0:T(8,128)S(1)} %get-tuple-element.72), channel_id=1, source_target_pairs={{1,0},{2,1},{3,2},{0,3},{5,4},{6,5},{7,6},{4,7},{9,8},{10,9},{11,1... | collective-permute-start | bytes 307208 | tf_op jit(solution)/shard_map/ppermute | solution.py:945
  4.9 19.0 %collective-permute-start.4 = (f32[512,128]{1,0:T(8,128)S(1)}, f32[512,128]{1,0:T(8,128)S(1)}, u32[]{:S(2)}, u32[]{:S(2)}) collective-permute-start(f32[512,128]{1,0:T(8,128)S(1)} %get-tuple-element.90), channel_id=1, source_target_pairs={{0,4},{4,8},{8,12},{12,16},{16,20},{20,24},{24,28},{28,0},{1,5},{5... | collective-permute-start | bytes 786440 | tf_op jit(solution)/shard_map/ppermute | solution.py:942
  8.1 9.4 %copy-start.3 = (s32[1,32,1]{1,2,0:T(1,128)S(1)}, s32[1,32,1]{1,2,0:T(1,128)}, u32[]{:S(2)}) copy-start(s32[1,32,1]{1,2,0:T(1,128)} %param.20) | copy-start | bytes 388
  8.1 9.4 %copy-start.4 = (s32[1,32]{1,0:T(1,128)S(1)}, s32[1,32]{1,0:T(1,128)}, u32[]{:S(2)}) copy-start(s32[1,32]{1,0:T(1,128)} %target.1) | copy-start | bytes 388
  9.6 14.3 %collective-permute-start.5 = (f32[464,128]{1,0:T(8,128)S(1)}, f32[464,128]{1,0:T(8,128)S(1)}, u32[]{:S(2)}, u32[]{:S(2)}) collective-permute-start(f32[464,128]{1,0:T(8,128)S(1)} %get-tuple-element.91), channel_id=1, source_target_pairs={{0,4},{4,8},{8,12},{12,16},{16,20},{20,24},{24,28},{28,0},{1,5},{5... | collective-permute-start | bytes 712712 | tf_op jit(solution)/shard_map/ppermute | solution.py:942
  11.1 5.1 %collective-permute-start.2 = (f32[376,128]{1,0:T(8,128)S(1)}, f32[376,128]{1,0:T(8,128)S(1)}, u32[]{:S(2)}, u32[]{:S(2)}) collective-permute-start(f32[376,128]{1,0:T(8,128)S(1)} %get-tuple-element.73), channel_id=1, source_target_pairs={{0,1},{1,2},{2,3},{3,0},{4,5},{5,6},{6,7},{7,4},{8,9},{9,10},{10,1... | collective-permute-start | bytes 577544 | tf_op jit(solution)/shard_map/ppermute | solution.py:942
  12.6 4.8 %collective-permute-start.3 = (f32[376,128]{1,0:T(8,128)S(1)}, f32[376,128]{1,0:T(8,128)S(1)}, u32[]{:S(2)}, u32[]{:S(2)}) collective-permute-start(f32[376,128]{1,0:T(8,128)S(1)} %get-tuple-element.74), channel_id=1, source_target_pairs={{1,0},{2,1},{3,2},{0,3},{5,4},{6,5},{7,6},{4,7},{9,8},{10,9},{11,1... | collective-permute-start | bytes 577544 | tf_op jit(solution)/shard_map/ppermute | solution.py:945
  12.9 11.0 %collective-permute-start.6 = (f32[240,128]{1,0:T(8,128)S(1)}, f32[240,128]{1,0:T(8,128)S(1)}, u32[]{:S(2)}, u32[]{:S(2)}) collective-permute-start(f32[240,128]{1,0:T(8,128)S(1)} %get-tuple-element.92), channel_id=1, source_target_pairs={{0,4},{4,8},{8,12},{12,16},{16,20},{20,24},{24,28},{28,0},{1,5},{5... | collective-permute-start | bytes 368648 | tf_op jit(solution)/shard_map/ppermute | solution.py:942
  23.9 3.0 %copy-start.1 = (f32[1,32,128]{2,1,0:T(8,128)S(1)}, f32[1,32,128]{2,1,0:T(8,128)}, u32[]{:S(2)}) copy-start(f32[1,32,128]{2,1,0:T(8,128)} %coef.1) | copy-start | bytes 49156
  25.6 18.0 %collective-permute-start.9 = (f32[920,128]{1,0:T(8,128)S(1)}, f32[920,128]{1,0:T(8,128)S(1)}, u32[]{:S(2)}, u32[]{:S(2)}) collective-permute-start(f32[920,128]{1,0:T(8,128)S(1)} %get-tuple-element.115), channel_id=1, source_target_pairs={{4,0},{8,4},{12,8},{16,12},{20,16},{24,20},{28,24},{5,1},{9,5},{13... | collective-permute-start | bytes 1413128 | tf_op jit(solution)/shard_map/ppermute | solution.py:1049
  43.1 2.9 %collective-permute-start.8 = (f32[8,128]{1,0:T(8,128)S(1)}, f32[8,128]{1,0:T(8,128)S(1)}, u32[]{:S(2)}, u32[]{:S(2)}) collective-permute-start(f32[8,128]{1,0:T(8,128)S(1)} %get-tuple-element.105), channel_id=1, source_target_pairs={{1,0},{2,1},{3,2},{0,3},{5,4},{6,5},{7,6},{4,7},{9,8},{10,9},{11,1... | collective-permute-start | bytes 12296 | tf_op jit(solution)/shard_map/ppermute | solution.py:945
  43.7 3.0 %collective-permute-start.7 = (f32[8,128]{1,0:T(8,128)S(1)}, f32[8,128]{1,0:T(8,128)S(1)}, u32[]{:S(2)}, u32[]{:S(2)}) collective-permute-start(f32[8,128]{1,0:T(8,128)S(1)} %get-tuple-element.104._.refs_10_), channel_id=1, source_target_pairs={{0,1},{1,2},{2,3},{3,0},{4,5},{5,6},{6,7},{7,4},{8,9},{9,10},{10,1... | collective-permute-start | bytes 12296 | tf_op jit(solution)/shard_map/ppermute | solution.py:942
  58.5 3.0 %collective-permute-start.12 = (f32[8,128]{1,0:T(8,128)S(1)}, f32[8,128]{1,0:T(8,128)S(1)}, u32[]{:S(2)}, u32[]{:S(2)}) collective-permute-start(f32[8,128]{1,0:T(8,128)S(1)} %shard_map.141), channel_id=1, source_target_pairs={{0,3},{1,2},{2,1},{3,0},{4,7},{5,6},{6,5},{7,4},{8,11},{9,10},{10,... | collective-permute-start | bytes 12296 | tf_op jit(solution)/shard_map/ppermute | solution.py:1148
  58.5 3.7 %collective-permute-start.11 = (f32[8,128]{1,0:T(8,128)S(1)}, f32[8,128]{1,0:T(8,128)S(1)}, u32[]{:S(2)}, u32[]{:S(2)}) collective-permute-start(f32[8,128]{1,0:T(8,128)S(1)} %shard_map.141), channel_id=1, source_target_pairs={{0,2},{1,3},{2,0},{3,1},{4,6},{5,7},{6,4},{7,5},{8,10},{9,11},{10,... | collective-permute-start | bytes 12296 | tf_op jit(solution)/shard_map/ppermute | solution.py:1148
  59.4 2.7 %collective-permute-start.10 = (f32[8,128]{1,0:T(8,128)S(1)}, f32[8,128]{1,0:T(8,128)S(1)}, u32[]{:S(2)}, u32[]{:S(2)}) collective-permute-start(f32[8,128]{1,0:T(8,128)S(1)} %shard_map.141), channel_id=1, source_target_pairs={{0,1},{1,0},{2,3},{3,2},{4,5},{5,4},{6,7},{7,6},{8,9},{9,8},{10,11... | collective-permute-start | bytes 12296 | tf_op jit(solution)/shard_map/ppermute | solution.py:1148
